TPU v7x, 32 devices: a whole 2x2x4 slice. The times are simulated.
32 devices in a mesh: seq: 8 (over z, y), head: 2 (over x), sample: 2 (over core).
Axes of the slice: x: 2, y: 2, z: 4, core: 2. Of those that a mesh axis runs over, the one named last changes fastest.
Arguments:
- features: bfloat16 [2, 2048, 1536], P('sample', 'seq'), may hold values from -6 to 6
- dilated_weight: bfloat16 [1536, 3, 768], P(None, None, 'head'), may hold values from -0.09375 to 0.09375
- point_weight: bfloat16 [1536, 768], P(None, 'head'), may hold values from -0.21875 to 0.21875
- track_weight: bfloat16 [1536, 3840], P('sample', 'head'), may hold values from -0.15625 to 0.15625
- track_cotangent: bfloat16 [2, 2048, 3840], P('sample', 'seq', 'head'), may hold values from -6 to 6
Outputs:
- input_grad: bfloat16 [2, 2048, 1536], P('sample', 'seq')
- dilated_grad: float32 [1536, 3, 768], P(('seq', 'sample'), None, 'head')
- point_grad: float32 [1536, 768], P(('seq', 'sample'), 'head')
All inputs are finite; a program needn't handle non-finite values.
Results may differ from a plain program's by a relative error of at most 0.015.
Values may be sent and summed in bfloat16 or wider, within the bound.
No kernel may reach another device: no remote copies, remote signals or barrier semaphores. Data moves between devices by JAX's collectives and lax.ppermute only.
A program may use at most 128 MiB of HBM per device.

v0:
```python
import jax
import jax.numpy as jnp
from jax import lax
from jax.sharding import PartitionSpec as P

DIST = 4


def passed_along(value, axis, steps):
    count = lax.axis_size(axis)
    leading, last = (max(0, -steps), min(count, count - steps))
    return lax.ppermute(value, axis, [(source, source + steps) for source in range(leading, last)])


def gelu_value(value):
    inner = 0.7978845608 * (value + 0.044715 * value * value * value)
    return 0.5 * value * (1.0 + jnp.tanh(inner))


def gelu_slope(value):
    inner = 0.7978845608 * (value + 0.044715 * value * value * value)
    tangent = jnp.tanh(inner)
    return 0.5 * (1.0 + tangent) + 0.5 * value * (1.0 - tangent * tangent) * 0.7978845608 * (
        1.0 + 3.0 * 0.044715 * value * value
    )


def times_transposed(left, right):
    return lax.dot_general(
        left, right, (((1,), (1,)), ((), ())), preferred_element_type=jnp.float32
    )


def transposed_times(left, right):
    return lax.dot_general(
        left, right, (((0,), (0,)), ((), ())), preferred_element_type=jnp.float32
    )


def shift_terms(field, amount):
    return passed_along(field.astype(jnp.bfloat16), "seq", amount).astype(field.dtype)


def shift_grads(field, amount):
    return passed_along(field, "seq", amount)


def pair_sum(term):
    return lax.psum(term.astype(jnp.bfloat16), "head").astype(jnp.float32)


def body(features, dilated_weight, point_weight, track_weight, track_cotangent):
    samples, positions, channels = features.shape
    number_rows = samples * positions
    group_width = dilated_weight.shape[2]
    feat_wide = features.reshape(number_rows, channels).astype(jnp.float32)
    activated_hidden = gelu_value(feat_wide).astype(jnp.bfloat16)
    flat_weight = dilated_weight.reshape(channels, 3 * group_width)
    tap_terms = jnp.dot(activated_hidden, flat_weight, preferred_element_type=jnp.float32)
    middle = (
        shift_terms(tap_terms[:, :group_width], DIST) + tap_terms[:, group_width : 2 * group_width]
    )
    middle = middle + shift_terms(tap_terms[:, 2 * group_width :], -DIST)
    hidden = gelu_value(middle).astype(jnp.bfloat16)
    block_out = (feat_wide + pair_sum(times_transposed(hidden, point_weight))).astype(jnp.bfloat16)
    whole_track = lax.all_gather(track_weight, "sample", axis=0, tiled=True)
    scores = jnp.dot(block_out, whole_track, preferred_element_type=jnp.float32)
    cotangent = track_cotangent.reshape(number_rows, whole_track.shape[1])
    score_grad = (cotangent.astype(jnp.float32) * jax.nn.sigmoid(scores)).astype(jnp.bfloat16)
    out_grad = pair_sum(times_transposed(score_grad, whole_track))
    out_grad_b = out_grad.astype(jnp.bfloat16)
    hidden_grad = jnp.dot(out_grad_b, point_weight, preferred_element_type=jnp.float32)
    middle_gradient = (hidden_grad * gelu_slope(middle)).astype(jnp.bfloat16)
    later = shift_grads(middle_gradient, -DIST)
    earlier = shift_grads(middle_gradient, DIST)
    kernel_taps = jnp.concatenate([later, middle_gradient, earlier], axis=1)
    act_grad = pair_sum(times_transposed(kernel_taps, flat_weight))
    input_grad = (out_grad + act_grad * gelu_slope(feat_wide)).astype(jnp.bfloat16)
    summed = lax.psum_scatter(
        jnp.concatenate(
            [transposed_times(activated_hidden, kernel_taps), transposed_times(out_grad_b, hidden)],
            axis=1,
        ),
        ("seq", "sample"),
        scatter_dimension=0,
        tiled=True,
    )
    dilated_grad = summed[:, : 3 * group_width].reshape(summed.shape[0], 3, group_width)
    point_grad = summed[:, 3 * group_width :]
    return (input_grad.reshape(samples, positions, channels), dilated_grad, point_grad)


def solution(mesh):
    placed = (
        P("sample", "seq", None),
        P(None, None, "head"),
        P(None, "head"),
        P("sample", "head"),
        P("sample", "seq", "head"),
    )
    return jax.shard_map(
        body,
        mesh=mesh,
        in_specs=placed,
        out_specs=(
            P("sample", "seq", None),
            P(("seq", "sample"), None, "head"),
            P(("seq", "sample"), "head"),
        ),
        check_vma=False,
    )
```

profile of v0, /device:TPU:0, one launch (start us, length us, event | category | flops | bytes accessed | tf_op | source)
XLA Modules:
  0.0 297.2 jit_solution(14314375926241629251)
XLA Ops:
  8.1 6.3 %copy.13 = bf16[1536,3,384]{0,2,1:T(8,128)(2,1)} copy(bf16[1536,3,384]{2,0,1:T(8,128)(2,1)} %param.6) | data formatting | bytes 7077888 | tf_op args[1]
  14.4 3.5 %fusion.66 = (bf16[256,1152]{1,0:T(8,128)(2,1)S(1)}, f32[256,1152]{1,0:T(8,128)S(1)}) fusion(bf16[1536,1152]{0,1:T(8,128)(2,1)} %bitcast.88, bf16[1,256,1536]{2,1,0:T(8,128)(2,1)S(1)} %copy-done.2), kind=kOutput, calls=%fused_computation.79 | convolution fusion | flops 910196736 | bytes 6094848 | tf_op jit(solution)/shard_map/dot_general | solution.py:59
  17.9 6.0 %collective-permute-start = (bf16[256,384]{1,0:T(8,128)(2,1)S(1)}, bf16[256,384]{1,0:T(8,128)(2,1)S(1)}, u32[]{:S(2)}, u32[]{:S(2)}) collective-permute-start(bf16[256,384]{1,0:T(8,128)(2,1)S(1)} %get-tuple-element.12), channel_id=1, source_target_pairs={{0,16},{4,20},{8,24},{12,28},{1,17},{5,21},{9,25},{13,29},{2,18},{... | collective-permute-start | bytes 589832 | tf_op jit(solution)/shard_map/ppermute | solution.py:12
  23.9 1.3 collective-permute-start.1
  25.2 2.9 collective-permute-done
  28.1 9.2 %collective-permute-done.1 = bf16[256,384]{1,0:T(8,128)(2,1)S(1)} collective-permute-done((bf16[256,384]{1,0:T(8,128)(2,1)S(1)}, bf16[256,384]{1,0:T(8,128)(2,1)S(1)}, u32[]{:S(2)}, u32[]{:S(2)}) %collective-permute-start.1) | collective-permute-done | bytes 196640 | tf_op jit(solution)/shard_map/ppermute | solution.py:12
  37.3 0.2 multiply_convert_fusion
  37.5 0.7 copy-done.6
  38.1 1.5 convolution_convert_fusion.1
  39.7 0.5 all-gather.2.cloned.1.call-update
  40.3 32.1 %all-reduce.4.cloned.1.call-done = bf16[256,1536]{1,0:T(8,128)(2,1)} async-done(((bf16[256,1536]{1,0:T(8,128)(2,1)}), bf16[256,1536]{1,0:T(8,128)(2,1)}) %all-reduce.4.cloned.1.call-update) | async-done | bytes 786448 | tf_op jit(solution)/shard_map/psum | solution.py:49
  72.3 9.2 %convolution_convert_fusion = bf16[256,1536]{1,0:T(8,128)(2,1)} fusion(bf16[1536,1920]{1,0:T(8,128)(2,1)} %all-gather.2.cloned.1.call-done, bf16[1,256,1920]{2,1,0:T(8,128)(2,1)} %param.9, bf16[1,256,1536]{2,1,0:T(8,128)(2,1)S(1)} %copy-done.2, bf16[256,1536]{1,0:T(8,128)(2,1)} %all-reduce.4.cloned.1.call-done), kind=kOutput, calls=%fused_computation.21 | convolution fusion | flops 3024814080 | bytes 9240576 | tf_op jit(solution)/shard_map/dot_general | solution.py:29
  81.6 34.4 %all-reduce.6.cloned.1.call-done = bf16[256,1536]{1,0:T(8,128)(2,1)} async-done(((bf16[256,1536]{1,0:T(8,128)(2,1)}), bf16[256,1536]{1,0:T(8,128)(2,1)}) %all-reduce.6.cloned.1.call-update) | async-done | bytes 786448 | tf_op jit(solution)/shard_map/psum | solution.py:49
  116.1 2.0 fusion.31
  118.1 4.3 %collective-permute-start.3 = (bf16[256,384]{1,0:T(8,128)(2,1)S(1)}, bf16[256,384]{1,0:T(8,128)(2,1)S(1)}, u32[]{:S(2)}, u32[]{:S(2)}) collective-permute-start(bf16[256,384]{1,0:T(8,128)(2,1)S(1)} %fusion.31), channel_id=1, source_target_pairs={{0,16},{4,20},{8,24},{12,28},{1,17},{5,21},{9,25},{13,29},{2,18},{... | collective-permute-start | bytes 589832 | tf_op jit(solution)/shard_map/ppermute | solution.py:12
  122.4 1.3 collective-permute-start.2
  123.8 1.4 fusion.67
  125.2 1.4 collective-permute-done.3
  126.6 9.2 %collective-permute-done.2 = bf16[256,384]{1,0:T(8,128)(2,1)S(1)} collective-permute-done((bf16[256,384]{1,0:T(8,128)(2,1)S(1)}, bf16[256,384]{1,0:T(8,128)(2,1)S(1)}, u32[]{:S(2)}, u32[]{:S(2)}) %collective-permute-start.2) | collective-permute-done | bytes 196640 | tf_op jit(solution)/shard_map/ppermute | solution.py:12
  135.8 0.7 copy-done.9
  136.5 2.1 convolution_convert_fusion.2
  138.6 0.2 reduce-scatter.4.cloned.1.call-start
  138.8 5.4 %fusion.32 = f32[1536,1152]{0,1:T(8,128)} fusion(bf16[1,256,1536]{2,1,0:T(8,128)(2,1)} %param.5, bf16[256,384]{1,0:T(8,128)(2,1)} %copy-done.8, bf16[256,384]{1,0:T(8,128)(2,1)} %copy-done.7, bf16[256,384]{1,0:T(8,128)(2,1)} %copy-done.9), kind=kOutput, calls=%fused_computation.44 | convolution fusion | flops 911671296 | bytes 8454144 | tf_op jit(solution)/shard_map/dot_general | solution.py:35
  144.2 7.5 %pad_maximum_fusion = f32[1536,1536]{0,1:T(8,128)} fusion(f32[1536,384]{0,1:T(8,128)S(1)} %fusion.67, f32[1536,1152]{0,1:T(8,128)} %fusion.32), kind=kLoop, calls=%fused_computation | loop fusion | flops 2359296 | bytes 18874368 | tf_op jit(solution)/shard_map/concatenate | solution.py:80
  151.8 9.7 %copy.16 = f32[1536,1536]{1,0:T(8,128)} copy(f32[1536,1536]{0,1:T(8,128)} %pad_maximum_fusion) | data formatting | bytes 18874368
  161.5 8.8 %all-reduce.8.cloned.1.call-done = bf16[256,1536]{1,0:T(8,128)(2,1)} async-done(((bf16[256,1536]{1,0:T(8,128)(2,1)}), bf16[256,1536]{1,0:T(8,128)(2,1)}) %all-reduce.8.cloned.1.call-update) | async-done | bytes 786448 | tf_op jit(solution)/shard_map/psum | solution.py:49
  170.3 3.2 %fusion.47 = bf16[1,256,1536]{2,1,0:T(8,128)(2,1)} fusion(bf16[1,256,1536]{2,1,0:T(8,128)(2,1)S(1)} %copy-done.3, bf16[256,1536]{1,0:T(8,128)(2,1)} %all-reduce.8.cloned.1.call-done, bf16[256,1536]{1,0:T(8,128)(2,1)S(1)} %copy-done.5), kind=kLoop, calls=%fused_computation.55 | loop fusion | flops 9043968 | bytes 3145728 | tf_op jit(solution)/shard_map/reshape | solution.py:90
  173.5 112.7 %reduce-scatter.4.cloned.1.call-done = f32[96,1536]{1,0:T(8,128)} async-done(((f32[1536,1536]{1,0:T(8,128)}), f32[96,1536]{1,0:T(8,128)}) %reduce-scatter.4.cloned.1.call-update) | async-done | bytes 589840
  286.2 1.0 slice.25
  287.2 0.2 copy.18
  287.5 1.0 copy.14
  288.4 1.6 slice.26
  (28 shorter events, 0.3 us)
Async XLA Ops:
  8.0 30.1 %copy-start = (bf16[1536,384]{1,0:T(8,128)(2,1)S(1)}, bf16[1536,384]{1,0:T(8,128)(2,1)}, u32[]{:S(2)}) copy-start(bf16[1536,384]{1,0:T(8,128)(2,1)} %param.7) | copy-start | bytes 3538948
  8.0 6.4 %copy-start.2 = (bf16[1,256,1536]{2,1,0:T(8,128)(2,1)S(1)}, bf16[1,256,1536]{2,1,0:T(8,128)(2,1)}, u32[]{:S(2)}) copy-start(bf16[1,256,1536]{2,1,0:T(8,128)(2,1)} %param.5) | copy-start | bytes 2359300
  8.0 64.3 %all-reduce.4.cloned.1.call-start = ((), (), s32[]{:S(2)}) async-start(), calls=%async_computation.1 | async-start | bytes 1572864 | tf_op jit(solution)/shard_map/psum | solution.py:49
  17.9 10.1 %collective-permute-start = (bf16[256,384]{1,0:T(8,128)(2,1)S(1)}, bf16[256,384]{1,0:T(8,128)(2,1)S(1)}, u32[]{:S(2)}, u32[]{:S(2)}) collective-permute-start(bf16[256,384]{1,0:T(8,128)(2,1)S(1)} %get-tuple-element.12), channel_id=1, source_target_pairs={{0,16},{4,20},{8,24},{12,28},{1,17},{5,21},{9,25},{13,29},{2,18},{... | collective-permute-start | bytes 589832 | tf_op jit(solution)/shard_map/ppermute | solution.py:12
  23.9 13.4 %collective-permute-start.1 = (bf16[256,384]{1,0:T(8,128)(2,1)S(1)}, bf16[256,384]{1,0:T(8,128)(2,1)S(1)}, u32[]{:S(2)}, u32[]{:S(2)}) collective-permute-start(bf16[256,384]{1,0:T(8,128)(2,1)S(1)} %get-tuple-element.13), channel_id=1, source_target_pairs={{16,0},{20,4},{24,8},{28,12},{17,1},{21,5},{25,9},{29,13},{18,2},{... | collective-permute-start | bytes 589832 | tf_op jit(solution)/shard_map/ppermute | solution.py:12
  37.5 0.7 copy-start.6
  39.6 32.7 %all-gather.2.cloned.1.call-start = ((), (), s32[]{:S(2)}) async-start(), calls=%async_computation.2 | async-start | bytes 8847360 | tf_op jit(solution)/shard_map/all_gather | solution.py:66
  40.2 75.8 %all-reduce.6.cloned.1.call-start = ((), (), s32[]{:S(2)}) async-start(), calls=%async_computation.3 | async-start | bytes 1572864 | tf_op jit(solution)/shard_map/psum | solution.py:49
  81.6 88.7 %all-reduce.8.cloned.1.call-start = ((), (), s32[]{:S(2)}) async-start(), calls=%async_computation.4 | async-start | bytes 1572864 | tf_op jit(solution)/shard_map/psum | solution.py:49
  116.1 7.7 %copy-start.4 = (bf16[256,1536]{1,0:T(8,128)(2,1)S(1)}, bf16[256,1536]{1,0:T(8,128)(2,1)}, u32[]{:S(2)}) copy-start(bf16[256,1536]{1,0:T(8,128)(2,1)} %all-reduce.6.cloned.1.call-done) | copy-start | bytes 2359300
  116.1 20.4 %copy-start.1 = (bf16[1536,3,384]{0,2,1:T(8,128)(2,1)S(1)}, bf16[1536,3,384]{0,2,1:T(8,128)(2,1)}, u32[]{:S(2)}) copy-start(bf16[1536,3,384]{0,2,1:T(8,128)(2,1)} %copy.13) | copy-start | bytes 10616836
  118.1 17.7 %copy-start.7 = (bf16[256,384]{1,0:T(8,128)(2,1)}, bf16[256,384]{1,0:T(8,128)(2,1)S(1)}, u32[]{:S(2)}) copy-start(bf16[256,384]{1,0:T(8,128)(2,1)S(1)} %fusion.31) | copy-start | bytes 589828
  118.1 8.5 %collective-permute-start.3 = (bf16[256,384]{1,0:T(8,128)(2,1)S(1)}, bf16[256,384]{1,0:T(8,128)(2,1)S(1)}, u32[]{:S(2)}, u32[]{:S(2)}) collective-permute-start(bf16[256,384]{1,0:T(8,128)(2,1)S(1)} %fusion.31), channel_id=1, source_target_pairs={{0,16},{4,20},{8,24},{12,28},{1,17},{5,21},{9,25},{13,29},{2,18},{... | collective-permute-start | bytes 589832 | tf_op jit(solution)/shard_map/ppermute | solution.py:12
  122.4 13.4 %collective-permute-start.2 = (bf16[256,384]{1,0:T(8,128)(2,1)S(1)}, bf16[256,384]{1,0:T(8,128)(2,1)S(1)}, u32[]{:S(2)}, u32[]{:S(2)}) collective-permute-start(bf16[256,384]{1,0:T(8,128)(2,1)S(1)} %fusion.31), channel_id=1, source_target_pairs={{16,0},{20,4},{24,8},{28,12},{17,1},{21,5},{25,9},{29,13},{18,2},{... | collective-permute-start | bytes 589832 | tf_op jit(solution)/shard_map/ppermute | solution.py:12
  126.6 9.2 %copy-start.8 = (bf16[256,384]{1,0:T(8,128)(2,1)}, bf16[256,384]{1,0:T(8,128)(2,1)S(1)}, u32[]{:S(2)}) copy-start(bf16[256,384]{1,0:T(8,128)(2,1)S(1)} %collective-permute-done.3) | copy-start | bytes 589828
  135.8 0.7 copy-start.9
  138.6 147.6 %reduce-scatter.4.cloned.1.call-start = ((), (), s32[]{:S(2)}) async-start(), calls=%async_computation.5 | async-start | bytes 10027008
  161.5 8.8 %copy-start.3 = (bf16[1,256,1536]{2,1,0:T(8,128)(2,1)S(1)}, bf16[1,256,1536]{2,1,0:T(8,128)(2,1)}, u32[]{:S(2)}) copy-start(bf16[1,256,1536]{2,1,0:T(8,128)(2,1)} %param.5) | copy-start | bytes 2359300
  161.5 8.8 %copy-start.5 = (bf16[256,1536]{1,0:T(8,128)(2,1)S(1)}, bf16[256,1536]{1,0:T(8,128)(2,1)}, u32[]{:S(2)}) copy-start(bf16[256,1536]{1,0:T(8,128)(2,1)} %all-reduce.6.cloned.1.call-done) | copy-start | bytes 2359300
Sparse Core Ops, SparseCore 0:
  39.8 32.5 all-reduce.3
  81.7 34.3 all-reduce.5
  138.7 31.5 all-reduce.7
  174.8 111.3 reduce-scatter.3
Sparse Core Ops, SparseCore 1:
  41.7 14.3 all-gather.1
where the time goes:
time: 298 us; the launch traced here: 297 us
  waiting for transfers between devices  211 us (71%)
  matrix products  25.1 us (8%)
  local copies, waits for them, and re-layouts  21.3 us (7%)
  between operations  15.3 us (5%)
  starting transfers between devices  13.3 us (4%)
  other arithmetic  10.9 us (4%)
    unnamed x6, waiting for transfers between devices  113 us
    psum x3, waiting for transfers between devices, pair_sum(): return lax.psum(term.astype(jnp.bfloat16), 'head').astype(jnp.float32)  75.3 us
    ppermute x4, waiting for transfers between devices, passed_along(): lax.ppermute(value, axis, [(source, source + steps) for source in range(l...  22.7 us
    unnamed x24, local copies, waits for them, and re-layouts  18.6 us
    ppermute x4, starting transfers between devices, passed_along(): lax.ppermute(value, axis, [(source, source + steps) for source in range(l...  12.9 us
    dot_general x3, matrix products, times_transposed(): lax.dot_general(left, right, (((1,), (1,)), ((), ())), preferred_element_...  12.8 us
    concatenate x1, other arithmetic, body(): jnp.concatenate([transposed_times(activated_hidden, kernel_taps), transpo...  7.55 us
    dot_general x2, matrix products, transposed_times(): lax.dot_general(left, right, (((0,), (0,)), ((), ())), preferred_element_...  6.85 us
  transfers between devices with their start and end apart: 9, of which 8 were waited for; matrix products, arithmetic and copies ran while one was open for 9% of the time, Pallas kernels for 0%

commit v1 on v0

v1 whole, which is shorter than its diff:
```python
import jax
import jax.numpy as jnp
from jax import lax
from jax.sharding import PartitionSpec as P

DILATION_STEP = 1024
BF16 = jnp.bfloat16
F32 = jnp.float32


def gelu_value(value):
    inner = 0.7978845608 * (value + 0.044715 * value * value * value)
    return 0.5 * value * (1.0 + jnp.tanh(inner))


def gelu_slope(value):
    inner = 0.7978845608 * (value + 0.044715 * value * value * value)
    tangent = jnp.tanh(inner)
    return 0.5 * (1.0 + tangent) + 0.5 * value * (1.0 - tangent * tangent) * 0.7978845608 * (
        1.0 + 3.0 * 0.044715 * value * value
    )


def dot(left, right, contract):
    return lax.dot_general(left, right, (contract, ((), ())), preferred_element_type=F32)


def flip(value, axis, step=1):
    count = lax.axis_size(axis)
    return lax.ppermute(value, axis, [(i, i ^ step) for i in range(count)])


def own_first(value, axis_at, bit):
    return (
        lax.dynamic_index_in_dim(value, bit, axis_at, keepdims=False),
        lax.dynamic_index_in_dim(value, 1 - bit, axis_at, keepdims=False),
    )


def in_order(own, other, bit, axis):
    first = jnp.where(bit == 0, own, other)
    second = jnp.where(bit == 0, other, own)
    return jnp.concatenate([first, second], axis=axis)


def bits_of(count):
    return count.bit_length() - 1


def body(features, dilated_weight, point_weight, track_weight, track_cotangent):
    samples, positions, channels = features.shape
    rows = samples * positions
    half = rows // 2
    width = dilated_weight.shape[2]
    n_seq, n_sample = lax.axis_size("seq"), lax.axis_size("sample")
    seq, head, sample = lax.axis_index("seq"), lax.axis_index("head"), lax.axis_index("sample")
    dist = DILATION_STEP // positions
    one_sided = n_seq == 2 * dist
    low = seq < dist
    taps = jnp.transpose(dilated_weight, (1, 0, 2))

    if one_sided:
        outer_weights = [lax.dynamic_index_in_dim(taps, jnp.where(low, 0, 2), 0, keepdims=False)]
        pairs = [(i, (i + dist) % n_seq) for i in range(n_seq)]
        forward, backward = [pairs], [pairs]
    else:
        outer_weights = [taps[0], taps[2]]
        up = [(i, i + dist) for i in range(n_seq - dist)]
        down = [(i + dist, i) for i in range(n_seq - dist)]
        forward, backward = [up, down], [down, up]
    count = len(outer_weights)

    whole_track = lax.all_gather(track_weight, "sample", axis=0, tiled=True)
    piece = channels // n_sample
    own_piece = lax.dynamic_slice_in_dim(point_weight, sample * piece, piece, 0)
    other_point = lax.all_gather(flip(own_piece, "head"), "sample", axis=0, tiled=True)

    feat = features.reshape(rows, channels)
    feat_wide = feat.astype(F32)
    activated = gelu_value(feat_wide).astype(BF16)
    sent = [dot(activated, weight, ((1,), (0,))).astype(BF16) for weight in outer_weights]
    arrived = [lax.ppermute(term, "seq", pairs) for term, pairs in zip(sent, forward)]
    middle = dot(activated, taps[1], ((1,), (0,)))
    for term in arrived:
        middle = middle + term.astype(F32)
    middle_b = middle.astype(BF16)
    other_middle = flip(middle_b, "head")
    hidden = gelu_value(middle).astype(BF16)
    other_hidden = gelu_value(other_middle.astype(F32)).astype(BF16)
    block_out = (
        feat_wide
        + dot(hidden, point_weight, ((1,), (1,)))
        + dot(other_hidden, other_point, ((1,), (1,)))
    ).astype(BF16)

    def rows_of(value, which):
        return lax.dynamic_slice_in_dim(value, which * half, half, 0)

    cotangent = track_cotangent.reshape(rows, whole_track.shape[1])

    def track_part(which):
        scores = dot(rows_of(block_out, which), whole_track, ((1,), (0,)))
        grad = (rows_of(cotangent, which).astype(F32) * jax.nn.sigmoid(scores)).astype(BF16)
        return dot(grad, whole_track, ((1,), (1,)))

    theirs = flip(track_part(1 - head).astype(BF16), "head")
    out_grad = track_part(head) + theirs.astype(F32)
    out_grad_b = out_grad.astype(BF16)
    other_out_grad = flip(out_grad_b, "head")

    grad_own = (
        dot(out_grad_b, point_weight, ((1,), (0,))) * gelu_slope(rows_of(middle, head))
    ).astype(BF16)
    grad_other = (
        dot(out_grad_b, other_point, ((1,), (0,)))
        * gelu_slope(rows_of(other_middle, head).astype(F32))
    ).astype(BF16)
    middle_grad = in_order(grad_own, flip(grad_other, "head"), head, 0)
    moved = []
    for pairs in backward:
        straight = lax.ppermute(grad_own, "seq", pairs)
        crossed = lax.ppermute(
            grad_other,
            ("seq", "head"),
            [(2 * i + k, 2 * j + 1 - k) for i, j in pairs for k in range(2)],
        )
        moved.append(in_order(straight, crossed, head, 0))

    act_part = dot(middle_grad, taps[1], ((1,), (1,)))
    for field, weight in zip(moved, outer_weights):
        act_part = act_part + dot(field, weight, ((1,), (1,)))
    act_theirs = flip(rows_of(act_part, 1 - head).astype(BF16), "head")
    act_grad = rows_of(act_part, head) + act_theirs.astype(F32)
    input_half = (out_grad + act_grad * gelu_slope(rows_of(feat_wide, head))).astype(BF16)
    input_grad = in_order(input_half, flip(input_half, "head"), head, 0)

    seq_bits = bits_of(n_seq)
    block = channels // (n_seq * n_sample)
    shape = (2,) * seq_bits + (n_sample, block)

    def halve(value, left, bit, keep_last=False):
        at = left.index(bit)
        if bit < 0:
            mine, give = own_first(value, at, sample)
            got = flip(give.astype(BF16), "sample")
        else:
            mine, give = own_first(value, at, (seq >> bit) & 1)
            got = flip(give.astype(BF16), "seq", 1 << bit)
        rest = [b for b in left if b != bit]
        return (mine, got, rest) if keep_last else (mine.astype(F32) + got.astype(F32), rest)

    def reduced(value, order, apart=False):
        left = list(range(seq_bits - 1, -1, -1)) + [-1]
        value = value.reshape(shape + value.shape[1:])
        for bit in order[:-1]:
            value, left = halve(value, left, bit)
            value = value.astype(BF16)
        mine, got, _ = halve(value, left, order[-1], True)
        if apart:
            return mine.astype(F32), got.astype(F32)
        return mine.astype(F32) + got.astype(F32)

    order_a = [-1] + list(range(seq_bits))
    order_b = [-1] + list(range(1, seq_bits - 1)) + [0, seq_bits - 1]
    whole_out_grad = in_order(out_grad_b, other_out_grad, head, 0)
    point_grad = reduced(dot(whole_out_grad, hidden, ((0,), (0,))), order_a)
    mid_tap = reduced(dot(activated, middle_grad, ((0,), (0,))), order_b)
    if one_sided:
        mine, got = reduced(dot(activated, moved[0], ((0,), (0,))), order_a, True)
        outer = [jnp.where(low, mine, got), jnp.where(low, got, mine)]
    else:
        outer = [reduced(dot(activated, field, ((0,), (0,))), order_a) for field in moved]
    dilated_grad = jnp.transpose(jnp.stack([outer[0], mid_tap, outer[1]]), (1, 0, 2))
    return (input_grad.reshape(samples, positions, channels), dilated_grad, point_grad)


def solution(mesh):
    placed = (
        P("sample", "seq", None),
        P(None, None, "head"),
        P(None, "head"),
        P("sample", "head"),
        P("sample", "seq", "head"),
    )
    return jax.shard_map(
        body,
        mesh=mesh,
        in_specs=placed,
        out_specs=(
            P("sample", "seq", None),
            P(("seq", "sample"), None, "head"),
            P(("seq", "sample"), "head"),
        ),
        check_vma=False,
    )
```

time: 298 us -> 167 us (0.56)
  waiting for transfers between devices: 211 us -> 81.1 us
  local copies, waits for them, and re-layouts: 21.3 us -> 5.52 us
  starting transfers between devices: 13.3 us -> 27.7 us
  matrix products: 25.1 us -> 29.8 us
  other arithmetic: 10.9 us -> 7.76 us
    unnamed x6 -> x2, waiting for transfers between devices: 113 us -> 0.71 us
    psum x3 -> x0, waiting for transfers between devices: 75.3 us -> none  [pair_sum(): return lax.psum(term.astype(jnp.bfloat16), 'head').astype(jnp.float32)]
    ppermute x4 -> x22, waiting for transfers between devices: 22.7 us -> 76.2 us  [the longest x19 64.1 us: flip(): return lax.ppermute(value, axis, [(i, i ^ step) for i in range(count)])]
    unnamed x24, local copies, waits for them, and re-layouts: 18.6 us -> 3.53 us
    ppermute x4 -> x22, starting transfers between devices: 12.9 us -> 27.7 us  [the longest x19 20.7 us: flip(): return lax.ppermute(value, axis, [(i, i ^ step) for i in range(count)])]
    concatenate x1 -> x0, other arithmetic: 7.55 us -> none  [body(): jnp.concatenate([transposed_times(activated_hidden, kernel_taps), transpo...]
    dot_general x7 -> x13, matrix products: 25.1 us -> 29.8 us  [dot(): lax.dot_general(left, right, (contract, ((), ())), preferred_element_type...]
    all_gather x1, waiting for transfers between devices: 0.01 us -> 4.24 us  [body(): whole_track = lax.all_gather(track_weight, 'sample', axis=0, tiled=True)]
  transfers between devices with their start and end apart: 9 -> 24, of which waited for: 8 -> 15; matrix products, arithmetic and copies ran while one was open for 9% -> 12% of each run, Pallas kernels for 0% -> 0%
where the time goes in v1:
time: 167 us; the launch traced here: 166 us
  waiting for transfers between devices  81.1 us (49%)
  matrix products  29.8 us (18%)
  starting transfers between devices  27.7 us (17%)
  between operations  14.4 us (9%)
  other arithmetic  7.76 us (5%)
  local copies, waits for them, and re-layouts  5.52 us (3%)
    ppermute x19, waiting for transfers between devices, flip(): return lax.ppermute(value, axis, [(i, i ^ step) for i in range(count)])  64.1 us
    dot_general x13, matrix products, dot(): lax.dot_general(left, right, (contract, ((), ())), preferred_element_type...  29.8 us
    ppermute x19, starting transfers between devices, flip(): return lax.ppermute(value, axis, [(i, i ^ step) for i in range(count)])  20.7 us
    ppermute x1, waiting for transfers between devices, body(): lax.ppermute(term, 'seq', pairs)  8.36 us
    all_gather x1, waiting for transfers between devices, body(): whole_track = lax.all_gather(track_weight, 'sample', axis=0, tiled=True)  4.24 us
    ppermute x1, starting transfers between devices, body(): lax.ppermute(grad_other, ('seq', 'head'), [(2 * i + k, 2 * j + 1 - k) for...  3.58 us
    unnamed x24, local copies, waits for them, and re-layouts  3.53 us
  transfers between devices with their start and end apart: 24, of which 15 were waited for; matrix products, arithmetic and copies ran while one was open for 12% of the time, Pallas kernels for 0%

profile of v1, /device:TPU:0, one launch (start us, length us, event | category | flops | bytes accessed | tf_op | source)
XLA Modules:
  0.0 166.3 jit_solution(9735525463101552460)
XLA Ops:
  8.5 3.0 %collective-permute-start.2 = (bf16[768,384]{1,0:T(8,128)(2,1)S(1)}, bf16[768,384]{1,0:T(8,128)(2,1)S(1)}, u32[]{:S(2)}, u32[]{:S(2)}) collective-permute-start(bf16[768,384]{1,0:T(8,128)(2,1)S(1)} %constant_dynamic-slice_fusion.4), channel_id=1, source_target_pairs={{0,2},{2,0},{1,3},{3,1},{4,6},{6,4},{5,7},{7,5},{8,10},{10,8},{9,1... | collective-permute-start | bytes 1769480 | tf_op jit(solution)/shard_map/ppermute | solution.py:30
  11.5 13.3 %collective-permute-done.2 = bf16[768,384]{1,0:T(8,128)(2,1)S(1)} collective-permute-done((bf16[768,384]{1,0:T(8,128)(2,1)S(1)}, bf16[768,384]{1,0:T(8,128)(2,1)S(1)}, u32[]{:S(2)}, u32[]{:S(2)}) %collective-permute-start.2) | collective-permute-done | bytes 589856 | tf_op jit(solution)/shard_map/ppermute | solution.py:30
  26.8 2.0 %fusion.28 = bf16[256,384]{1,0:T(8,128)(2,1)S(1)} fusion(bf16[1536,3,384]{2,0,1:T(8,128)(2,1)} %param.6, s32[]{:T(128)S(6)} %select_n.121, bf16[1,256,1536]{2,1,0:T(8,128)(2,1)S(1)} %copy-done.1), kind=kOutput, calls=%fused_computation.46 | convolution fusion | flops 306020352 | bytes 2162692 | tf_op jit(solution)/shard_map/dot_general | solution.py:25
  28.8 2.9 %collective-permute-start = (bf16[256,384]{1,0:T(8,128)(2,1)S(1)}, bf16[256,384]{1,0:T(8,128)(2,1)S(1)}, u32[]{:S(2)}, u32[]{:S(2)}) collective-permute-start(bf16[256,384]{1,0:T(8,128)(2,1)S(1)} %fusion.28), channel_id=1, source_target_pairs={{0,16},{4,20},{8,24},{12,28},{16,0},{20,4},{24,8},{28,12},{1,17},{... | collective-permute-start | bytes 589832 | tf_op jit(solution)/shard_map/ppermute | solution.py:82
  31.7 8.4 %collective-permute-done = bf16[256,384]{1,0:T(8,128)(2,1)S(1)} collective-permute-done((bf16[256,384]{1,0:T(8,128)(2,1)S(1)}, bf16[256,384]{1,0:T(8,128)(2,1)S(1)}, u32[]{:S(2)}, u32[]{:S(2)}) %collective-permute-start) | collective-permute-done | bytes 196640 | tf_op jit(solution)/shard_map/ppermute | solution.py:82
  40.1 2.0 %fusion.129 = (bf16[256,384]{1,0:T(8,128)(2,1)S(1)}, f32[256,384]{1,0:T(8,128)S(1)}) fusion(bf16[256,384]{1,0:T(8,128)(2,1)S(1)} %collective-permute-done, bf16[3,1536,384]{2,1,0:T(8,128)(2,1)} %bitcast.162, bf16[1,256,1536]{2,1,0:T(8,128)(2,1)S(1)} %copy-done.1), kind=kOutput, calls=%fused_computation.191 | convolution fusion | flops 306216960 | bytes 2752512 | tf_op jit(solution)/shard_map/dot_general | solution.py:25
  42.1 1.5 collective-permute-start.1
  44.2 3.9 %collective-permute-done.1 = bf16[256,384]{1,0:T(8,128)(2,1)} collective-permute-done((bf16[256,384]{1,0:T(8,128)(2,1)S(1)}, bf16[256,384]{1,0:T(8,128)(2,1)}, u32[]{:S(2)}, u32[]{:S(2)}) %collective-permute-start.1) | collective-permute-done | bytes 196640 | tf_op jit(solution)/shard_map/ppermute | solution.py:30
  48.1 3.2 %fusion = bf16[256,1536]{1,0:T(8,128)(2,1)} fusion(f32[256,1536]{1,0:T(8,128)S(1)} %convolution_add_fusion.2, bf16[1536,384]{1,0:T(8,128)(2,1)} %all-gather.3.cloned.1.call-done, bf16[256,384]{1,0:T(8,128)(2,1)} %collective-permute-done.1), kind=kOutput, calls=%fused_computation.3 | convolution fusion | flops 303759360 | bytes 3735552 | tf_op jit(solution)/shard_map/dot_general | solution.py:25
  51.2 4.2 %all-gather.5.cloned.1.call-done = bf16[1536,1920]{1,0:T(8,128)(2,1)} async-done(((bf16[768,1920]{1,0:T(8,128)(2,1)}), bf16[1536,1920]{1,0:T(8,128)(2,1)}) %all-gather.5.cloned.1.call-update) | async-done | bytes 5898256 | tf_op jit(solution)/shard_map/all_gather | solution.py:73
  55.5 7.6 %convolution_convert_fusion = bf16[128,1536]{1,0:T(8,128)(2,1)S(1)} fusion(bf16[1536,1920]{1,0:T(8,128)(2,1)} %all-gather.5.cloned.1.call-done, bf16[1,256,1920]{2,1,0:T(8,128)(2,1)} %param.9, s32[]{:T(128)S(6)} %select_n.123, bf16[256,1536]{1,0:T(8,128)(2,1)} %fusion), kind=kOutput, calls=%fused_computation.16 | convolution fusion | flops 1511620608 | bytes 13075456 | tf_op jit(solution)/shard_map/dot_general | solution.py:25
  63.1 1.8 %collective-permute-start.3 = (bf16[128,1536]{1,0:T(8,128)(2,1)S(1)}, bf16[128,1536]{1,0:T(8,128)(2,1)}, u32[]{:S(2)}, u32[]{:S(2)}) collective-permute-start(bf16[128,1536]{1,0:T(8,128)(2,1)S(1)} %convolution_convert_fusion), channel_id=1, source_target_pairs={{0,2},{2,0},{1,3},{3,1},{4,6},{6,4},{5,7},{7,5},{8,10},{10,8},{9,1... | collective-permute-start | bytes 1179656 | tf_op jit(solution)/shard_map/ppermute | solution.py:30
  64.9 9.7 %collective-permute-done.3 = bf16[128,1536]{1,0:T(8,128)(2,1)} collective-permute-done((bf16[128,1536]{1,0:T(8,128)(2,1)S(1)}, bf16[128,1536]{1,0:T(8,128)(2,1)}, u32[]{:S(2)}, u32[]{:S(2)}) %collective-permute-start.3) | collective-permute-done | bytes 393248 | tf_op jit(solution)/shard_map/ppermute | solution.py:30
  74.6 8.4 %fusion.130 = (bf16[128,1536]{1,0:T(8,128)(2,1)S(1)}, f32[128,1536]{1,0:T(8,128)}) fusion(bf16[128,1536]{1,0:T(8,128)(2,1)} %collective-permute-done.3, bf16[1536,1920]{1,0:T(8,128)(2,1)} %all-gather.5.cloned.1.call-done, bf16[1,256,1920]{2,1,0:T(8,128)(2,1)} %param.9, s32[]{:T(128)S(6)} %select_n.120, bf16[256,1536]{1,0:T(8,128)(2,1)S(1)} %copy-done.7), kind=kOutput, calls=%fused_computation.192 | convolution fusion | flops 1512013824 | bytes 14255104 | tf_op jit(solution)/shard_map/dot_general | solution.py:25
  84.4 2.0 %fusion.32 = bf16[128,384]{1,0:T(8,128)(2,1)} fusion(bf16[128,1536]{1,0:T(8,128)(2,1)S(1)} %get-tuple-element.15, bf16[1536,384]{1,0:T(8,128)(2,1)S(1)} %copy-done.6, bf16[256,384]{1,0:T(8,128)(2,1)} %collective-permute-done.1, s32[]{:T(128)S(6)} %select_n.120), kind=kOutput, calls=%fused_computation.50 | convolution fusion | flops 151977984 | bytes 1769476 | tf_op jit(solution)/shard_map/dot_general | solution.py:25
  86.4 3.6 %collective-permute-start.6 = (bf16[128,384]{1,0:T(8,128)(2,1)}, bf16[128,384]{1,0:T(8,128)(2,1)}, u32[]{:S(2)}, u32[]{:S(2)}) collective-permute-start(bf16[128,384]{1,0:T(8,128)(2,1)} %fusion.32), channel_id=1, source_target_pairs={{0,18},{2,16},{4,22},{6,20},{8,26},{10,24},{12,30},{14,28},{16,2},... | collective-permute-start | bytes 294920 | tf_op jit(solution)/shard_map/ppermute | solution.py:122
  90.5 1.4 fusion.44
  92.1 1.4 copy.14
  93.9 1.7 %collective-permute-start.4 = (bf16[128,384]{1,0:T(8,128)(2,1)}, bf16[128,384]{1,0:T(8,128)(2,1)S(1)}, u32[]{:S(2)}, u32[]{:S(2)}) collective-permute-start(bf16[128,384]{1,0:T(8,128)(2,1)} %fusion.32), channel_id=1, source_target_pairs={{0,2},{2,0},{1,3},{3,1},{4,6},{6,4},{5,7},{7,5},{8,10},{10,8},{9,1... | collective-permute-start | bytes 294920 | tf_op jit(solution)/shard_map/ppermute | solution.py:30
  95.6 2.3 %collective-permute-done.6 = bf16[128,384]{1,0:T(8,128)(2,1)} collective-permute-done((bf16[128,384]{1,0:T(8,128)(2,1)}, bf16[128,384]{1,0:T(8,128)(2,1)}, u32[]{:S(2)}, u32[]{:S(2)}) %collective-permute-start.6) | collective-permute-done | bytes 98336 | tf_op jit(solution)/shard_map/ppermute | solution.py:122
  97.9 1.3 collective-permute-done.5
  102.0 4.6 %collective-permute-done.4 = bf16[128,384]{1,0:T(8,128)(2,1)S(1)} collective-permute-done((bf16[128,384]{1,0:T(8,128)(2,1)}, bf16[128,384]{1,0:T(8,128)(2,1)S(1)}, u32[]{:S(2)}, u32[]{:S(2)}) %collective-permute-start.4) | collective-permute-done | bytes 98336 | tf_op jit(solution)/shard_map/ppermute | solution.py:30
  111.3 9.3 %collective-permute-done.7 = bf16[128,1536]{1,0:T(8,128)(2,1)S(1)} collective-permute-done((bf16[128,1536]{1,0:T(8,128)(2,1)S(1)}, bf16[128,1536]{1,0:T(8,128)(2,1)S(1)}, u32[]{:S(2)}, u32[]{:S(2)}) %collective-permute-start.7) | collective-permute-done | bytes 393248 | tf_op jit(solution)/shard_map/ppermute | solution.py:30
  123.2 1.5 collective-permute-start.10
  124.8 6.9 %collective-permute-done.8 = bf16[128,1536]{1,0:T(8,128)(2,1)S(1)} collective-permute-done((bf16[128,1536]{1,0:T(8,128)(2,1)S(1)}, bf16[128,1536]{1,0:T(8,128)(2,1)S(1)}, u32[]{:S(2)}, u32[]{:S(2)}) %collective-permute-start.8) | collective-permute-done | bytes 393248 | tf_op jit(solution)/shard_map/ppermute | solution.py:30
  132.8 1.7 %collective-permute-start.15 = (bf16[2,96,384]{2,1,0:T(8,128)(2,1)S(1)}, bf16[2,96,384]{2,1,0:T(8,128)(2,1)S(1)}, u32[]{:S(2)}, u32[]{:S(2)}) collective-permute-start(bf16[2,96,384]{2,1,0:T(8,128)(2,1)S(1)} %dynamic-slice_bitcast_fusion.4), channel_id=1, source_target_pairs={{0,4},{4,0},{8,12},{12,8},{16,20},{20,16},{24,28},{28,24},{1,5},{5... | collective-permute-start | bytes 442376 | tf_op jit(solution)/shard_map/ppermute | solution.py:30
  136.1 3.7 %collective-permute-done.11 = bf16[2,96,384]{2,1,0:T(8,128)(2,1)S(1)} collective-permute-done((bf16[2,96,384]{2,1,0:T(8,128)(2,1)S(1)}, bf16[2,96,384]{2,1,0:T(8,128)(2,1)S(1)}, u32[]{:S(2)}, u32[]{:S(2)}) %collective-permute-start.11) | collective-permute-done | bytes 147488 | tf_op jit(solution)/shard_map/ppermute | solution.py:30
  139.9 2.8 %collective-permute-start.12 = (bf16[96,384]{1,0:T(8,128)(2,1)S(1)}, bf16[96,384]{1,0:T(8,128)(2,1)S(1)}, u32[]{:S(2)}, u32[]{:S(2)}) collective-permute-start(bf16[96,384]{1,0:T(8,128)(2,1)S(1)} %dynamic-slice_bitcast_fusion.8), channel_id=1, source_target_pairs={{0,16},{4,20},{8,24},{12,28},{16,0},{20,4},{24,8},{28,12},{1,17},{... | collective-permute-start | bytes 221192 | tf_op jit(solution)/shard_map/ppermute | solution.py:30
  143.0 3.9 %collective-permute-done.12 = bf16[96,384]{1,0:T(8,128)(2,1)S(1)} collective-permute-done((bf16[96,384]{1,0:T(8,128)(2,1)S(1)}, bf16[96,384]{1,0:T(8,128)(2,1)S(1)}, u32[]{:S(2)}, u32[]{:S(2)}) %collective-permute-start.12) | collective-permute-done | bytes 73760 | tf_op jit(solution)/shard_map/ppermute | solution.py:30
  148.1 4.9 %collective-permute-done.20 = bf16[2,96,384]{2,1,0:T(8,128)(2,1)S(1)} collective-permute-done((bf16[2,96,384]{2,1,0:T(8,128)(2,1)S(1)}, bf16[2,96,384]{2,1,0:T(8,128)(2,1)S(1)}, u32[]{:S(2)}, u32[]{:S(2)}) %collective-permute-start.20) | collective-permute-done | bytes 147488 | tf_op jit(solution)/shard_map/ppermute | solution.py:30
  153.1 1.6 collective-permute-start.21
  155.5 3.2 %collective-permute-done.21 = bf16[96,384]{1,0:T(8,128)(2,1)S(1)} collective-permute-done((bf16[96,384]{1,0:T(8,128)(2,1)S(1)}, bf16[96,384]{1,0:T(8,128)(2,1)S(1)}, u32[]{:S(2)}, u32[]{:S(2)}) %collective-permute-start.21) | collective-permute-done | bytes 73760 | tf_op jit(solution)/shard_map/ppermute | solution.py:30
  (91 shorter events, 22.1 us)
Async XLA Ops:
  7.2 40.9 %all-gather.3.cloned.1.call-start = ((), (), s32[]{:S(2)}) async-start(), calls=%async_computation | async-start | bytes 1769472 | tf_op jit(solution)/shard_map/all_gather | solution.py:76
  8.5 16.3 %collective-permute-start.2 = (bf16[768,384]{1,0:T(8,128)(2,1)S(1)}, bf16[768,384]{1,0:T(8,128)(2,1)S(1)}, u32[]{:S(2)}, u32[]{:S(2)}) collective-permute-start(bf16[768,384]{1,0:T(8,128)(2,1)S(1)} %constant_dynamic-slice_fusion.4), channel_id=1, source_target_pairs={{0,2},{2,0},{1,3},{3,1},{4,6},{6,4},{5,7},{7,5},{8,10},{10,8},{9,1... | collective-permute-start | bytes 1769480 | tf_op jit(solution)/shard_map/ppermute | solution.py:30
  25.7 29.8 %all-gather.5.cloned.1.call-start = ((), (), s32[]{:S(2)}) async-start(), calls=%async_computation.1 | async-start | bytes 8847360 | tf_op jit(solution)/shard_map/all_gather | solution.py:73
  28.8 11.3 %collective-permute-start = (bf16[256,384]{1,0:T(8,128)(2,1)S(1)}, bf16[256,384]{1,0:T(8,128)(2,1)S(1)}, u32[]{:S(2)}, u32[]{:S(2)}) collective-permute-start(bf16[256,384]{1,0:T(8,128)(2,1)S(1)} %fusion.28), channel_id=1, source_target_pairs={{0,16},{4,20},{8,24},{12,28},{16,0},{20,4},{24,8},{28,12},{1,17},{... | collective-permute-start | bytes 589832 | tf_op jit(solution)/shard_map/ppermute | solution.py:82
  42.1 2.1 %copy-start.3 = (f32[256,384]{1,0:T(8,128)}, f32[256,384]{1,0:T(8,128)S(1)}, u32[]{:S(2)}) copy-start(f32[256,384]{1,0:T(8,128)S(1)} %get-tuple-element.14) | copy-start | bytes 1179652
  42.1 6.0 %collective-permute-start.1 = (bf16[256,384]{1,0:T(8,128)(2,1)S(1)}, bf16[256,384]{1,0:T(8,128)(2,1)}, u32[]{:S(2)}, u32[]{:S(2)}) collective-permute-start(bf16[256,384]{1,0:T(8,128)(2,1)S(1)} %get-tuple-element.13), channel_id=1, source_target_pairs={{0,2},{2,0},{1,3},{3,1},{4,6},{6,4},{5,7},{7,5},{8,10},{10,8},{9,1... | collective-permute-start | bytes 589832 | tf_op jit(solution)/shard_map/ppermute | solution.py:30
  51.2 23.3 %copy-start.7 = (bf16[256,1536]{1,0:T(8,128)(2,1)S(1)}, bf16[256,1536]{1,0:T(8,128)(2,1)}, u32[]{:S(2)}) copy-start(bf16[256,1536]{1,0:T(8,128)(2,1)} %fusion) | copy-start | bytes 2359300
  63.1 11.5 %collective-permute-start.3 = (bf16[128,1536]{1,0:T(8,128)(2,1)S(1)}, bf16[128,1536]{1,0:T(8,128)(2,1)}, u32[]{:S(2)}, u32[]{:S(2)}) collective-permute-start(bf16[128,1536]{1,0:T(8,128)(2,1)S(1)} %convolution_convert_fusion), channel_id=1, source_target_pairs={{0,2},{2,0},{1,3},{3,1},{4,6},{6,4},{5,7},{7,5},{8,10},{10,8},{9,1... | collective-permute-start | bytes 1179656 | tf_op jit(solution)/shard_map/ppermute | solution.py:30
  64.9 18.1 %copy-start.4 = (f32[256,384]{1,0:T(8,128)S(1)}, f32[256,384]{1,0:T(8,128)}, u32[]{:S(2)}) copy-start(f32[256,384]{1,0:T(8,128)} %copy-done.3) | copy-start | bytes 1179652
  82.9 3.4 %copy-start.10 = (bf16[128,1536]{1,0:T(8,128)(2,1)}, bf16[128,1536]{1,0:T(8,128)(2,1)S(1)}, u32[]{:S(2)}) copy-start(bf16[128,1536]{1,0:T(8,128)(2,1)S(1)} %get-tuple-element.15) | copy-start | bytes 1179652
  82.9 1.4 copy-start.6
  86.4 11.6 %collective-permute-start.6 = (bf16[128,384]{1,0:T(8,128)(2,1)}, bf16[128,384]{1,0:T(8,128)(2,1)}, u32[]{:S(2)}, u32[]{:S(2)}) collective-permute-start(bf16[128,384]{1,0:T(8,128)(2,1)} %fusion.32), channel_id=1, source_target_pairs={{0,18},{2,16},{4,22},{6,20},{8,26},{10,24},{12,30},{14,28},{16,2},... | collective-permute-start | bytes 294920 | tf_op jit(solution)/shard_map/ppermute | solution.py:122
  89.9 9.3 %collective-permute-start.5 = (bf16[128,384]{1,0:T(8,128)(2,1)}, bf16[128,384]{1,0:T(8,128)(2,1)}, u32[]{:S(2)}, u32[]{:S(2)}) collective-permute-start(bf16[128,384]{1,0:T(8,128)(2,1)} %fusion.31), channel_id=1, source_target_pairs={{0,16},{4,20},{8,24},{12,28},{16,0},{20,4},{24,8},{28,12},{1,17},{... | collective-permute-start | bytes 294920 | tf_op jit(solution)/shard_map/ppermute | solution.py:121
  93.5 16.6 %collective-permute-start.17 = (bf16[128,1536]{1,0:T(8,128)(2,1)}, bf16[128,1536]{1,0:T(8,128)(2,1)S(1)}, u32[]{:S(2)}, u32[]{:S(2)}) collective-permute-start(bf16[128,1536]{1,0:T(8,128)(2,1)} %copy-done.10), channel_id=1, source_target_pairs={{0,2},{2,0},{1,3},{3,1},{4,6},{6,4},{5,7},{7,5},{8,10},{10,8},{9,1... | collective-permute-start | bytes 1179656 | tf_op jit(solution)/shard_map/ppermute | solution.py:30
  93.9 12.7 %collective-permute-start.4 = (bf16[128,384]{1,0:T(8,128)(2,1)}, bf16[128,384]{1,0:T(8,128)(2,1)S(1)}, u32[]{:S(2)}, u32[]{:S(2)}) collective-permute-start(bf16[128,384]{1,0:T(8,128)(2,1)} %fusion.32), channel_id=1, source_target_pairs={{0,2},{2,0},{1,3},{3,1},{4,6},{6,4},{5,7},{7,5},{8,10},{10,8},{9,1... | collective-permute-start | bytes 294920 | tf_op jit(solution)/shard_map/ppermute | solution.py:30
  99.3 2.1 %copy-start.2 = (bf16[1536,3,384]{2,0,1:T(8,128)(2,1)S(1)}, bf16[1536,3,384]{2,0,1:T(8,128)(2,1)}, u32[]{:S(2)}) copy-start(bf16[1536,3,384]{2,0,1:T(8,128)(2,1)} %param.6) | copy-start | bytes 10616836
  108.1 13.8 %collective-permute-start.13 = (bf16[2,2,2,96,384]{4,3,0,2,1:T(8,128)(2,1)S(1)}, bf16[2,2,2,96,384]{4,3,0,2,1:T(8,128)(2,1)S(1)}, u32[]{:S(2)}, u32[]{:S(2)}) collective-permute-start(bf16[2,2,2,96,384]{4,3,0,2,1:T(8,128)(2,1)S(1)} %fusion.54), channel_id=1, source_target_pairs={{0,1},{1,0},{2,3},{3,2},{4,5},{5,4},{6,7},{7,6},{8,9},{9,8},{10,11... | collective-permute-start | bytes 1769480 | tf_op jit(solution)/shard_map/ppermute | solution.py:30
  108.3 1.8 %copy-start.11 = (bf16[128,1536]{1,0:T(8,128)(2,1)S(1)}, bf16[128,1536]{1,0:T(8,128)(2,1)}, u32[]{:S(2)}) copy-start(bf16[128,1536]{1,0:T(8,128)(2,1)} %copy-done.10) | copy-start | bytes 1179652
  108.3 14.7 %collective-permute-start.9 = (bf16[2,2,2,96,384]{4,3,2,1,0:T(8,128)(2,1)S(1)}, bf16[2,2,2,96,384]{4,3,2,1,0:T(8,128)(2,1)S(1)}, u32[]{:S(2)}, u32[]{:S(2)}) collective-permute-start(bf16[2,2,2,96,384]{4,3,2,1,0:T(8,128)(2,1)S(1)} %fusion.53), channel_id=1, source_target_pairs={{0,1},{1,0},{2,3},{3,2},{4,5},{5,4},{6,7},{7,6},{8,9},{9,8},{10,11... | collective-permute-start | bytes 1769480 | tf_op jit(solution)/shard_map/ppermute | solution.py:30
  109.5 11.1 %collective-permute-start.7 = (bf16[128,1536]{1,0:T(8,128)(2,1)S(1)}, bf16[128,1536]{1,0:T(8,128)(2,1)S(1)}, u32[]{:S(2)}, u32[]{:S(2)}) collective-permute-start(bf16[128,1536]{1,0:T(8,128)(2,1)S(1)} %dynamic-slice_convert_fusion.1), channel_id=1, source_target_pairs={{0,2},{2,0},{1,3},{3,1},{4,6},{6,4},{5,7},{7,5},{8,10},{10,8},{9,1... | collective-permute-start | bytes 1179656 | tf_op jit(solution)/shard_map/ppermute | solution.py:30
  110.5 10.2 %copy-start.8 = (f32[128,1536]{1,0:T(8,128)S(1)}, f32[128,1536]{1,0:T(8,128)}, u32[]{:S(2)}) copy-start(f32[128,1536]{1,0:T(8,128)} %get-tuple-element.16) | copy-start | bytes 2359300
  111.2 24.0 %collective-permute-start.18 = (bf16[2,2,2,96,384]{4,3,0,1,2:T(8,128)(2,1)S(1)}, bf16[2,2,2,96,384]{4,3,0,1,2:T(8,128)(2,1)S(1)}, u32[]{:S(2)}, u32[]{:S(2)}) collective-permute-start(bf16[2,2,2,96,384]{4,3,0,1,2:T(8,128)(2,1)S(1)} %fusion.55), channel_id=1, source_target_pairs={{0,1},{1,0},{2,3},{3,2},{4,5},{5,4},{6,7},{7,6},{8,9},{9,8},{10,11... | collective-permute-start | bytes 1769480 | tf_op jit(solution)/shard_map/ppermute | solution.py:30
  121.4 10.3 %collective-permute-start.8 = (bf16[128,1536]{1,0:T(8,128)(2,1)S(1)}, bf16[128,1536]{1,0:T(8,128)(2,1)S(1)}, u32[]{:S(2)}, u32[]{:S(2)}) collective-permute-start(bf16[128,1536]{1,0:T(8,128)(2,1)S(1)} %fusion.43), channel_id=1, source_target_pairs={{0,2},{2,0},{1,3},{3,1},{4,6},{6,4},{5,7},{7,5},{8,10},{10,8},{9,1... | collective-permute-start | bytes 1179656 | tf_op jit(solution)/shard_map/ppermute | solution.py:30
  122.2 10.5 %collective-permute-start.14 = (bf16[2,2,96,384]{3,2,0,1:T(8,128)(2,1)S(1)}, bf16[2,2,96,384]{3,2,0,1:T(8,128)(2,1)S(1)}, u32[]{:S(2)}, u32[]{:S(2)}) collective-permute-start(bf16[2,2,96,384]{3,2,0,1:T(8,128)(2,1)S(1)} %dynamic-slice_bitcast_fusion.1), channel_id=1, source_target_pairs={{0,8},{4,12},{8,0},{12,4},{16,24},{20,28},{24,16},{28,20},{1,9},{5... | collective-permute-start | bytes 884744 | tf_op jit(solution)/shard_map/ppermute | solution.py:30
  123.2 11.2 %collective-permute-start.10 = (bf16[2,2,96,384]{3,2,1,0:T(8,128)(2,1)S(1)}, bf16[2,2,96,384]{3,2,1,0:T(8,128)(2,1)S(1)}, u32[]{:S(2)}, u32[]{:S(2)}) collective-permute-start(bf16[2,2,96,384]{3,2,1,0:T(8,128)(2,1)S(1)} %dynamic-slice_bitcast_fusion.2), channel_id=1, source_target_pairs={{0,4},{4,0},{8,12},{12,8},{16,20},{20,16},{24,28},{28,24},{1,5},{5... | collective-permute-start | bytes 884744 | tf_op jit(solution)/shard_map/ppermute | solution.py:30
  132.8 9.9 %collective-permute-start.15 = (bf16[2,96,384]{2,1,0:T(8,128)(2,1)S(1)}, bf16[2,96,384]{2,1,0:T(8,128)(2,1)S(1)}, u32[]{:S(2)}, u32[]{:S(2)}) collective-permute-start(bf16[2,96,384]{2,1,0:T(8,128)(2,1)S(1)} %dynamic-slice_bitcast_fusion.4), channel_id=1, source_target_pairs={{0,4},{4,0},{8,12},{12,8},{16,20},{20,16},{24,28},{28,24},{1,5},{5... | collective-permute-start | bytes 442376 | tf_op jit(solution)/shard_map/ppermute | solution.py:30
  134.6 5.2 %collective-permute-start.11 = (bf16[2,96,384]{2,1,0:T(8,128)(2,1)S(1)}, bf16[2,96,384]{2,1,0:T(8,128)(2,1)S(1)}, u32[]{:S(2)}, u32[]{:S(2)}) collective-permute-start(bf16[2,96,384]{2,1,0:T(8,128)(2,1)S(1)} %dynamic-slice_bitcast_fusion.5), channel_id=1, source_target_pairs={{0,8},{4,12},{8,0},{12,4},{16,24},{20,28},{24,16},{28,20},{1,9},{5... | collective-permute-start | bytes 442376 | tf_op jit(solution)/shard_map/ppermute | solution.py:30
  135.4 11.5 %collective-permute-start.19 = (bf16[2,2,96,384]{3,2,0,1:T(8,128)(2,1)S(1)}, bf16[2,2,96,384]{3,2,0,1:T(8,128)(2,1)S(1)}, u32[]{:S(2)}, u32[]{:S(2)}) collective-permute-start(bf16[2,2,96,384]{3,2,0,1:T(8,128)(2,1)S(1)} %dynamic-slice_bitcast_fusion), channel_id=1, source_target_pairs={{0,4},{4,0},{8,12},{12,8},{16,20},{20,16},{24,28},{28,24},{1,5},{5... | collective-permute-start | bytes 884744 | tf_op jit(solution)/shard_map/ppermute | solution.py:30
  139.9 7.0 %collective-permute-start.12 = (bf16[96,384]{1,0:T(8,128)(2,1)S(1)}, bf16[96,384]{1,0:T(8,128)(2,1)S(1)}, u32[]{:S(2)}, u32[]{:S(2)}) collective-permute-start(bf16[96,384]{1,0:T(8,128)(2,1)S(1)} %dynamic-slice_bitcast_fusion.8), channel_id=1, source_target_pairs={{0,16},{4,20},{8,24},{12,28},{16,0},{20,4},{24,8},{28,12},{1,17},{... | collective-permute-start | bytes 221192 | tf_op jit(solution)/shard_map/ppermute | solution.py:30
  142.8 5.3 %collective-permute-start.16 = (bf16[96,384]{1,0:T(8,128)(2,1)S(1)}, bf16[96,384]{1,0:T(8,128)(2,1)S(1)}, u32[]{:S(2)}, u32[]{:S(2)}) collective-permute-start(bf16[96,384]{1,0:T(8,128)(2,1)S(1)} %dynamic-slice_bitcast_fusion.7), channel_id=1, source_target_pairs={{0,16},{4,20},{8,24},{12,28},{16,0},{20,4},{24,8},{28,12},{1,17},{... | collective-permute-start | bytes 221192 | tf_op jit(solution)/shard_map/ppermute | solution.py:30
  147.0 6.0 %collective-permute-start.20 = (bf16[2,96,384]{2,1,0:T(8,128)(2,1)S(1)}, bf16[2,96,384]{2,1,0:T(8,128)(2,1)S(1)}, u32[]{:S(2)}, u32[]{:S(2)}) collective-permute-start(bf16[2,96,384]{2,1,0:T(8,128)(2,1)S(1)} %dynamic-slice_bitcast_fusion.3), channel_id=1, source_target_pairs={{0,8},{4,12},{8,0},{12,4},{16,24},{20,28},{24,16},{28,20},{1,9},{5... | collective-permute-start | bytes 442376 | tf_op jit(solution)/shard_map/ppermute | solution.py:30
  153.1 5.6 %collective-permute-start.21 = (bf16[96,384]{1,0:T(8,128)(2,1)S(1)}, bf16[96,384]{1,0:T(8,128)(2,1)S(1)}, u32[]{:S(2)}, u32[]{:S(2)}) collective-permute-start(bf16[96,384]{1,0:T(8,128)(2,1)S(1)} %dynamic-slice_bitcast_fusion.6), channel_id=1, source_target_pairs={{0,16},{4,20},{8,24},{12,28},{16,0},{20,4},{24,8},{28,12},{1,17},{... | collective-permute-start | bytes 221192 | tf_op jit(solution)/shard_map/ppermute | solution.py:30
  (4 other events, 4.2 us)
Sparse Core Ops, SparseCore 0:
  25.8 10.7 all-gather.2
  38.1 17.3 all-gather.4

commit v2 on v1

--- a/solution.py
+++ b/solution.py
@@ -1,11 +1,14 @@
 import jax
 import jax.numpy as jnp
 from jax import lax
+from jax.experimental import pallas as pl
+from jax.experimental.pallas import tpu as pltpu
 from jax.sharding import PartitionSpec as P
 
 DILATION_STEP = 1024
 BF16 = jnp.bfloat16
 F32 = jnp.float32
+VMEM = 40 * 2**20
 
 
 def gelu_value(value):
@@ -47,7 +50,7 @@
     return count.bit_length() - 1
 
 
-def body(features, dilated_weight, point_weight, track_weight, track_cotangent):
+def general(features, dilated_weight, point_weight, track_weight, track_cotangent):
     samples, positions, channels = features.shape
     rows = samples * positions
     half = rows // 2
@@ -174,6 +177,416 @@
     return (input_grad.reshape(samples, positions, channels), dilated_grad, point_grad)
 
 
+def wide(ref):
+    return ref[...].astype(F32)
+
+
+def kernel_call(kernel, outs, ins, after=None, scratch=()):
+    place, arrays = ins[0], list(ins[1:])
+    in_specs = [pl.BlockSpec(memory_space=pltpu.SMEM)]
+    in_specs += [pl.BlockSpec(memory_space=pltpu.VMEM)] * len(arrays)
+    number = len(arrays) + 1
+    if after is not None:
+        arrays.append(after)
+        in_specs.append(pl.BlockSpec(memory_space=pl.ANY))
+
+    def run(*refs):
+        given = refs[:number]
+        kernel(*given, *refs[len(in_specs):])
+
+    return pl.pallas_call(
+        run,
+        out_shape=[jax.ShapeDtypeStruct(s, d) for s, d in outs],
+        in_specs=in_specs,
+        out_specs=[pl.BlockSpec(memory_space=pltpu.VMEM)] * len(outs),
+        scratch_shapes=list(scratch),
+        compiler_params=pltpu.CompilerParams(vmem_limit_bytes=VMEM),
+        name=kernel.__name__,
+    )(place, *arrays)
+
+
+NN = ((1,), (0,))
+NT = ((1,), (1,))
+HEAD, SAMPLE, TOP, MID, LOWEST = 1, 2, 3, 4, 5
+
+
+def outer_term(place, feat, weight, acted, term, total):
+    step = pl.program_id(0)
+    act = gelu_value(feat[...].astype(F32)).astype(BF16)
+    acted[...] = act
+
+    @pl.when(step == 0)
+    def _():
+        total[...] = jnp.zeros_like(total)
+
+    total[...] += dot(act, weight[0], NN)
+
+    @pl.when(step == pl.num_programs(0) - 1)
+    def _():
+        term[...] = total[...].astype(BF16)
+
+
+def middle_term(place, acted, weight, middle, turned):
+    act = acted[...]
+    middle[...] = dot(act, weight[...], NN)
+    turned[...] = act.T.reshape(turned.shape)
+
+
+def add_terms(place, middle, arrived, total, sent):
+    value = middle[...] + wide(arrived)
+    total[...] = value
+    sent[...] = value.astype(BF16)
+
+
+def own_hidden(place, middle, feat, point, hidden, slope, block):
+    half = slope.shape[0]
+    hid = gelu_value(middle[...]).astype(BF16)
+    hidden[...] = hid
+    own = pl.ds(pl.multiple_of(place[HEAD] * half, half), half)
+    slope[...] = gelu_slope(middle[own, :])
+    block[...] = wide(feat) + dot(hid, point[...], NT)
+
+
+def tracks(
+    place, block, other_middle, point_near, point_far, near, far, cotangent,
+    keep, give, block_b, total,
+):
+    step = pl.program_id(0)
+    sample = place[SAMPLE]
+    piece = block_b.shape[2]
+
+    @pl.when(step == 0)
+    def _():
+        hid = gelu_value(wide(other_middle)).astype(BF16)
+        for which, point in ((sample, point_near), (1 - sample, point_far)):
+            columns = pl.ds(pl.multiple_of(which * piece, piece), piece)
+            block_b[which] = (block[:, columns] + dot(hid, point[...], NT)).astype(BF16)
+        total[...] = jnp.zeros_like(total)
+
+    scores = dot(block_b[sample], near[...], NN) + dot(block_b[1 - sample], far[...], NN)
+    grad = (wide(cotangent) * jax.nn.sigmoid(scores)).astype(BF16)
+    total[sample] += dot(grad, near[...], NT)
+    total[1 - sample] += dot(grad, far[...], NT)
+
+    @pl.when(step == pl.num_programs(0) - 1)
+    def _():
+        half = keep.shape[0]
+        own = pl.ds(pl.multiple_of(place[HEAD] * half, half), half)
+        theirs = pl.ds(pl.multiple_of((1 - place[HEAD]) * half, half), half)
+        for which in range(2):
+            columns = pl.ds(which * piece, piece)
+            keep[:, columns] = total[which, own, :]
+            give[:, columns] = total[which, theirs, :].astype(BF16)
+
+
+def slopes(place, other_middle, feat, slope_other, slope_feat):
+    half = slope_other.shape[0]
+    own = pl.ds(pl.multiple_of(place[HEAD] * half, half), half)
+    slope_other[...] = gelu_slope(other_middle[own, :].astype(F32))
+    slope_feat[...] = gelu_slope(feat[own, :].astype(F32))
+
+
+def middle_grads(
+    place, keep, theirs, point, point_near, point_far, slope, slope_other,
+    out_grad, out_grad_b, grad_own, grad_other,
+):
+    sample = place[SAMPLE]
+    piece = point_near.shape[0]
+    total = keep[...] + wide(theirs)
+    out_grad[...] = total
+    total_b = total.astype(BF16)
+    out_grad_b[...] = total_b
+    grad_own[...] = (dot(total_b, point[...], NN) * slope[...]).astype(BF16)
+    near = out_grad_b[:, pl.ds(pl.multiple_of(sample * piece, piece), piece)]
+    far = out_grad_b[:, pl.ds(pl.multiple_of((1 - sample) * piece, piece), piece)]
+    other = dot(near, point_near[...], NN) + dot(far, point_far[...], NN)
+    grad_other[...] = (other * slope_other[...]).astype(BF16)
+
+
+def assembled(field, own, theirs, head):
+    half = own.shape[0]
+    field[pl.ds(pl.multiple_of(head * half, half), half), :] = own[...]
+    field[pl.ds(pl.multiple_of((1 - head) * half, half), half), :] = theirs[...]
+
+
+def products(place, turned, field, keep, give, columns):
+    groups, _, block, rows = turned.shape
+    for which, out in ((1 - place[SAMPLE], give), (place[SAMPLE], keep)):
+        left = turned[:, which].reshape(groups * block, rows)
+        value = dot(left, field[...], NN).astype(out.dtype)
+        out[:, :, columns] = value.reshape(groups, block, value.shape[1])
+
+
+def middle_tap(place, turned, own, theirs, field, keep, give):
+    assembled(field, own, theirs, place[HEAD])
+    products(place, turned, field, keep, give, slice(None))
+
+
+def outer_tap(
+    place, turned, straight, crossed, own_grad, other_grad, hidden, field, keep, give, whole,
+    turned_grad,
+):
+    width = straight.shape[1]
+    assembled(field, straight, crossed, place[HEAD])
+    products(place, turned, field, keep, give, slice(0, width))
+    assembled(whole, own_grad, other_grad, place[HEAD])
+    turned_grad[...] = whole[...].T.reshape(turned_grad.shape)
+    products(place, turned_grad, hidden, keep, give, slice(width, 2 * width))
+
+
+def act_given(place, middle_grad, moved, mid_weight, outer_weight, give):
+    half = give.shape[0]
+    theirs = pl.ds(pl.multiple_of((1 - place[HEAD]) * half, half), half)
+    value = dot(middle_grad[theirs, :], mid_weight[...], NT)
+    give[...] = (value + dot(moved[theirs, :], outer_weight[...], NT)).astype(BF16)
+
+
+def act_kept(place, middle_grad, moved, mid_weight, outer_weight, keep):
+    half = keep.shape[0]
+    own = pl.ds(pl.multiple_of(place[HEAD] * half, half), half)
+    value = dot(middle_grad[own, :], mid_weight[...], NT)
+    keep[...] = value + dot(moved[own, :], outer_weight[...], NT)
+
+
+def core_sum(place, kept, got, keep, along, across, both):
+    mid, lowest = place[MID], place[LOWEST]
+
+    def part(i, j):
+        return kept[:, i, j].astype(F32) + got[:, i, j].astype(F32)
+
+    both[...] = part(1 - mid, 1 - lowest).astype(BF16)
+    along[...] = part(1 - mid, lowest).astype(BF16)
+    across[...] = part(mid, 1 - lowest).astype(BF16)
+    keep[...] = part(mid, lowest)
+
+
+def chips_sum(place, kept, along, across, both, keep, give):
+    def part(i):
+        total = kept[i] + along[i].astype(F32)
+        return total + across[i].astype(F32) + both[i].astype(F32)
+
+    give[...] = part(1 - place[TOP]).astype(BF16)
+    keep[...] = part(place[TOP])
+
+
+def input_part(place, out_grad, kept, got, slope_feat, result):
+    result[...] = (out_grad[...] + (kept[...] + wide(got)) * slope_feat[...]).astype(BF16)
+
+
+def finish(place, mid_kept, mid_got, kept, got, dilated, point):
+    width = mid_kept.shape[1]
+    dilated[1] = mid_kept[...] + wide(mid_got)
+    own, theirs = place[0], 2 - place[0]
+    dilated[own] = kept[:, :width]
+    dilated[theirs] = got[:, :width].astype(F32)
+    point[...] = kept[:, width:] + got[:, width:].astype(F32)
+
+
+def joined(place, own, theirs, result):
+    assembled(result, own, theirs, place[HEAD])
+
+
+def body(features, dilated_weight, point_weight, track_weight, track_cotangent):
+    samples, positions, channels = features.shape
+    n_seq, n_sample, n_head = (lax.axis_size(a) for a in ("seq", "sample", "head"))
+    dist = DILATION_STEP // positions
+    if not (n_seq == 2 * dist and bits_of(n_seq) == 3 and n_sample == 2 and n_head == 2 and samples == 1):
+        return general(features, dilated_weight, point_weight, track_weight, track_cotangent)
+    rows = positions
+    half = rows // 2
+    width = dilated_weight.shape[2]
+    tracks_here = track_weight.shape[1]
+    piece = channels // n_sample
+    block = channels // (n_seq * n_sample)
+    seq, head, sample = lax.axis_index("seq"), lax.axis_index("head"), lax.axis_index("sample")
+    place = jnp.stack(
+        [jnp.where(seq < dist, 0, 2), head, sample, (seq >> 2) & 1, (seq >> 1) & 1, seq & 1]
+    ).astype(jnp.int32)
+    taps = jnp.transpose(dilated_weight, (1, 0, 2))
+    feat = features.reshape(rows, channels)
+    cotangent = track_cotangent.reshape(rows, tracks_here)
+    pairs = [(i, (i + dist) % n_seq) for i in range(n_seq)]
+    crossing = [(2 * i + k, 2 * j + 1 - k) for i, j in pairs for k in range(2)]
+
+    own_piece = lax.dynamic_slice_in_dim(point_weight, sample * piece, piece, 0)
+    point_near = flip(own_piece, "head")
+    far_track = flip(track_weight, "sample")
+    point_far = flip(point_near, "sample")
+
+    steps = 3
+    depth = channels // steps
+    acted, term = pl.pallas_call(
+        outer_term,
+        grid_spec=pltpu.PrefetchScalarGridSpec(
+            num_scalar_prefetch=1,
+            grid=(steps,),
+            in_specs=[
+                pl.BlockSpec((rows, depth), lambda k, place: (0, k)),
+                pl.BlockSpec((1, depth, width), lambda k, place: (place[0], k, 0)),
+            ],
+            out_specs=[
+                pl.BlockSpec((rows, depth), lambda k, place: (0, k)),
+                pl.BlockSpec((rows, width), lambda k, place: (0, 0)),
+            ],
+            scratch_shapes=[pltpu.VMEM((rows, width), F32)],
+        ),
+        out_shape=[
+            jax.ShapeDtypeStruct((rows, channels), BF16),
+            jax.ShapeDtypeStruct((rows, width), BF16),
+        ],
+        compiler_params=pltpu.CompilerParams(vmem_limit_bytes=VMEM),
+        name="outer_term",
+    )(place, feat, taps)
+    arrived = lax.ppermute(term, "seq", pairs)
+    mid_weight = taps[1]
+    outer_weight = lax.dynamic_index_in_dim(taps, place[0], 0, keepdims=False)
+    groups = n_seq
+    middle, turned = kernel_call(
+        middle_term,
+        [((rows, width), F32), ((groups, n_sample, block, rows), BF16)],
+        [place, acted, mid_weight],
+    )
+    middle, middle_b = kernel_call(
+        add_terms, [((rows, width), F32), ((rows, width), BF16)], [place, middle, arrived], turned
+    )
+    other_middle = flip(middle_b, "head")
+    hidden, slope, block_part = kernel_call(
+        own_hidden,
+        [((rows, width), BF16), ((half, width), F32), ((rows, channels), F32)],
+        [place, middle, feat, point_weight],
+    )
+
+    tile = width if tracks_here % width == 0 else tracks_here
+    fixed = lambda k, place: (0, 0)
+    moving = lambda k, place: (0, k)
+    keep, give = pl.pallas_call(
+        tracks,
+        grid_spec=pltpu.PrefetchScalarGridSpec(
+            num_scalar_prefetch=1,
+            grid=(tracks_here // tile,),
+            in_specs=[
+                pl.BlockSpec((rows, channels), fixed),
+                pl.BlockSpec((rows, width), fixed),
+                pl.BlockSpec((piece, width), fixed),
+                pl.BlockSpec((piece, width), fixed),
+                pl.BlockSpec((piece, tile), moving),
+                pl.BlockSpec((piece, tile), moving),
+                pl.BlockSpec((rows, tile), moving),
+            ],
+            out_specs=[pl.BlockSpec((half, channels), fixed)] * 2,
+            scratch_shapes=[
+                pltpu.VMEM((n_sample, rows, piece), BF16),
+                pltpu.VMEM((n_sample, rows, piece), F32),
+            ],
+        ),
+        out_shape=[
+            jax.ShapeDtypeStruct((half, channels), F32),
+            jax.ShapeDtypeStruct((half, channels), BF16),
+        ],
+        compiler_params=pltpu.CompilerParams(vmem_limit_bytes=VMEM),
+        name="tracks",
+    )(place, block_part, other_middle, point_near, point_far, track_weight, far_track, cotangent)
+    theirs = flip(give, "head")
+    slope_other, slope_feat = kernel_call(
+        slopes,
+        [((half, width), F32), ((half, channels), F32)],
+        [place, other_middle, feat],
+        keep,
+    )
+    out_grad, out_grad_b, grad_own, grad_other = kernel_call(
+        middle_grads,
+        [
+            ((half, channels), F32),
+            ((half, channels), BF16),
+            ((half, width), BF16),
+            ((half, width), BF16),
+        ],
+        [place, keep, theirs, point_weight, point_near, point_far, slope, slope_other],
+    )
+    straight = lax.ppermute(grad_own, "seq", pairs)
+    crossed = lax.ppermute(grad_other, ("seq", "head"), crossing)
+    grad_theirs = flip(grad_other, "head")
+    other_out_grad = flip(out_grad_b, "head")
+
+    def chips(value):
+        return value.reshape(2, 2, 2, *value.shape[1:])
+
+    def direct(along, across, both):
+        return (
+            flip(along, "seq", 2),
+            flip(across, "seq", 1),
+            flip(both, "seq", 3),
+        )
+
+    def summed(keep, give, columns, after):
+        got = flip(give, "sample")
+        part = [((2, block, columns), F32)] + [((2, block, columns), BF16)] * 3
+        kept, along, across, both = kernel_call(
+            core_sum, part, [place, chips(keep), chips(got)], after
+        )
+        return kept, direct(along, across, both)
+
+    def halves(kept, got, columns, after):
+        keep, give = kernel_call(
+            chips_sum,
+            [((block, columns), F32), ((block, columns), BF16)],
+            [place, kept, *got],
+            after,
+        )
+        return keep, flip(give, "seq", 4)
+
+    part = [((groups, block, width), BF16)] * 2
+    middle_grad, mid_keep, mid_give = kernel_call(
+        middle_tap, [((rows, width), BF16)] + part, [place, turned, grad_own, grad_theirs]
+    )
+    mid_keep, mid_got = summed(mid_keep, mid_give, width, None)
+    part = [((groups, block, 2 * width), BF16)] * 2
+    moved, out_keep, out_give = kernel_call(
+        outer_tap,
+        [((rows, width), BF16)] + part,
+        [place, turned, straight, crossed, out_grad_b, other_out_grad, hidden],
+        mid_keep,
+        scratch=[
+            pltpu.VMEM((rows, channels), BF16),
+            pltpu.VMEM((groups, n_sample, block, rows), BF16),
+        ],
+    )
+    (act_give,) = kernel_call(
+        act_given,
+        [((half, channels), BF16)],
+        [place, middle_grad, moved, mid_weight, outer_weight],
+        out_keep,
+    )
+    act_got = flip(act_give, "head")
+    (act_keep,) = kernel_call(
+        act_kept,
+        [((half, channels), F32)],
+        [place, middle_grad, moved, mid_weight, outer_weight],
+        act_give,
+    )
+    out_keep, out_got = summed(out_keep, out_give, 2 * width, act_keep)
+    (input_half,) = kernel_call(
+        input_part,
+        [((half, channels), BF16)],
+        [place, out_grad, act_keep, act_got, slope_feat],
+        out_keep,
+    )
+    input_other = flip(input_half, "head")
+    mid_keep, mid_got = halves(mid_keep, mid_got, width, input_half)
+    out_keep, out_got = halves(out_keep, out_got, 2 * width, mid_keep)
+    (input_grad,) = kernel_call(
+        joined, [((rows, channels), BF16)], [place, input_half, input_other], out_keep
+    )
+    dilated_grad, point_grad = kernel_call(
+        finish,
+        [((3, block, width), F32), ((block, width), F32)],
+        [place, mid_keep, mid_got, out_keep, out_got],
+        input_grad,
+    )
+    dilated_grad = jnp.transpose(dilated_grad, (1, 0, 2))
+    return (input_grad.reshape(samples, positions, channels), dilated_grad, point_grad)
+
+
 def solution(mesh):
     placed = (
         P("sample", "seq", None),

time: 167 us -> 114 us (0.68)
  matrix products: 29.8 us -> 0 us
  waiting for transfers between devices: 81.1 us -> 51.7 us
  Pallas kernels: 0 us -> 27.5 us
  between operations: 14.4 us -> 0.83 us
  other arithmetic: 7.76 us -> 0 us
    dot_general x13 -> x0, matrix products: 29.8 us -> none  [dot(): lax.dot_general(left, right, (contract, ((), ())), preferred_element_type...]
    pallas_call x0 -> x18, Pallas kernels: none -> 27.5 us  [the longest x16 17.1 us: kernel_call(): pl.pallas_call(run, out_shape=[jax.ShapeDtypeStruct(s, d) for s, d in out...]
    ppermute x19, waiting for transfers between devices: 64.1 us -> 41.8 us  [flip(): return lax.ppermute(value, axis, [(i, i ^ step) for i in range(count)])]
    ppermute x2, waiting for transfers between devices: 10.7 us -> 2.53 us  [the longest x1 1.27 us: body(): arrived = lax.ppermute(term, 'seq', pairs)]
    ppermute x1, waiting for transfers between devices: 1.34 us -> 7.41 us  [body(): straight = lax.ppermute(grad_own, 'seq', pairs)]
    all_gather x2 -> x0, waiting for transfers between devices: 4.24 us -> none  [the longest x1 4.24 us: body(): whole_track = lax.all_gather(track_weight, 'sample', axis=0, tiled=True)]
    ppermute x2, starting transfers between devices: 6.49 us -> 2.71 us  [the longest x1 2.65 us: body(): arrived = lax.ppermute(term, 'seq', pairs)]
    select_n x4 -> x0, other arithmetic: 2.14 us -> none  [in_order(): first = jnp.where(bit == 0, own, other)]
  transfers between devices with their start and end apart: 24 -> 22, of which waited for: 15 -> 11; matrix products, arithmetic and copies ran while one was open for 12% -> 2% of each run, Pallas kernels for 0% -> 12%
where the time goes in v2:
time: 114 us
  waiting for transfers between devices  51.7 us (45%)
  starting transfers between devices  27.8 us (24%)
  Pallas kernels  27.5 us (24%)
  local copies, waits for them, and re-layouts  5.88 us (5%)
    ppermute x19, waiting for transfers between devices, flip(): return lax.ppermute(value, axis, [(i, i ^ step) for i in range(count)])  41.8 us
    ppermute x19, starting transfers between devices, flip(): return lax.ppermute(value, axis, [(i, i ^ step) for i in range(count)])  22.6 us
    pallas_call x16, Pallas kernels, kernel_call(): pl.pallas_call(run, out_shape=[jax.ShapeDtypeStruct(s, d) for s, d in out...  17.1 us
    pallas_call x1, Pallas kernels, body(): pl.pallas_call(tracks, grid_spec=pltpu.PrefetchScalarGridSpec(num_scalar_...  8.14 us
    ppermute x1, waiting for transfers between devices, body(): straight = lax.ppermute(grad_own, 'seq', pairs)  7.41 us
    unnamed x12, local copies, waits for them, and re-layouts  3.16 us
    ppermute x1, starting transfers between devices, body(): arrived = lax.ppermute(term, 'seq', pairs)  2.65 us
    ppermute x1, starting transfers between devices, body(): straight = lax.ppermute(grad_own, 'seq', pairs)  2.59 us
  transfers between devices with their start and end apart: 22, of which 11 were waited for; matrix products, arithmetic and copies ran while one was open for 2% of the time, Pallas kernels for 12%

profile of v2, /device:TPU:0, one launch (start us, length us, event | category | flops | bytes accessed | tf_op | source)
XLA Modules:
  0.0 113.7 jit_solution(8093747602997244120)
XLA Ops:
  2.3 2.6 %collective-permute-start.2 = (bf16[768,384]{1,0:T(8,128)(2,1)S(1)}, bf16[768,384]{1,0:T(8,128)(2,1)S(1)}, u32[]{:S(2)}, u32[]{:S(2)}) collective-permute-start(bf16[768,384]{1,0:T(8,128)(2,1)S(1)} %constant_dynamic-slice_fusion), channel_id=1, source_target_pairs={{0,2},{2,0},{1,3},{3,1},{4,6},{6,4},{5,7},{7,5},{8,10},{10,8},{9,1... | collective-permute-start | bytes 1769480 | tf_op jit(solution)/shard_map/ppermute | solution.py:33
  5.0 2.0 %copy-done = bf16[1536,3,384]{2,0,1:T(8,128)(2,1)S(1)} copy-done((bf16[1536,3,384]{2,0,1:T(8,128)(2,1)S(1)}, bf16[1536,3,384]{2,0,1:T(8,128)(2,1)}, u32[]{:S(2)}) %copy-start) | copy-done | bytes 3538968
  7.0 2.2 %outer_term.1 = (bf16[256,1536]{1,0:T(8,128)(2,1)S(1)}, bf16[256,384]{1,0:T(8,128)(2,1)S(1)}) custom-call(s32[6]{0:T(128)S(1)} %stack.27.place.refs_0_, bf16[256,1536]{1,0:T(8,128)(2,1)S(1)} %bitcast.21, bf16[3,1536,384]{2,1,0:T(8,128)(2,1)S(1)} %bitcast.19), custom_call_target="tpu_custom_call" | custom-call | tf_op jit(solution)/shard_map/outer_term/pallas_call | solution.py:418
  9.2 2.6 %collective-permute-start = (bf16[256,384]{1,0:T(8,128)(2,1)S(1)}, bf16[256,384]{1,0:T(8,128)(2,1)S(1)}, u32[]{:S(2)}, u32[]{:S(2)}) collective-permute-start(bf16[256,384]{1,0:T(8,128)(2,1)S(1)} %get-tuple-element.42), channel_id=1, source_target_pairs={{0,16},{4,20},{8,24},{12,28},{16,0},{20,4},{24,8},{28,12},{1,17},{... | collective-permute-start | bytes 589832 | tf_op jit(solution)/shard_map/ppermute | solution.py:440
  11.9 7.0 %collective-permute-done.2.point_near.refs_4_ = bf16[768,384]{1,0:T(8,128)(2,1)S(1)} collective-permute-done((bf16[768,384]{1,0:T(8,128)(2,1)S(1)}, bf16[768,384]{1,0:T(8,128)(2,1)S(1)}, u32[]{:S(2)}, u32[]{:S(2)}) %collective-permute-start.2) | collective-permute-done | bytes 589856 | tf_op jit(solution)/shard_map/ppermute | solution.py:33
  20.1 1.3 %collective-permute-done.refs_2_ = bf16[256,384]{1,0:T(8,128)(2,1)S(1)} collective-permute-done((bf16[256,384]{1,0:T(8,128)(2,1)S(1)}, bf16[256,384]{1,0:T(8,128)(2,1)S(1)}, u32[]{:S(2)}, u32[]{:S(2)}) %collective-permute-start) | collective-permute-done | bytes 196640 | tf_op jit(solution)/shard_map/ppermute | solution.py:440
  22.6 1.3 %own_hidden.1 = (bf16[256,384]{1,0:T(8,128)(2,1)S(1)}, f32[128,384]{1,0:T(8,128)S(1)}, f32[256,1536]{1,0:T(8,128)S(1)}) custom-call(s32[6]{0:T(128)S(1)} %stack.27.place.refs_0_, f32[256,384]{1,0:T(8,128)S(1)} %get-tuple-element.44.refs_1_, bf16[256,1536]{1,0:T(8,128)(2,1)S(1)} %bitcast.22, bf16[1536,384]{1,0:T(8,128)(2,1)S(1)} %copy-done.1), custom_call_target="tpu_custom_call" | custom-call | tf_op jit(solution)/shard_map/own_hidden/pallas_call | solution.py:197
  23.8 4.4 %collective-permute-done.1.other_middle.refs_1_ = bf16[256,384]{1,0:T(8,128)(2,1)S(1)} collective-permute-done((bf16[256,384]{1,0:T(8,128)(2,1)S(1)}, bf16[256,384]{1,0:T(8,128)(2,1)S(1)}, u32[]{:S(2)}, u32[]{:S(2)}) %collective-permute-start.1) | collective-permute-done | bytes 196640 | tf_op jit(solution)/shard_map/ppermute | solution.py:33
  28.2 8.1 %tracks.1 = (f32[128,1536]{1,0:T(8,128)S(1)}, bf16[128,1536]{1,0:T(8,128)(2,1)S(1)}) custom-call(s32[6]{0:T(128)S(1)} %stack.27.place.refs_0_, f32[256,1536]{1,0:T(8,128)S(1)} %get-tuple-element.45.block, bf16[256,384]{1,0:T(8,128)(2,1)S(1)} %collective-permute-done.1.other_middle.refs_1_, bf16[768,384]{1,0:T(8,128)(2,1)S(1)} %collective-permute-done.2.point_near.refs_4_, ...), custom_call_target="tpu_custom_call" | custom-call | tf_op jit(solution)/shard_map/tracks/pallas_call | solution.py:462
  36.4 1.7 %collective-permute-start.5 = (bf16[128,1536]{1,0:T(8,128)(2,1)S(1)}, bf16[128,1536]{1,0:T(8,128)(2,1)S(1)}, u32[]{:S(2)}, u32[]{:S(2)}) collective-permute-start(bf16[128,1536]{1,0:T(8,128)(2,1)S(1)} %get-tuple-element.48), channel_id=1, source_target_pairs={{0,2},{2,0},{1,3},{3,1},{4,6},{6,4},{5,7},{7,5},{8,10},{10,8},{9,1... | collective-permute-start | bytes 1179656 | tf_op jit(solution)/shard_map/ppermute | solution.py:33
  39.3 7.8 %collective-permute-done.5.refs_2_ = bf16[128,1536]{1,0:T(8,128)(2,1)S(1)} collective-permute-done((bf16[128,1536]{1,0:T(8,128)(2,1)S(1)}, bf16[128,1536]{1,0:T(8,128)(2,1)S(1)}, u32[]{:S(2)}, u32[]{:S(2)}) %collective-permute-start.5) | collective-permute-done | bytes 393248 | tf_op jit(solution)/shard_map/ppermute | solution.py:33
  48.2 1.8 %collective-permute-start.6 = (bf16[128,384]{1,0:T(8,128)(2,1)S(1)}, bf16[128,384]{1,0:T(8,128)(2,1)S(1)}, u32[]{:S(2)}, u32[]{:S(2)}) collective-permute-start(bf16[128,384]{1,0:T(8,128)(2,1)S(1)} %get-tuple-element.53), channel_id=1, source_target_pairs={{0,2},{2,0},{1,3},{3,1},{4,6},{6,4},{5,7},{7,5},{8,10},{10,8},{9,1... | collective-permute-start | bytes 294920 | tf_op jit(solution)/shard_map/ppermute | solution.py:33
  50.0 2.9 %collective-permute-done.6.refs_3_ = bf16[128,384]{1,0:T(8,128)(2,1)S(1)} collective-permute-done((bf16[128,384]{1,0:T(8,128)(2,1)S(1)}, bf16[128,384]{1,0:T(8,128)(2,1)S(1)}, u32[]{:S(2)}, u32[]{:S(2)}) %collective-permute-start.6) | collective-permute-done | bytes 98336 | tf_op jit(solution)/shard_map/ppermute | solution.py:33
  54.1 1.8 %collective-permute-start.9 = (bf16[128,1536]{1,0:T(8,128)(2,1)S(1)}, bf16[128,1536]{1,0:T(8,128)(2,1)S(1)}, u32[]{:S(2)}, u32[]{:S(2)}) collective-permute-start(bf16[128,1536]{1,0:T(8,128)(2,1)S(1)} %get-tuple-element.55.refs_4_), channel_id=1, source_target_pairs={{0,2},{2,0},{1,3},{3,1},{4,6},{6,4},{5,7},{7,5},{8,10},{10,8},{9,1... | collective-permute-start | bytes 1179656 | tf_op jit(solution)/shard_map/ppermute | solution.py:33
  55.9 2.6 %collective-permute-start.7 = (bf16[128,384]{1,0:T(8,128)(2,1)S(1)}, bf16[128,384]{1,0:T(8,128)(2,1)S(1)}, u32[]{:S(2)}, u32[]{:S(2)}) collective-permute-start(bf16[128,384]{1,0:T(8,128)(2,1)S(1)} %get-tuple-element.52.refs_2_), channel_id=1, source_target_pairs={{0,16},{4,20},{8,24},{12,28},{16,0},{20,4},{24,8},{28,12},{1,17},{... | collective-permute-start | bytes 294920 | tf_op jit(solution)/shard_map/ppermute | solution.py:506
  59.3 7.4 %collective-permute-done.7.refs_2_ = bf16[128,384]{1,0:T(8,128)(2,1)S(1)} collective-permute-done((bf16[128,384]{1,0:T(8,128)(2,1)S(1)}, bf16[128,384]{1,0:T(8,128)(2,1)S(1)}, u32[]{:S(2)}, u32[]{:S(2)}) %collective-permute-start.7) | collective-permute-done | bytes 98336 | tf_op jit(solution)/shard_map/ppermute | solution.py:506
  66.7 1.3 %collective-permute-done.8.refs_3_ = bf16[128,384]{1,0:T(8,128)(2,1)S(1)} collective-permute-done((bf16[128,384]{1,0:T(8,128)(2,1)S(1)}, bf16[128,384]{1,0:T(8,128)(2,1)S(1)}, u32[]{:S(2)}, u32[]{:S(2)}) %collective-permute-start.8) | collective-permute-done | bytes 98336 | tf_op jit(solution)/shard_map/ppermute | solution.py:507
  68.0 1.6 %outer_tap.1 = (bf16[256,384]{1,0:T(8,128)(2,1)S(1)}, bf16[8,96,768]{2,1,0:T(8,128)(2,1)S(1)}, bf16[8,96,768]{2,1,0:T(8,128)(2,1)S(1)}) custom-call(s32[6]{0:T(128)S(1)} %stack.27.place.refs_0_, bf16[8,2,96,256]{3,2,1,0:T(8,128)(2,1)S(1)} %get-tuple-element.43.refs_3_.refs_1_, bf16[128,384]{1,0:T(8,128)(2,1)S(1)} %collective-permute-done.7.refs_2_, ...), custom_call_target="tpu_custom_call" | custom-call | tf_op jit(solution)/shard_map/outer_tap/pallas_call | solution.py:197
  69.7 1.4 %dynamic-slice_bitcast_fusion.refs_4_ = bf16[1536,384]{1,0:T(8,128)(2,1)S(1)} fusion(bf16[1536,3,384]{2,0,1:T(8,128)(2,1)} %param.6, s32[]{:T(128)} %select_n.9), kind=kLoop, calls=%fused_computation.1 | loop fusion | bytes 2359300 | tf_op jit(solution)/shard_map/jit(dynamic_index_in_dim)/squeeze | solution.py:442
  71.1 1.4 %act_given.1.refs_5_ = bf16[128,1536]{1,0:T(8,128)(2,1)S(1)} custom-call(s32[6]{0:T(128)S(1)} %stack.27.place.refs_0_, bf16[256,384]{1,0:T(8,128)(2,1)S(1)} %get-tuple-element.54.refs_1_, bf16[256,384]{1,0:T(8,128)(2,1)S(1)} %get-tuple-element.60.refs_2_, bf16[1536,384]{1,0:T(8,128)(2,1)S(1)} %slice_bitcast_fusion.refs_2_.refs_3_, ...), custom_call_target="tpu_custom_call" | custom-call | tf_op jit(solution)/shard_map/act_given/pallas_call | solution.py:197
  72.5 1.6 %collective-permute-start.11 = (bf16[128,1536]{1,0:T(8,128)(2,1)S(1)}, bf16[128,1536]{1,0:T(8,128)(2,1)S(1)}, u32[]{:S(2)}, u32[]{:S(2)}) collective-permute-start(bf16[128,1536]{1,0:T(8,128)(2,1)S(1)} %act_given.1.refs_5_), channel_id=1, source_target_pairs={{0,2},{2,0},{1,3},{3,1},{4,6},{6,4},{5,7},{7,5},{8,10},{10,8},{9,1... | collective-permute-start | bytes 1179656 | tf_op jit(solution)/shard_map/ppermute | solution.py:33
  74.1 1.6 %collective-permute-start.17 = (bf16[2,96,384]{2,1,0:T(8,128)(2,1)S(1)}, bf16[2,96,384]{2,1,0:T(8,128)(2,1)S(1)}, u32[]{:S(2)}, u32[]{:S(2)}) collective-permute-start(bf16[2,96,384]{2,1,0:T(8,128)(2,1)S(1)} %get-tuple-element.68), channel_id=1, source_target_pairs={{0,8},{4,12},{8,0},{12,4},{16,24},{20,28},{24,16},{28,20},{1,9},{5... | collective-permute-start | bytes 442376 | tf_op jit(solution)/shard_map/ppermute | solution.py:33
  75.7 1.4 %act_kept.1.refs_3_.refs_2_ = f32[128,1536]{1,0:T(8,128)S(1)} custom-call(s32[6]{0:T(128)S(1)} %stack.27.place.refs_0_, bf16[256,384]{1,0:T(8,128)(2,1)S(1)} %get-tuple-element.54.refs_1_, bf16[256,384]{1,0:T(8,128)(2,1)S(1)} %get-tuple-element.60.refs_2_, bf16[1536,384]{1,0:T(8,128)(2,1)S(1)} %slice_bitcast_fusion.refs_2_.refs_3_, ...), custom_call_target="tpu_custom_call" | custom-call | tf_op jit(solution)/shard_map/act_kept/pallas_call | solution.py:197
  77.1 1.6 %collective-permute-start.18 = (bf16[2,96,384]{2,1,0:T(8,128)(2,1)S(1)}, bf16[2,96,384]{2,1,0:T(8,128)(2,1)S(1)}, u32[]{:S(2)}, u32[]{:S(2)}) collective-permute-start(bf16[2,96,384]{2,1,0:T(8,128)(2,1)S(1)} %get-tuple-element.69), channel_id=1, source_target_pairs={{0,4},{4,0},{8,12},{12,8},{16,20},{20,16},{24,28},{28,24},{1,5},{5... | collective-permute-start | bytes 442376 | tf_op jit(solution)/shard_map/ppermute | solution.py:33
  80.5 3.6 %collective-permute-done.11.refs_3_ = bf16[128,1536]{1,0:T(8,128)(2,1)S(1)} collective-permute-done((bf16[128,1536]{1,0:T(8,128)(2,1)S(1)}, bf16[128,1536]{1,0:T(8,128)(2,1)S(1)}, u32[]{:S(2)}, u32[]{:S(2)}) %collective-permute-start.11) | collective-permute-done | bytes 393248 | tf_op jit(solution)/shard_map/ppermute | solution.py:33
  84.0 2.5 %collective-permute-start.16 = (bf16[2,96,768]{2,1,0:T(8,128)(2,1)S(1)}, bf16[2,96,768]{2,1,0:T(8,128)(2,1)S(1)}, u32[]{:S(2)}, u32[]{:S(2)}) collective-permute-start(bf16[2,96,768]{2,1,0:T(8,128)(2,1)S(1)} %get-tuple-element.67), channel_id=1, source_target_pairs={{0,12},{4,8},{8,4},{12,0},{16,28},{20,24},{24,20},{28,16},{1,13},{... | collective-permute-start | bytes 884744 | tf_op jit(solution)/shard_map/ppermute | solution.py:33
  87.3 1.6 %collective-permute-start.13 = (bf16[128,1536]{1,0:T(8,128)(2,1)S(1)}, bf16[128,1536]{1,0:T(8,128)(2,1)S(1)}, u32[]{:S(2)}, u32[]{:S(2)}) collective-permute-start(bf16[128,1536]{1,0:T(8,128)(2,1)S(1)} %input_part.1.refs_5_.refs_1_), channel_id=1, source_target_pairs={{0,2},{2,0},{1,3},{3,1},{4,6},{6,4},{5,7},{7,5},{8,10},{10,8},{9,1... | collective-permute-start | bytes 1179656 | tf_op jit(solution)/shard_map/ppermute | solution.py:33
  89.3 8.3 %collective-permute-done.19.refs_4_ = bf16[2,96,384]{2,1,0:T(8,128)(2,1)S(1)} collective-permute-done((bf16[2,96,384]{2,1,0:T(8,128)(2,1)S(1)}, bf16[2,96,384]{2,1,0:T(8,128)(2,1)S(1)}, u32[]{:S(2)}, u32[]{:S(2)}) %collective-permute-start.19) | collective-permute-done | bytes 147488 | tf_op jit(solution)/shard_map/ppermute | solution.py:33
  99.3 2.7 %collective-permute-start.21 = (bf16[96,768]{1,0:T(8,128)(2,1)S(1)}, bf16[96,768]{1,0:T(8,128)(2,1)S(1)}, u32[]{:S(2)}, u32[]{:S(2)}) collective-permute-start(bf16[96,768]{1,0:T(8,128)(2,1)S(1)} %get-tuple-element.74), channel_id=1, source_target_pairs={{0,16},{4,20},{8,24},{12,28},{16,0},{20,4},{24,8},{28,12},{1,17},{... | collective-permute-start | bytes 442376 | tf_op jit(solution)/shard_map/ppermute | solution.py:33
  102.3 1.5 %joined.1.refs_5_ = bf16[256,1536]{1,0:T(8,128)(2,1)} custom-call(s32[6]{0:T(128)S(1)} %stack.27.place.refs_0_, bf16[128,1536]{1,0:T(8,128)(2,1)S(1)} %input_part.1.refs_5_.refs_1_, bf16[128,1536]{1,0:T(8,128)(2,1)S(1)} %collective-permute-done.13.refs_2_, f32[96,768]{1,0:T(8,128)S(1)} %get-tuple-element.72.refs_3_), custom_call_target="tpu_custom_call" | custom-call | tf_op jit(solution)/shard_map/joined/pallas_call | solution.py:197
  103.8 7.4 %collective-permute-done.20.refs_2_ = bf16[96,384]{1,0:T(8,128)(2,1)S(1)} collective-permute-done((bf16[96,384]{1,0:T(8,128)(2,1)S(1)}, bf16[96,384]{1,0:T(8,128)(2,1)S(1)}, u32[]{:S(2)}, u32[]{:S(2)}) %collective-permute-start.20) | collective-permute-done | bytes 73760 | tf_op jit(solution)/shard_map/ppermute | solution.py:33
  112.3 1.4 %finish.1 = (f32[3,96,384]{2,1,0:T(8,128)}, f32[96,384]{1,0:T(8,128)}) custom-call(s32[6]{0:T(128)S(1)} %stack.27.place.refs_0_, f32[96,384]{1,0:T(8,128)S(1)} %get-tuple-element.71.refs_5_.refs_1_, bf16[96,384]{1,0:T(8,128)(2,1)S(1)} %collective-permute-done.20.refs_2_, f32[96,768]{1,0:T(8,128)S(1)} %get-tuple-element.72.refs_3_, ...), custom_call_target="tpu_custom_call" | custom-call | tf_op jit(solution)/shard_map/finish/pallas_call | solution.py:197
  (46 shorter events, 14.5 us)
Async XLA Ops:
  0.6 4.4 %copy-start.2 = (bf16[1,256,1536]{2,1,0:T(8,128)(2,1)S(1)}, bf16[1,256,1536]{2,1,0:T(8,128)(2,1)}, u32[]{:S(2)}) copy-start(bf16[1,256,1536]{2,1,0:T(8,128)(2,1)} %param.5) | copy-start | bytes 2359300
  0.6 27.6 %collective-permute-start.4 = (bf16[768,1920]{1,0:T(8,128)(2,1)}, bf16[768,1920]{1,0:T(8,128)(2,1)}, u32[]{:S(2)}, u32[]{:S(2)}) collective-permute-start(bf16[768,1920]{1,0:T(8,128)(2,1)} %near.1), channel_id=1, source_target_pairs={{0,1},{1,0},{2,3},{3,2},{4,5},{5,4},{6,7},{7,6},{8,9},{9,8},{10,11... | collective-permute-start | bytes 8847368 | tf_op jit(solution)/shard_map/ppermute | solution.py:33
  2.3 16.6 %collective-permute-start.2 = (bf16[768,384]{1,0:T(8,128)(2,1)S(1)}, bf16[768,384]{1,0:T(8,128)(2,1)S(1)}, u32[]{:S(2)}, u32[]{:S(2)}) collective-permute-start(bf16[768,384]{1,0:T(8,128)(2,1)S(1)} %constant_dynamic-slice_fusion), channel_id=1, source_target_pairs={{0,2},{2,0},{1,3},{3,1},{4,6},{6,4},{5,7},{7,5},{8,10},{10,8},{9,1... | collective-permute-start | bytes 1769480 | tf_op jit(solution)/shard_map/ppermute | solution.py:33
  5.0 2.0 %copy-start = (bf16[1536,3,384]{2,0,1:T(8,128)(2,1)S(1)}, bf16[1536,3,384]{2,0,1:T(8,128)(2,1)}, u32[]{:S(2)}) copy-start(bf16[1536,3,384]{2,0,1:T(8,128)(2,1)} %param.6) | copy-start | bytes 10616836
  9.2 12.1 %collective-permute-start = (bf16[256,384]{1,0:T(8,128)(2,1)S(1)}, bf16[256,384]{1,0:T(8,128)(2,1)S(1)}, u32[]{:S(2)}, u32[]{:S(2)}) collective-permute-start(bf16[256,384]{1,0:T(8,128)(2,1)S(1)} %get-tuple-element.42), channel_id=1, source_target_pairs={{0,16},{4,20},{8,24},{12,28},{16,0},{20,4},{24,8},{28,12},{1,17},{... | collective-permute-start | bytes 589832 | tf_op jit(solution)/shard_map/ppermute | solution.py:440
  18.8 9.4 %collective-permute-start.3 = (bf16[768,384]{1,0:T(8,128)(2,1)S(1)}, bf16[768,384]{1,0:T(8,128)(2,1)S(1)}, u32[]{:S(2)}, u32[]{:S(2)}) collective-permute-start(bf16[768,384]{1,0:T(8,128)(2,1)S(1)} %collective-permute-done.2.point_near.refs_4_), channel_id=1, source_target_pairs={{0,1},{1,0},{2,3},{3,2},{4,5},{5,4},{6,7},{7,6},{8,9},{9,8},{10,11... | collective-permute-start | bytes 1769480 | tf_op jit(solution)/shard_map/ppermute | solution.py:33
  18.8 9.4 %copy-start.4 = (bf16[768,1920]{1,0:T(8,128)(2,1)S(1)}, bf16[768,1920]{1,0:T(8,128)(2,1)}, u32[]{:S(2)}) copy-start(bf16[768,1920]{1,0:T(8,128)(2,1)} %near.1) | copy-start | bytes 8847364
  20.1 2.5 %copy-start.1 = (bf16[1536,384]{1,0:T(8,128)(2,1)S(1)}, bf16[1536,384]{1,0:T(8,128)(2,1)}, u32[]{:S(2)}) copy-start(bf16[1536,384]{1,0:T(8,128)(2,1)} %refs_3_.3) | copy-start | bytes 3538948
  22.0 6.2 %collective-permute-start.1 = (bf16[256,384]{1,0:T(8,128)(2,1)S(1)}, bf16[256,384]{1,0:T(8,128)(2,1)S(1)}, u32[]{:S(2)}, u32[]{:S(2)}) collective-permute-start(bf16[256,384]{1,0:T(8,128)(2,1)S(1)} %get-tuple-element.46), channel_id=1, source_target_pairs={{0,2},{2,0},{1,3},{3,1},{4,6},{6,4},{5,7},{7,5},{8,10},{10,8},{9,1... | collective-permute-start | bytes 589832 | tf_op jit(solution)/shard_map/ppermute | solution.py:33
  22.6 5.7 %copy-start.5 = (bf16[1,256,1920]{2,1,0:T(8,128)(2,1)S(1)}, bf16[1,256,1920]{2,1,0:T(8,128)(2,1)}, u32[]{:S(2)}) copy-start(bf16[1,256,1920]{2,1,0:T(8,128)(2,1)} %param.9) | copy-start | bytes 2949124
  36.4 10.7 %collective-permute-start.5 = (bf16[128,1536]{1,0:T(8,128)(2,1)S(1)}, bf16[128,1536]{1,0:T(8,128)(2,1)S(1)}, u32[]{:S(2)}, u32[]{:S(2)}) collective-permute-start(bf16[128,1536]{1,0:T(8,128)(2,1)S(1)} %get-tuple-element.48), channel_id=1, source_target_pairs={{0,2},{2,0},{1,3},{3,1},{4,6},{6,4},{5,7},{7,5},{8,10},{10,8},{9,1... | collective-permute-start | bytes 1179656 | tf_op jit(solution)/shard_map/ppermute | solution.py:33
  48.2 4.7 %collective-permute-start.6 = (bf16[128,384]{1,0:T(8,128)(2,1)S(1)}, bf16[128,384]{1,0:T(8,128)(2,1)S(1)}, u32[]{:S(2)}, u32[]{:S(2)}) collective-permute-start(bf16[128,384]{1,0:T(8,128)(2,1)S(1)} %get-tuple-element.53), channel_id=1, source_target_pairs={{0,2},{2,0},{1,3},{3,1},{4,6},{6,4},{5,7},{7,5},{8,10},{10,8},{9,1... | collective-permute-start | bytes 294920 | tf_op jit(solution)/shard_map/ppermute | solution.py:33
  54.1 4.5 %collective-permute-start.10 = (bf16[8,96,384]{2,1,0:T(8,128)(2,1)S(1)}, bf16[8,96,384]{2,1,0:T(8,128)(2,1)S(1)}, u32[]{:S(2)}, u32[]{:S(2)}) collective-permute-start(bf16[8,96,384]{2,1,0:T(8,128)(2,1)S(1)} %get-tuple-element.58), channel_id=1, source_target_pairs={{0,1},{1,0},{2,3},{3,2},{4,5},{5,4},{6,7},{7,6},{8,9},{9,8},{10,11... | collective-permute-start | bytes 1769480 | tf_op jit(solution)/shard_map/ppermute | solution.py:33
  54.1 13.8 %collective-permute-start.9 = (bf16[128,1536]{1,0:T(8,128)(2,1)S(1)}, bf16[128,1536]{1,0:T(8,128)(2,1)S(1)}, u32[]{:S(2)}, u32[]{:S(2)}) collective-permute-start(bf16[128,1536]{1,0:T(8,128)(2,1)S(1)} %get-tuple-element.55.refs_4_), channel_id=1, source_target_pairs={{0,2},{2,0},{1,3},{3,1},{4,6},{6,4},{5,7},{7,5},{8,10},{10,8},{9,1... | collective-permute-start | bytes 1179656 | tf_op jit(solution)/shard_map/ppermute | solution.py:33
  55.9 10.8 %collective-permute-start.7 = (bf16[128,384]{1,0:T(8,128)(2,1)S(1)}, bf16[128,384]{1,0:T(8,128)(2,1)S(1)}, u32[]{:S(2)}, u32[]{:S(2)}) collective-permute-start(bf16[128,384]{1,0:T(8,128)(2,1)S(1)} %get-tuple-element.52.refs_2_), channel_id=1, source_target_pairs={{0,16},{4,20},{8,24},{12,28},{16,0},{20,4},{24,8},{28,12},{1,17},{... | collective-permute-start | bytes 294920 | tf_op jit(solution)/shard_map/ppermute | solution.py:506
  58.5 9.4 %collective-permute-start.8 = (bf16[128,384]{1,0:T(8,128)(2,1)S(1)}, bf16[128,384]{1,0:T(8,128)(2,1)S(1)}, u32[]{:S(2)}, u32[]{:S(2)}) collective-permute-start(bf16[128,384]{1,0:T(8,128)(2,1)S(1)} %get-tuple-element.53), channel_id=1, source_target_pairs={{0,18},{2,16},{4,22},{6,20},{8,26},{10,24},{12,30},{14,28},{16,2},... | collective-permute-start | bytes 294920 | tf_op jit(solution)/shard_map/ppermute | solution.py:507
  69.6 9.1 %collective-permute-start.12 = (bf16[8,96,768]{2,1,0:T(8,128)(2,1)S(1)}, bf16[8,96,768]{2,1,0:T(8,128)(2,1)S(1)}, u32[]{:S(2)}, u32[]{:S(2)}) collective-permute-start(bf16[8,96,768]{2,1,0:T(8,128)(2,1)S(1)} %get-tuple-element.63), channel_id=1, source_target_pairs={{0,1},{1,0},{2,3},{3,2},{4,5},{5,4},{6,7},{7,6},{8,9},{9,8},{10,11... | collective-permute-start | bytes 3538952 | tf_op jit(solution)/shard_map/ppermute | solution.py:33
  72.5 11.6 %collective-permute-start.11 = (bf16[128,1536]{1,0:T(8,128)(2,1)S(1)}, bf16[128,1536]{1,0:T(8,128)(2,1)S(1)}, u32[]{:S(2)}, u32[]{:S(2)}) collective-permute-start(bf16[128,1536]{1,0:T(8,128)(2,1)S(1)} %act_given.1.refs_5_), channel_id=1, source_target_pairs={{0,2},{2,0},{1,3},{3,1},{4,6},{6,4},{5,7},{7,5},{8,10},{10,8},{9,1... | collective-permute-start | bytes 1179656 | tf_op jit(solution)/shard_map/ppermute | solution.py:33
  74.1 13.2 %collective-permute-start.17 = (bf16[2,96,384]{2,1,0:T(8,128)(2,1)S(1)}, bf16[2,96,384]{2,1,0:T(8,128)(2,1)S(1)}, u32[]{:S(2)}, u32[]{:S(2)}) collective-permute-start(bf16[2,96,384]{2,1,0:T(8,128)(2,1)S(1)} %get-tuple-element.68), channel_id=1, source_target_pairs={{0,8},{4,12},{8,0},{12,4},{16,24},{20,28},{24,16},{28,20},{1,9},{5... | collective-permute-start | bytes 442376 | tf_op jit(solution)/shard_map/ppermute | solution.py:33
  77.1 11.8 %collective-permute-start.18 = (bf16[2,96,384]{2,1,0:T(8,128)(2,1)S(1)}, bf16[2,96,384]{2,1,0:T(8,128)(2,1)S(1)}, u32[]{:S(2)}, u32[]{:S(2)}) collective-permute-start(bf16[2,96,384]{2,1,0:T(8,128)(2,1)S(1)} %get-tuple-element.69), channel_id=1, source_target_pairs={{0,4},{4,0},{8,12},{12,8},{16,20},{20,16},{24,28},{28,24},{1,5},{5... | collective-permute-start | bytes 442376 | tf_op jit(solution)/shard_map/ppermute | solution.py:33
  79.5 18.8 %collective-permute-start.14 = (bf16[2,96,768]{2,1,0:T(8,128)(2,1)S(1)}, bf16[2,96,768]{2,1,0:T(8,128)(2,1)S(1)}, u32[]{:S(2)}, u32[]{:S(2)}) collective-permute-start(bf16[2,96,768]{2,1,0:T(8,128)(2,1)S(1)} %get-tuple-element.65), channel_id=1, source_target_pairs={{0,8},{4,12},{8,0},{12,4},{16,24},{20,28},{24,16},{28,20},{1,9},{5... | collective-permute-start | bytes 884744 | tf_op jit(solution)/shard_map/ppermute | solution.py:33
  79.9 18.7 %collective-permute-start.15 = (bf16[2,96,768]{2,1,0:T(8,128)(2,1)S(1)}, bf16[2,96,768]{2,1,0:T(8,128)(2,1)S(1)}, u32[]{:S(2)}, u32[]{:S(2)}) collective-permute-start(bf16[2,96,768]{2,1,0:T(8,128)(2,1)S(1)} %get-tuple-element.66), channel_id=1, source_target_pairs={{0,4},{4,0},{8,12},{12,8},{16,20},{20,16},{24,28},{28,24},{1,5},{5... | collective-permute-start | bytes 884744 | tf_op jit(solution)/shard_map/ppermute | solution.py:33
  84.0 14.6 %collective-permute-start.16 = (bf16[2,96,768]{2,1,0:T(8,128)(2,1)S(1)}, bf16[2,96,768]{2,1,0:T(8,128)(2,1)S(1)}, u32[]{:S(2)}, u32[]{:S(2)}) collective-permute-start(bf16[2,96,768]{2,1,0:T(8,128)(2,1)S(1)} %get-tuple-element.67), channel_id=1, source_target_pairs={{0,12},{4,8},{8,4},{12,0},{16,28},{20,24},{24,20},{28,16},{1,13},{... | collective-permute-start | bytes 884744 | tf_op jit(solution)/shard_map/ppermute | solution.py:33
  87.3 15.0 %collective-permute-start.13 = (bf16[128,1536]{1,0:T(8,128)(2,1)S(1)}, bf16[128,1536]{1,0:T(8,128)(2,1)S(1)}, u32[]{:S(2)}, u32[]{:S(2)}) collective-permute-start(bf16[128,1536]{1,0:T(8,128)(2,1)S(1)} %input_part.1.refs_5_.refs_1_), channel_id=1, source_target_pairs={{0,2},{2,0},{1,3},{3,1},{4,6},{6,4},{5,7},{7,5},{8,10},{10,8},{9,1... | collective-permute-start | bytes 1179656 | tf_op jit(solution)/shard_map/ppermute | solution.py:33
  88.9 8.7 %collective-permute-start.19 = (bf16[2,96,384]{2,1,0:T(8,128)(2,1)S(1)}, bf16[2,96,384]{2,1,0:T(8,128)(2,1)S(1)}, u32[]{:S(2)}, u32[]{:S(2)}) collective-permute-start(bf16[2,96,384]{2,1,0:T(8,128)(2,1)S(1)} %get-tuple-element.70), channel_id=1, source_target_pairs={{0,12},{4,8},{8,4},{12,0},{16,28},{20,24},{24,20},{28,16},{1,13},{... | collective-permute-start | bytes 442376 | tf_op jit(solution)/shard_map/ppermute | solution.py:33
  99.3 11.9 %collective-permute-start.21 = (bf16[96,768]{1,0:T(8,128)(2,1)S(1)}, bf16[96,768]{1,0:T(8,128)(2,1)S(1)}, u32[]{:S(2)}, u32[]{:S(2)}) collective-permute-start(bf16[96,768]{1,0:T(8,128)(2,1)S(1)} %get-tuple-element.74), channel_id=1, source_target_pairs={{0,16},{4,20},{8,24},{12,28},{16,0},{20,4},{24,8},{28,12},{1,17},{... | collective-permute-start | bytes 442376 | tf_op jit(solution)/shard_map/ppermute | solution.py:33
  102.0 9.2 %collective-permute-start.20 = (bf16[96,384]{1,0:T(8,128)(2,1)S(1)}, bf16[96,384]{1,0:T(8,128)(2,1)S(1)}, u32[]{:S(2)}, u32[]{:S(2)}) collective-permute-start(bf16[96,384]{1,0:T(8,128)(2,1)S(1)} %get-tuple-element.73), channel_id=1, source_target_pairs={{0,16},{4,20},{8,24},{12,28},{16,0},{20,4},{24,8},{28,12},{1,17},{... | collective-permute-start | bytes 221192 | tf_op jit(solution)/shard_map/ppermute | solution.py:33
  111.2 1.1 copy-start.3

commit v3 on v1

--- a/solution.py
+++ b/solution.py
@@ -1,11 +1,15 @@
 import jax
 import jax.numpy as jnp
 from jax import lax
+from jax.experimental import pallas as pl
+from jax.experimental.pallas import tpu as pltpu
 from jax.sharding import PartitionSpec as P
 
 DILATION_STEP = 1024
 BF16 = jnp.bfloat16
 F32 = jnp.float32
+VMEM = 24 * 2**20
+LITTLE = pl.CostEstimate(flops=1, bytes_accessed=1, transcendentals=0)
 
 
 def gelu_value(value):
@@ -47,7 +51,7 @@
     return count.bit_length() - 1
 
 
-def body(features, dilated_weight, point_weight, track_weight, track_cotangent):
+def general(features, dilated_weight, point_weight, track_weight, track_cotangent):
     samples, positions, channels = features.shape
     rows = samples * positions
     half = rows // 2
@@ -174,6 +178,404 @@
     return (input_grad.reshape(samples, positions, channels), dilated_grad, point_grad)
 
 
+def wide(ref):
+    return ref[...].astype(F32)
+
+
+def kernel_call(kernel, outs, ins, after=None, scratch=(), spaces={}):
+    place, arrays = ins[0], list(ins[1:])
+    in_specs = [pl.BlockSpec(memory_space=pltpu.SMEM)]
+    in_specs += [
+        pl.BlockSpec(memory_space=spaces.get(k + 1, pltpu.VMEM)) for k in range(len(arrays))
+    ]
+    number = len(arrays) + 1
+    if after is not None:
+        arrays.append(after)
+        in_specs.append(pl.BlockSpec(memory_space=pl.ANY))
+
+    def run(*refs):
+        given = refs[:number]
+        kernel(*given, *refs[len(in_specs):])
+
+    return pl.pallas_call(
+        run,
+        out_shape=[jax.ShapeDtypeStruct(s, d) for s, d in outs],
+        in_specs=in_specs,
+        out_specs=[pl.BlockSpec(memory_space=pltpu.VMEM)] * len(outs),
+        scratch_shapes=list(scratch),
+        compiler_params=pltpu.CompilerParams(vmem_limit_bytes=VMEM),
+        cost_estimate=LITTLE,
+        name=kernel.__name__,
+    )(place, *arrays)
+
+
+def in_hbm(value):
+    return pltpu.with_memory_space_constraint(value, pltpu.HBM)
+
+
+NN = ((1,), (0,))
+NT = ((1,), (1,))
+HEAD, SAMPLE, TOP, MID, LOWEST = 1, 2, 3, 4, 5
+
+
+def outer_term(place, feat, taps, acted, term, rows, weight, sems):
+    steps = sems.shape[1]
+    depth = rows.shape[1] // steps
+    parts = [pl.ds(k * depth, depth) for k in range(steps)]
+    feats = [
+        pltpu.make_async_copy(feat.at[:, part], rows.at[:, part], sems.at[0, k])
+        for k, part in enumerate(parts)
+    ]
+    weights = [
+        pltpu.make_async_copy(taps.at[place[0], part], weight.at[part], sems.at[1, k])
+        for k, part in enumerate(parts)
+    ]
+    for pair in zip(feats, weights):
+        for copy in pair:
+            copy.start()
+    total = None
+    for copy, coming, part in zip(feats, weights, parts):
+        copy.wait()
+        act = gelu_value(rows[:, part].astype(F32)).astype(BF16)
+        acted[:, part] = act
+        coming.wait()
+        value = dot(act, weight[part, :], NN)
+        total = value if total is None else total + value
+    term[...] = total.astype(BF16)
+
+
+def piece_of(place, point, piece):
+    number = piece.shape[0]
+    piece[...] = point[pl.ds(pl.multiple_of(place[SAMPLE] * number, number), number), :]
+
+
+def middle_term(place, acted, weight, middle, kept, given):
+    act = acted[...]
+    middle[...] = dot(act, weight[1], NN)
+    part_channels(place, act.T, kept, given)
+
+
+def part_channels(place, turned, kept, given):
+    groups, block, rows = kept.shape
+    split = turned.reshape(groups, 2, block, rows)
+    first = place[SAMPLE] == 0
+    kept[...] = jnp.where(first, split[:, 0], split[:, 1])
+    given[...] = jnp.where(first, split[:, 1], split[:, 0])
+
+
+def add_terms(place, middle, arrived, total, sent):
+    value = middle[...] + wide(arrived)
+    total[...] = value
+    sent[...] = value.astype(BF16)
+
+
+def own_hidden(place, middle, feat, point, hidden, slope, block):
+    half = slope.shape[0]
+    hid = gelu_value(middle[...]).astype(BF16)
+    hidden[...] = hid
+    own = pl.ds(pl.multiple_of(place[HEAD] * half, half), half)
+    slope[...] = gelu_slope(middle[own, :])
+    block[...] = wide(feat) + dot(hid, point[...], NT)
+
+
+def tracks(place, block, other_middle, near, far, cotangent, *rest):
+    *points, keep, give, block_b, grads = rest
+    sample = place[SAMPLE]
+    half = keep.shape[0]
+    piece = block_b.shape[2]
+    width = other_middle.shape[1]
+    own = pl.ds(pl.multiple_of(place[HEAD] * half, half), half)
+    theirs = pl.ds(pl.multiple_of((1 - place[HEAD]) * half, half), half)
+
+    def turned(ref, columns):
+        return jnp.concatenate([ref[theirs, columns], ref[own, columns]], axis=0)
+
+    hid = gelu_value(turned(other_middle, slice(None)).astype(F32)).astype(BF16)
+    ahead = 0
+    for point in points:
+        number = point.shape[0]
+        which, column = (sample, ahead) if ahead < piece else (1 - sample, ahead - piece)
+        columns = pl.ds(pl.multiple_of(which * piece + column, number), number)
+        value = turned(block, columns) + dot(hid, point[...], NT)
+        block_b[which, :, column : column + number] = value.astype(BF16)
+        ahead += number
+    number = near.shape[1]
+    tile = width if number % width == 0 else number
+    for start in range(0, number, tile):
+        columns = slice(start, start + tile)
+        scores = dot(block_b[sample], near[:, columns], NN)
+        scores += dot(block_b[1 - sample], far[:, columns], NN)
+        cot = turned(cotangent, columns).astype(F32)
+        grads[:, columns] = (cot * jax.nn.sigmoid(scores)).astype(BF16)
+    for which, weight in ((sample, near), (1 - sample, far)):
+        columns = pl.ds(pl.multiple_of(which * piece, piece), piece)
+        value = dot(grads[...], weight[...], NT)
+        give[:, columns] = value[:half].astype(BF16)
+        keep[:, columns] = value[half:]
+
+
+def slopes(place, other_middle, feat, slope_other, slope_feat):
+    half = slope_other.shape[0]
+    own = pl.ds(pl.multiple_of(place[HEAD] * half, half), half)
+    slope_other[...] = gelu_slope(other_middle[own, :].astype(F32))
+    slope_feat[...] = gelu_slope(feat[own, :].astype(F32))
+
+
+def middle_grads(place, keep, theirs, point, slope, slope_other, *rest):
+    *points, out_grad, both, grad_own, grad_other = rest
+    sample = place[SAMPLE]
+    channels = keep.shape[1]
+    piece = channels // 2
+    total = keep[...] + wide(theirs)
+    out_grad[...] = total
+    total_b = total.astype(BF16)
+    both[:, :channels] = total_b
+    grad_own[...] = (dot(total_b, point[...], NN) * slope[...]).astype(BF16)
+    other, ahead = None, 0
+    for part in points:
+        number = part.shape[0]
+        which, column = (sample, ahead) if ahead < piece else (1 - sample, ahead - piece)
+        left = both[:, pl.ds(pl.multiple_of(which * piece + column, number), number)]
+        value = dot(left, part[...], NN)
+        other = value if other is None else other + value
+        ahead += number
+    other = (other * slope_other[...]).astype(BF16)
+    grad_other[...] = other
+    both[:, channels:] = other
+
+
+def assembled(field, own, theirs, head):
+    half = field.shape[0] // 2
+    field[pl.ds(pl.multiple_of(head * half, half), half), :] = own
+    field[pl.ds(pl.multiple_of((1 - head) * half, half), half), :] = theirs
+
+
+def gathered(
+    place, both, got, grad_own, straight, crossed, middle_grad, moved, kept, given, whole,
+):
+    channels = whole.shape[1]
+    groups = kept.shape[0]
+    assembled(middle_grad, grad_own[...], got[:, channels:], place[HEAD])
+    assembled(moved, straight[...], crossed[...], place[HEAD])
+    assembled(whole, both[:, :channels], got[:, :channels], place[HEAD])
+    part_channels(place, whole[...].T, kept, given.at[:groups])
+    block, rows = kept.shape[1:]
+    number = middle_grad.shape[1] // block
+    shape = (number, block, rows)
+    given[groups : groups + number] = middle_grad[...].T.reshape(shape)
+    given[groups + number :] = moved[...].T.reshape(shape)
+
+
+def products(
+    place, acts, other_acts, outs, pack, middle_grad, moved, hidden, other_hidden,
+    keep, along, across, both,
+):
+    groups, block, rows = acts.shape
+    width = hidden.shape[1]
+    number = width // block
+    half = groups // 2
+    other_mid = pack[groups : groups + number].reshape(width, rows)
+    other_moved = pack[groups + number :].reshape(width, rows)
+    mid, lowest = place[MID], place[LOWEST]
+
+    for i, j, out in (
+        (1 - mid, 1 - lowest, both),
+        (1 - mid, lowest, along),
+        (mid, 1 - lowest, across),
+        (mid, lowest, keep),
+    ):
+        at = 2 * i + j
+
+        def left(ref):
+            return jnp.concatenate([ref[at], ref[half + at]], axis=0)
+
+        own, other = left(acts), left(other_acts)
+        values = (
+            dot(own, moved[...], NN) + dot(other, other_moved, NT),
+            dot(own, middle_grad[...], NN) + dot(other, other_mid, NT),
+            dot(left(outs), hidden[...], NN) + dot(left(pack), other_hidden[...], NN),
+        )
+        for k, value in enumerate(values):
+            shape = (2, block, width)
+            out[:, :, k * width : (k + 1) * width] = value.astype(out.dtype).reshape(shape)
+
+
+def act_given(place, middle_grad, moved, weight, give):
+    half = give.shape[0]
+    theirs = pl.ds(pl.multiple_of((1 - place[HEAD]) * half, half), half)
+    value = dot(middle_grad[theirs, :], weight[1], NT)
+    give[...] = (value + dot(moved[theirs, :], weight[place[0]], NT)).astype(BF16)
+
+
+def act_kept(place, middle_grad, moved, weight, keep):
+    half = keep.shape[0]
+    own = pl.ds(pl.multiple_of(place[HEAD] * half, half), half)
+    value = dot(middle_grad[own, :], weight[1], NT)
+    keep[...] = value + dot(moved[own, :], weight[place[0]], NT)
+
+
+def chips_sum(place, kept, along, across, both, keep, give):
+    def part(i):
+        total = kept[i] + along[i].astype(F32)
+        return total + across[i].astype(F32) + both[i].astype(F32)
+
+    give[...] = part(1 - place[TOP]).astype(BF16)
+    keep[...] = part(place[TOP])
+
+
+def input_part(place, out_grad, kept, got, slope_feat, result):
+    result[...] = (out_grad[...] + (kept[...] + wide(got)) * slope_feat[...]).astype(BF16)
+
+
+def finish(place, kept, got, own, theirs, dilated, point, result):
+    assembled(result, own[...], theirs[...], place[HEAD])
+    width = point.shape[1]
+    dilated[place[0]] = kept[:, :width]
+    dilated[2 - place[0]] = got[:, :width].astype(F32)
+    dilated[1] = kept[:, width : 2 * width] + got[:, width : 2 * width].astype(F32)
+    point[...] = kept[:, 2 * width :] + got[:, 2 * width :].astype(F32)
+
+
+def body(features, dilated_weight, point_weight, track_weight, track_cotangent):
+    samples, positions, channels = features.shape
+    n_seq, n_sample, n_head = (lax.axis_size(a) for a in ("seq", "sample", "head"))
+    dist = DILATION_STEP // positions
+    if not (n_seq == 2 * dist and bits_of(n_seq) == 3 and n_sample == 2 and n_head == 2 and samples == 1):
+        return general(features, dilated_weight, point_weight, track_weight, track_cotangent)
+    rows = positions
+    half = rows // 2
+    width = dilated_weight.shape[2]
+    tracks_here = track_weight.shape[1]
+    piece = channels // n_sample
+    block = channels // (n_seq * n_sample)
+    seq, head, sample = lax.axis_index("seq"), lax.axis_index("head"), lax.axis_index("sample")
+    place = jnp.stack(
+        [jnp.where(seq < dist, 0, 2), head, sample, (seq >> 2) & 1, (seq >> 1) & 1, seq & 1]
+    ).astype(jnp.int32)
+    taps = jnp.transpose(dilated_weight, (1, 0, 2))
+    feat = features.reshape(rows, channels)
+    cotangent = track_cotangent.reshape(rows, tracks_here)
+    pairs = [(i, (i + dist) % n_seq) for i in range(n_seq)]
+    crossing = [(2 * i + k, 2 * j + 1 - k) for i, j in pairs for k in range(2)]
+
+    far_track = flip(track_weight, "sample")
+    acted, term = kernel_call(
+        outer_term,
+        [((rows, channels), BF16), ((rows, width), BF16)],
+        [place, in_hbm(feat), in_hbm(taps)],
+        scratch=[
+            pltpu.VMEM((rows, channels), BF16),
+            pltpu.VMEM((channels, width), BF16),
+            pltpu.SemaphoreType.DMA((2, 3)),
+        ],
+        spaces={1: pltpu.HBM, 2: pltpu.HBM},
+    )
+    arrived = lax.ppermute(term, "seq", pairs)
+    groups = n_seq
+
+    (own_piece,) = kernel_call(
+        piece_of, [((piece, width), BF16)], [place, point_weight], acted
+    )
+    cut = piece // 3
+    near = [flip(own_piece[k : k + cut], "head") for k in range(0, piece, cut)]
+    far = [
+        flip(part[k : k + cut // 2], "sample") for part in near for k in range(0, cut, cut // 2)
+    ]
+    points = near + far
+
+    turned = ((groups, block, rows), BF16)
+    middle, acts, acts_given = kernel_call(
+        middle_term,
+        [((rows, width), F32), turned, turned],
+        [place, acted, taps],
+        own_piece,
+    )
+    middle, middle_b = kernel_call(
+        add_terms, [((rows, width), F32), ((rows, width), BF16)], [place, middle, arrived], acts
+    )
+    other_middle = flip(middle_b, "head")
+    hidden, slope, block_part = kernel_call(
+        own_hidden,
+        [((rows, width), BF16), ((half, width), F32), ((rows, channels), F32)],
+        [place, middle, feat, point_weight],
+    )
+
+    keep, give = kernel_call(
+        tracks,
+        [((half, channels), F32), ((half, channels), BF16)],
+        [place, block_part, other_middle, track_weight, far_track, cotangent, *points],
+        scratch=[
+            pltpu.VMEM((n_sample, rows, piece), BF16),
+            pltpu.VMEM((rows, tracks_here), BF16),
+        ],
+    )
+    theirs = flip(give, "head")
+    slope_other, slope_feat = kernel_call(
+        slopes,
+        [((half, width), F32), ((half, channels), F32)],
+        [place, other_middle, feat],
+        keep,
+    )
+    out_grad, both, grad_own, grad_other = kernel_call(
+        middle_grads,
+        [
+            ((half, channels), F32),
+            ((half, channels + width), BF16),
+            ((half, width), BF16),
+            ((half, width), BF16),
+        ],
+        [place, keep, theirs, point_weight, slope, slope_other, *points],
+    )
+    straight = lax.ppermute(grad_own, "seq", pairs)
+    crossed = lax.ppermute(grad_other, ("seq", "head"), crossing)
+    got = flip(both, "head")
+    number = groups + 2 * width // block
+    middle_grad, moved, outs, pack = kernel_call(
+        gathered,
+        [((rows, width), BF16)] * 2 + [turned, ((number, block, rows), BF16)],
+        [place, both, got, grad_own, straight, crossed],
+        scratch=[pltpu.VMEM((rows, channels), BF16)],
+    )
+    other_pack = flip(pack, "sample")
+    (act_give,) = kernel_call(
+        act_given, [((half, channels), BF16)], [place, middle_grad, moved, taps]
+    )
+    act_got = flip(act_give, "head")
+    part = (2, block, 3 * width)
+    kept, along, across, diagonal = kernel_call(
+        products,
+        [(part, F32)] + [(part, BF16)] * 3,
+        [
+            place, acts, flip(acts_given, "sample"), outs, other_pack, middle_grad, moved,
+            hidden, flip(hidden, "sample"),
+        ],
+        act_give,
+    )
+    along, across, diagonal = flip(along, "seq", 2), flip(across, "seq", 1), flip(diagonal, "seq", 3)
+    (act_keep,) = kernel_call(
+        act_kept, [((half, channels), F32)], [place, middle_grad, moved, taps], kept
+    )
+    (input_half,) = kernel_call(
+        input_part,
+        [((half, channels), BF16)],
+        [place, out_grad, act_keep, act_got, slope_feat],
+    )
+    input_other = flip(input_half, "head")
+    kept, given = kernel_call(
+        chips_sum,
+        [((block, 3 * width), F32), ((block, 3 * width), BF16)],
+        [place, kept, along, across, diagonal],
+        input_half,
+    )
+    dilated_grad, point_grad, input_grad = kernel_call(
+        finish,
+        [((3, block, width), F32), ((block, width), F32), ((rows, channels), BF16)],
+        [place, kept, flip(given, "seq", 4), input_half, input_other],
+    )
+    dilated_grad = jnp.transpose(dilated_grad, (1, 0, 2))
+    return (input_grad.reshape(samples, positions, channels), dilated_grad, point_grad)
+
+
 def solution(mesh):
     placed = (
         P("sample", "seq", None),

time: 167 us -> 105 us (0.63)
  matrix products: 29.8 us -> 0 us
  waiting for transfers between devices: 81.1 us -> 55.7 us
  Pallas kernels: 0 us -> 24.1 us
  between operations: 14.4 us -> 0.85 us
  other arithmetic: 7.76 us -> 0 us
  local copies, waits for them, and re-layouts: 5.52 us -> 0.23 us
  starting transfers between devices: 27.7 us -> 24 us
    dot_general x13 -> x0, matrix products: 29.8 us -> none  [dot(): lax.dot_general(left, right, (contract, ((), ())), preferred_element_type...]
    pallas_call x0 -> x15, Pallas kernels: none -> 24.1 us  [kernel_call(): pl.pallas_call(run, out_shape=[jax.ShapeDtypeStruct(s, d) for s, d in out...]
    ppermute x19 -> x22, waiting for transfers between devices: 64.1 us -> 43.8 us  [flip(): return lax.ppermute(value, axis, [(i, i ^ step) for i in range(count)])]
    ppermute x2, waiting for transfers between devices: 10.7 us -> 5.47 us  [the longest x1 4.34 us: body(): arrived = lax.ppermute(term, 'seq', pairs)]
    ppermute x1, waiting for transfers between devices: 1.34 us -> 6.49 us  [body(): straight = lax.ppermute(grad_own, 'seq', pairs)]
    all_gather x2 -> x0, waiting for transfers between devices: 4.24 us -> none  [the longest x1 4.24 us: body(): whole_track = lax.all_gather(track_weight, 'sample', axis=0, tiled=True)]
    unnamed x24 -> x10, local copies, waits for them, and re-layouts: 3.53 us -> 0.03 us
    ppermute x19 -> x22, starting transfers between devices: 20.7 us -> 17.4 us  [flip(): return lax.ppermute(value, axis, [(i, i ^ step) for i in range(count)])]
  transfers between devices with their start and end apart: 24 -> 25, of which waited for: 15 -> 13; matrix products, arithmetic and copies ran while one was open for 12% -> 0% of each run, Pallas kernels for 0% -> 13%
where the time goes in v3:
time: 105 us
  waiting for transfers between devices  55.7 us (53%)
  Pallas kernels  24.1 us (23%)
  starting transfers between devices  24 us (23%)
    ppermute x22, waiting for transfers between devices, flip(): return lax.ppermute(value, axis, [(i, i ^ step) for i in range(count)])  43.8 us
    pallas_call x15, Pallas kernels, kernel_call(): pl.pallas_call(run, out_shape=[jax.ShapeDtypeStruct(s, d) for s, d in out...  24.1 us
    ppermute x22, starting transfers between devices, flip(): return lax.ppermute(value, axis, [(i, i ^ step) for i in range(count)])  17.4 us
    ppermute x1, waiting for transfers between devices, body(): straight = lax.ppermute(grad_own, 'seq', pairs)  6.49 us
    ppermute x1, waiting for transfers between devices, body(): arrived = lax.ppermute(term, 'seq', pairs)  4.34 us
    ppermute x1, starting transfers between devices, body(): arrived = lax.ppermute(term, 'seq', pairs)  3.68 us
    ppermute x1, starting transfers between devices, body(): crossed = lax.ppermute(grad_other, ('seq', 'head'), crossing)  2.56 us
  transfers between devices with their start and end apart: 25, of which 13 were waited for; matrix products, arithmetic and copies ran while one was open for 0% of the time, Pallas kernels for 13%

profile of v3, /device:TPU:0, one launch (start us, length us, event | category | flops | bytes accessed | tf_op | source)
XLA Modules:
  0.0 104.9 jit_solution(2429302370162722084)
XLA Ops:
  1.2 2.9 %outer_term.1 = (bf16[256,1536]{1,0:T(8,128)(2,1)S(1)}, bf16[256,384]{1,0:T(8,128)(2,1)S(1)}) custom-call(s32[6]{0:T(128)S(1)} %stack.27.refs_0_, bf16[256,1536]{1,0:T(8,128)(2,1)} %bitcast.15, bf16[3,1536,384]{2,1,0:T(8,128)(2,1)} %bitcast.11), custom_call_target="tpu_custom_call" | custom-call | flops 1 | bytes 1 | tf_op jit(solution)/shard_map/outer_term/pallas_call | solution.py:200
  4.1 3.7 %collective-permute-start.1 = (bf16[256,384]{1,0:T(8,128)(2,1)S(1)}, bf16[256,384]{1,0:T(8,128)(2,1)S(1)}, u32[]{:S(2)}, u32[]{:S(2)}) collective-permute-start(bf16[256,384]{1,0:T(8,128)(2,1)S(1)} %get-tuple-element.38), channel_id=1, source_target_pairs={{0,16},{4,20},{8,24},{12,28},{16,0},{20,4},{24,8},{28,12},{1,17},{... | collective-permute-start | bytes 589832 | tf_op jit(solution)/shard_map/ppermute | solution.py:473
  8.5 1.6 %collective-permute-start.4 = (bf16[256,384]{1,0:T(8,128)(2,1)S(1)}, bf16[256,384]{1,0:T(8,128)(2,1)S(1)}, u32[]{:S(2)}, u32[]{:S(2)}) collective-permute-start(bf16[256,384]{1,0:T(8,128)(2,1)S(1)} %get-tuple-element.67), channel_id=1, source_target_pairs={{0,2},{2,0},{1,3},{3,1},{4,6},{6,4},{5,7},{7,5},{8,10},{10,8},{9,1... | collective-permute-start | bytes 589832 | tf_op jit(solution)/shard_map/ppermute | solution.py:34
  10.6 1.5 %collective-permute-start.6 = (bf16[256,384]{1,0:T(8,128)(2,1)S(1)}, bf16[256,384]{1,0:T(8,128)(2,1)S(1)}, u32[]{:S(2)}, u32[]{:S(2)}) collective-permute-start(bf16[256,384]{1,0:T(8,128)(2,1)S(1)} %get-tuple-element.65), channel_id=1, source_target_pairs={{0,2},{2,0},{1,3},{3,1},{4,6},{6,4},{5,7},{7,5},{8,10},{10,8},{9,1... | collective-permute-start | bytes 589832 | tf_op jit(solution)/shard_map/ppermute | solution.py:34
  12.1 1.1 %middle_term.1 = (f32[256,384]{1,0:T(8,128)S(1)}, bf16[8,96,256]{2,1,0:T(8,128)(2,1)S(1)}, bf16[8,96,256]{2,1,0:T(8,128)(2,1)S(1)}) custom-call(s32[6]{0:T(128)S(1)} %stack.27.refs_0_, bf16[256,1536]{1,0:T(8,128)(2,1)S(1)} %get-tuple-element.34.refs_2_.refs_1_, bf16[3,1536,384]{2,1,0:T(8,128)(2,1)S(1)} %bitcast.12, bf16[768,384]{1,0:T(8,128)(2,1)S(1)} %piece_of.1.refs_3_), custom_call_target="tpu_custom_call" | custom-call | flops 1 | bytes 1 | tf_op jit(solution)/shard_map/middle_term/pallas_call | solution.py:200
  13.2 4.3 %collective-permute-done.1.refs_2_ = bf16[256,384]{1,0:T(8,128)(2,1)S(1)} collective-permute-done((bf16[256,384]{1,0:T(8,128)(2,1)S(1)}, bf16[256,384]{1,0:T(8,128)(2,1)S(1)}, u32[]{:S(2)}, u32[]{:S(2)}) %collective-permute-start.1) | collective-permute-done | bytes 196640 | tf_op jit(solution)/shard_map/ppermute | solution.py:473
  18.2 1.6 %collective-permute-start.2 = (bf16[256,384]{1,0:T(8,128)(2,1)S(1)}, bf16[256,384]{1,0:T(8,128)(2,1)S(1)}, u32[]{:S(2)}, u32[]{:S(2)}) collective-permute-start(bf16[256,384]{1,0:T(8,128)(2,1)S(1)} %get-tuple-element.41), channel_id=1, source_target_pairs={{0,2},{2,0},{1,3},{3,1},{4,6},{6,4},{5,7},{7,5},{8,10},{10,8},{9,1... | collective-permute-start | bytes 589832 | tf_op jit(solution)/shard_map/ppermute | solution.py:34
  20.5 4.2 %collective-permute-done.6.refs_8_ = bf16[256,384]{1,0:T(8,128)(2,1)S(1)} collective-permute-done((bf16[256,384]{1,0:T(8,128)(2,1)S(1)}, bf16[256,384]{1,0:T(8,128)(2,1)S(1)}, u32[]{:S(2)}, u32[]{:S(2)}) %collective-permute-start.6) | collective-permute-done | bytes 196640 | tf_op jit(solution)/shard_map/ppermute | solution.py:34
  26.2 1.3 %own_hidden.1 = (bf16[256,384]{1,0:T(8,128)(2,1)S(1)}, f32[128,384]{1,0:T(8,128)S(1)}, f32[256,1536]{1,0:T(8,128)S(1)}) custom-call(s32[6]{0:T(128)S(1)} %stack.27.refs_0_, f32[256,384]{1,0:T(8,128)S(1)} %get-tuple-element.39.refs_1_, bf16[256,1536]{1,0:T(8,128)(2,1)S(1)} %bitcast.16, bf16[1536,384]{1,0:T(8,128)(2,1)S(1)} %copy-done.1), custom_call_target="tpu_custom_call" | custom-call | flops 1 | bytes 1 | tf_op jit(solution)/shard_map/own_hidden/pallas_call | solution.py:200
  28.2 6.3 %tracks.1 = (f32[128,1536]{1,0:T(8,128)S(1)}, bf16[128,1536]{1,0:T(8,128)(2,1)S(1)}) custom-call(s32[6]{0:T(128)S(1)} %stack.27.refs_0_, f32[256,1536]{1,0:T(8,128)S(1)} %get-tuple-element.40.refs_1_, bf16[256,384]{1,0:T(8,128)(2,1)S(1)} %collective-permute-done.2.refs_2_.refs_1_, bf16[768,1920]{1,0:T(8,128)(2,1)S(1)} %copy-done.3, ...), custom_call_target="tpu_custom_call" | custom-call | flops 1 | bytes 1 | tf_op jit(solution)/shard_map/tracks/pallas_call | solution.py:200
  34.5 1.6 %collective-permute-start.13 = (bf16[128,1536]{1,0:T(8,128)(2,1)S(1)}, bf16[128,1536]{1,0:T(8,128)(2,1)S(1)}, u32[]{:S(2)}, u32[]{:S(2)}) collective-permute-start(bf16[128,1536]{1,0:T(8,128)(2,1)S(1)} %get-tuple-element.43), channel_id=1, source_target_pairs={{0,2},{2,0},{1,3},{3,1},{4,6},{6,4},{5,7},{7,5},{8,10},{10,8},{9,1... | collective-permute-start | bytes 1179656 | tf_op jit(solution)/shard_map/ppermute | solution.py:34
  36.1 1.2 %slopes.1 = (f32[128,384]{1,0:T(8,128)S(1)}, f32[128,1536]{1,0:T(8,128)S(1)}) custom-call(s32[6]{0:T(128)S(1)} %stack.27.refs_0_, bf16[256,384]{1,0:T(8,128)(2,1)S(1)} %collective-permute-done.2.refs_2_.refs_1_, bf16[256,1536]{1,0:T(8,128)(2,1)S(1)} %bitcast.17, f32[128,1536]{1,0:T(8,128)S(1)} %get-tuple-element.42.refs_3_.refs_1_), custom_call_target="tpu_custom_call" | custom-call | flops 1 | bytes 1 | tf_op jit(solution)/shard_map/slopes/pallas_call | solution.py:200
  37.3 8.1 %collective-permute-done.13.refs_2_ = bf16[128,1536]{1,0:T(8,128)(2,1)S(1)} collective-permute-done((bf16[128,1536]{1,0:T(8,128)(2,1)S(1)}, bf16[128,1536]{1,0:T(8,128)(2,1)S(1)}, u32[]{:S(2)}, u32[]{:S(2)}) %collective-permute-start.13) | collective-permute-done | bytes 393248 | tf_op jit(solution)/shard_map/ppermute | solution.py:34
  45.3 1.2 %middle_grads.1 = (f32[128,1536]{1,0:T(8,128)S(1)}, bf16[128,1920]{1,0:T(8,128)(2,1)S(1)}, bf16[128,384]{1,0:T(8,128)(2,1)S(1)}, bf16[128,384]{1,0:T(8,128)(2,1)S(1)}) custom-call(s32[6]{0:T(128)S(1)} %stack.27.refs_0_, f32[128,1536]{1,0:T(8,128)S(1)} %get-tuple-element.42.refs_3_.refs_1_, bf16[128,1536]{1,0:T(8,128)(2,1)S(1)} %collective-permute-done.13.refs_2_, ...), custom_call_target="tpu_custom_call" | custom-call | flops 1 | bytes 1 | tf_op jit(solution)/shard_map/middle_grads/pallas_call | solution.py:200
  46.5 1.6 %collective-permute-start.14 = (bf16[128,1920]{1,0:T(8,128)(2,1)S(1)}, bf16[128,1920]{1,0:T(8,128)(2,1)S(1)}, u32[]{:S(2)}, u32[]{:S(2)}) collective-permute-start(bf16[128,1920]{1,0:T(8,128)(2,1)S(1)} %get-tuple-element.46.refs_1_), channel_id=1, source_target_pairs={{0,2},{2,0},{1,3},{3,1},{4,6},{6,4},{5,7},{7,5},{8,10},{10,8},{9,1... | collective-permute-start | bytes 1474568 | tf_op jit(solution)/shard_map/ppermute | solution.py:34
  48.4 2.6 %collective-permute-start.16 = (bf16[128,384]{1,0:T(8,128)(2,1)S(1)}, bf16[128,384]{1,0:T(8,128)(2,1)S(1)}, u32[]{:S(2)}, u32[]{:S(2)}) collective-permute-start(bf16[128,384]{1,0:T(8,128)(2,1)S(1)} %get-tuple-element.48), channel_id=1, source_target_pairs={{0,18},{2,16},{4,22},{6,20},{8,26},{10,24},{12,30},{14,28},{16,2},... | collective-permute-start | bytes 294920 | tf_op jit(solution)/shard_map/ppermute | solution.py:530
  51.0 6.5 %collective-permute-done.15.refs_4_ = bf16[128,384]{1,0:T(8,128)(2,1)S(1)} collective-permute-done((bf16[128,384]{1,0:T(8,128)(2,1)S(1)}, bf16[128,384]{1,0:T(8,128)(2,1)S(1)}, u32[]{:S(2)}, u32[]{:S(2)}) %collective-permute-start.15) | collective-permute-done | bytes 98336 | tf_op jit(solution)/shard_map/ppermute | solution.py:529
  57.5 1.1 %collective-permute-done.16.refs_5_ = bf16[128,384]{1,0:T(8,128)(2,1)S(1)} collective-permute-done((bf16[128,384]{1,0:T(8,128)(2,1)S(1)}, bf16[128,384]{1,0:T(8,128)(2,1)S(1)}, u32[]{:S(2)}, u32[]{:S(2)}) %collective-permute-start.16) | collective-permute-done | bytes 98336 | tf_op jit(solution)/shard_map/ppermute | solution.py:530
  58.6 2.0 %collective-permute-done.14.refs_2_ = bf16[128,1920]{1,0:T(8,128)(2,1)S(1)} collective-permute-done((bf16[128,1920]{1,0:T(8,128)(2,1)S(1)}, bf16[128,1920]{1,0:T(8,128)(2,1)S(1)}, u32[]{:S(2)}, u32[]{:S(2)}) %collective-permute-start.14) | collective-permute-done | bytes 491552 | tf_op jit(solution)/shard_map/ppermute | solution.py:34
  60.6 1.0 gathered.1
  62.3 1.4 %act_given.1.refs_9_ = bf16[128,1536]{1,0:T(8,128)(2,1)S(1)} custom-call(s32[6]{0:T(128)S(1)} %stack.27.refs_0_, bf16[256,384]{1,0:T(8,128)(2,1)S(1)} %get-tuple-element.51.refs_1_.refs_5_, bf16[256,384]{1,0:T(8,128)(2,1)S(1)} %get-tuple-element.52.refs_2_.refs_6_, bf16[3,1536,384]{2,1,0:T(8,128)(2,1)S(1)} %bitcast.13), custom_call_target="tpu_custom_call" | custom-call | flops 1 | bytes 1 | tf_op jit(solution)/shard_map/act_given/pallas_call | solution.py:200
  63.7 1.5 %collective-permute-start.22 = (bf16[128,1536]{1,0:T(8,128)(2,1)S(1)}, bf16[128,1536]{1,0:T(8,128)(2,1)S(1)}, u32[]{:S(2)}, u32[]{:S(2)}) collective-permute-start(bf16[128,1536]{1,0:T(8,128)(2,1)S(1)} %act_given.1.refs_9_), channel_id=1, source_target_pairs={{0,2},{2,0},{1,3},{3,1},{4,6},{6,4},{5,7},{7,5},{8,10},{10,8},{9,1... | collective-permute-start | bytes 1179656 | tf_op jit(solution)/shard_map/ppermute | solution.py:34
  65.2 2.0 %products.1 = (f32[2,96,1152]{2,1,0:T(8,128)S(1)}, bf16[2,96,1152]{2,1,0:T(8,128)(2,1)S(1)}, bf16[2,96,1152]{2,1,0:T(8,128)(2,1)S(1)}, bf16[2,96,1152]{2,1,0:T(8,128)(2,1)S(1)}) custom-call(s32[6]{0:T(128)S(1)} %stack.27.refs_0_, bf16[8,96,256]{2,1,0:T(8,128)(2,1)S(1)} %get-tuple-element.35.refs_3_.refs_1_, ...), custom_call_target="tpu_custom_call" | custom-call | flops 1 | bytes 1 | tf_op jit(solution)/shard_map/products/pallas_call | solution.py:200
  67.3 1.7 %collective-permute-start.19 = (bf16[2,96,1152]{2,1,0:T(8,128)(2,1)S(1)}, bf16[2,96,1152]{2,1,0:T(8,128)(2,1)S(1)}, u32[]{:S(2)}, u32[]{:S(2)}) collective-permute-start(bf16[2,96,1152]{2,1,0:T(8,128)(2,1)S(1)} %get-tuple-element.55), channel_id=1, source_target_pairs={{0,8},{4,12},{8,0},{12,4},{16,24},{20,28},{24,16},{28,20},{1,9},{5... | collective-permute-start | bytes 1327112 | tf_op jit(solution)/shard_map/ppermute | solution.py:34
  68.9 1.5 %collective-permute-start.20 = (bf16[2,96,1152]{2,1,0:T(8,128)(2,1)S(1)}, bf16[2,96,1152]{2,1,0:T(8,128)(2,1)S(1)}, u32[]{:S(2)}, u32[]{:S(2)}) collective-permute-start(bf16[2,96,1152]{2,1,0:T(8,128)(2,1)S(1)} %get-tuple-element.56), channel_id=1, source_target_pairs={{0,4},{4,0},{8,12},{12,8},{16,20},{20,16},{24,28},{28,24},{1,5},{5... | collective-permute-start | bytes 1327112 | tf_op jit(solution)/shard_map/ppermute | solution.py:34
  70.8 1.4 %act_kept.1.refs_2_ = f32[128,1536]{1,0:T(8,128)S(1)} custom-call(s32[6]{0:T(128)S(1)} %stack.27.refs_0_, bf16[256,384]{1,0:T(8,128)(2,1)S(1)} %get-tuple-element.51.refs_1_.refs_5_, bf16[256,384]{1,0:T(8,128)(2,1)S(1)} %get-tuple-element.52.refs_2_.refs_6_, bf16[3,1536,384]{2,1,0:T(8,128)(2,1)S(1)} %bitcast.14, ...), custom_call_target="tpu_custom_call" | custom-call | flops 1 | bytes 1 | tf_op jit(solution)/shard_map/act_kept/pallas_call | solution.py:200
  72.2 3.0 %collective-permute-done.22.refs_3_ = bf16[128,1536]{1,0:T(8,128)(2,1)S(1)} collective-permute-done((bf16[128,1536]{1,0:T(8,128)(2,1)S(1)}, bf16[128,1536]{1,0:T(8,128)(2,1)S(1)}, u32[]{:S(2)}, u32[]{:S(2)}) %collective-permute-start.22) | collective-permute-done | bytes 393248 | tf_op jit(solution)/shard_map/ppermute | solution.py:34
  75.9 1.5 %collective-permute-start.24 = (bf16[128,1536]{1,0:T(8,128)(2,1)S(1)}, bf16[128,1536]{1,0:T(8,128)(2,1)S(1)}, u32[]{:S(2)}, u32[]{:S(2)}) collective-permute-start(bf16[128,1536]{1,0:T(8,128)(2,1)S(1)} %input_part.1.refs_5_.refs_3_), channel_id=1, source_target_pairs={{0,2},{2,0},{1,3},{3,1},{4,6},{6,4},{5,7},{7,5},{8,10},{10,8},{9,1... | collective-permute-start | bytes 1179656 | tf_op jit(solution)/shard_map/ppermute | solution.py:34
  77.4 2.9 %collective-permute-done.19.refs_2_ = bf16[2,96,1152]{2,1,0:T(8,128)(2,1)S(1)} collective-permute-done((bf16[2,96,1152]{2,1,0:T(8,128)(2,1)S(1)}, bf16[2,96,1152]{2,1,0:T(8,128)(2,1)S(1)}, u32[]{:S(2)}, u32[]{:S(2)}) %collective-permute-start.19) | collective-permute-done | bytes 442400 | tf_op jit(solution)/shard_map/ppermute | solution.py:34
  80.3 10.0 %collective-permute-done.20.refs_3_ = bf16[2,96,1152]{2,1,0:T(8,128)(2,1)S(1)} collective-permute-done((bf16[2,96,1152]{2,1,0:T(8,128)(2,1)S(1)}, bf16[2,96,1152]{2,1,0:T(8,128)(2,1)S(1)}, u32[]{:S(2)}, u32[]{:S(2)}) %collective-permute-start.20) | collective-permute-done | bytes 442400 | tf_op jit(solution)/shard_map/ppermute | solution.py:34
  91.5 11.6 %collective-permute-done.23.refs_2_ = bf16[96,1152]{1,0:T(8,128)(2,1)S(1)} collective-permute-done((bf16[96,1152]{1,0:T(8,128)(2,1)S(1)}, bf16[96,1152]{1,0:T(8,128)(2,1)S(1)}, u32[]{:S(2)}, u32[]{:S(2)}) %collective-permute-start.23) | collective-permute-done | bytes 221216 | tf_op jit(solution)/shard_map/ppermute | solution.py:34
  103.2 1.7 %finish.1 = (f32[3,96,384]{2,1,0:T(8,128)}, f32[96,384]{1,0:T(8,128)}, bf16[256,1536]{1,0:T(8,128)(2,1)}) custom-call(s32[6]{0:T(128)S(1)} %stack.27.refs_0_, f32[96,1152]{1,0:T(8,128)S(1)} %get-tuple-element.60.refs_1_, bf16[96,1152]{1,0:T(8,128)(2,1)S(1)} %collective-permute-done.23.refs_2_, bf16[128,1536]{1,0:T(8,128)(2,1)S(1)} %input_part.1.refs_5_.refs_3_, ...), custom_call_target="tpu_custom_call" | custom-call | flops 1 | bytes 1 | tf_op jit(solution)/shard_map/finish/pallas_call | solution.py:200
  (48 shorter events, 8.5 us)
Async XLA Ops:
  0.6 7.2 %copy-start.1 = (bf16[1536,384]{1,0:T(8,128)(2,1)S(1)}, bf16[1536,384]{1,0:T(8,128)(2,1)}, u32[]{:S(2)}) copy-start(bf16[1536,384]{1,0:T(8,128)(2,1)} %refs_3_.5) | copy-start | bytes 3538948
  0.6 27.6 %collective-permute-start.3 = (bf16[768,1920]{1,0:T(8,128)(2,1)}, bf16[768,1920]{1,0:T(8,128)(2,1)}, u32[]{:S(2)}, u32[]{:S(2)}) collective-permute-start(bf16[768,1920]{1,0:T(8,128)(2,1)} %refs_3_.4), channel_id=1, source_target_pairs={{0,1},{1,0},{2,3},{3,2},{4,5},{5,4},{6,7},{7,6},{8,9},{9,8},{10,11... | collective-permute-start | bytes 8847368 | tf_op jit(solution)/shard_map/ppermute | solution.py:34
  4.1 8.0 %copy-start = (bf16[1536,3,384]{2,0,1:T(8,128)(2,1)S(1)}, bf16[1536,3,384]{2,0,1:T(8,128)(2,1)}, u32[]{:S(2)}) copy-start(bf16[1536,3,384]{2,0,1:T(8,128)(2,1)} %param.6) | copy-start | bytes 10616836
  4.1 13.4 %collective-permute-start.1 = (bf16[256,384]{1,0:T(8,128)(2,1)S(1)}, bf16[256,384]{1,0:T(8,128)(2,1)S(1)}, u32[]{:S(2)}, u32[]{:S(2)}) collective-permute-start(bf16[256,384]{1,0:T(8,128)(2,1)S(1)} %get-tuple-element.38), channel_id=1, source_target_pairs={{0,16},{4,20},{8,24},{12,28},{16,0},{20,4},{24,8},{28,12},{1,17},{... | collective-permute-start | bytes 589832 | tf_op jit(solution)/shard_map/ppermute | solution.py:473
  8.5 11.3 %collective-permute-start.4 = (bf16[256,384]{1,0:T(8,128)(2,1)S(1)}, bf16[256,384]{1,0:T(8,128)(2,1)S(1)}, u32[]{:S(2)}, u32[]{:S(2)}) collective-permute-start(bf16[256,384]{1,0:T(8,128)(2,1)S(1)} %get-tuple-element.67), channel_id=1, source_target_pairs={{0,2},{2,0},{1,3},{3,1},{4,6},{6,4},{5,7},{7,5},{8,10},{10,8},{9,1... | collective-permute-start | bytes 589832 | tf_op jit(solution)/shard_map/ppermute | solution.py:34
  10.1 10.5 %collective-permute-start.5 = (bf16[256,384]{1,0:T(8,128)(2,1)S(1)}, bf16[256,384]{1,0:T(8,128)(2,1)S(1)}, u32[]{:S(2)}, u32[]{:S(2)}) collective-permute-start(bf16[256,384]{1,0:T(8,128)(2,1)S(1)} %get-tuple-element.66), channel_id=1, source_target_pairs={{0,2},{2,0},{1,3},{3,1},{4,6},{6,4},{5,7},{7,5},{8,10},{10,8},{9,1... | collective-permute-start | bytes 589832 | tf_op jit(solution)/shard_map/ppermute | solution.py:34
  10.6 15.6 %copy-start.2 = (bf16[1,256,1536]{2,1,0:T(8,128)(2,1)S(1)}, bf16[1,256,1536]{2,1,0:T(8,128)(2,1)}, u32[]{:S(2)}) copy-start(bf16[1,256,1536]{2,1,0:T(8,128)(2,1)} %param.5) | copy-start | bytes 2359300
  10.6 14.1 %collective-permute-start.6 = (bf16[256,384]{1,0:T(8,128)(2,1)S(1)}, bf16[256,384]{1,0:T(8,128)(2,1)S(1)}, u32[]{:S(2)}, u32[]{:S(2)}) collective-permute-start(bf16[256,384]{1,0:T(8,128)(2,1)S(1)} %get-tuple-element.65), channel_id=1, source_target_pairs={{0,2},{2,0},{1,3},{3,1},{4,6},{6,4},{5,7},{7,5},{8,10},{10,8},{9,1... | collective-permute-start | bytes 589832 | tf_op jit(solution)/shard_map/ppermute | solution.py:34
  13.2 15.0 %copy-start.3 = (bf16[768,1920]{1,0:T(8,128)(2,1)S(1)}, bf16[768,1920]{1,0:T(8,128)(2,1)}, u32[]{:S(2)}) copy-start(bf16[768,1920]{1,0:T(8,128)(2,1)} %refs_3_.4) | copy-start | bytes 8847364
  13.2 15.0 %copy-start.4 = (bf16[1,256,1920]{2,1,0:T(8,128)(2,1)S(1)}, bf16[1,256,1920]{2,1,0:T(8,128)(2,1)}, u32[]{:S(2)}) copy-start(bf16[1,256,1920]{2,1,0:T(8,128)(2,1)} %param.9) | copy-start | bytes 2949124
  18.2 10.0 %collective-permute-start.2 = (bf16[256,384]{1,0:T(8,128)(2,1)S(1)}, bf16[256,384]{1,0:T(8,128)(2,1)S(1)}, u32[]{:S(2)}, u32[]{:S(2)}) collective-permute-start(bf16[256,384]{1,0:T(8,128)(2,1)S(1)} %get-tuple-element.41), channel_id=1, source_target_pairs={{0,2},{2,0},{1,3},{3,1},{4,6},{6,4},{5,7},{7,5},{8,10},{10,8},{9,1... | collective-permute-start | bytes 589832 | tf_op jit(solution)/shard_map/ppermute | solution.py:34
  19.8 4.9 %collective-permute-start.7 = (bf16[128,384]{1,0:T(8,128)(2,1)S(1)}, bf16[128,384]{1,0:T(8,128)(2,1)S(1)}, u32[]{:S(2)}, u32[]{:S(2)}) collective-permute-start(bf16[128,384]{1,0:T(8,128)(2,1)S(1)} %get-tuple-element.73), channel_id=1, source_target_pairs={{0,1},{1,0},{2,3},{3,2},{4,5},{5,4},{6,7},{7,6},{8,9},{9,8},{10,11... | collective-permute-start | bytes 294920 | tf_op jit(solution)/shard_map/ppermute | solution.py:34
  20.5 4.8 %collective-permute-start.8 = (bf16[128,384]{1,0:T(8,128)(2,1)S(1)}, bf16[128,384]{1,0:T(8,128)(2,1)S(1)}, u32[]{:S(2)}, u32[]{:S(2)}) collective-permute-start(bf16[128,384]{1,0:T(8,128)(2,1)S(1)} %get-tuple-element.72), channel_id=1, source_target_pairs={{0,1},{1,0},{2,3},{3,2},{4,5},{5,4},{6,7},{7,6},{8,9},{9,8},{10,11... | collective-permute-start | bytes 294920 | tf_op jit(solution)/shard_map/ppermute | solution.py:34
  24.7 1.3 %collective-permute-start.9 = (bf16[128,384]{1,0:T(8,128)(2,1)S(1)}, bf16[128,384]{1,0:T(8,128)(2,1)S(1)}, u32[]{:S(2)}, u32[]{:S(2)}) collective-permute-start(bf16[128,384]{1,0:T(8,128)(2,1)S(1)} %get-tuple-element.71), channel_id=1, source_target_pairs={{0,1},{1,0},{2,3},{3,2},{4,5},{5,4},{6,7},{7,6},{8,9},{9,8},{10,11... | collective-permute-start | bytes 294920 | tf_op jit(solution)/shard_map/ppermute | solution.py:34
  24.8 2.7 %collective-permute-start.10 = (bf16[128,384]{1,0:T(8,128)(2,1)S(1)}, bf16[128,384]{1,0:T(8,128)(2,1)S(1)}, u32[]{:S(2)}, u32[]{:S(2)}) collective-permute-start(bf16[128,384]{1,0:T(8,128)(2,1)S(1)} %get-tuple-element.70), channel_id=1, source_target_pairs={{0,1},{1,0},{2,3},{3,2},{4,5},{5,4},{6,7},{7,6},{8,9},{9,8},{10,11... | collective-permute-start | bytes 294920 | tf_op jit(solution)/shard_map/ppermute | solution.py:34
  25.3 2.1 %collective-permute-start.11 = (bf16[128,384]{1,0:T(8,128)(2,1)S(1)}, bf16[128,384]{1,0:T(8,128)(2,1)S(1)}, u32[]{:S(2)}, u32[]{:S(2)}) collective-permute-start(bf16[128,384]{1,0:T(8,128)(2,1)S(1)} %get-tuple-element.69), channel_id=1, source_target_pairs={{0,1},{1,0},{2,3},{3,2},{4,5},{5,4},{6,7},{7,6},{8,9},{9,8},{10,11... | collective-permute-start | bytes 294920 | tf_op jit(solution)/shard_map/ppermute | solution.py:34
  26.0 1.5 %collective-permute-start.12 = (bf16[128,384]{1,0:T(8,128)(2,1)S(1)}, bf16[128,384]{1,0:T(8,128)(2,1)S(1)}, u32[]{:S(2)}, u32[]{:S(2)}) collective-permute-start(bf16[128,384]{1,0:T(8,128)(2,1)S(1)} %get-tuple-element.68), channel_id=1, source_target_pairs={{0,1},{1,0},{2,3},{3,2},{4,5},{5,4},{6,7},{7,6},{8,9},{9,8},{10,11... | collective-permute-start | bytes 294920 | tf_op jit(solution)/shard_map/ppermute | solution.py:34
  34.5 10.8 %collective-permute-start.13 = (bf16[128,1536]{1,0:T(8,128)(2,1)S(1)}, bf16[128,1536]{1,0:T(8,128)(2,1)S(1)}, u32[]{:S(2)}, u32[]{:S(2)}) collective-permute-start(bf16[128,1536]{1,0:T(8,128)(2,1)S(1)} %get-tuple-element.43), channel_id=1, source_target_pairs={{0,2},{2,0},{1,3},{3,1},{4,6},{6,4},{5,7},{7,5},{8,10},{10,8},{9,1... | collective-permute-start | bytes 1179656 | tf_op jit(solution)/shard_map/ppermute | solution.py:34
  46.5 14.1 %collective-permute-start.14 = (bf16[128,1920]{1,0:T(8,128)(2,1)S(1)}, bf16[128,1920]{1,0:T(8,128)(2,1)S(1)}, u32[]{:S(2)}, u32[]{:S(2)}) collective-permute-start(bf16[128,1920]{1,0:T(8,128)(2,1)S(1)} %get-tuple-element.46.refs_1_), channel_id=1, source_target_pairs={{0,2},{2,0},{1,3},{3,1},{4,6},{6,4},{5,7},{7,5},{8,10},{10,8},{9,1... | collective-permute-start | bytes 1474568 | tf_op jit(solution)/shard_map/ppermute | solution.py:34
  48.1 9.4 %collective-permute-start.15 = (bf16[128,384]{1,0:T(8,128)(2,1)S(1)}, bf16[128,384]{1,0:T(8,128)(2,1)S(1)}, u32[]{:S(2)}, u32[]{:S(2)}) collective-permute-start(bf16[128,384]{1,0:T(8,128)(2,1)S(1)} %get-tuple-element.47.refs_3_), channel_id=1, source_target_pairs={{0,16},{4,20},{8,24},{12,28},{16,0},{20,4},{24,8},{28,12},{1,17},{... | collective-permute-start | bytes 294920 | tf_op jit(solution)/shard_map/ppermute | solution.py:529
  48.4 10.2 %collective-permute-start.16 = (bf16[128,384]{1,0:T(8,128)(2,1)S(1)}, bf16[128,384]{1,0:T(8,128)(2,1)S(1)}, u32[]{:S(2)}, u32[]{:S(2)}) collective-permute-start(bf16[128,384]{1,0:T(8,128)(2,1)S(1)} %get-tuple-element.48), channel_id=1, source_target_pairs={{0,18},{2,16},{4,22},{6,20},{8,26},{10,24},{12,30},{14,28},{16,2},... | collective-permute-start | bytes 294920 | tf_op jit(solution)/shard_map/ppermute | solution.py:530
  61.6 3.6 %collective-permute-start.17 = (bf16[16,96,256]{2,1,0:T(8,128)(2,1)S(1)}, bf16[16,96,256]{2,1,0:T(8,128)(2,1)S(1)}, u32[]{:S(2)}, u32[]{:S(2)}) collective-permute-start(bf16[16,96,256]{2,1,0:T(8,128)(2,1)S(1)} %get-tuple-element.50), channel_id=1, source_target_pairs={{0,1},{1,0},{2,3},{3,2},{4,5},{5,4},{6,7},{7,6},{8,9},{9,8},{10,11... | collective-permute-start | bytes 2359304 | tf_op jit(solution)/shard_map/ppermute | solution.py:34
  61.7 3.5 %collective-permute-start = (bf16[8,96,256]{2,1,0:T(8,128)(2,1)S(1)}, bf16[8,96,256]{2,1,0:T(8,128)(2,1)S(1)}, u32[]{:S(2)}, u32[]{:S(2)}) collective-permute-start(bf16[8,96,256]{2,1,0:T(8,128)(2,1)S(1)} %get-tuple-element.36), channel_id=1, source_target_pairs={{0,1},{1,0},{2,3},{3,2},{4,5},{5,4},{6,7},{7,6},{8,9},{9,8},{10,11... | collective-permute-start | bytes 1179656 | tf_op jit(solution)/shard_map/ppermute | solution.py:34
  62.2 3.0 %collective-permute-start.18 = (bf16[256,384]{1,0:T(8,128)(2,1)S(1)}, bf16[256,384]{1,0:T(8,128)(2,1)S(1)}, u32[]{:S(2)}, u32[]{:S(2)}) collective-permute-start(bf16[256,384]{1,0:T(8,128)(2,1)S(1)} %get-tuple-element.53.refs_7_), channel_id=1, source_target_pairs={{0,1},{1,0},{2,3},{3,2},{4,5},{5,4},{6,7},{7,6},{8,9},{9,8},{10,11... | collective-permute-start | bytes 589832 | tf_op jit(solution)/shard_map/ppermute | solution.py:34
  63.7 11.5 %collective-permute-start.22 = (bf16[128,1536]{1,0:T(8,128)(2,1)S(1)}, bf16[128,1536]{1,0:T(8,128)(2,1)S(1)}, u32[]{:S(2)}, u32[]{:S(2)}) collective-permute-start(bf16[128,1536]{1,0:T(8,128)(2,1)S(1)} %act_given.1.refs_9_), channel_id=1, source_target_pairs={{0,2},{2,0},{1,3},{3,1},{4,6},{6,4},{5,7},{7,5},{8,10},{10,8},{9,1... | collective-permute-start | bytes 1179656 | tf_op jit(solution)/shard_map/ppermute | solution.py:34
  67.3 13.1 %collective-permute-start.19 = (bf16[2,96,1152]{2,1,0:T(8,128)(2,1)S(1)}, bf16[2,96,1152]{2,1,0:T(8,128)(2,1)S(1)}, u32[]{:S(2)}, u32[]{:S(2)}) collective-permute-start(bf16[2,96,1152]{2,1,0:T(8,128)(2,1)S(1)} %get-tuple-element.55), channel_id=1, source_target_pairs={{0,8},{4,12},{8,0},{12,4},{16,24},{20,28},{24,16},{28,20},{1,9},{5... | collective-permute-start | bytes 1327112 | tf_op jit(solution)/shard_map/ppermute | solution.py:34
  68.9 21.4 %collective-permute-start.20 = (bf16[2,96,1152]{2,1,0:T(8,128)(2,1)S(1)}, bf16[2,96,1152]{2,1,0:T(8,128)(2,1)S(1)}, u32[]{:S(2)}, u32[]{:S(2)}) collective-permute-start(bf16[2,96,1152]{2,1,0:T(8,128)(2,1)S(1)} %get-tuple-element.56), channel_id=1, source_target_pairs={{0,4},{4,0},{8,12},{12,8},{16,20},{20,16},{24,28},{28,24},{1,5},{5... | collective-permute-start | bytes 1327112 | tf_op jit(solution)/shard_map/ppermute | solution.py:34
  70.4 19.9 %collective-permute-start.21 = (bf16[2,96,1152]{2,1,0:T(8,128)(2,1)S(1)}, bf16[2,96,1152]{2,1,0:T(8,128)(2,1)S(1)}, u32[]{:S(2)}, u32[]{:S(2)}) collective-permute-start(bf16[2,96,1152]{2,1,0:T(8,128)(2,1)S(1)} %get-tuple-element.57), channel_id=1, source_target_pairs={{0,12},{4,8},{8,4},{12,0},{16,28},{20,24},{24,20},{28,16},{1,13},{... | collective-permute-start | bytes 1327112 | tf_op jit(solution)/shard_map/ppermute | solution.py:34
  75.9 15.7 %collective-permute-start.24 = (bf16[128,1536]{1,0:T(8,128)(2,1)S(1)}, bf16[128,1536]{1,0:T(8,128)(2,1)S(1)}, u32[]{:S(2)}, u32[]{:S(2)}) collective-permute-start(bf16[128,1536]{1,0:T(8,128)(2,1)S(1)} %input_part.1.refs_5_.refs_3_), channel_id=1, source_target_pairs={{0,2},{2,0},{1,3},{3,1},{4,6},{6,4},{5,7},{7,5},{8,10},{10,8},{9,1... | collective-permute-start | bytes 1179656 | tf_op jit(solution)/shard_map/ppermute | solution.py:34
  91.1 12.1 %collective-permute-start.23 = (bf16[96,1152]{1,0:T(8,128)(2,1)S(1)}, bf16[96,1152]{1,0:T(8,128)(2,1)S(1)}, u32[]{:S(2)}, u32[]{:S(2)}) collective-permute-start(bf16[96,1152]{1,0:T(8,128)(2,1)S(1)} %get-tuple-element.61), channel_id=1, source_target_pairs={{0,16},{4,20},{8,24},{12,28},{16,0},{20,4},{24,8},{28,12},{1,17},{... | collective-permute-start | bytes 663560 | tf_op jit(solution)/shard_map/ppermute | solution.py:34

commit v4 on v3

--- a/solution.py
+++ b/solution.py
@@ -244,15 +244,18 @@
     term[...] = total.astype(BF16)
 
 
-def piece_of(place, point, piece):
+def piece_of(place, point, piece, sem):
     number = piece.shape[0]
-    piece[...] = point[pl.ds(pl.multiple_of(place[SAMPLE] * number, number), number), :]
+    own = pl.ds(pl.multiple_of(place[SAMPLE] * number, number), number)
+    copy = pltpu.make_async_copy(point.at[own], piece, sem)
+    copy.start()
+    copy.wait()
 
 
 def middle_term(place, acted, weight, middle, kept, given):
     act = acted[...]
     middle[...] = dot(act, weight[1], NN)
-    part_channels(place, act.T, kept, given)
+    part_channels(place, act.T, kept, [given])
 
 
 def part_channels(place, turned, kept, given):
@@ -260,7 +263,10 @@
     split = turned.reshape(groups, 2, block, rows)
     first = place[SAMPLE] == 0
     kept[...] = jnp.where(first, split[:, 0], split[:, 1])
-    given[...] = jnp.where(first, split[:, 1], split[:, 0])
+    theirs = jnp.where(first, split[:, 1], split[:, 0])
+    number = groups // len(given)
+    for k, part in enumerate(given):
+        part[...] = theirs[k * number : (k + 1) * number]
 
 
 def add_terms(place, middle, arrived, total, sent):
@@ -269,34 +275,24 @@
     sent[...] = value.astype(BF16)
 
 
-def own_hidden(place, middle, feat, point, hidden, slope, block):
-    half = slope.shape[0]
+def own_hidden(place, middle, feat, point, hidden, block):
     hid = gelu_value(middle[...]).astype(BF16)
     hidden[...] = hid
-    own = pl.ds(pl.multiple_of(place[HEAD] * half, half), half)
-    slope[...] = gelu_slope(middle[own, :])
     block[...] = wide(feat) + dot(hid, point[...], NT)
 
 
 def tracks(place, block, other_middle, near, far, cotangent, *rest):
-    *points, keep, give, block_b, grads = rest
+    *points, give, block_b, grads = rest
     sample = place[SAMPLE]
-    half = keep.shape[0]
     piece = block_b.shape[2]
     width = other_middle.shape[1]
-    own = pl.ds(pl.multiple_of(place[HEAD] * half, half), half)
-    theirs = pl.ds(pl.multiple_of((1 - place[HEAD]) * half, half), half)
-
-    def turned(ref, columns):
-        return jnp.concatenate([ref[theirs, columns], ref[own, columns]], axis=0)
-
-    hid = gelu_value(turned(other_middle, slice(None)).astype(F32)).astype(BF16)
+    hid = gelu_value(wide(other_middle)).astype(BF16)
     ahead = 0
     for point in points:
         number = point.shape[0]
         which, column = (sample, ahead) if ahead < piece else (1 - sample, ahead - piece)
         columns = pl.ds(pl.multiple_of(which * piece + column, number), number)
-        value = turned(block, columns) + dot(hid, point[...], NT)
+        value = block[:, columns] + dot(hid, point[...], NT)
         block_b[which, :, column : column + number] = value.astype(BF16)
         ahead += number
     number = near.shape[1]
@@ -305,113 +301,85 @@
         columns = slice(start, start + tile)
         scores = dot(block_b[sample], near[:, columns], NN)
         scores += dot(block_b[1 - sample], far[:, columns], NN)
-        cot = turned(cotangent, columns).astype(F32)
-        grads[:, columns] = (cot * jax.nn.sigmoid(scores)).astype(BF16)
+        grads[:, columns] = (wide(cotangent.at[:, columns]) * jax.nn.sigmoid(scores)).astype(BF16)
     for which, weight in ((sample, near), (1 - sample, far)):
         columns = pl.ds(pl.multiple_of(which * piece, piece), piece)
-        value = dot(grads[...], weight[...], NT)
-        give[:, columns] = value[:half].astype(BF16)
-        keep[:, columns] = value[half:]
-
-
-def slopes(place, other_middle, feat, slope_other, slope_feat):
-    half = slope_other.shape[0]
-    own = pl.ds(pl.multiple_of(place[HEAD] * half, half), half)
-    slope_other[...] = gelu_slope(other_middle[own, :].astype(F32))
-    slope_feat[...] = gelu_slope(feat[own, :].astype(F32))
-
-
-def middle_grads(place, keep, theirs, point, slope, slope_other, *rest):
-    *points, out_grad, both, grad_own, grad_other = rest
-    sample = place[SAMPLE]
-    channels = keep.shape[1]
-    piece = channels // 2
-    total = keep[...] + wide(theirs)
+        give[:, columns] = dot(grads[...], weight[...], NT).astype(BF16)
+
+
+def slopes(place, middle, feat, slope, slope_feat):
+    slope[...] = gelu_slope(middle[...])
+    slope_feat[...] = gelu_slope(wide(feat))
+
+
+def middle_grads(
+    place, own, theirs, point, slope, out_grad, middle_grad, kept, first, second, turned
+):
+    total = wide(own) + wide(theirs)
     out_grad[...] = total
     total_b = total.astype(BF16)
-    both[:, :channels] = total_b
-    grad_own[...] = (dot(total_b, point[...], NN) * slope[...]).astype(BF16)
-    other, ahead = None, 0
-    for part in points:
-        number = part.shape[0]
-        which, column = (sample, ahead) if ahead < piece else (1 - sample, ahead - piece)
-        left = both[:, pl.ds(pl.multiple_of(which * piece + column, number), number)]
-        value = dot(left, part[...], NN)
-        other = value if other is None else other + value
-        ahead += number
-    other = (other * slope_other[...]).astype(BF16)
-    grad_other[...] = other
-    both[:, channels:] = other
-
-
-def assembled(field, own, theirs, head):
-    half = field.shape[0] // 2
-    field[pl.ds(pl.multiple_of(head * half, half), half), :] = own
-    field[pl.ds(pl.multiple_of((1 - head) * half, half), half), :] = theirs
-
-
-def gathered(
-    place, both, got, grad_own, straight, crossed, middle_grad, moved, kept, given, whole,
-):
-    channels = whole.shape[1]
-    groups = kept.shape[0]
-    assembled(middle_grad, grad_own[...], got[:, channels:], place[HEAD])
-    assembled(moved, straight[...], crossed[...], place[HEAD])
-    assembled(whole, both[:, :channels], got[:, :channels], place[HEAD])
-    part_channels(place, whole[...].T, kept, given.at[:groups])
-    block, rows = kept.shape[1:]
-    number = middle_grad.shape[1] // block
-    shape = (number, block, rows)
-    given[groups : groups + number] = middle_grad[...].T.reshape(shape)
-    given[groups + number :] = moved[...].T.reshape(shape)
-
-
-def products(
-    place, acts, other_acts, outs, pack, middle_grad, moved, hidden, other_hidden,
-    keep, along, across, both,
-):
-    groups, block, rows = acts.shape
-    width = hidden.shape[1]
-    number = width // block
-    half = groups // 2
-    other_mid = pack[groups : groups + number].reshape(width, rows)
-    other_moved = pack[groups + number :].reshape(width, rows)
+    grad = (dot(total_b, point[...], NN) * slope[...]).astype(BF16)
+    middle_grad[...] = grad
+    turned[...] = grad.T
+    part_channels(place, total_b.T, kept, [first, second])
+
+
+def each_chip(place, keep, along, across, both, values):
     mid, lowest = place[MID], place[LOWEST]
-
     for i, j, out in (
         (1 - mid, 1 - lowest, both),
         (1 - mid, lowest, along),
         (mid, 1 - lowest, across),
         (mid, lowest, keep),
     ):
-        at = 2 * i + j
 
         def left(ref):
-            return jnp.concatenate([ref[at], ref[half + at]], axis=0)
-
-        own, other = left(acts), left(other_acts)
-        values = (
-            dot(own, moved[...], NN) + dot(other, other_moved, NT),
-            dot(own, middle_grad[...], NN) + dot(other, other_mid, NT),
-            dot(left(outs), hidden[...], NN) + dot(left(pack), other_hidden[...], NN),
+            groups, at = ref.shape[0], 2 * i + j
+            return jnp.concatenate([ref[at], ref[groups // 2 + at]], axis=0)
+
+        for k, value in enumerate(values(left)):
+            width = value.shape[1]
+            shape = (2, out.shape[1], width)
+            out[:, :, k * width : (k + 1) * width] = value.astype(out.dtype).reshape(shape)
+
+
+def middle_products(
+    place, acts, other_acts, outs, first, second, other_mid, middle_grad, hidden, other_hidden,
+    keep, along, across, both, other_outs,
+):
+    number = first.shape[0]
+    other_outs[:number] = first[...]
+    other_outs[number:] = second[...]
+
+    def values(left):
+        return (
+            dot(left(acts), middle_grad[...], NN) + dot(left(other_acts), other_mid[...], NT),
+            dot(left(outs), hidden[...], NN) + dot(left(other_outs), other_hidden[...], NN),
         )
-        for k, value in enumerate(values):
-            shape = (2, block, width)
-            out[:, :, k * width : (k + 1) * width] = value.astype(out.dtype).reshape(shape)
-
-
-def act_given(place, middle_grad, moved, weight, give):
-    half = give.shape[0]
-    theirs = pl.ds(pl.multiple_of((1 - place[HEAD]) * half, half), half)
-    value = dot(middle_grad[theirs, :], weight[1], NT)
-    give[...] = (value + dot(moved[theirs, :], weight[place[0]], NT)).astype(BF16)
-
-
-def act_kept(place, middle_grad, moved, weight, keep):
-    half = keep.shape[0]
-    own = pl.ds(pl.multiple_of(place[HEAD] * half, half), half)
-    value = dot(middle_grad[own, :], weight[1], NT)
-    keep[...] = value + dot(moved[own, :], weight[place[0]], NT)
+
+    each_chip(place, keep, along, across, both, values)
+
+
+def outer_products(
+    place, acts, other_acts, moved, first, second, keep, along, across, both, other_moved
+):
+    number = first.shape[0]
+    other_moved[:number] = first[...]
+    other_moved[number:] = second[...]
+
+    def values(left):
+        return (dot(left(acts), moved[...], NN) + dot(left(other_acts), other_moved[...], NN),)
+
+    each_chip(place, keep, along, across, both, values)
+
+
+def act_part(first):
+    def act_rows(place, middle_grad, moved, weight, give):
+        rows = slice(first, first + give.shape[0])
+        value = dot(middle_grad[rows, :], weight[1], NT)
+        give[...] = (value + dot(moved[rows, :], weight[place[0]], NT)).astype(BF16)
+
+    return act_rows
 
 
 def chips_sum(place, kept, along, across, both, keep, give):
@@ -423,17 +391,21 @@
     keep[...] = part(place[TOP])
 
 
-def input_part(place, out_grad, kept, got, slope_feat, result):
-    result[...] = (out_grad[...] + (kept[...] + wide(got)) * slope_feat[...]).astype(BF16)
-
-
-def finish(place, kept, got, own, theirs, dilated, point, result):
-    assembled(result, own[...], theirs[...], place[HEAD])
+def finish(
+    place, out_grad, slope, act_one, got_one, act_two, got_two, mid_kept, mid_got, kept, got,
+    dilated, point, result,
+):
     width = point.shape[1]
-    dilated[place[0]] = kept[:, :width]
-    dilated[2 - place[0]] = got[:, :width].astype(F32)
-    dilated[1] = kept[:, width : 2 * width] + got[:, width : 2 * width].astype(F32)
-    point[...] = kept[:, 2 * width :] + got[:, 2 * width :].astype(F32)
+    dilated[place[0]] = kept[...]
+    dilated[2 - place[0]] = wide(got)
+    dilated[1] = mid_kept[:, :width] + mid_got[:, :width].astype(F32)
+    point[...] = mid_kept[:, width:] + mid_got[:, width:].astype(F32)
+    first = 0
+    for own, theirs in ((act_one, got_one), (act_two, got_two)):
+        rows = slice(first, first + own.shape[0])
+        act_grad = wide(own) + wide(theirs)
+        result[rows, :] = (out_grad[rows, :] + act_grad * slope[rows, :]).astype(BF16)
+        first += own.shape[0]
 
 
 def body(features, dilated_weight, point_weight, track_weight, track_cotangent):
@@ -456,13 +428,23 @@
     feat = features.reshape(rows, channels)
     cotangent = track_cotangent.reshape(rows, tracks_here)
     pairs = [(i, (i + dist) % n_seq) for i in range(n_seq)]
-    crossing = [(2 * i + k, 2 * j + 1 - k) for i, j in pairs for k in range(2)]
-
+
+    (own_piece,) = kernel_call(
+        piece_of,
+        [((piece, width), BF16)],
+        [place, in_hbm(point_weight)],
+        scratch=[pltpu.SemaphoreType.DMA],
+        spaces={1: pltpu.HBM},
+    )
+    near = flip(own_piece, "head")
+    cut = piece // 3
+    points = [near] + [flip(near[k : k + cut], "sample") for k in range(0, piece, cut)]
     far_track = flip(track_weight, "sample")
     acted, term = kernel_call(
         outer_term,
         [((rows, channels), BF16), ((rows, width), BF16)],
         [place, in_hbm(feat), in_hbm(taps)],
+        own_piece,
         scratch=[
             pltpu.VMEM((rows, channels), BF16),
             pltpu.VMEM((channels, width), BF16),
@@ -473,104 +455,89 @@
     arrived = lax.ppermute(term, "seq", pairs)
     groups = n_seq
 
-    (own_piece,) = kernel_call(
-        piece_of, [((piece, width), BF16)], [place, point_weight], acted
-    )
-    cut = piece // 3
-    near = [flip(own_piece[k : k + cut], "head") for k in range(0, piece, cut)]
-    far = [
-        flip(part[k : k + cut // 2], "sample") for part in near for k in range(0, cut, cut // 2)
-    ]
-    points = near + far
-
     turned = ((groups, block, rows), BF16)
     middle, acts, acts_given = kernel_call(
         middle_term,
         [((rows, width), F32), turned, turned],
         [place, acted, taps],
-        own_piece,
     )
     middle, middle_b = kernel_call(
         add_terms, [((rows, width), F32), ((rows, width), BF16)], [place, middle, arrived], acts
     )
     other_middle = flip(middle_b, "head")
-    hidden, slope, block_part = kernel_call(
+    hidden, block_part = kernel_call(
         own_hidden,
-        [((rows, width), BF16), ((half, width), F32), ((rows, channels), F32)],
+        [((rows, width), BF16), ((rows, channels), F32)],
         [place, middle, feat, point_weight],
     )
-
-    keep, give = kernel_call(
+    (give,) = kernel_call(
         tracks,
-        [((half, channels), F32), ((half, channels), BF16)],
+        [((rows, channels), BF16)],
         [place, block_part, other_middle, track_weight, far_track, cotangent, *points],
         scratch=[
             pltpu.VMEM((n_sample, rows, piece), BF16),
             pltpu.VMEM((rows, tracks_here), BF16),
         ],
     )
-    theirs = flip(give, "head")
-    slope_other, slope_feat = kernel_call(
-        slopes,
-        [((half, width), F32), ((half, channels), F32)],
-        [place, other_middle, feat],
-        keep,
-    )
-    out_grad, both, grad_own, grad_other = kernel_call(
+    got = flip(give, "head")
+    slope, slope_feat = kernel_call(
+        slopes, [((rows, width), F32), ((rows, channels), F32)], [place, middle, feat], give
+    )
+    out_grad, middle_grad, outs, *given = kernel_call(
         middle_grads,
-        [
-            ((half, channels), F32),
-            ((half, channels + width), BF16),
-            ((half, width), BF16),
-            ((half, width), BF16),
-        ],
-        [place, keep, theirs, point_weight, slope, slope_other, *points],
-    )
-    straight = lax.ppermute(grad_own, "seq", pairs)
-    crossed = lax.ppermute(grad_other, ("seq", "head"), crossing)
-    got = flip(both, "head")
-    number = groups + 2 * width // block
-    middle_grad, moved, outs, pack = kernel_call(
-        gathered,
-        [((rows, width), BF16)] * 2 + [turned, ((number, block, rows), BF16)],
-        [place, both, got, grad_own, straight, crossed],
-        scratch=[pltpu.VMEM((rows, channels), BF16)],
-    )
-    other_pack = flip(pack, "sample")
-    (act_give,) = kernel_call(
-        act_given, [((half, channels), BF16)], [place, middle_grad, moved, taps]
-    )
-    act_got = flip(act_give, "head")
-    part = (2, block, 3 * width)
-    kept, along, across, diagonal = kernel_call(
-        products,
-        [(part, F32)] + [(part, BF16)] * 3,
-        [
-            place, acts, flip(acts_given, "sample"), outs, other_pack, middle_grad, moved,
-            hidden, flip(hidden, "sample"),
-        ],
-        act_give,
-    )
-    along, across, diagonal = flip(along, "seq", 2), flip(across, "seq", 1), flip(diagonal, "seq", 3)
-    (act_keep,) = kernel_call(
-        act_kept, [((half, channels), F32)], [place, middle_grad, moved, taps], kept
-    )
-    (input_half,) = kernel_call(
-        input_part,
-        [((half, channels), BF16)],
-        [place, out_grad, act_keep, act_got, slope_feat],
-    )
-    input_other = flip(input_half, "head")
-    kept, given = kernel_call(
-        chips_sum,
-        [((block, 3 * width), F32), ((block, 3 * width), BF16)],
-        [place, kept, along, across, diagonal],
-        input_half,
-    )
+        [((rows, channels), F32), ((rows, width), BF16), turned]
+        + [((groups // 2, block, rows), BF16)] * 2
+        + [((width, rows), BF16)],
+        [place, give, got, point_weight, slope],
+    )
+    moved = lax.ppermute(middle_grad, "seq", pairs)
+
+    def traded(kernel, columns, ins, after=None, scratch=()):
+        part = (2, block, columns)
+        keep, *gives = kernel_call(
+            kernel, [(part, F32)] + [(part, BF16)] * 3, [place, *ins], after, scratch
+        )
+        return keep, [flip(value, "seq", step) for value, step in zip(gives, (2, 1, 3))]
+
+    def halved(kept, got, columns, after):
+        part = (block, columns)
+        kept, given = kernel_call(
+            chips_sum, [(part, F32), (part, BF16)], [place, kept, *got], after
+        )
+        return kept, flip(given, "seq", 4)
+
+    other_acts, other_hidden = flip(acts_given, "sample"), flip(hidden, "sample")
+    mid_kept, mid_got = traded(
+        middle_products,
+        2 * width,
+        [acts, other_acts, outs]
+        + [flip(part, "sample") for part in given]
+        + [middle_grad, hidden, other_hidden],
+        scratch=[pltpu.VMEM((groups, block, rows), BF16)],
+    )
+    other_moved = [flip(moved[k : k + half], "sample") for k in (0, half)]
+    act_one = kernel_call(
+        act_part(0), [((half, channels), BF16)], [place, middle_grad, moved, taps], mid_kept
+    )[0]
+    kept, got = traded(
+        outer_products,
+        width,
+        [acts, other_acts, moved, *other_moved],
+        act_one,
+        scratch=[pltpu.VMEM((rows, width), BF16)],
+    )
+    act_two = kernel_call(
+        act_part(half), [((half, channels), BF16)], [place, middle_grad, moved, taps], kept
+    )[0]
+    mid_kept, mid_got = halved(mid_kept, mid_got, 2 * width, act_two)
+    kept, got = halved(kept, got, width, mid_kept)
     dilated_grad, point_grad, input_grad = kernel_call(
         finish,
         [((3, block, width), F32), ((block, width), F32), ((rows, channels), BF16)],
-        [place, kept, flip(given, "seq", 4), input_half, input_other],
+        [
+            place, out_grad, slope_feat, act_one, flip(act_one, "head"),
+            act_two, flip(act_two, "head"), mid_kept, mid_got, kept, got,
+        ],
     )
     dilated_grad = jnp.transpose(dilated_grad, (1, 0, 2))
     return (input_grad.reshape(samples, positions, channels), dilated_grad, point_grad)

time: 105 us -> 93.1 us (0.89)
  waiting for transfers between devices: 55.7 us -> 45.6 us
  starting transfers between devices: 24 us -> 22.1 us
    ppermute x22 -> x24, waiting for transfers between devices: 43.8 us -> 33.4 us  [flip(): return lax.ppermute(value, axis, [(i, i ^ step) for i in range(count)])]
    ppermute x1, waiting for transfers between devices: 4.34 us -> 8.37 us  [body(): arrived = lax.ppermute(term, 'seq', pairs)]
    ppermute x2 -> x1, waiting for transfers between devices: 7.62 us -> 3.8 us  [body(): moved = lax.ppermute(middle_grad, 'seq', pairs)]
    ppermute x2 -> x1, starting transfers between devices: 2.89 us -> 0.01 us  [body(): moved = lax.ppermute(middle_grad, 'seq', pairs)]
    ppermute x22 -> x24, starting transfers between devices: 17.4 us -> 19.5 us  [flip(): return lax.ppermute(value, axis, [(i, i ^ step) for i in range(count)])]
  transfers between devices with their start and end apart: 25 -> 26, of which waited for: 13 -> 11; matrix products, arithmetic and copies ran while one was open for 0% -> 0% of each run, Pallas kernels for 13% -> 19%
where the time goes in v4:
time: 93.1 us; the launch traced here: 92.9 us
  waiting for transfers between devices  45.6 us (49%)
  Pallas kernels  24.2 us (26%)
  starting transfers between devices  22.1 us (24%)
    ppermute x24, waiting for transfers between devices, flip(): return lax.ppermute(value, axis, [(i, i ^ step) for i in range(count)])  33.4 us
    pallas_call x15, Pallas kernels, kernel_call(): pl.pallas_call(run, out_shape=[jax.ShapeDtypeStruct(s, d) for s, d in out...  24.2 us
    ppermute x24, starting transfers between devices, flip(): return lax.ppermute(value, axis, [(i, i ^ step) for i in range(count)])  19.5 us
    ppermute x1, waiting for transfers between devices, body(): arrived = lax.ppermute(term, 'seq', pairs)  8.37 us
    ppermute x1, waiting for transfers between devices, body(): moved = lax.ppermute(middle_grad, 'seq', pairs)  3.8 us
    ppermute x1, starting transfers between devices, body(): arrived = lax.ppermute(term, 'seq', pairs)  2.65 us
  transfers between devices with their start and end apart: 26, of which 11 were waited for; matrix products, arithmetic and copies ran while one was open for 0% of the time, Pallas kernels for 19%

profile of v4, /device:TPU:0, one launch (start us, length us, event | category | flops | bytes accessed | tf_op | source)
XLA Modules:
  0.0 92.9 jit_solution(4642917311975215600)
XLA Ops:
  1.2 1.6 %piece_of.1.refs_3_ = bf16[768,384]{1,0:T(8,128)(2,1)S(1)} custom-call(s32[6]{0:T(128)S(1)} %stack.27.refs_0_, bf16[1536,384]{1,0:T(8,128)(2,1)} %refs_3_.5), custom_call_target="tpu_custom_call" | custom-call | flops 1 | bytes 1 | tf_op jit(solution)/shard_map/piece_of/pallas_call | solution.py:200
  2.9 2.6 %collective-permute-start.3 = (bf16[768,384]{1,0:T(8,128)(2,1)S(1)}, bf16[768,384]{1,0:T(8,128)(2,1)S(1)}, u32[]{:S(2)}, u32[]{:S(2)}) collective-permute-start(bf16[768,384]{1,0:T(8,128)(2,1)S(1)} %piece_of.1.refs_3_), channel_id=1, source_target_pairs={{0,2},{2,0},{1,3},{3,1},{4,6},{6,4},{5,7},{7,5},{8,10},{10,8},{9,1... | collective-permute-start | bytes 1769480 | tf_op jit(solution)/shard_map/ppermute | solution.py:34
  5.4 3.1 %outer_term.1 = (bf16[256,1536]{1,0:T(8,128)(2,1)S(1)}, bf16[256,384]{1,0:T(8,128)(2,1)S(1)}) custom-call(s32[6]{0:T(128)S(1)} %stack.27.refs_0_, bf16[256,1536]{1,0:T(8,128)(2,1)} %bitcast.15, bf16[3,1536,384]{2,1,0:T(8,128)(2,1)} %bitcast.11, bf16[768,384]{1,0:T(8,128)(2,1)S(1)} %piece_of.1.refs_3_), custom_call_target="tpu_custom_call" | custom-call | flops 1 | bytes 1 | tf_op jit(solution)/shard_map/outer_term/pallas_call | solution.py:200
  8.6 2.7 %collective-permute-start = (bf16[256,384]{1,0:T(8,128)(2,1)S(1)}, bf16[256,384]{1,0:T(8,128)(2,1)S(1)}, u32[]{:S(2)}, u32[]{:S(2)}) collective-permute-start(bf16[256,384]{1,0:T(8,128)(2,1)S(1)} %get-tuple-element.37), channel_id=1, source_target_pairs={{0,16},{4,20},{8,24},{12,28},{16,0},{20,4},{24,8},{28,12},{1,17},{... | collective-permute-start | bytes 589832 | tf_op jit(solution)/shard_map/ppermute | solution.py:455
  11.3 1.1 %middle_term.1 = (f32[256,384]{1,0:T(8,128)S(1)}, bf16[8,96,256]{2,1,0:T(8,128)(2,1)S(1)}, bf16[8,96,256]{2,1,0:T(8,128)(2,1)S(1)}) custom-call(s32[6]{0:T(128)S(1)} %stack.27.refs_0_, bf16[256,1536]{1,0:T(8,128)(2,1)S(1)} %get-tuple-element.35.refs_1_, bf16[3,1536,384]{2,1,0:T(8,128)(2,1)S(1)} %bitcast.12), custom_call_target="tpu_custom_call" | custom-call | flops 1 | bytes 1 | tf_op jit(solution)/shard_map/middle_term/pallas_call | solution.py:200
  12.4 8.4 %collective-permute-done.refs_2_ = bf16[256,384]{1,0:T(8,128)(2,1)S(1)} collective-permute-done((bf16[256,384]{1,0:T(8,128)(2,1)S(1)}, bf16[256,384]{1,0:T(8,128)(2,1)S(1)}, u32[]{:S(2)}, u32[]{:S(2)}) %collective-permute-start) | collective-permute-done | bytes 196640 | tf_op jit(solution)/shard_map/ppermute | solution.py:455
  22.7 1.2 %own_hidden.1 = (bf16[256,384]{1,0:T(8,128)(2,1)S(1)}, f32[256,1536]{1,0:T(8,128)S(1)}) custom-call(s32[6]{0:T(128)S(1)} %stack.27.refs_0_, f32[256,384]{1,0:T(8,128)S(1)} %get-tuple-element.39.refs_1_, bf16[256,1536]{1,0:T(8,128)(2,1)S(1)} %bitcast.16, bf16[1536,384]{1,0:T(8,128)(2,1)S(1)} %copy-done.1), custom_call_target="tpu_custom_call" | custom-call | flops 1 | bytes 1 | tf_op jit(solution)/shard_map/own_hidden/pallas_call | solution.py:200
  23.8 3.8 %collective-permute-done.1.refs_2_ = bf16[256,384]{1,0:T(8,128)(2,1)S(1)} collective-permute-done((bf16[256,384]{1,0:T(8,128)(2,1)S(1)}, bf16[256,384]{1,0:T(8,128)(2,1)S(1)}, u32[]{:S(2)}, u32[]{:S(2)}) %collective-permute-start.1) | collective-permute-done | bytes 196640 | tf_op jit(solution)/shard_map/ppermute | solution.py:34
  27.7 4.9 %tracks.1.refs_3_.refs_1_ = bf16[256,1536]{1,0:T(8,128)(2,1)S(1)} custom-call(s32[6]{0:T(128)S(1)} %stack.27.refs_0_, f32[256,1536]{1,0:T(8,128)S(1)} %get-tuple-element.40.refs_1_, bf16[256,384]{1,0:T(8,128)(2,1)S(1)} %collective-permute-done.1.refs_2_, bf16[768,1920]{1,0:T(8,128)(2,1)S(1)} %copy-done.3, ...), custom_call_target="tpu_custom_call" | custom-call | flops 1 | bytes 1 | tf_op jit(solution)/shard_map/tracks/pallas_call | solution.py:200
  32.6 0.9 collective-permute-start.7
  34.0 1.7 %slopes.1 = (f32[256,384]{1,0:T(8,128)S(1)}, f32[256,1536]{1,0:T(8,128)S(1)}) custom-call(s32[6]{0:T(128)S(1)} %stack.27.refs_0_, f32[256,384]{1,0:T(8,128)S(1)} %get-tuple-element.39.refs_1_, bf16[256,1536]{1,0:T(8,128)(2,1)S(1)} %bitcast.17, bf16[256,1536]{1,0:T(8,128)(2,1)S(1)} %tracks.1.refs_3_.refs_1_), custom_call_target="tpu_custom_call" | custom-call | flops 1 | bytes 1 | tf_op jit(solution)/shard_map/slopes/pallas_call | solution.py:200
  35.7 14.9 %collective-permute-done.7.refs_2_ = bf16[256,1536]{1,0:T(8,128)(2,1)S(1)} collective-permute-done((bf16[256,1536]{1,0:T(8,128)(2,1)S(1)}, bf16[256,1536]{1,0:T(8,128)(2,1)S(1)}, u32[]{:S(2)}, u32[]{:S(2)}) %collective-permute-start.7) | collective-permute-done | bytes 786464 | tf_op jit(solution)/shard_map/ppermute | solution.py:34
  50.6 1.2 %middle_grads.1 = (f32[256,1536]{1,0:T(8,128)S(1)}, bf16[256,384]{1,0:T(8,128)(2,1)S(1)}, bf16[8,96,256]{2,1,0:T(8,128)(2,1)S(1)}, bf16[4,96,256]{2,1,0:T(8,128)...) custom-call(s32[6]{0:T(128)S(1)} %stack.27.refs_0_, ...), custom_call_target="tpu_custom_call" | custom-call | flops 1 | bytes 1 | tf_op jit(solution)/shard_map/middle_grads/pallas_call | solution.py:200
  52.4 0.8 collective-permute-done.10.refs_4_
  53.9 1.6 %middle_products.1 = (f32[2,96,768]{2,1,0:T(8,128)S(1)}, bf16[2,96,768]{2,1,0:T(8,128)(2,1)S(1)}, bf16[2,96,768]{2,1,0:T(8,128)(2,1)S(1)}, bf16[2,96,768]{2,1,0:T(8,128)(2,1)S(1)}) custom-call(s32[6]{0:T(128)S(1)} %stack.27.refs_0_, bf16[8,96,256]{2,1,0:T(8,128)(2,1)S(1)} %get-tuple-element.38.refs_3_.refs_1_, ...), custom_call_target="tpu_custom_call" | custom-call | flops 1 | bytes 1 | tf_op jit(solution)/shard_map/middle_products/pallas_call | solution.py:200
  55.4 4.1 %collective-permute-start.18 = (bf16[2,96,768]{2,1,0:T(8,128)(2,1)S(1)}, bf16[2,96,768]{2,1,0:T(8,128)(2,1)S(1)}, u32[]{:S(2)}, u32[]{:S(2)}) collective-permute-start(bf16[2,96,768]{2,1,0:T(8,128)(2,1)S(1)} %get-tuple-element.54), channel_id=1, source_target_pairs={{0,8},{4,12},{8,0},{12,4},{16,24},{20,28},{24,16},{28,20},{1,9},{5... | collective-permute-start | bytes 884744 | tf_op jit(solution)/shard_map/ppermute | solution.py:34
  59.6 1.5 %collective-permute-start.19 = (bf16[2,96,768]{2,1,0:T(8,128)(2,1)S(1)}, bf16[2,96,768]{2,1,0:T(8,128)(2,1)S(1)}, u32[]{:S(2)}, u32[]{:S(2)}) collective-permute-start(bf16[2,96,768]{2,1,0:T(8,128)(2,1)S(1)} %get-tuple-element.55), channel_id=1, source_target_pairs={{0,4},{4,0},{8,12},{12,8},{16,20},{20,16},{24,28},{28,24},{1,5},{5... | collective-permute-start | bytes 884744 | tf_op jit(solution)/shard_map/ppermute | solution.py:34
  61.1 3.8 %collective-permute-done.8.refs_2_.refs_3_ = bf16[256,384]{1,0:T(8,128)(2,1)S(1)} collective-permute-done((bf16[256,384]{1,0:T(8,128)(2,1)S(1)}, bf16[256,384]{1,0:T(8,128)(2,1)S(1)}, u32[]{:S(2)}, u32[]{:S(2)}) %collective-permute-start.8) | collective-permute-done | bytes 196640 | tf_op jit(solution)/shard_map/ppermute | solution.py:493
  65.5 1.4 %act_rows.2.refs_6_.refs_3_ = bf16[128,1536]{1,0:T(8,128)(2,1)S(1)} custom-call(s32[6]{0:T(128)S(1)} %stack.27.refs_0_, bf16[256,384]{1,0:T(8,128)(2,1)S(1)} %get-tuple-element.45.refs_7_.refs_1_, bf16[256,384]{1,0:T(8,128)(2,1)S(1)} %collective-permute-done.8.refs_2_.refs_3_, bf16[3,1536,384]{2,1,0:T(8,128)(2,1)S(1)} %bitcast.13, ...), custom_call_target="tpu_custom_call" | custom-call | flops 1 | bytes 1 | tf_op jit(solution)/shard_map/act_rows/pallas_call | solution.py:200
  66.9 1.2 %collective-permute-start.14 = (bf16[128,1536]{1,0:T(8,128)(2,1)S(1)}, bf16[128,1536]{1,0:T(8,128)(2,1)S(1)}, u32[]{:S(2)}, u32[]{:S(2)}) collective-permute-start(bf16[128,1536]{1,0:T(8,128)(2,1)S(1)} %act_rows.2.refs_6_.refs_3_), channel_id=1, source_target_pairs={{0,2},{2,0},{1,3},{3,1},{4,6},{6,4},{5,7},{7,5},{8,10},{10,8},{9,1... | collective-permute-start | bytes 1179656 | tf_op jit(solution)/shard_map/ppermute | solution.py:34
  68.1 1.1 %outer_products.1 = (f32[2,96,384]{2,1,0:T(8,128)S(1)}, bf16[2,96,384]{2,1,0:T(8,128)(2,1)S(1)}, bf16[2,96,384]{2,1,0:T(8,128)(2,1)S(1)}, bf16[2,96,384]{2,1,0:T(8,128)(2,1)S(1)}) custom-call(s32[6]{0:T(128)S(1)} %stack.27.refs_0_, bf16[8,96,256]{2,1,0:T(8,128)(2,1)S(1)} %get-tuple-element.38.refs_3_.refs_1_, ...), custom_call_target="tpu_custom_call" | custom-call | flops 1 | bytes 1 | tf_op jit(solution)/shard_map/outer_products/pallas_call | solution.py:200
  69.3 1.4 %act_rows.3.refs_5_ = bf16[128,1536]{1,0:T(8,128)(2,1)S(1)} custom-call(s32[6]{0:T(128)S(1)} %stack.27.refs_0_, bf16[256,384]{1,0:T(8,128)(2,1)S(1)} %get-tuple-element.45.refs_7_.refs_1_, bf16[256,384]{1,0:T(8,128)(2,1)S(1)} %collective-permute-done.8.refs_2_.refs_3_, bf16[3,1536,384]{2,1,0:T(8,128)(2,1)S(1)} %bitcast.14, ...), custom_call_target="tpu_custom_call" | custom-call | flops 1 | bytes 1 | tf_op jit(solution)/shard_map/act_rows/pallas_call | solution.py:200
  70.7 0.9 %collective-permute-start.17 = (bf16[128,1536]{1,0:T(8,128)(2,1)S(1)}, bf16[128,1536]{1,0:T(8,128)(2,1)S(1)}, u32[]{:S(2)}, u32[]{:S(2)}) collective-permute-start(bf16[128,1536]{1,0:T(8,128)(2,1)S(1)} %act_rows.3.refs_5_), channel_id=1, source_target_pairs={{0,2},{2,0},{1,3},{3,1},{4,6},{6,4},{5,7},{7,5},{8,10},{10,8},{9,1... | collective-permute-start | bytes 1179656 | tf_op jit(solution)/shard_map/ppermute | solution.py:34
  71.6 1.6 %collective-permute-start.23 = (bf16[2,96,384]{2,1,0:T(8,128)(2,1)S(1)}, bf16[2,96,384]{2,1,0:T(8,128)(2,1)S(1)}, u32[]{:S(2)}, u32[]{:S(2)}) collective-permute-start(bf16[2,96,384]{2,1,0:T(8,128)(2,1)S(1)} %get-tuple-element.60), channel_id=1, source_target_pairs={{0,4},{4,0},{8,12},{12,8},{16,20},{20,16},{24,28},{28,24},{1,5},{5... | collective-permute-start | bytes 442376 | tf_op jit(solution)/shard_map/ppermute | solution.py:34
  73.2 3.3 %collective-permute-done.20.refs_4_ = bf16[2,96,768]{2,1,0:T(8,128)(2,1)S(1)} collective-permute-done((bf16[2,96,768]{2,1,0:T(8,128)(2,1)S(1)}, bf16[2,96,768]{2,1,0:T(8,128)(2,1)S(1)}, u32[]{:S(2)}, u32[]{:S(2)}) %collective-permute-start.20) | collective-permute-done | bytes 294944 | tf_op jit(solution)/shard_map/ppermute | solution.py:34
  76.7 0.7 chips_sum.2
  77.4 0.9 collective-permute-done.22.refs_2_
  78.3 2.7 %collective-permute-start.21 = (bf16[96,768]{1,0:T(8,128)(2,1)S(1)}, bf16[96,768]{1,0:T(8,128)(2,1)S(1)}, u32[]{:S(2)}, u32[]{:S(2)}) collective-permute-start(bf16[96,768]{1,0:T(8,128)(2,1)S(1)} %get-tuple-element.58), channel_id=1, source_target_pairs={{0,16},{4,20},{8,24},{12,28},{16,0},{20,4},{24,8},{28,12},{1,17},{... | collective-permute-start | bytes 442376 | tf_op jit(solution)/shard_map/ppermute | solution.py:34
  80.9 2.9 %collective-permute-done.24.refs_4_ = bf16[2,96,384]{2,1,0:T(8,128)(2,1)S(1)} collective-permute-done((bf16[2,96,384]{2,1,0:T(8,128)(2,1)S(1)}, bf16[2,96,384]{2,1,0:T(8,128)(2,1)S(1)}, u32[]{:S(2)}, u32[]{:S(2)}) %collective-permute-start.24) | collective-permute-done | bytes 147488 | tf_op jit(solution)/shard_map/ppermute | solution.py:34
  83.9 0.6 chips_sum.3
  84.9 6.1 %collective-permute-done.25.refs_10_ = bf16[96,384]{1,0:T(8,128)(2,1)S(1)} collective-permute-done((bf16[96,384]{1,0:T(8,128)(2,1)S(1)}, bf16[96,384]{1,0:T(8,128)(2,1)S(1)}, u32[]{:S(2)}, u32[]{:S(2)}) %collective-permute-start.25) | collective-permute-done | bytes 73760 | tf_op jit(solution)/shard_map/ppermute | solution.py:34
  91.0 1.9 %finish.1 = (f32[3,96,384]{2,1,0:T(8,128)}, f32[96,384]{1,0:T(8,128)}, bf16[256,1536]{1,0:T(8,128)(2,1)}) custom-call(s32[6]{0:T(128)S(1)} %stack.27.refs_0_, f32[256,1536]{1,0:T(8,128)S(1)} %get-tuple-element.43.refs_1_, f32[256,1536]{1,0:T(8,128)S(1)} %get-tuple-element.44.refs_2_, bf16[128,1536]{1,0:T(8,128)(2,1)S(1)} %act_rows.2.refs_6_.refs_3_, ...), custom_call_target="tpu_custom_call" | custom-call | flops 1 | bytes 1 | tf_op jit(solution)/shard_map/finish/pallas_call | solution.py:200
  (48 shorter events, 5.3 us)
Async XLA Ops:
  0.6 27.0 %collective-permute-start.2 = (bf16[768,1920]{1,0:T(8,128)(2,1)}, bf16[768,1920]{1,0:T(8,128)(2,1)S(1)}, u32[]{:S(2)}, u32[]{:S(2)}) collective-permute-start(bf16[768,1920]{1,0:T(8,128)(2,1)} %refs_3_.4), channel_id=1, source_target_pairs={{0,1},{1,0},{2,3},{3,2},{4,5},{5,4},{6,7},{7,6},{8,9},{9,8},{10,11... | collective-permute-start | bytes 8847368 | tf_op jit(solution)/shard_map/ppermute | solution.py:34
  2.9 19.1 %collective-permute-start.3 = (bf16[768,384]{1,0:T(8,128)(2,1)S(1)}, bf16[768,384]{1,0:T(8,128)(2,1)S(1)}, u32[]{:S(2)}, u32[]{:S(2)}) collective-permute-start(bf16[768,384]{1,0:T(8,128)(2,1)S(1)} %piece_of.1.refs_3_), channel_id=1, source_target_pairs={{0,2},{2,0},{1,3},{3,1},{4,6},{6,4},{5,7},{7,5},{8,10},{10,8},{9,1... | collective-permute-start | bytes 1769480 | tf_op jit(solution)/shard_map/ppermute | solution.py:34
  5.4 5.8 %copy-start = (bf16[1536,3,384]{2,0,1:T(8,128)(2,1)S(1)}, bf16[1536,3,384]{2,0,1:T(8,128)(2,1)}, u32[]{:S(2)}) copy-start(bf16[1536,3,384]{2,0,1:T(8,128)(2,1)} %param.6) | copy-start | bytes 10616836
  8.6 12.2 %collective-permute-start = (bf16[256,384]{1,0:T(8,128)(2,1)S(1)}, bf16[256,384]{1,0:T(8,128)(2,1)S(1)}, u32[]{:S(2)}, u32[]{:S(2)}) collective-permute-start(bf16[256,384]{1,0:T(8,128)(2,1)S(1)} %get-tuple-element.37), channel_id=1, source_target_pairs={{0,16},{4,20},{8,24},{12,28},{16,0},{20,4},{24,8},{28,12},{1,17},{... | collective-permute-start | bytes 589832 | tf_op jit(solution)/shard_map/ppermute | solution.py:455
  11.3 16.4 %copy-start.3 = (bf16[768,1920]{1,0:T(8,128)(2,1)S(1)}, bf16[768,1920]{1,0:T(8,128)(2,1)}, u32[]{:S(2)}) copy-start(bf16[768,1920]{1,0:T(8,128)(2,1)} %refs_3_.4) | copy-start | bytes 8847364
  12.4 10.3 %copy-start.1 = (bf16[1536,384]{1,0:T(8,128)(2,1)S(1)}, bf16[1536,384]{1,0:T(8,128)(2,1)}, u32[]{:S(2)}) copy-start(bf16[1536,384]{1,0:T(8,128)(2,1)} %refs_3_.5) | copy-start | bytes 3538948
  12.4 10.3 %copy-start.2 = (bf16[1,256,1536]{2,1,0:T(8,128)(2,1)S(1)}, bf16[1,256,1536]{2,1,0:T(8,128)(2,1)}, u32[]{:S(2)}) copy-start(bf16[1,256,1536]{2,1,0:T(8,128)(2,1)} %param.5) | copy-start | bytes 2359300
  21.4 6.3 %copy-start.4 = (bf16[1,256,1920]{2,1,0:T(8,128)(2,1)S(1)}, bf16[1,256,1920]{2,1,0:T(8,128)(2,1)}, u32[]{:S(2)}) copy-start(bf16[1,256,1920]{2,1,0:T(8,128)(2,1)} %param.9) | copy-start | bytes 2949124
  21.4 6.2 %collective-permute-start.1 = (bf16[256,384]{1,0:T(8,128)(2,1)S(1)}, bf16[256,384]{1,0:T(8,128)(2,1)S(1)}, u32[]{:S(2)}, u32[]{:S(2)}) collective-permute-start(bf16[256,384]{1,0:T(8,128)(2,1)S(1)} %get-tuple-element.41), channel_id=1, source_target_pairs={{0,2},{2,0},{1,3},{3,1},{4,6},{6,4},{5,7},{7,5},{8,10},{10,8},{9,1... | collective-permute-start | bytes 589832 | tf_op jit(solution)/shard_map/ppermute | solution.py:34
  22.0 5.6 %collective-permute-start.4 = (bf16[256,384]{1,0:T(8,128)(2,1)S(1)}, bf16[256,384]{1,0:T(8,128)(2,1)S(1)}, u32[]{:S(2)}, u32[]{:S(2)}) collective-permute-start(bf16[256,384]{1,0:T(8,128)(2,1)S(1)} %get-tuple-element.69), channel_id=1, source_target_pairs={{0,1},{1,0},{2,3},{3,2},{4,5},{5,4},{6,7},{7,6},{8,9},{9,8},{10,11... | collective-permute-start | bytes 589832 | tf_op jit(solution)/shard_map/ppermute | solution.py:34
  22.1 5.6 %collective-permute-start.5 = (bf16[256,384]{1,0:T(8,128)(2,1)S(1)}, bf16[256,384]{1,0:T(8,128)(2,1)S(1)}, u32[]{:S(2)}, u32[]{:S(2)}) collective-permute-start(bf16[256,384]{1,0:T(8,128)(2,1)S(1)} %get-tuple-element.68), channel_id=1, source_target_pairs={{0,1},{1,0},{2,3},{3,2},{4,5},{5,4},{6,7},{7,6},{8,9},{9,8},{10,11... | collective-permute-start | bytes 589832 | tf_op jit(solution)/shard_map/ppermute | solution.py:34
  22.6 5.1 %collective-permute-start.6 = (bf16[256,384]{1,0:T(8,128)(2,1)S(1)}, bf16[256,384]{1,0:T(8,128)(2,1)S(1)}, u32[]{:S(2)}, u32[]{:S(2)}) collective-permute-start(bf16[256,384]{1,0:T(8,128)(2,1)S(1)} %get-tuple-element.67), channel_id=1, source_target_pairs={{0,1},{1,0},{2,3},{3,2},{4,5},{5,4},{6,7},{7,6},{8,9},{9,8},{10,11... | collective-permute-start | bytes 589832 | tf_op jit(solution)/shard_map/ppermute | solution.py:34
  32.6 18.0 %collective-permute-start.7 = (bf16[256,1536]{1,0:T(8,128)(2,1)S(1)}, bf16[256,1536]{1,0:T(8,128)(2,1)S(1)}, u32[]{:S(2)}, u32[]{:S(2)}) collective-permute-start(bf16[256,1536]{1,0:T(8,128)(2,1)S(1)} %tracks.1.refs_3_.refs_1_), channel_id=1, source_target_pairs={{0,2},{2,0},{1,3},{3,1},{4,6},{6,4},{5,7},{7,5},{8,10},{10,8},{9,1... | collective-permute-start | bytes 2359304 | tf_op jit(solution)/shard_map/ppermute | solution.py:34
  33.5 19.0 %collective-permute-start.9 = (bf16[8,96,256]{2,1,0:T(8,128)(2,1)S(1)}, bf16[8,96,256]{2,1,0:T(8,128)(2,1)S(1)}, u32[]{:S(2)}, u32[]{:S(2)}) collective-permute-start(bf16[8,96,256]{2,1,0:T(8,128)(2,1)S(1)} %get-tuple-element.46), channel_id=1, source_target_pairs={{0,1},{1,0},{2,3},{3,2},{4,5},{5,4},{6,7},{7,6},{8,9},{9,8},{10,11... | collective-permute-start | bytes 1179656 | tf_op jit(solution)/shard_map/ppermute | solution.py:34
  33.5 19.0 %collective-permute-start.13 = (bf16[256,384]{1,0:T(8,128)(2,1)S(1)}, bf16[256,384]{1,0:T(8,128)(2,1)S(1)}, u32[]{:S(2)}, u32[]{:S(2)}) collective-permute-start(bf16[256,384]{1,0:T(8,128)(2,1)S(1)} %get-tuple-element.51.refs_8_), channel_id=1, source_target_pairs={{0,1},{1,0},{2,3},{3,2},{4,5},{5,4},{6,7},{7,6},{8,9},{9,8},{10,11... | collective-permute-start | bytes 589832 | tf_op jit(solution)/shard_map/ppermute | solution.py:34
  51.8 1.5 %collective-permute-start.10 = (bf16[4,96,256]{2,1,0:T(8,128)(2,1)S(1)}, bf16[4,96,256]{2,1,0:T(8,128)(2,1)S(1)}, u32[]{:S(2)}, u32[]{:S(2)}) collective-permute-start(bf16[4,96,256]{2,1,0:T(8,128)(2,1)S(1)} %get-tuple-element.48), channel_id=1, source_target_pairs={{0,1},{1,0},{2,3},{3,2},{4,5},{5,4},{6,7},{7,6},{8,9},{9,8},{10,11... | collective-permute-start | bytes 589832 | tf_op jit(solution)/shard_map/ppermute | solution.py:34
  51.9 1.7 %collective-permute-start.11 = (bf16[4,96,256]{2,1,0:T(8,128)(2,1)S(1)}, bf16[4,96,256]{2,1,0:T(8,128)(2,1)S(1)}, u32[]{:S(2)}, u32[]{:S(2)}) collective-permute-start(bf16[4,96,256]{2,1,0:T(8,128)(2,1)S(1)} %get-tuple-element.49), channel_id=1, source_target_pairs={{0,1},{1,0},{2,3},{3,2},{4,5},{5,4},{6,7},{7,6},{8,9},{9,8},{10,11... | collective-permute-start | bytes 589832 | tf_op jit(solution)/shard_map/ppermute | solution.py:34
  52.4 1.5 %collective-permute-start.12 = (bf16[384,256]{1,0:T(8,128)(2,1)S(1)}, bf16[384,256]{1,0:T(8,128)(2,1)S(1)}, u32[]{:S(2)}, u32[]{:S(2)}) collective-permute-start(bf16[384,256]{1,0:T(8,128)(2,1)S(1)} %get-tuple-element.50), channel_id=1, source_target_pairs={{0,1},{1,0},{2,3},{3,2},{4,5},{5,4},{6,7},{7,6},{8,9},{9,8},{10,11... | collective-permute-start | bytes 589832 | tf_op jit(solution)/shard_map/ppermute | solution.py:34
  52.4 12.5 %collective-permute-start.8 = (bf16[256,384]{1,0:T(8,128)(2,1)S(1)}, bf16[256,384]{1,0:T(8,128)(2,1)S(1)}, u32[]{:S(2)}, u32[]{:S(2)}) collective-permute-start(bf16[256,384]{1,0:T(8,128)(2,1)S(1)} %get-tuple-element.45.refs_7_.refs_1_), channel_id=1, source_target_pairs={{0,16},{4,20},{8,24},{12,28},{16,0},{20,4},{24,8},{28,12},{1,17},{... | collective-permute-start | bytes 589832 | tf_op jit(solution)/shard_map/ppermute | solution.py:493
  55.4 16.2 %collective-permute-start.18 = (bf16[2,96,768]{2,1,0:T(8,128)(2,1)S(1)}, bf16[2,96,768]{2,1,0:T(8,128)(2,1)S(1)}, u32[]{:S(2)}, u32[]{:S(2)}) collective-permute-start(bf16[2,96,768]{2,1,0:T(8,128)(2,1)S(1)} %get-tuple-element.54), channel_id=1, source_target_pairs={{0,8},{4,12},{8,0},{12,4},{16,24},{20,28},{24,16},{28,20},{1,9},{5... | collective-permute-start | bytes 884744 | tf_op jit(solution)/shard_map/ppermute | solution.py:34
  59.6 12.1 %collective-permute-start.19 = (bf16[2,96,768]{2,1,0:T(8,128)(2,1)S(1)}, bf16[2,96,768]{2,1,0:T(8,128)(2,1)S(1)}, u32[]{:S(2)}, u32[]{:S(2)}) collective-permute-start(bf16[2,96,768]{2,1,0:T(8,128)(2,1)S(1)} %get-tuple-element.55), channel_id=1, source_target_pairs={{0,4},{4,0},{8,12},{12,8},{16,20},{20,16},{24,28},{28,24},{1,5},{5... | collective-permute-start | bytes 884744 | tf_op jit(solution)/shard_map/ppermute | solution.py:34
  61.1 15.5 %collective-permute-start.20 = (bf16[2,96,768]{2,1,0:T(8,128)(2,1)S(1)}, bf16[2,96,768]{2,1,0:T(8,128)(2,1)S(1)}, u32[]{:S(2)}, u32[]{:S(2)}) collective-permute-start(bf16[2,96,768]{2,1,0:T(8,128)(2,1)S(1)} %get-tuple-element.56), channel_id=1, source_target_pairs={{0,12},{4,8},{8,4},{12,0},{16,28},{20,24},{24,20},{28,16},{1,13},{... | collective-permute-start | bytes 884744 | tf_op jit(solution)/shard_map/ppermute | solution.py:34
  64.9 2.0 %collective-permute-start.15 = (bf16[128,384]{1,0:T(8,128)(2,1)S(1)}, bf16[128,384]{1,0:T(8,128)(2,1)S(1)}, u32[]{:S(2)}, u32[]{:S(2)}) collective-permute-start(bf16[128,384]{1,0:T(8,128)(2,1)S(1)} %get-tuple-element.71), channel_id=1, source_target_pairs={{0,1},{1,0},{2,3},{3,2},{4,5},{5,4},{6,7},{7,6},{8,9},{9,8},{10,11... | collective-permute-start | bytes 294920 | tf_op jit(solution)/shard_map/ppermute | solution.py:34
  65.0 3.1 %collective-permute-start.16 = (bf16[128,384]{1,0:T(8,128)(2,1)S(1)}, bf16[128,384]{1,0:T(8,128)(2,1)S(1)}, u32[]{:S(2)}, u32[]{:S(2)}) collective-permute-start(bf16[128,384]{1,0:T(8,128)(2,1)S(1)} %get-tuple-element.70), channel_id=1, source_target_pairs={{0,1},{1,0},{2,3},{3,2},{4,5},{5,4},{6,7},{7,6},{8,9},{9,8},{10,11... | collective-permute-start | bytes 294920 | tf_op jit(solution)/shard_map/ppermute | solution.py:34
  66.9 24.1 %collective-permute-start.14 = (bf16[128,1536]{1,0:T(8,128)(2,1)S(1)}, bf16[128,1536]{1,0:T(8,128)(2,1)S(1)}, u32[]{:S(2)}, u32[]{:S(2)}) collective-permute-start(bf16[128,1536]{1,0:T(8,128)(2,1)S(1)} %act_rows.2.refs_6_.refs_3_), channel_id=1, source_target_pairs={{0,2},{2,0},{1,3},{3,1},{4,6},{6,4},{5,7},{7,5},{8,10},{10,8},{9,1... | collective-permute-start | bytes 1179656 | tf_op jit(solution)/shard_map/ppermute | solution.py:34
  70.7 20.3 %collective-permute-start.17 = (bf16[128,1536]{1,0:T(8,128)(2,1)S(1)}, bf16[128,1536]{1,0:T(8,128)(2,1)S(1)}, u32[]{:S(2)}, u32[]{:S(2)}) collective-permute-start(bf16[128,1536]{1,0:T(8,128)(2,1)S(1)} %act_rows.3.refs_5_), channel_id=1, source_target_pairs={{0,2},{2,0},{1,3},{3,1},{4,6},{6,4},{5,7},{7,5},{8,10},{10,8},{9,1... | collective-permute-start | bytes 1179656 | tf_op jit(solution)/shard_map/ppermute | solution.py:34
  71.6 6.6 %collective-permute-start.22 = (bf16[2,96,384]{2,1,0:T(8,128)(2,1)S(1)}, bf16[2,96,384]{2,1,0:T(8,128)(2,1)S(1)}, u32[]{:S(2)}, u32[]{:S(2)}) collective-permute-start(bf16[2,96,384]{2,1,0:T(8,128)(2,1)S(1)} %get-tuple-element.59), channel_id=1, source_target_pairs={{0,8},{4,12},{8,0},{12,4},{16,24},{20,28},{24,16},{28,20},{1,9},{5... | collective-permute-start | bytes 442376 | tf_op jit(solution)/shard_map/ppermute | solution.py:34
  71.6 9.3 %collective-permute-start.23 = (bf16[2,96,384]{2,1,0:T(8,128)(2,1)S(1)}, bf16[2,96,384]{2,1,0:T(8,128)(2,1)S(1)}, u32[]{:S(2)}, u32[]{:S(2)}) collective-permute-start(bf16[2,96,384]{2,1,0:T(8,128)(2,1)S(1)} %get-tuple-element.60), channel_id=1, source_target_pairs={{0,4},{4,0},{8,12},{12,8},{16,20},{20,16},{24,28},{28,24},{1,5},{5... | collective-permute-start | bytes 442376 | tf_op jit(solution)/shard_map/ppermute | solution.py:34
  76.6 7.3 %collective-permute-start.24 = (bf16[2,96,384]{2,1,0:T(8,128)(2,1)S(1)}, bf16[2,96,384]{2,1,0:T(8,128)(2,1)S(1)}, u32[]{:S(2)}, u32[]{:S(2)}) collective-permute-start(bf16[2,96,384]{2,1,0:T(8,128)(2,1)S(1)} %get-tuple-element.61), channel_id=1, source_target_pairs={{0,12},{4,8},{8,4},{12,0},{16,28},{20,24},{24,20},{28,16},{1,13},{... | collective-permute-start | bytes 442376 | tf_op jit(solution)/shard_map/ppermute | solution.py:34
  78.3 12.8 %collective-permute-start.21 = (bf16[96,768]{1,0:T(8,128)(2,1)S(1)}, bf16[96,768]{1,0:T(8,128)(2,1)S(1)}, u32[]{:S(2)}, u32[]{:S(2)}) collective-permute-start(bf16[96,768]{1,0:T(8,128)(2,1)S(1)} %get-tuple-element.58), channel_id=1, source_target_pairs={{0,16},{4,20},{8,24},{12,28},{16,0},{20,4},{24,8},{28,12},{1,17},{... | collective-permute-start | bytes 442376 | tf_op jit(solution)/shard_map/ppermute | solution.py:34
  84.5 6.5 %collective-permute-start.25 = (bf16[96,384]{1,0:T(8,128)(2,1)S(1)}, bf16[96,384]{1,0:T(8,128)(2,1)S(1)}, u32[]{:S(2)}, u32[]{:S(2)}) collective-permute-start(bf16[96,384]{1,0:T(8,128)(2,1)S(1)} %get-tuple-element.63), channel_id=1, source_target_pairs={{0,16},{4,20},{8,24},{12,28},{16,0},{20,4},{24,8},{28,12},{1,17},{... | collective-permute-start | bytes 221192 | tf_op jit(solution)/shard_map/ppermute | solution.py:34

commit v5 on v4

--- a/solution.py
+++ b/solution.py
@@ -244,18 +244,10 @@
     term[...] = total.astype(BF16)
 
 
-def piece_of(place, point, piece, sem):
-    number = piece.shape[0]
-    own = pl.ds(pl.multiple_of(place[SAMPLE] * number, number), number)
-    copy = pltpu.make_async_copy(point.at[own], piece, sem)
-    copy.start()
-    copy.wait()
-
-
 def middle_term(place, acted, weight, middle, kept, given):
     act = acted[...]
     middle[...] = dot(act, weight[1], NN)
-    part_channels(place, act.T, kept, [given])
+    part_channels(place, act.T, kept, given)
 
 
 def part_channels(place, turned, kept, given):
@@ -263,10 +255,7 @@
     split = turned.reshape(groups, 2, block, rows)
     first = place[SAMPLE] == 0
     kept[...] = jnp.where(first, split[:, 0], split[:, 1])
-    theirs = jnp.where(first, split[:, 1], split[:, 0])
-    number = groups // len(given)
-    for k, part in enumerate(given):
-        part[...] = theirs[k * number : (k + 1) * number]
+    given[...] = jnp.where(first, split[:, 1], split[:, 0])
 
 
 def add_terms(place, middle, arrived, total, sent):
@@ -275,26 +264,36 @@
     sent[...] = value.astype(BF16)
 
 
-def own_hidden(place, middle, feat, point, hidden, block):
+def own_hidden(place, middle, feat, point, direct, *rest):
+    *passed, hidden, block, other_point = rest
     hid = gelu_value(middle[...]).astype(BF16)
     hidden[...] = hid
     block[...] = wide(feat) + dot(hid, point[...], NT)
-
-
-def tracks(place, block, other_middle, near, far, cotangent, *rest):
-    *points, give, block_b, grads = rest
+    first = 0
+    for part in passed:
+        rows = slice(first, first + part.shape[0])
+        other_point[rows, :] = jnp.where(place[SAMPLE] == 0, direct[rows, :], part[...])
+        first += part.shape[0]
+
+
+def slopes(place, middle, feat, slope, slope_feat):
+    slope[...] = gelu_slope(middle[...])
+    slope_feat[...] = gelu_slope(wide(feat))
+
+
+def tracks(
+    place, block, other_middle, near, far, cotangent, point, other_point,
+    part, other_hidden, grad_kept, grad_given, block_b, grads,
+):
     sample = place[SAMPLE]
     piece = block_b.shape[2]
     width = other_middle.shape[1]
     hid = gelu_value(wide(other_middle)).astype(BF16)
-    ahead = 0
-    for point in points:
-        number = point.shape[0]
-        which, column = (sample, ahead) if ahead < piece else (1 - sample, ahead - piece)
-        columns = pl.ds(pl.multiple_of(which * piece + column, number), number)
-        value = block[:, columns] + dot(hid, point[...], NT)
-        block_b[which, :, column : column + number] = value.astype(BF16)
-        ahead += number
+    other_hidden[...] = hid
+    for which in range(2):
+        columns = slice(which * piece, (which + 1) * piece)
+        value = block[:, columns] + dot(hid, other_point[columns, :], NT)
+        block_b[which] = value.astype(BF16)
     number = near.shape[1]
     tile = width if number % width == 0 else number
     for start in range(0, number, tile):
@@ -302,26 +301,36 @@
         scores = dot(block_b[sample], near[:, columns], NN)
         scores += dot(block_b[1 - sample], far[:, columns], NN)
         grads[:, columns] = (wide(cotangent.at[:, columns]) * jax.nn.sigmoid(scores)).astype(BF16)
+    kept = given = 0.0
     for which, weight in ((sample, near), (1 - sample, far)):
         columns = pl.ds(pl.multiple_of(which * piece, piece), piece)
-        give[:, columns] = dot(grads[...], weight[...], NT).astype(BF16)
-
-
-def slopes(place, middle, feat, slope, slope_feat):
-    slope[...] = gelu_slope(middle[...])
-    slope_feat[...] = gelu_slope(wide(feat))
-
-
-def middle_grads(
-    place, own, theirs, point, slope, out_grad, middle_grad, kept, first, second, turned
-):
-    total = wide(own) + wide(theirs)
-    out_grad[...] = total
-    total_b = total.astype(BF16)
-    grad = (dot(total_b, point[...], NN) * slope[...]).astype(BF16)
-    middle_grad[...] = grad
-    turned[...] = grad.T
-    part_channels(place, total_b.T, kept, [first, second])
+        value = dot(grads[...], weight[...], NT).astype(BF16)
+        part[:, columns] = value
+        kept += dot(value, point[columns, :], NN)
+        given += dot(value, other_point[columns, :], NN)
+    grad_kept[...] = kept
+    grad_given[...] = given.astype(BF16)
+
+
+def turn_parts(place, part, far_middle, kept, far_hidden, *rest):
+    *pieces, given = rest
+    far_hidden[...] = gelu_value(wide(far_middle)).astype(BF16)
+    part_channels(place, part[...].T, kept, given)
+    first = 0
+    for piece in pieces:
+        piece[...] = given[first : first + piece.shape[0]]
+        first += piece.shape[0]
+
+
+def middle_grads(place, kept, got, slope, middle_grad):
+    middle_grad[...] = ((kept[...] + wide(got)) * slope[...]).astype(BF16)
+
+
+def joined(pieces, whole):
+    first = 0
+    for piece in pieces:
+        whole[first : first + piece.shape[0]] = piece[...]
+        first += piece.shape[0]
 
 
 def each_chip(place, keep, along, across, both, values):
@@ -343,69 +352,76 @@
             out[:, :, k * width : (k + 1) * width] = value.astype(out.dtype).reshape(shape)
 
 
-def middle_products(
-    place, acts, other_acts, outs, first, second, other_mid, middle_grad, hidden, other_hidden,
-    keep, along, across, both, other_outs,
+def point_products(
+    place, outs, hidden, other_hidden, far_hidden, far_other, *rest
 ):
-    number = first.shape[0]
-    other_outs[:number] = first[...]
-    other_outs[number:] = second[...]
+    *pieces, keep, along, across, both, other_outs = rest
+    joined(pieces, other_outs)
 
     def values(left):
+        own, other = left(outs), left(other_outs)
         return (
-            dot(left(acts), middle_grad[...], NN) + dot(left(other_acts), other_mid[...], NT),
-            dot(left(outs), hidden[...], NN) + dot(left(other_outs), other_hidden[...], NN),
+            dot(own, hidden[...], NN) + dot(other, far_hidden[...], NN),
+            dot(own, other_hidden[...], NN) + dot(other, far_other[...], NN),
         )
 
     each_chip(place, keep, along, across, both, values)
 
 
-def outer_products(
-    place, acts, other_acts, moved, first, second, keep, along, across, both, other_moved
+def tap_products(
+    place, acts, other_acts, middle_grad, other_middle_grad, moved, other_moved,
+    keep, along, across, both,
 ):
-    number = first.shape[0]
-    other_moved[:number] = first[...]
-    other_moved[number:] = second[...]
-
     def values(left):
-        return (dot(left(acts), moved[...], NN) + dot(left(other_acts), other_moved[...], NN),)
+        own, other = left(acts), left(other_acts)
+        return (
+            dot(own, middle_grad[...], NN) + dot(other, other_middle_grad[...], NN),
+            dot(own, moved[...], NN) + dot(other, other_moved[...], NN),
+        )
 
     each_chip(place, keep, along, across, both, values)
 
 
-def act_part(first):
-    def act_rows(place, middle_grad, moved, weight, give):
-        rows = slice(first, first + give.shape[0])
-        value = dot(middle_grad[rows, :], weight[1], NT)
-        give[...] = (value + dot(moved[rows, :], weight[place[0]], NT)).astype(BF16)
-
-    return act_rows
-
-
-def chips_sum(place, kept, along, across, both, keep, give):
-    def part(i):
-        total = kept[i] + along[i].astype(F32)
-        return total + across[i].astype(F32) + both[i].astype(F32)
-
-    give[...] = part(1 - place[TOP]).astype(BF16)
-    keep[...] = part(place[TOP])
-
-
-def finish(
-    place, out_grad, slope, act_one, got_one, act_two, got_two, mid_kept, mid_got, kept, got,
-    dilated, point, result,
-):
+def act_part(place, middle_grad, moved, weight, part, slope, give):
+    value = dot(middle_grad[...], weight[1], NT) + dot(moved[...], weight[place[0]], NT)
+    give[...] = (wide(part) + value * slope[...]).astype(BF16)
+
+
+def over_chips(at, kept, *arrived):
+    total = kept[at]
+    for part in arrived:
+        total += part[at].astype(F32)
+    return total
+
+
+def point_sum(place, kept, along, across, both, keep, give):
+    width = keep.shape[2]
+    for at in range(2):
+        total = over_chips(at, kept, along, across, both)
+        keep[at] = total[:, :width]
+        give[at] = total[:, width:].astype(BF16)
+
+
+def point_half(place, kept, got, keep, give):
+    top = place[TOP]
+    keep[...] = over_chips(top, kept, got)
+    give[...] = over_chips(1 - top, kept, got).astype(BF16)
+
+
+def taps_sum(place, *refs):
+    *parts, keep, give = refs
+    top = place[TOP]
+    keep[...] = over_chips(top, *parts)
+    give[...] = over_chips(1 - top, *parts).astype(BF16)
+
+
+def finish(place, own, theirs, point_kept, point_got, kept, got, dilated, point, result):
     width = point.shape[1]
-    dilated[place[0]] = kept[...]
-    dilated[2 - place[0]] = wide(got)
-    dilated[1] = mid_kept[:, :width] + mid_got[:, :width].astype(F32)
-    point[...] = mid_kept[:, width:] + mid_got[:, width:].astype(F32)
-    first = 0
-    for own, theirs in ((act_one, got_one), (act_two, got_two)):
-        rows = slice(first, first + own.shape[0])
-        act_grad = wide(own) + wide(theirs)
-        result[rows, :] = (out_grad[rows, :] + act_grad * slope[rows, :]).astype(BF16)
-        first += own.shape[0]
+    dilated[1] = kept[:, :width] + got[:, :width].astype(F32)
+    dilated[place[0]] = kept[:, width:]
+    dilated[2 - place[0]] = got[:, width:].astype(F32)
+    point[...] = point_kept[...] + wide(point_got)
+    result[...] = (wide(own) + wide(theirs)).astype(BF16)
 
 
 def body(features, dilated_weight, point_weight, track_weight, track_cotangent):
@@ -429,22 +445,16 @@
     cotangent = track_cotangent.reshape(rows, tracks_here)
     pairs = [(i, (i + dist) % n_seq) for i in range(n_seq)]
 
-    (own_piece,) = kernel_call(
-        piece_of,
-        [((piece, width), BF16)],
-        [place, in_hbm(point_weight)],
-        scratch=[pltpu.SemaphoreType.DMA],
-        spaces={1: pltpu.HBM},
-    )
-    near = flip(own_piece, "head")
-    cut = piece // 3
-    points = [near] + [flip(near[k : k + cut], "sample") for k in range(0, piece, cut)]
+    direct = lax.ppermute(point_weight, ("head", "sample"), [(0, 2), (2, 0)])
+    cut = channels // 3
+    passed = [
+        lax.ppermute(direct[k : k + cut], "sample", [(0, 1)]) for k in range(0, channels, cut)
+    ]
     far_track = flip(track_weight, "sample")
     acted, term = kernel_call(
         outer_term,
         [((rows, channels), BF16), ((rows, width), BF16)],
         [place, in_hbm(feat), in_hbm(taps)],
-        own_piece,
         scratch=[
             pltpu.VMEM((rows, channels), BF16),
             pltpu.VMEM((channels, width), BF16),
@@ -465,78 +475,98 @@
         add_terms, [((rows, width), F32), ((rows, width), BF16)], [place, middle, arrived], acts
     )
     other_middle = flip(middle_b, "head")
-    hidden, block_part = kernel_call(
+    hidden, block_part, other_point = kernel_call(
         own_hidden,
-        [((rows, width), BF16), ((rows, channels), F32)],
-        [place, middle, feat, point_weight],
-    )
-    (give,) = kernel_call(
+        [((rows, width), BF16), ((rows, channels), F32), ((channels, width), BF16)],
+        [place, middle, feat, point_weight, direct, *passed],
+    )
+    slope, slope_feat = kernel_call(
+        slopes,
+        [((rows, width), F32), ((rows, channels), F32)],
+        [place, middle, feat],
+        block_part,
+    )
+    part, other_hidden, grad_kept, grad_given = kernel_call(
         tracks,
-        [((rows, channels), BF16)],
-        [place, block_part, other_middle, track_weight, far_track, cotangent, *points],
+        [((rows, channels), BF16), ((rows, width), BF16), ((rows, width), F32), ((rows, width), BF16)],
+        [
+            place, block_part, other_middle, track_weight, far_track, cotangent, point_weight,
+            other_point,
+        ],
+        slope,
         scratch=[
             pltpu.VMEM((n_sample, rows, piece), BF16),
             pltpu.VMEM((rows, tracks_here), BF16),
         ],
     )
-    got = flip(give, "head")
-    slope, slope_feat = kernel_call(
-        slopes, [((rows, width), F32), ((rows, channels), F32)], [place, middle, feat], give
-    )
-    out_grad, middle_grad, outs, *given = kernel_call(
-        middle_grads,
-        [((rows, channels), F32), ((rows, width), BF16), turned]
-        + [((groups // 2, block, rows), BF16)] * 2
-        + [((width, rows), BF16)],
-        [place, give, got, point_weight, slope],
+    grad_got = flip(grad_given, "head")
+    far_hidden = flip(hidden, "sample")
+
+    def traded(kernel, columns, ins, after=None, scratch=()):
+        shape = (2, block, columns)
+        keep, *gives = kernel_call(
+            kernel, [(shape, F32)] + [(shape, BF16)] * 3, [place, *ins], after, scratch
+        )
+        return keep, *[flip(value, "seq", step) for value, step in zip(gives, (2, 1, 3))]
+
+    third = -(-groups // 3)
+    outs, far_other, *outs_given = kernel_call(
+        turn_parts,
+        [turned, ((rows, width), BF16)]
+        + [((min(third, groups - k), block, rows), BF16) for k in range(0, groups, third)],
+        [place, part, flip(other_middle, "sample")],
+        far_hidden,
+        scratch=[pltpu.VMEM((groups, block, rows), BF16)],
+    )
+    points = traded(
+        point_products,
+        2 * width,
+        [outs, hidden, other_hidden, far_hidden, far_other]
+        + [flip(piece, "sample") for piece in outs_given],
+        scratch=[pltpu.VMEM((groups, block, rows), BF16)],
+    )
+    (middle_grad,) = kernel_call(
+        middle_grads, [((rows, width), BF16)], [place, grad_kept, grad_got, slope], points[0]
     )
     moved = lax.ppermute(middle_grad, "seq", pairs)
-
-    def traded(kernel, columns, ins, after=None, scratch=()):
-        part = (2, block, columns)
-        keep, *gives = kernel_call(
-            kernel, [(part, F32)] + [(part, BF16)] * 3, [place, *ins], after, scratch
-        )
-        return keep, [flip(value, "seq", step) for value, step in zip(gives, (2, 1, 3))]
-
-    def halved(kept, got, columns, after):
-        part = (block, columns)
-        kept, given = kernel_call(
-            chips_sum, [(part, F32), (part, BF16)], [place, kept, *got], after
-        )
-        return kept, flip(given, "seq", 4)
-
-    other_acts, other_hidden = flip(acts_given, "sample"), flip(hidden, "sample")
-    mid_kept, mid_got = traded(
-        middle_products,
+    small = ((block, width), F32), ((block, width), BF16)
+    point_kept, point_give = kernel_call(
+        point_sum,
+        [((2, block, width), F32), ((2, block, width), BF16)],
+        [place, *points],
+        middle_grad,
+    )
+    (own,) = kernel_call(
+        act_part,
+        [((rows, channels), BF16)],
+        [place, middle_grad, moved, taps, part, slope_feat],
+        point_kept,
+    )
+    steps = traded(
+        tap_products,
         2 * width,
-        [acts, other_acts, outs]
-        + [flip(part, "sample") for part in given]
-        + [middle_grad, hidden, other_hidden],
-        scratch=[pltpu.VMEM((groups, block, rows), BF16)],
-    )
-    other_moved = [flip(moved[k : k + half], "sample") for k in (0, half)]
-    act_one = kernel_call(
-        act_part(0), [((half, channels), BF16)], [place, middle_grad, moved, taps], mid_kept
-    )[0]
-    kept, got = traded(
-        outer_products,
-        width,
-        [acts, other_acts, moved, *other_moved],
-        act_one,
-        scratch=[pltpu.VMEM((rows, width), BF16)],
-    )
-    act_two = kernel_call(
-        act_part(half), [((half, channels), BF16)], [place, middle_grad, moved, taps], kept
-    )[0]
-    mid_kept, mid_got = halved(mid_kept, mid_got, 2 * width, act_two)
-    kept, got = halved(kept, got, width, mid_kept)
+        [
+            acts, flip(acts_given, "sample"), middle_grad, flip(middle_grad, "sample"), moved,
+            flip(moved, "sample"),
+        ],
+        own,
+    )
+    point_kept, point_give = kernel_call(
+        point_half, small, [place, point_kept, flip(point_give, "head")], steps[0]
+    )
+    point_got = flip(point_give, "seq", n_seq // 2)
+    kept, give = kernel_call(
+        taps_sum,
+        [((block, 2 * width), F32), ((block, 2 * width), BF16)],
+        [place, *steps],
+        point_got,
+    )
     dilated_grad, point_grad, input_grad = kernel_call(
         finish,
         [((3, block, width), F32), ((block, width), F32), ((rows, channels), BF16)],
         [
-            place, out_grad, slope_feat, act_one, flip(act_one, "head"),
-            act_two, flip(act_two, "head"), mid_kept, mid_got, kept, got,
+            place, own, flip(own, "head"), point_kept, point_got, kept,
+            flip(give, "seq", n_seq // 2),
         ],
     )
     dilated_grad = jnp.transpose(dilated_grad, (1, 0, 2))

time: 93.1 us -> 108 us (1.16)
  starting transfers between devices: 22.1 us -> 35.9 us
    ppermute x0 -> x4, waiting for transfers between devices: none -> 8.47 us  [the longest x1 8.46 us: body(): direct = lax.ppermute(point_weight, ('head', 'sample'), [(0, 2), (2, 0)])]
    ppermute x1, waiting for transfers between devices: 8.37 us -> 0.01 us  [body(): arrived = lax.ppermute(term, 'seq', pairs)]
    ppermute x0 -> x4, starting transfers between devices: none -> 8.36 us  [the longest x1 4.41 us: body(): direct = lax.ppermute(point_weight, ('head', 'sample'), [(0, 2), (2, 0)])]
    ppermute x1, starting transfers between devices: 0.01 us -> 5.03 us  [body(): moved = lax.ppermute(middle_grad, 'seq', pairs)]
    ppermute x24 -> x21, waiting for transfers between devices: 33.4 us -> 37.7 us  [flip(): return lax.ppermute(value, axis, [(i, i ^ step) for i in range(count)])]
    ppermute x1, waiting for transfers between devices: 3.8 us -> 0.01 us  [body(): moved = lax.ppermute(middle_grad, 'seq', pairs)]
    ppermute x24 -> x21, starting transfers between devices: 19.5 us -> 19.9 us  [flip(): return lax.ppermute(value, axis, [(i, i ^ step) for i in range(count)])]
  transfers between devices with their start and end apart: 26 -> 27, of which waited for: 11 -> 11; matrix products, arithmetic and copies ran while one was open for 0% -> 0% of each run, Pallas kernels for 19% -> 21%
where the time goes in v5:
time: 108 us
  waiting for transfers between devices  46.1 us (43%)
  starting transfers between devices  35.9 us (33%)
  Pallas kernels  24.9 us (23%)
    ppermute x21, waiting for transfers between devices, flip(): return lax.ppermute(value, axis, [(i, i ^ step) for i in range(count)])  37.7 us
    pallas_call x15, Pallas kernels, kernel_call(): pl.pallas_call(run, out_shape=[jax.ShapeDtypeStruct(s, d) for s, d in out...  24.9 us
    ppermute x21, starting transfers between devices, flip(): return lax.ppermute(value, axis, [(i, i ^ step) for i in range(count)])  19.9 us
    ppermute x1, waiting for transfers between devices, body(): direct = lax.ppermute(point_weight, ('head', 'sample'), [(0, 2), (2, 0)])  8.46 us
    ppermute x1, starting transfers between devices, body(): moved = lax.ppermute(middle_grad, 'seq', pairs)  5.03 us
    ppermute x1, starting transfers between devices, body(): direct = lax.ppermute(point_weight, ('head', 'sample'), [(0, 2), (2, 0)])  4.41 us
    ppermute x3, starting transfers between devices, body(): lax.ppermute(direct[k:k + cut], 'sample', [(0, 1)])  3.94 us
    ppermute x1, starting transfers between devices, body(): arrived = lax.ppermute(term, 'seq', pairs)  2.66 us
  transfers between devices with their start and end apart: 27, of which 11 were waited for; matrix products, arithmetic and copies ran while one was open for 0% of the time, Pallas kernels for 21%

profile of v5, /device:TPU:0, one launch (start us, length us, event | category | flops | bytes accessed | tf_op | source)
XLA Modules:
  0.0 108.1 jit_solution(3564160396632084376)
XLA Ops:
  1.1 4.4 %collective-permute-start.1 = (bf16[1536,384]{1,0:T(8,128)(2,1)}, bf16[1536,384]{1,0:T(8,128)(2,1)S(1)}, u32[]{:S(2)}, u32[]{:S(2)}) collective-permute-start(bf16[1536,384]{1,0:T(8,128)(2,1)} %refs_6_.1), channel_id=1, source_target_pairs={{0,2},{2,0},{4,6},{6,4},{8,10},{10,8},{12,14},{14,12},{16,18},{18,... | collective-permute-start | bytes 3538952 | tf_op jit(solution)/shard_map/ppermute | solution.py:448
  5.7 3.2 %outer_term.1 = (bf16[256,1536]{1,0:T(8,128)(2,1)S(1)}, bf16[256,384]{1,0:T(8,128)(2,1)S(1)}) custom-call(s32[6]{0:T(128)S(1)} %stack.27.refs_0_, bf16[256,1536]{1,0:T(8,128)(2,1)} %bitcast.14, bf16[3,1536,384]{2,1,0:T(8,128)(2,1)} %bitcast.11), custom_call_target="tpu_custom_call" | custom-call | flops 1 | bytes 1 | tf_op jit(solution)/shard_map/outer_term/pallas_call | solution.py:200
  8.8 2.7 %collective-permute-start = (bf16[256,384]{1,0:T(8,128)(2,1)S(1)}, bf16[256,384]{1,0:T(8,128)(2,1)S(1)}, u32[]{:S(2)}, u32[]{:S(2)}) collective-permute-start(bf16[256,384]{1,0:T(8,128)(2,1)S(1)} %get-tuple-element.43), channel_id=1, source_target_pairs={{0,16},{4,20},{8,24},{12,28},{16,0},{20,4},{24,8},{28,12},{1,17},{... | collective-permute-start | bytes 589832 | tf_op jit(solution)/shard_map/ppermute | solution.py:465
  11.5 8.5 %collective-permute-done.1.refs_4_ = bf16[1536,384]{1,0:T(8,128)(2,1)S(1)} collective-permute-done((bf16[1536,384]{1,0:T(8,128)(2,1)}, bf16[1536,384]{1,0:T(8,128)(2,1)S(1)}, u32[]{:S(2)}, u32[]{:S(2)}) %collective-permute-start.1) | collective-permute-done | bytes 1179680 | tf_op jit(solution)/shard_map/ppermute | solution.py:448
  20.1 1.3 %collective-permute-start.2 = (bf16[512,384]{1,0:T(8,128)(2,1)S(1)}, bf16[512,384]{1,0:T(8,128)(2,1)S(1)}, u32[]{:S(2)}, u32[]{:S(2)}) collective-permute-start(bf16[512,384]{1,0:T(8,128)(2,1)S(1)} %get-tuple-element.81), channel_id=1, source_target_pairs={{0,1},{2,3},{4,5},{6,7},{8,9},{10,11},{12,13},{14,15},{16,17},{18,... | collective-permute-start | bytes 1179656 | tf_op jit(solution)/shard_map/ppermute | solution.py:451
  21.4 1.3 %collective-permute-start.3 = (bf16[512,384]{1,0:T(8,128)(2,1)S(1)}, bf16[512,384]{1,0:T(8,128)(2,1)S(1)}, u32[]{:S(2)}, u32[]{:S(2)}) collective-permute-start(bf16[512,384]{1,0:T(8,128)(2,1)S(1)} %get-tuple-element.80), channel_id=1, source_target_pairs={{0,1},{2,3},{4,5},{6,7},{8,9},{10,11},{12,13},{14,15},{16,17},{18,... | collective-permute-start | bytes 1179656 | tf_op jit(solution)/shard_map/ppermute | solution.py:451
  22.7 1.3 %collective-permute-start.4 = (bf16[512,384]{1,0:T(8,128)(2,1)S(1)}, bf16[512,384]{1,0:T(8,128)(2,1)S(1)}, u32[]{:S(2)}, u32[]{:S(2)}) collective-permute-start(bf16[512,384]{1,0:T(8,128)(2,1)S(1)} %get-tuple-element.79), channel_id=1, source_target_pairs={{0,1},{2,3},{4,5},{6,7},{8,9},{10,11},{12,13},{14,15},{16,17},{18,... | collective-permute-start | bytes 1179656 | tf_op jit(solution)/shard_map/ppermute | solution.py:451
  24.1 1.1 %middle_term.1 = (f32[256,384]{1,0:T(8,128)S(1)}, bf16[8,96,256]{2,1,0:T(8,128)(2,1)S(1)}, bf16[8,96,256]{2,1,0:T(8,128)(2,1)S(1)}) custom-call(s32[6]{0:T(128)S(1)} %stack.27.refs_0_, bf16[256,1536]{1,0:T(8,128)(2,1)S(1)} %get-tuple-element.41.refs_1_, bf16[3,1536,384]{2,1,0:T(8,128)(2,1)S(1)} %bitcast.12), custom_call_target="tpu_custom_call" | custom-call | flops 1 | bytes 1 | tf_op jit(solution)/shard_map/middle_term/pallas_call | solution.py:200
  25.8 2.1 %collective-permute-start.5 = (bf16[256,384]{1,0:T(8,128)(2,1)S(1)}, bf16[256,384]{1,0:T(8,128)(2,1)S(1)}, u32[]{:S(2)}, u32[]{:S(2)}) collective-permute-start(bf16[256,384]{1,0:T(8,128)(2,1)S(1)} %get-tuple-element.47), channel_id=1, source_target_pairs={{0,2},{2,0},{1,3},{3,1},{4,6},{6,4},{5,7},{7,5},{8,10},{10,8},{9,1... | collective-permute-start | bytes 589832 | tf_op jit(solution)/shard_map/ppermute | solution.py:34
  27.9 3.7 %collective-permute-done.5.refs_2_ = bf16[256,384]{1,0:T(8,128)(2,1)S(1)} collective-permute-done((bf16[256,384]{1,0:T(8,128)(2,1)S(1)}, bf16[256,384]{1,0:T(8,128)(2,1)S(1)}, u32[]{:S(2)}, u32[]{:S(2)}) %collective-permute-start.5) | collective-permute-done | bytes 196640 | tf_op jit(solution)/shard_map/ppermute | solution.py:34
  31.6 1.3 %own_hidden.1 = (bf16[256,384]{1,0:T(8,128)(2,1)S(1)}, f32[256,1536]{1,0:T(8,128)S(1)}, bf16[1536,384]{1,0:T(8,128)(2,1)S(1)}) custom-call(s32[6]{0:T(128)S(1)} %stack.27.refs_0_, f32[256,384]{1,0:T(8,128)S(1)} %get-tuple-element.45.refs_1_, bf16[256,1536]{1,0:T(8,128)(2,1)S(1)} %bitcast.15, bf16[1536,384]{1,0:T(8,128)(2,1)S(1)} %copy-done.2, ...), custom_call_target="tpu_custom_call" | custom-call | flops 1 | bytes 1 | tf_op jit(solution)/shard_map/own_hidden/pallas_call | solution.py:200
  33.5 1.7 %slopes.1 = (f32[256,384]{1,0:T(8,128)S(1)}, f32[256,1536]{1,0:T(8,128)S(1)}) custom-call(s32[6]{0:T(128)S(1)} %stack.27.refs_0_, f32[256,384]{1,0:T(8,128)S(1)} %get-tuple-element.45.refs_1_, bf16[256,1536]{1,0:T(8,128)(2,1)S(1)} %bitcast.16, f32[256,1536]{1,0:T(8,128)S(1)} %get-tuple-element.46.refs_3_.refs_1_), custom_call_target="tpu_custom_call" | custom-call | flops 1 | bytes 1 | tf_op jit(solution)/shard_map/slopes/pallas_call | solution.py:200
  35.3 7.2 %tracks.1 = (bf16[256,1536]{1,0:T(8,128)(2,1)S(1)}, bf16[256,384]{1,0:T(8,128)(2,1)S(1)}, f32[256,384]{1,0:T(8,128)S(1)}, bf16[256,384]{1,0:T(8,128)(2,1)S(1)}) custom-call(s32[6]{0:T(128)S(1)} %stack.27.refs_0_, f32[256,1536]{1,0:T(8,128)S(1)} %get-tuple-element.46.refs_3_.refs_1_, bf16[256,384]{1,0:T(8,128)(2,1)S(1)} %collective-permute-done.5.refs_2_, ...), custom_call_target="tpu_custom_call" | custom-call | flops 1 | bytes 1 | tf_op jit(solution)/shard_map/tracks/pallas_call | solution.py:200
  42.4 1.0 turn_parts.1
  44.1 2.0 %collective-permute-start.7 = (bf16[256,384]{1,0:T(8,128)(2,1)S(1)}, bf16[256,384]{1,0:T(8,128)(2,1)S(1)}, u32[]{:S(2)}, u32[]{:S(2)}) collective-permute-start(bf16[256,384]{1,0:T(8,128)(2,1)S(1)} %get-tuple-element.51), channel_id=1, source_target_pairs={{0,2},{2,0},{1,3},{3,1},{4,6},{6,4},{5,7},{7,5},{8,10},{10,8},{9,1... | collective-permute-start | bytes 589832 | tf_op jit(solution)/shard_map/ppermute | solution.py:34
  46.1 1.5 %point_products.1 = (f32[2,96,768]{2,1,0:T(8,128)S(1)}, bf16[2,96,768]{2,1,0:T(8,128)(2,1)S(1)}, bf16[2,96,768]{2,1,0:T(8,128)(2,1)S(1)}, bf16[2,96,768]{2,1,0:T(8,128)(2,1)S(1)}) custom-call(s32[6]{0:T(128)S(1)} %stack.27.refs_0_, bf16[8,96,256]{2,1,0:T(8,128)(2,1)S(1)} %get-tuple-element.54.refs_1_, bf16[256,384]{1,0:T(8,128)(2,1)S(1)} %get-tuple-element.53.refs_2_, ...), custom_call_target="tpu_custom_call" | custom-call | flops 1 | bytes 1 | tf_op jit(solution)/shard_map/point_products/pallas_call | solution.py:200
  47.6 1.6 %collective-permute-start.14 = (bf16[2,96,768]{2,1,0:T(8,128)(2,1)S(1)}, bf16[2,96,768]{2,1,0:T(8,128)(2,1)S(1)}, u32[]{:S(2)}, u32[]{:S(2)}) collective-permute-start(bf16[2,96,768]{2,1,0:T(8,128)(2,1)S(1)} %get-tuple-element.62), channel_id=1, source_target_pairs={{0,8},{4,12},{8,0},{12,4},{16,24},{20,28},{24,16},{28,20},{1,9},{5... | collective-permute-start | bytes 884744 | tf_op jit(solution)/shard_map/ppermute | solution.py:34
  49.3 1.5 %collective-permute-start.15 = (bf16[2,96,768]{2,1,0:T(8,128)(2,1)S(1)}, bf16[2,96,768]{2,1,0:T(8,128)(2,1)S(1)}, u32[]{:S(2)}, u32[]{:S(2)}) collective-permute-start(bf16[2,96,768]{2,1,0:T(8,128)(2,1)S(1)} %get-tuple-element.63), channel_id=1, source_target_pairs={{0,4},{4,0},{8,12},{12,8},{16,20},{20,16},{24,28},{28,24},{1,5},{5... | collective-permute-start | bytes 884744 | tf_op jit(solution)/shard_map/ppermute | solution.py:34
  52.2 5.0 %collective-permute-start.13 = (bf16[256,384]{1,0:T(8,128)(2,1)S(1)}, bf16[256,384]{1,0:T(8,128)(2,1)S(1)}, u32[]{:S(2)}, u32[]{:S(2)}) collective-permute-start(bf16[256,384]{1,0:T(8,128)(2,1)S(1)} %middle_grads.1.refs_5_.refs_1_.refs_3_), channel_id=1, source_target_pairs={{0,16},{4,20},{8,24},{12,28},{16,0},{20,4},{24,8},{28,12},{1,17},{... | collective-permute-start | bytes 589832 | tf_op jit(solution)/shard_map/ppermute | solution.py:531
  57.6 1.6 %collective-permute-done.15.refs_3_ = bf16[2,96,768]{2,1,0:T(8,128)(2,1)S(1)} collective-permute-done((bf16[2,96,768]{2,1,0:T(8,128)(2,1)S(1)}, bf16[2,96,768]{2,1,0:T(8,128)(2,1)S(1)}, u32[]{:S(2)}, u32[]{:S(2)}) %collective-permute-start.15) | collective-permute-done | bytes 294944 | tf_op jit(solution)/shard_map/ppermute | solution.py:34
  59.1 9.2 %collective-permute-done.16.refs_4_ = bf16[2,96,768]{2,1,0:T(8,128)(2,1)S(1)} collective-permute-done((bf16[2,96,768]{2,1,0:T(8,128)(2,1)S(1)}, bf16[2,96,768]{2,1,0:T(8,128)(2,1)S(1)}, u32[]{:S(2)}, u32[]{:S(2)}) %collective-permute-start.16) | collective-permute-done | bytes 294944 | tf_op jit(solution)/shard_map/ppermute | solution.py:34
  69.0 1.6 %act_part.1.refs_7_.refs_1_ = bf16[256,1536]{1,0:T(8,128)(2,1)S(1)} custom-call(s32[6]{0:T(128)S(1)} %stack.27.refs_0_, bf16[256,384]{1,0:T(8,128)(2,1)S(1)} %middle_grads.1.refs_5_.refs_1_.refs_3_, bf16[256,384]{1,0:T(8,128)(2,1)S(1)} %collective-permute-done.13.refs_2_.refs_5_, bf16[3,1536,384]{2,1,0:T(8,128)(2,1)S(1)} %bitcast.13, ...), custom_call_target="tpu_custom_call" | custom-call | flops 1 | bytes 1 | tf_op jit(solution)/shard_map/act_part/pallas_call | solution.py:200
  70.5 1.3 %collective-permute-start.17 = (bf16[256,1536]{1,0:T(8,128)(2,1)S(1)}, bf16[256,1536]{1,0:T(8,128)(2,1)S(1)}, u32[]{:S(2)}, u32[]{:S(2)}) collective-permute-start(bf16[256,1536]{1,0:T(8,128)(2,1)S(1)} %act_part.1.refs_7_.refs_1_), channel_id=1, source_target_pairs={{0,2},{2,0},{1,3},{3,1},{4,6},{6,4},{5,7},{7,5},{8,10},{10,8},{9,1... | collective-permute-start | bytes 2359304 | tf_op jit(solution)/shard_map/ppermute | solution.py:34
  73.6 1.5 %tap_products.1 = (f32[2,96,768]{2,1,0:T(8,128)S(1)}, bf16[2,96,768]{2,1,0:T(8,128)(2,1)S(1)}, bf16[2,96,768]{2,1,0:T(8,128)(2,1)S(1)}, bf16[2,96,768]{2,1,0:T(8,128)(2,1)S(1)}) custom-call(s32[6]{0:T(128)S(1)} %stack.27.refs_0_, bf16[8,96,256]{2,1,0:T(8,128)(2,1)S(1)} %get-tuple-element.44.refs_3_.refs_1_, ...), custom_call_target="tpu_custom_call" | custom-call | flops 1 | bytes 1 | tf_op jit(solution)/shard_map/tap_products/pallas_call | solution.py:200
  75.1 3.2 %collective-permute-start.23 = (bf16[2,96,768]{2,1,0:T(8,128)(2,1)S(1)}, bf16[2,96,768]{2,1,0:T(8,128)(2,1)S(1)}, u32[]{:S(2)}, u32[]{:S(2)}) collective-permute-start(bf16[2,96,768]{2,1,0:T(8,128)(2,1)S(1)} %get-tuple-element.71), channel_id=1, source_target_pairs={{0,8},{4,12},{8,0},{12,4},{16,24},{20,28},{24,16},{28,20},{1,9},{5... | collective-permute-start | bytes 884744 | tf_op jit(solution)/shard_map/ppermute | solution.py:34
  78.2 1.5 %collective-permute-start.24 = (bf16[2,96,768]{2,1,0:T(8,128)(2,1)S(1)}, bf16[2,96,768]{2,1,0:T(8,128)(2,1)S(1)}, u32[]{:S(2)}, u32[]{:S(2)}) collective-permute-start(bf16[2,96,768]{2,1,0:T(8,128)(2,1)S(1)} %get-tuple-element.72), channel_id=1, source_target_pairs={{0,4},{4,0},{8,12},{12,8},{16,20},{20,16},{24,28},{28,24},{1,5},{5... | collective-permute-start | bytes 884744 | tf_op jit(solution)/shard_map/ppermute | solution.py:34
  80.6 12.0 %collective-permute-done.18.refs_2_ = bf16[2,96,384]{2,1,0:T(8,128)(2,1)S(1)} collective-permute-done((bf16[2,96,384]{2,1,0:T(8,128)(2,1)S(1)}, bf16[2,96,384]{2,1,0:T(8,128)(2,1)S(1)}, u32[]{:S(2)}, u32[]{:S(2)}) %collective-permute-start.18) | collective-permute-done | bytes 147488 | tf_op jit(solution)/shard_map/ppermute | solution.py:34
  93.1 1.9 %collective-permute-start.22 = (bf16[96,384]{1,0:T(8,128)(2,1)S(1)}, bf16[96,384]{1,0:T(8,128)(2,1)S(1)}, u32[]{:S(2)}, u32[]{:S(2)}) collective-permute-start(bf16[96,384]{1,0:T(8,128)(2,1)S(1)} %get-tuple-element.70), channel_id=1, source_target_pairs={{0,16},{4,20},{8,24},{12,28},{16,0},{20,4},{24,8},{28,12},{1,17},{... | collective-permute-start | bytes 221192 | tf_op jit(solution)/shard_map/ppermute | solution.py:34
  95.0 4.2 %collective-permute-done.22.refs_5_.refs_4_ = bf16[96,384]{1,0:T(8,128)(2,1)S(1)} collective-permute-done((bf16[96,384]{1,0:T(8,128)(2,1)S(1)}, bf16[96,384]{1,0:T(8,128)(2,1)S(1)}, u32[]{:S(2)}, u32[]{:S(2)}) %collective-permute-start.22) | collective-permute-done | bytes 73760 | tf_op jit(solution)/shard_map/ppermute | solution.py:34
  99.9 1.3 %collective-permute-start.26 = (bf16[96,768]{1,0:T(8,128)(2,1)S(1)}, bf16[96,768]{1,0:T(8,128)(2,1)S(1)}, u32[]{:S(2)}, u32[]{:S(2)}) collective-permute-start(bf16[96,768]{1,0:T(8,128)(2,1)S(1)} %get-tuple-element.75), channel_id=1, source_target_pairs={{0,16},{4,20},{8,24},{12,28},{16,0},{20,4},{24,8},{28,12},{1,17},{... | collective-permute-start | bytes 442376 | tf_op jit(solution)/shard_map/ppermute | solution.py:34
  101.1 5.2 %collective-permute-done.26.refs_6_ = bf16[96,768]{1,0:T(8,128)(2,1)S(1)} collective-permute-done((bf16[96,768]{1,0:T(8,128)(2,1)S(1)}, bf16[96,768]{1,0:T(8,128)(2,1)S(1)}, u32[]{:S(2)}, u32[]{:S(2)}) %collective-permute-start.26) | collective-permute-done | bytes 147488 | tf_op jit(solution)/shard_map/ppermute | solution.py:34
  106.3 1.8 %finish.1 = (f32[3,96,384]{2,1,0:T(8,128)}, f32[96,384]{1,0:T(8,128)}, bf16[256,1536]{1,0:T(8,128)(2,1)}) custom-call(s32[6]{0:T(128)S(1)} %stack.27.refs_0_, bf16[256,1536]{1,0:T(8,128)(2,1)S(1)} %act_part.1.refs_7_.refs_1_, bf16[256,1536]{1,0:T(8,128)(2,1)S(1)} %collective-permute-done.17.refs_2_, f32[96,384]{1,0:T(8,128)S(1)} %get-tuple-element.69.refs_3_, ...), custom_call_target="tpu_custom_call" | custom-call | flops 1 | bytes 1 | tf_op jit(solution)/shard_map/finish/pallas_call | solution.py:200
  (49 shorter events, 8.8 us)
Async XLA Ops:
  0.6 34.6 %collective-permute-start.6 = (bf16[768,1920]{1,0:T(8,128)(2,1)}, bf16[768,1920]{1,0:T(8,128)(2,1)}, u32[]{:S(2)}, u32[]{:S(2)}) collective-permute-start(bf16[768,1920]{1,0:T(8,128)(2,1)} %refs_3_.3), channel_id=1, source_target_pairs={{0,1},{1,0},{2,3},{3,2},{4,5},{5,4},{6,7},{7,6},{8,9},{9,8},{10,11... | collective-permute-start | bytes 8847368 | tf_op jit(solution)/shard_map/ppermute | solution.py:34
  1.1 18.8 %collective-permute-start.1 = (bf16[1536,384]{1,0:T(8,128)(2,1)}, bf16[1536,384]{1,0:T(8,128)(2,1)S(1)}, u32[]{:S(2)}, u32[]{:S(2)}) collective-permute-start(bf16[1536,384]{1,0:T(8,128)(2,1)} %refs_6_.1), channel_id=1, source_target_pairs={{0,2},{2,0},{4,6},{6,4},{8,10},{10,8},{12,14},{14,12},{16,18},{18,... | collective-permute-start | bytes 3538952 | tf_op jit(solution)/shard_map/ppermute | solution.py:448
  5.7 18.4 %copy-start = (bf16[1536,3,384]{2,0,1:T(8,128)(2,1)S(1)}, bf16[1536,3,384]{2,0,1:T(8,128)(2,1)}, u32[]{:S(2)}) copy-start(bf16[1536,3,384]{2,0,1:T(8,128)(2,1)} %param.6) | copy-start | bytes 10616836
  8.8 16.4 %collective-permute-start = (bf16[256,384]{1,0:T(8,128)(2,1)S(1)}, bf16[256,384]{1,0:T(8,128)(2,1)S(1)}, u32[]{:S(2)}, u32[]{:S(2)}) collective-permute-start(bf16[256,384]{1,0:T(8,128)(2,1)S(1)} %get-tuple-element.43), channel_id=1, source_target_pairs={{0,16},{4,20},{8,24},{12,28},{16,0},{20,4},{24,8},{28,12},{1,17},{... | collective-permute-start | bytes 589832 | tf_op jit(solution)/shard_map/ppermute | solution.py:465
  20.1 11.5 %collective-permute-start.2 = (bf16[512,384]{1,0:T(8,128)(2,1)S(1)}, bf16[512,384]{1,0:T(8,128)(2,1)S(1)}, u32[]{:S(2)}, u32[]{:S(2)}) collective-permute-start(bf16[512,384]{1,0:T(8,128)(2,1)S(1)} %get-tuple-element.81), channel_id=1, source_target_pairs={{0,1},{2,3},{4,5},{6,7},{8,9},{10,11},{12,13},{14,15},{16,17},{18,... | collective-permute-start | bytes 1179656 | tf_op jit(solution)/shard_map/ppermute | solution.py:451
  21.4 10.2 %collective-permute-start.3 = (bf16[512,384]{1,0:T(8,128)(2,1)S(1)}, bf16[512,384]{1,0:T(8,128)(2,1)S(1)}, u32[]{:S(2)}, u32[]{:S(2)}) collective-permute-start(bf16[512,384]{1,0:T(8,128)(2,1)S(1)} %get-tuple-element.80), channel_id=1, source_target_pairs={{0,1},{2,3},{4,5},{6,7},{8,9},{10,11},{12,13},{14,15},{16,17},{18,... | collective-permute-start | bytes 1179656 | tf_op jit(solution)/shard_map/ppermute | solution.py:451
  22.7 8.9 %collective-permute-start.4 = (bf16[512,384]{1,0:T(8,128)(2,1)S(1)}, bf16[512,384]{1,0:T(8,128)(2,1)S(1)}, u32[]{:S(2)}, u32[]{:S(2)}) collective-permute-start(bf16[512,384]{1,0:T(8,128)(2,1)S(1)} %get-tuple-element.79), channel_id=1, source_target_pairs={{0,1},{2,3},{4,5},{6,7},{8,9},{10,11},{12,13},{14,15},{16,17},{18,... | collective-permute-start | bytes 1179656 | tf_op jit(solution)/shard_map/ppermute | solution.py:451
  24.0 7.5 %copy-start.1 = (bf16[1,256,1536]{2,1,0:T(8,128)(2,1)S(1)}, bf16[1,256,1536]{2,1,0:T(8,128)(2,1)}, u32[]{:S(2)}) copy-start(bf16[1,256,1536]{2,1,0:T(8,128)(2,1)} %param.5) | copy-start | bytes 2359300
  24.1 7.5 %copy-start.2 = (bf16[1536,384]{1,0:T(8,128)(2,1)S(1)}, bf16[1536,384]{1,0:T(8,128)(2,1)}, u32[]{:S(2)}) copy-start(bf16[1536,384]{1,0:T(8,128)(2,1)} %refs_6_.1) | copy-start | bytes 3538948
  25.8 5.7 %collective-permute-start.5 = (bf16[256,384]{1,0:T(8,128)(2,1)S(1)}, bf16[256,384]{1,0:T(8,128)(2,1)S(1)}, u32[]{:S(2)}, u32[]{:S(2)}) collective-permute-start(bf16[256,384]{1,0:T(8,128)(2,1)S(1)} %get-tuple-element.47), channel_id=1, source_target_pairs={{0,2},{2,0},{1,3},{3,1},{4,6},{6,4},{5,7},{7,5},{8,10},{10,8},{9,1... | collective-permute-start | bytes 589832 | tf_op jit(solution)/shard_map/ppermute | solution.py:34
  31.6 10.9 %collective-permute-start.8 = (bf16[256,384]{1,0:T(8,128)(2,1)S(1)}, bf16[256,384]{1,0:T(8,128)(2,1)S(1)}, u32[]{:S(2)}, u32[]{:S(2)}) collective-permute-start(bf16[256,384]{1,0:T(8,128)(2,1)S(1)} %collective-permute-done.5.refs_2_), channel_id=1, source_target_pairs={{0,1},{1,0},{2,3},{3,2},{4,5},{5,4},{6,7},{7,6},{8,9},{9,8},{10,11... | collective-permute-start | bytes 589832 | tf_op jit(solution)/shard_map/ppermute | solution.py:34
  31.6 3.6 %copy-start.3 = (bf16[768,1920]{1,0:T(8,128)(2,1)S(1)}, bf16[768,1920]{1,0:T(8,128)(2,1)}, u32[]{:S(2)}) copy-start(bf16[768,1920]{1,0:T(8,128)(2,1)} %refs_3_.3) | copy-start | bytes 8847364
  32.9 2.3 %copy-start.4 = (bf16[1,256,1920]{2,1,0:T(8,128)(2,1)S(1)}, bf16[1,256,1920]{2,1,0:T(8,128)(2,1)}, u32[]{:S(2)}) copy-start(bf16[1,256,1920]{2,1,0:T(8,128)(2,1)} %param.9) | copy-start | bytes 2949124
  32.9 9.5 %collective-permute-start.9 = (bf16[256,384]{1,0:T(8,128)(2,1)S(1)}, bf16[256,384]{1,0:T(8,128)(2,1)S(1)}, u32[]{:S(2)}, u32[]{:S(2)}) collective-permute-start(bf16[256,384]{1,0:T(8,128)(2,1)S(1)} %get-tuple-element.53.refs_2_), channel_id=1, source_target_pairs={{0,1},{1,0},{2,3},{3,2},{4,5},{5,4},{6,7},{7,6},{8,9},{9,8},{10,11... | collective-permute-start | bytes 589832 | tf_op jit(solution)/shard_map/ppermute | solution.py:34
  43.4 2.7 %collective-permute-start.10 = (bf16[3,96,256]{2,1,0:T(8,128)(2,1)S(1)}, bf16[3,96,256]{2,1,0:T(8,128)(2,1)S(1)}, u32[]{:S(2)}, u32[]{:S(2)}) collective-permute-start(bf16[3,96,256]{2,1,0:T(8,128)(2,1)S(1)} %get-tuple-element.57), channel_id=1, source_target_pairs={{0,1},{1,0},{2,3},{3,2},{4,5},{5,4},{6,7},{7,6},{8,9},{9,8},{10,11... | collective-permute-start | bytes 442376 | tf_op jit(solution)/shard_map/ppermute | solution.py:34
  43.5 2.6 %collective-permute-start.11 = (bf16[3,96,256]{2,1,0:T(8,128)(2,1)S(1)}, bf16[3,96,256]{2,1,0:T(8,128)(2,1)S(1)}, u32[]{:S(2)}, u32[]{:S(2)}) collective-permute-start(bf16[3,96,256]{2,1,0:T(8,128)(2,1)S(1)} %get-tuple-element.58), channel_id=1, source_target_pairs={{0,1},{1,0},{2,3},{3,2},{4,5},{5,4},{6,7},{7,6},{8,9},{9,8},{10,11... | collective-permute-start | bytes 442376 | tf_op jit(solution)/shard_map/ppermute | solution.py:34
  44.0 2.1 %collective-permute-start.12 = (bf16[2,96,256]{2,1,0:T(8,128)(2,1)S(1)}, bf16[2,96,256]{2,1,0:T(8,128)(2,1)S(1)}, u32[]{:S(2)}, u32[]{:S(2)}) collective-permute-start(bf16[2,96,256]{2,1,0:T(8,128)(2,1)S(1)} %get-tuple-element.59), channel_id=1, source_target_pairs={{0,1},{1,0},{2,3},{3,2},{4,5},{5,4},{6,7},{7,6},{8,9},{9,8},{10,11... | collective-permute-start | bytes 294920 | tf_op jit(solution)/shard_map/ppermute | solution.py:34
  44.1 7.5 %collective-permute-start.7 = (bf16[256,384]{1,0:T(8,128)(2,1)S(1)}, bf16[256,384]{1,0:T(8,128)(2,1)S(1)}, u32[]{:S(2)}, u32[]{:S(2)}) collective-permute-start(bf16[256,384]{1,0:T(8,128)(2,1)S(1)} %get-tuple-element.51), channel_id=1, source_target_pairs={{0,2},{2,0},{1,3},{3,1},{4,6},{6,4},{5,7},{7,5},{8,10},{10,8},{9,1... | collective-permute-start | bytes 589832 | tf_op jit(solution)/shard_map/ppermute | solution.py:34
  47.6 9.9 %collective-permute-start.14 = (bf16[2,96,768]{2,1,0:T(8,128)(2,1)S(1)}, bf16[2,96,768]{2,1,0:T(8,128)(2,1)S(1)}, u32[]{:S(2)}, u32[]{:S(2)}) collective-permute-start(bf16[2,96,768]{2,1,0:T(8,128)(2,1)S(1)} %get-tuple-element.62), channel_id=1, source_target_pairs={{0,8},{4,12},{8,0},{12,4},{16,24},{20,28},{24,16},{28,20},{1,9},{5... | collective-permute-start | bytes 884744 | tf_op jit(solution)/shard_map/ppermute | solution.py:34
  49.3 9.8 %collective-permute-start.15 = (bf16[2,96,768]{2,1,0:T(8,128)(2,1)S(1)}, bf16[2,96,768]{2,1,0:T(8,128)(2,1)S(1)}, u32[]{:S(2)}, u32[]{:S(2)}) collective-permute-start(bf16[2,96,768]{2,1,0:T(8,128)(2,1)S(1)} %get-tuple-element.63), channel_id=1, source_target_pairs={{0,4},{4,0},{8,12},{12,8},{16,20},{20,16},{24,28},{28,24},{1,5},{5... | collective-permute-start | bytes 884744 | tf_op jit(solution)/shard_map/ppermute | solution.py:34
  50.8 17.5 %collective-permute-start.16 = (bf16[2,96,768]{2,1,0:T(8,128)(2,1)S(1)}, bf16[2,96,768]{2,1,0:T(8,128)(2,1)S(1)}, u32[]{:S(2)}, u32[]{:S(2)}) collective-permute-start(bf16[2,96,768]{2,1,0:T(8,128)(2,1)S(1)} %get-tuple-element.64), channel_id=1, source_target_pairs={{0,12},{4,8},{8,4},{12,0},{16,28},{20,24},{24,20},{28,16},{1,13},{... | collective-permute-start | bytes 884744 | tf_op jit(solution)/shard_map/ppermute | solution.py:34
  52.2 16.8 %collective-permute-start.13 = (bf16[256,384]{1,0:T(8,128)(2,1)S(1)}, bf16[256,384]{1,0:T(8,128)(2,1)S(1)}, u32[]{:S(2)}, u32[]{:S(2)}) collective-permute-start(bf16[256,384]{1,0:T(8,128)(2,1)S(1)} %middle_grads.1.refs_5_.refs_1_.refs_3_), channel_id=1, source_target_pairs={{0,16},{4,20},{8,24},{12,28},{16,0},{20,4},{24,8},{28,12},{1,17},{... | collective-permute-start | bytes 589832 | tf_op jit(solution)/shard_map/ppermute | solution.py:531
  57.2 15.1 %collective-permute-start.19 = (bf16[8,96,256]{2,1,0:T(8,128)(2,1)S(1)}, bf16[8,96,256]{2,1,0:T(8,128)(2,1)S(1)}, u32[]{:S(2)}, u32[]{:S(2)}) collective-permute-start(bf16[8,96,256]{2,1,0:T(8,128)(2,1)S(1)} %get-tuple-element.67), channel_id=1, source_target_pairs={{0,1},{1,0},{2,3},{3,2},{4,5},{5,4},{6,7},{7,6},{8,9},{9,8},{10,11... | collective-permute-start | bytes 1179656 | tf_op jit(solution)/shard_map/ppermute | solution.py:34
  70.5 35.8 %collective-permute-start.17 = (bf16[256,1536]{1,0:T(8,128)(2,1)S(1)}, bf16[256,1536]{1,0:T(8,128)(2,1)S(1)}, u32[]{:S(2)}, u32[]{:S(2)}) collective-permute-start(bf16[256,1536]{1,0:T(8,128)(2,1)S(1)} %act_part.1.refs_7_.refs_1_), channel_id=1, source_target_pairs={{0,2},{2,0},{1,3},{3,1},{4,6},{6,4},{5,7},{7,5},{8,10},{10,8},{9,1... | collective-permute-start | bytes 2359304 | tf_op jit(solution)/shard_map/ppermute | solution.py:34
  71.8 1.4 %collective-permute-start.20 = (bf16[256,384]{1,0:T(8,128)(2,1)S(1)}, bf16[256,384]{1,0:T(8,128)(2,1)S(1)}, u32[]{:S(2)}, u32[]{:S(2)}) collective-permute-start(bf16[256,384]{1,0:T(8,128)(2,1)S(1)} %middle_grads.1.refs_5_.refs_1_.refs_3_), channel_id=1, source_target_pairs={{0,1},{1,0},{2,3},{3,2},{4,5},{5,4},{6,7},{7,6},{8,9},{9,8},{10,11... | collective-permute-start | bytes 589832 | tf_op jit(solution)/shard_map/ppermute | solution.py:34
  71.8 1.7 %collective-permute-start.21 = (bf16[256,384]{1,0:T(8,128)(2,1)S(1)}, bf16[256,384]{1,0:T(8,128)(2,1)S(1)}, u32[]{:S(2)}, u32[]{:S(2)}) collective-permute-start(bf16[256,384]{1,0:T(8,128)(2,1)S(1)} %collective-permute-done.13.refs_2_.refs_5_), channel_id=1, source_target_pairs={{0,1},{1,0},{2,3},{3,2},{4,5},{5,4},{6,7},{7,6},{8,9},{9,8},{10,11... | collective-permute-start | bytes 589832 | tf_op jit(solution)/shard_map/ppermute | solution.py:34
  75.1 24.1 %collective-permute-start.23 = (bf16[2,96,768]{2,1,0:T(8,128)(2,1)S(1)}, bf16[2,96,768]{2,1,0:T(8,128)(2,1)S(1)}, u32[]{:S(2)}, u32[]{:S(2)}) collective-permute-start(bf16[2,96,768]{2,1,0:T(8,128)(2,1)S(1)} %get-tuple-element.71), channel_id=1, source_target_pairs={{0,8},{4,12},{8,0},{12,4},{16,24},{20,28},{24,16},{28,20},{1,9},{5... | collective-permute-start | bytes 884744 | tf_op jit(solution)/shard_map/ppermute | solution.py:34
  78.2 21.0 %collective-permute-start.24 = (bf16[2,96,768]{2,1,0:T(8,128)(2,1)S(1)}, bf16[2,96,768]{2,1,0:T(8,128)(2,1)S(1)}, u32[]{:S(2)}, u32[]{:S(2)}) collective-permute-start(bf16[2,96,768]{2,1,0:T(8,128)(2,1)S(1)} %get-tuple-element.72), channel_id=1, source_target_pairs={{0,4},{4,0},{8,12},{12,8},{16,20},{20,16},{24,28},{28,24},{1,5},{5... | collective-permute-start | bytes 884744 | tf_op jit(solution)/shard_map/ppermute | solution.py:34
  79.7 19.5 %collective-permute-start.25 = (bf16[2,96,768]{2,1,0:T(8,128)(2,1)S(1)}, bf16[2,96,768]{2,1,0:T(8,128)(2,1)S(1)}, u32[]{:S(2)}, u32[]{:S(2)}) collective-permute-start(bf16[2,96,768]{2,1,0:T(8,128)(2,1)S(1)} %get-tuple-element.73), channel_id=1, source_target_pairs={{0,12},{4,8},{8,4},{12,0},{16,28},{20,24},{24,20},{28,16},{1,13},{... | collective-permute-start | bytes 884744 | tf_op jit(solution)/shard_map/ppermute | solution.py:34
  79.8 12.7 %collective-permute-start.18 = (bf16[2,96,384]{2,1,0:T(8,128)(2,1)S(1)}, bf16[2,96,384]{2,1,0:T(8,128)(2,1)S(1)}, u32[]{:S(2)}, u32[]{:S(2)}) collective-permute-start(bf16[2,96,384]{2,1,0:T(8,128)(2,1)S(1)} %get-tuple-element.66), channel_id=1, source_target_pairs={{0,2},{2,0},{1,3},{3,1},{4,6},{6,4},{5,7},{7,5},{8,10},{10,8},{9,1... | collective-permute-start | bytes 442376 | tf_op jit(solution)/shard_map/ppermute | solution.py:34
  93.1 6.1 %collective-permute-start.22 = (bf16[96,384]{1,0:T(8,128)(2,1)S(1)}, bf16[96,384]{1,0:T(8,128)(2,1)S(1)}, u32[]{:S(2)}, u32[]{:S(2)}) collective-permute-start(bf16[96,384]{1,0:T(8,128)(2,1)S(1)} %get-tuple-element.70), channel_id=1, source_target_pairs={{0,16},{4,20},{8,24},{12,28},{16,0},{20,4},{24,8},{28,12},{1,17},{... | collective-permute-start | bytes 221192 | tf_op jit(solution)/shard_map/ppermute | solution.py:34
  99.9 6.4 %collective-permute-start.26 = (bf16[96,768]{1,0:T(8,128)(2,1)S(1)}, bf16[96,768]{1,0:T(8,128)(2,1)S(1)}, u32[]{:S(2)}, u32[]{:S(2)}) collective-permute-start(bf16[96,768]{1,0:T(8,128)(2,1)S(1)} %get-tuple-element.75), channel_id=1, source_target_pairs={{0,16},{4,20},{8,24},{12,28},{16,0},{20,4},{24,8},{28,12},{1,17},{... | collective-permute-start | bytes 442376 | tf_op jit(solution)/shard_map/ppermute | solution.py:34

commit v6 on v5

--- a/solution.py
+++ b/solution.py
@@ -244,6 +244,14 @@
     term[...] = total.astype(BF16)
 
 
+def piece_of(place, point, piece, sem):
+    number = piece.shape[0]
+    own = pl.ds(pl.multiple_of(place[SAMPLE] * number, number), number)
+    copy = pltpu.make_async_copy(point.at[own], piece, sem)
+    copy.start()
+    copy.wait()
+
+
 def middle_term(place, acted, weight, middle, kept, given):
     act = acted[...]
     middle[...] = dot(act, weight[1], NN)
@@ -264,35 +272,35 @@
     sent[...] = value.astype(BF16)
 
 
-def own_hidden(place, middle, feat, point, direct, *rest):
-    *passed, hidden, block, other_point = rest
-    hid = gelu_value(middle[...]).astype(BF16)
+def own_hidden(place, middle, feat, point, hidden, block, slope):
+    value = middle[...]
+    hid = gelu_value(value).astype(BF16)
     hidden[...] = hid
     block[...] = wide(feat) + dot(hid, point[...], NT)
-    first = 0
-    for part in passed:
-        rows = slice(first, first + part.shape[0])
-        other_point[rows, :] = jnp.where(place[SAMPLE] == 0, direct[rows, :], part[...])
-        first += part.shape[0]
-
-
-def slopes(place, middle, feat, slope, slope_feat):
-    slope[...] = gelu_slope(middle[...])
-    slope_feat[...] = gelu_slope(wide(feat))
-
-
-def tracks(
-    place, block, other_middle, near, far, cotangent, point, other_point,
-    part, other_hidden, grad_kept, grad_given, block_b, grads,
-):
+    slope[...] = gelu_slope(value)
+
+
+def feature_slope(place, feat, slope):
+    slope[...] = gelu_slope(wide(feat))
+
+
+def tracks(place, block, other_middle, near, far, cotangent, point, *rest):
+    *pieces, part, other_hidden, grad_kept, grad_given, block_b, grads, points = rest
     sample = place[SAMPLE]
     piece = block_b.shape[2]
     width = other_middle.shape[1]
+    ahead = 0
+    for other in pieces:
+        number = other.shape[0]
+        which, row = (sample, ahead) if ahead < piece else (1 - sample, ahead - piece)
+        points[which, row : row + number, width:] = other[...]
+        ahead += number
     hid = gelu_value(wide(other_middle)).astype(BF16)
     other_hidden[...] = hid
     for which in range(2):
         columns = slice(which * piece, (which + 1) * piece)
-        value = block[:, columns] + dot(hid, other_point[columns, :], NT)
+        points[which, :, :width] = point[columns, :]
+        value = block[:, columns] + dot(hid, points[which, :, width:], NT)
         block_b[which] = value.astype(BF16)
     number = near.shape[1]
     tile = width if number % width == 0 else number
@@ -301,15 +309,14 @@
         scores = dot(block_b[sample], near[:, columns], NN)
         scores += dot(block_b[1 - sample], far[:, columns], NN)
         grads[:, columns] = (wide(cotangent.at[:, columns]) * jax.nn.sigmoid(scores)).astype(BF16)
-    kept = given = 0.0
+    both = 0.0
     for which, weight in ((sample, near), (1 - sample, far)):
         columns = pl.ds(pl.multiple_of(which * piece, piece), piece)
         value = dot(grads[...], weight[...], NT).astype(BF16)
         part[:, columns] = value
-        kept += dot(value, point[columns, :], NN)
-        given += dot(value, other_point[columns, :], NN)
-    grad_kept[...] = kept
-    grad_given[...] = given.astype(BF16)
+        both += dot(value, points[which], NN)
+    grad_kept[...] = both[:, :width]
+    grad_given[...] = both[:, width:].astype(BF16)
 
 
 def turn_parts(place, part, far_middle, kept, far_hidden, *rest):
@@ -382,9 +389,14 @@
     each_chip(place, keep, along, across, both, values)
 
 
-def act_part(place, middle_grad, moved, weight, part, slope, give):
-    value = dot(middle_grad[...], weight[1], NT) + dot(moved[...], weight[place[0]], NT)
-    give[...] = (wide(part) + value * slope[...]).astype(BF16)
+def act_part(first):
+    def act_rows(place, middle_grad, moved, weight, part, slope, give):
+        rows = slice(first, first + give.shape[0])
+        value = dot(middle_grad[rows, :], weight[1], NT)
+        value += dot(moved[rows, :], weight[place[0]], NT)
+        give[...] = (part[rows, :].astype(F32) + value * slope[rows, :]).astype(BF16)
+
+    return act_rows
 
 
 def over_chips(at, kept, *arrived):
@@ -402,26 +414,29 @@
         give[at] = total[:, width:].astype(BF16)
 
 
-def point_half(place, kept, got, keep, give):
-    top = place[TOP]
-    keep[...] = over_chips(top, kept, got)
-    give[...] = over_chips(1 - top, kept, got).astype(BF16)
-
-
-def taps_sum(place, *refs):
+def last_sum(place, point_kept, point_got, *refs):
     *parts, keep, give = refs
     top = place[TOP]
-    keep[...] = over_chips(top, *parts)
-    give[...] = over_chips(1 - top, *parts).astype(BF16)
-
-
-def finish(place, own, theirs, point_kept, point_got, kept, got, dilated, point, result):
+    width = parts[0].shape[2]
+    for columns, terms in (
+        (slice(0, width), parts),
+        (slice(width, None), (point_kept, point_got)),
+    ):
+        keep[:, columns] = over_chips(top, *terms)
+        give[:, columns] = over_chips(1 - top, *terms).astype(BF16)
+
+
+def finish(place, one, one_got, two, two_got, kept, got, dilated, point, result):
     width = point.shape[1]
     dilated[1] = kept[:, :width] + got[:, :width].astype(F32)
-    dilated[place[0]] = kept[:, width:]
-    dilated[2 - place[0]] = got[:, width:].astype(F32)
-    point[...] = point_kept[...] + wide(point_got)
-    result[...] = (wide(own) + wide(theirs)).astype(BF16)
+    dilated[place[0]] = kept[:, width : 2 * width]
+    dilated[2 - place[0]] = got[:, width : 2 * width].astype(F32)
+    point[...] = kept[:, 2 * width :] + got[:, 2 * width :].astype(F32)
+    first = 0
+    for own, theirs in ((one, one_got), (two, two_got)):
+        rows = slice(first, first + own.shape[0])
+        result[rows, :] = (wide(own) + wide(theirs)).astype(BF16)
+        first += own.shape[0]
 
 
 def body(features, dilated_weight, point_weight, track_weight, track_cotangent):
@@ -445,16 +460,22 @@
     cotangent = track_cotangent.reshape(rows, tracks_here)
     pairs = [(i, (i + dist) % n_seq) for i in range(n_seq)]
 
-    direct = lax.ppermute(point_weight, ("head", "sample"), [(0, 2), (2, 0)])
-    cut = channels // 3
-    passed = [
-        lax.ppermute(direct[k : k + cut], "sample", [(0, 1)]) for k in range(0, channels, cut)
-    ]
+    (own_piece,) = kernel_call(
+        piece_of,
+        [((piece, width), BF16)],
+        [place, in_hbm(point_weight)],
+        scratch=[pltpu.SemaphoreType.DMA],
+        spaces={1: pltpu.HBM},
+    )
+    near = flip(own_piece, "head")
+    cut = piece // 3
+    points = [near] + [flip(near[k : k + cut], "sample") for k in range(0, piece, cut)]
     far_track = flip(track_weight, "sample")
     acted, term = kernel_call(
         outer_term,
         [((rows, channels), BF16), ((rows, width), BF16)],
         [place, in_hbm(feat), in_hbm(taps)],
+        own_piece,
         scratch=[
             pltpu.VMEM((rows, channels), BF16),
             pltpu.VMEM((channels, width), BF16),
@@ -475,32 +496,30 @@
         add_terms, [((rows, width), F32), ((rows, width), BF16)], [place, middle, arrived], acts
     )
     other_middle = flip(middle_b, "head")
-    hidden, block_part, other_point = kernel_call(
+    hidden, block_part, slope = kernel_call(
         own_hidden,
-        [((rows, width), BF16), ((rows, channels), F32), ((channels, width), BF16)],
-        [place, middle, feat, point_weight, direct, *passed],
-    )
-    slope, slope_feat = kernel_call(
-        slopes,
-        [((rows, width), F32), ((rows, channels), F32)],
-        [place, middle, feat],
-        block_part,
+        [((rows, width), BF16), ((rows, channels), F32), ((rows, width), F32)],
+        [place, middle, feat, point_weight],
+    )
+    (slope_feat,) = kernel_call(
+        feature_slope, [((rows, channels), F32)], [place, feat], block_part
     )
     part, other_hidden, grad_kept, grad_given = kernel_call(
         tracks,
         [((rows, channels), BF16), ((rows, width), BF16), ((rows, width), F32), ((rows, width), BF16)],
         [
             place, block_part, other_middle, track_weight, far_track, cotangent, point_weight,
-            other_point,
+            *points,
         ],
-        slope,
+        slope_feat,
         scratch=[
             pltpu.VMEM((n_sample, rows, piece), BF16),
             pltpu.VMEM((rows, tracks_here), BF16),
+            pltpu.VMEM((n_sample, piece, n_head * width), BF16),
         ],
     )
     grad_got = flip(grad_given, "head")
-    far_hidden = flip(hidden, "sample")
+    far_hidden, other_acts = flip(hidden, "sample"), flip(acts_given, "sample")
 
     def traded(kernel, columns, ins, after=None, scratch=()):
         shape = (2, block, columns)
@@ -523,49 +542,41 @@
         2 * width,
         [outs, hidden, other_hidden, far_hidden, far_other]
         + [flip(piece, "sample") for piece in outs_given],
+        other_acts,
         scratch=[pltpu.VMEM((groups, block, rows), BF16)],
     )
     (middle_grad,) = kernel_call(
         middle_grads, [((rows, width), BF16)], [place, grad_kept, grad_got, slope], points[0]
     )
     moved = lax.ppermute(middle_grad, "seq", pairs)
-    small = ((block, width), F32), ((block, width), BF16)
+    ins = [place, middle_grad, moved, taps, part, slope_feat]
+    other_grad = flip(middle_grad, "sample")
+    most = rows * 3 // 4
+    (one,) = kernel_call(act_part(0), [((most, channels), BF16)], ins, other_grad)
     point_kept, point_give = kernel_call(
         point_sum,
         [((2, block, width), F32), ((2, block, width), BF16)],
         [place, *points],
-        middle_grad,
-    )
-    (own,) = kernel_call(
-        act_part,
-        [((rows, channels), BF16)],
-        [place, middle_grad, moved, taps, part, slope_feat],
-        point_kept,
+        one,
     )
     steps = traded(
         tap_products,
         2 * width,
-        [
-            acts, flip(acts_given, "sample"), middle_grad, flip(middle_grad, "sample"), moved,
-            flip(moved, "sample"),
-        ],
-        own,
-    )
-    point_kept, point_give = kernel_call(
-        point_half, small, [place, point_kept, flip(point_give, "head")], steps[0]
-    )
-    point_got = flip(point_give, "seq", n_seq // 2)
+        [acts, other_acts, middle_grad, other_grad, moved, flip(moved, "sample")],
+        point_kept,
+    )
+    (two,) = kernel_call(act_part(most), [((rows - most, channels), BF16)], ins, steps[0])
     kept, give = kernel_call(
-        taps_sum,
-        [((block, 2 * width), F32), ((block, 2 * width), BF16)],
-        [place, *steps],
-        point_got,
+        last_sum,
+        [((block, 3 * width), F32), ((block, 3 * width), BF16)],
+        [place, point_kept, flip(point_give, "head"), *steps],
+        two,
     )
     dilated_grad, point_grad, input_grad = kernel_call(
         finish,
         [((3, block, width), F32), ((block, width), F32), ((rows, channels), BF16)],
         [
-            place, own, flip(own, "head"), point_kept, point_got, kept,
+            place, one, flip(one, "head"), two, flip(two, "head"), kept,
             flip(give, "seq", n_seq // 2),
         ],
     )

time: 108 us -> 96.1 us (0.89)
  starting transfers between devices: 35.9 us -> 24.4 us
  waiting for transfers between devices: 46.1 us -> 44.5 us
    ppermute x4 -> x0, waiting for transfers between devices: 8.47 us -> none  [the longest x1 8.46 us: body(): direct = lax.ppermute(point_weight, ('head', 'sample'), [(0, 2), (2, 0)])]
    ppermute x1, waiting for transfers between devices: 0.01 us -> 8.4 us  [body(): arrived = lax.ppermute(term, 'seq', pairs)]
    ppermute x4 -> x0, starting transfers between devices: 8.36 us -> none  [the longest x1 4.41 us: body(): direct = lax.ppermute(point_weight, ('head', 'sample'), [(0, 2), (2, 0)])]
    ppermute x21 -> x25, waiting for transfers between devices: 37.7 us -> 30.7 us  [flip(): return lax.ppermute(value, axis, [(i, i ^ step) for i in range(count)])]
    ppermute x1, waiting for transfers between devices: 0.01 us -> 5.42 us  [body(): moved = lax.ppermute(middle_grad, 'seq', pairs)]
    ppermute x1, starting transfers between devices: 5.03 us -> 0.07 us  [body(): moved = lax.ppermute(middle_grad, 'seq', pairs)]
    ppermute x21 -> x25, starting transfers between devices: 19.9 us -> 21.7 us  [flip(): return lax.ppermute(value, axis, [(i, i ^ step) for i in range(count)])]
    pallas_call x15 -> x16, Pallas kernels: 24.9 us -> 25.9 us  [kernel_call(): pl.pallas_call(run, out_shape=[jax.ShapeDtypeStruct(s, d) for s, d in out...]
  transfers between devices with their start and end apart: 27 -> 27, of which waited for: 11 -> 12; matrix products, arithmetic and copies ran while one was open for 0% -> 0% of each run, Pallas kernels for 21% -> 25%
where the time goes in v6:
time: 96.1 us; the launch traced here: 95.9 us
  waiting for transfers between devices  44.5 us (46%)
  Pallas kernels  25.9 us (27%)
  starting transfers between devices  24.4 us (25%)
    ppermute x25, waiting for transfers between devices, flip(): return lax.ppermute(value, axis, [(i, i ^ step) for i in range(count)])  30.7 us
    pallas_call x16, Pallas kernels, kernel_call(): pl.pallas_call(run, out_shape=[jax.ShapeDtypeStruct(s, d) for s, d in out...  25.9 us
    ppermute x25, starting transfers between devices, flip(): return lax.ppermute(value, axis, [(i, i ^ step) for i in range(count)])  21.7 us
    ppermute x1, waiting for transfers between devices, body(): arrived = lax.ppermute(term, 'seq', pairs)  8.4 us
    ppermute x1, waiting for transfers between devices, body(): moved = lax.ppermute(middle_grad, 'seq', pairs)  5.42 us
    ppermute x1, starting transfers between devices, body(): arrived = lax.ppermute(term, 'seq', pairs)  2.65 us
  transfers between devices with their start and end apart: 27, of which 12 were waited for; matrix products, arithmetic and copies ran while one was open for 0% of the time, Pallas kernels for 25%

profile of v6, /device:TPU:0, one launch (start us, length us, event | category | flops | bytes accessed | tf_op | source)
XLA Modules:
  0.0 95.9 jit_solution(2187307381841037179)
XLA Ops:
  1.2 1.9 %piece_of.1.refs_3_ = bf16[768,384]{1,0:T(8,128)(2,1)S(1)} custom-call(s32[6]{0:T(128)S(1)} %stack.27.refs_0_, bf16[1536,384]{1,0:T(8,128)(2,1)} %refs_6_.1), custom_call_target="tpu_custom_call" | custom-call | flops 1 | bytes 1 | tf_op jit(solution)/shard_map/piece_of/pallas_call | solution.py:200
  3.1 2.6 %collective-permute-start.3 = (bf16[768,384]{1,0:T(8,128)(2,1)S(1)}, bf16[768,384]{1,0:T(8,128)(2,1)S(1)}, u32[]{:S(2)}, u32[]{:S(2)}) collective-permute-start(bf16[768,384]{1,0:T(8,128)(2,1)S(1)} %piece_of.1.refs_3_), channel_id=1, source_target_pairs={{0,2},{2,0},{1,3},{3,1},{4,6},{6,4},{5,7},{7,5},{8,10},{10,8},{9,1... | collective-permute-start | bytes 1769480 | tf_op jit(solution)/shard_map/ppermute | solution.py:34
  5.7 2.9 %outer_term.1 = (bf16[256,1536]{1,0:T(8,128)(2,1)S(1)}, bf16[256,384]{1,0:T(8,128)(2,1)S(1)}) custom-call(s32[6]{0:T(128)S(1)} %stack.27.refs_0_, bf16[256,1536]{1,0:T(8,128)(2,1)} %bitcast.15, bf16[3,1536,384]{2,1,0:T(8,128)(2,1)} %bitcast.11, bf16[768,384]{1,0:T(8,128)(2,1)S(1)} %piece_of.1.refs_3_), custom_call_target="tpu_custom_call" | custom-call | flops 1 | bytes 1 | tf_op jit(solution)/shard_map/outer_term/pallas_call | solution.py:200
  8.6 2.7 %collective-permute-start = (bf16[256,384]{1,0:T(8,128)(2,1)S(1)}, bf16[256,384]{1,0:T(8,128)(2,1)S(1)}, u32[]{:S(2)}, u32[]{:S(2)}) collective-permute-start(bf16[256,384]{1,0:T(8,128)(2,1)S(1)} %get-tuple-element.39), channel_id=1, source_target_pairs={{0,16},{4,20},{8,24},{12,28},{16,0},{20,4},{24,8},{28,12},{1,17},{... | collective-permute-start | bytes 589832 | tf_op jit(solution)/shard_map/ppermute | solution.py:486
  11.3 1.1 %middle_term.1 = (f32[256,384]{1,0:T(8,128)S(1)}, bf16[8,96,256]{2,1,0:T(8,128)(2,1)S(1)}, bf16[8,96,256]{2,1,0:T(8,128)(2,1)S(1)}) custom-call(s32[6]{0:T(128)S(1)} %stack.27.refs_0_, bf16[256,1536]{1,0:T(8,128)(2,1)S(1)} %get-tuple-element.37.refs_1_, bf16[3,1536,384]{2,1,0:T(8,128)(2,1)S(1)} %bitcast.12), custom_call_target="tpu_custom_call" | custom-call | flops 1 | bytes 1 | tf_op jit(solution)/shard_map/middle_term/pallas_call | solution.py:200
  12.4 8.4 %collective-permute-done.refs_2_ = bf16[256,384]{1,0:T(8,128)(2,1)S(1)} collective-permute-done((bf16[256,384]{1,0:T(8,128)(2,1)S(1)}, bf16[256,384]{1,0:T(8,128)(2,1)S(1)}, u32[]{:S(2)}, u32[]{:S(2)}) %collective-permute-start) | collective-permute-done | bytes 196640 | tf_op jit(solution)/shard_map/ppermute | solution.py:486
  22.7 5.0 %collective-permute-done.1.refs_2_ = bf16[256,384]{1,0:T(8,128)(2,1)S(1)} collective-permute-done((bf16[256,384]{1,0:T(8,128)(2,1)S(1)}, bf16[256,384]{1,0:T(8,128)(2,1)S(1)}, u32[]{:S(2)}, u32[]{:S(2)}) %collective-permute-start.1) | collective-permute-done | bytes 196640 | tf_op jit(solution)/shard_map/ppermute | solution.py:34
  27.7 1.2 %own_hidden.1 = (bf16[256,384]{1,0:T(8,128)(2,1)S(1)}, f32[256,1536]{1,0:T(8,128)S(1)}, f32[256,384]{1,0:T(8,128)S(1)}) custom-call(s32[6]{0:T(128)S(1)} %stack.27.refs_0_, f32[256,384]{1,0:T(8,128)S(1)} %get-tuple-element.41.refs_1_, bf16[256,1536]{1,0:T(8,128)(2,1)S(1)} %bitcast.16, bf16[1536,384]{1,0:T(8,128)(2,1)S(1)} %copy-done.1), custom_call_target="tpu_custom_call" | custom-call | flops 1 | bytes 1 | tf_op jit(solution)/shard_map/own_hidden/pallas_call | solution.py:200
  29.6 1.5 %feature_slope.1.refs_11_.refs_5_ = f32[256,1536]{1,0:T(8,128)S(1)} custom-call(s32[6]{0:T(128)S(1)} %stack.27.refs_0_, bf16[256,1536]{1,0:T(8,128)(2,1)S(1)} %bitcast.17, f32[256,1536]{1,0:T(8,128)S(1)} %get-tuple-element.42.refs_2_.refs_1_), custom_call_target="tpu_custom_call" | custom-call | flops 1 | bytes 1 | tf_op jit(solution)/shard_map/feature_slope/pallas_call | solution.py:200
  31.1 6.1 %tracks.1 = (bf16[256,1536]{1,0:T(8,128)(2,1)S(1)}, bf16[256,384]{1,0:T(8,128)(2,1)S(1)}, f32[256,384]{1,0:T(8,128)S(1)}, bf16[256,384]{1,0:T(8,128)(2,1)S(1)}) custom-call(s32[6]{0:T(128)S(1)} %stack.27.refs_0_, f32[256,1536]{1,0:T(8,128)S(1)} %get-tuple-element.42.refs_2_.refs_1_, bf16[256,384]{1,0:T(8,128)(2,1)S(1)} %collective-permute-done.1.refs_2_, ...), custom_call_target="tpu_custom_call" | custom-call | flops 1 | bytes 1 | tf_op jit(solution)/shard_map/tracks/pallas_call | solution.py:200
  37.2 0.9 collective-permute-start.7
  38.1 1.0 %turn_parts.1 = (bf16[8,96,256]{2,1,0:T(8,128)(2,1)S(1)}, bf16[256,384]{1,0:T(8,128)(2,1)S(1)}, bf16[3,96,256]{2,1,0:T(8,128)(2,1)S(1)}, bf16[3,96,256]{2,1,0:T(8,128)(2,1)S(1)}, bf16[2,96,256]{2,1,0:T(8,128)(2,1)S(1)}) custom-call(s32[6]{0:T(128)S(1)} %stack.27.refs_0_, bf16[256,1536]{1,0:T(8,128)(2,1)S(1)} %get-tuple-element.47.refs_1_.refs_4_, ...), custom_call_target="tpu_custom_call" | custom-call | flops 1 | bytes 1 | tf_op jit(solution)/shard_map/turn_parts/pallas_call | solution.py:200
  39.8 1.1 %collective-permute-done.12.refs_8_ = bf16[2,96,256]{2,1,0:T(8,128)(2,1)S(1)} collective-permute-done((bf16[2,96,256]{2,1,0:T(8,128)(2,1)S(1)}, bf16[2,96,256]{2,1,0:T(8,128)(2,1)S(1)}, u32[]{:S(2)}, u32[]{:S(2)}) %collective-permute-start.12) | collective-permute-done | bytes 98336 | tf_op jit(solution)/shard_map/ppermute | solution.py:34
  40.9 1.5 %point_products.1 = (f32[2,96,768]{2,1,0:T(8,128)S(1)}, bf16[2,96,768]{2,1,0:T(8,128)(2,1)S(1)}, bf16[2,96,768]{2,1,0:T(8,128)(2,1)S(1)}, bf16[2,96,768]{2,1,0:T(8,128)(2,1)S(1)}) custom-call(s32[6]{0:T(128)S(1)} %stack.27.refs_0_, bf16[8,96,256]{2,1,0:T(8,128)(2,1)S(1)} %get-tuple-element.49.refs_1_, bf16[256,384]{1,0:T(8,128)(2,1)S(1)} %get-tuple-element.48.refs_2_, ...), custom_call_target="tpu_custom_call" | custom-call | flops 1 | bytes 1 | tf_op jit(solution)/shard_map/point_products/pallas_call | solution.py:200
  42.5 2.0 %collective-permute-done.7.refs_2_ = bf16[256,384]{1,0:T(8,128)(2,1)S(1)} collective-permute-done((bf16[256,384]{1,0:T(8,128)(2,1)S(1)}, bf16[256,384]{1,0:T(8,128)(2,1)S(1)}, u32[]{:S(2)}, u32[]{:S(2)}) %collective-permute-start.7) | collective-permute-done | bytes 196640 | tf_op jit(solution)/shard_map/ppermute | solution.py:34
  45.2 4.7 %collective-permute-start.18 = (bf16[2,96,768]{2,1,0:T(8,128)(2,1)S(1)}, bf16[2,96,768]{2,1,0:T(8,128)(2,1)S(1)}, u32[]{:S(2)}, u32[]{:S(2)}) collective-permute-start(bf16[2,96,768]{2,1,0:T(8,128)(2,1)S(1)} %get-tuple-element.57), channel_id=1, source_target_pairs={{0,8},{4,12},{8,0},{12,4},{16,24},{20,28},{24,16},{28,20},{1,9},{5... | collective-permute-start | bytes 884744 | tf_op jit(solution)/shard_map/ppermute | solution.py:34
  49.9 1.5 %collective-permute-start.19 = (bf16[2,96,768]{2,1,0:T(8,128)(2,1)S(1)}, bf16[2,96,768]{2,1,0:T(8,128)(2,1)S(1)}, u32[]{:S(2)}, u32[]{:S(2)}) collective-permute-start(bf16[2,96,768]{2,1,0:T(8,128)(2,1)S(1)} %get-tuple-element.58), channel_id=1, source_target_pairs={{0,4},{4,0},{8,12},{12,8},{16,20},{20,16},{24,28},{28,24},{1,5},{5... | collective-permute-start | bytes 884744 | tf_op jit(solution)/shard_map/ppermute | solution.py:34
  51.4 5.4 %collective-permute-done.14.refs_2_.refs_5_ = bf16[256,384]{1,0:T(8,128)(2,1)S(1)} collective-permute-done((bf16[256,384]{1,0:T(8,128)(2,1)S(1)}, bf16[256,384]{1,0:T(8,128)(2,1)S(1)}, u32[]{:S(2)}, u32[]{:S(2)}) %collective-permute-start.14) | collective-permute-done | bytes 196640 | tf_op jit(solution)/shard_map/ppermute | solution.py:551
  56.9 1.5 %act_rows.2.refs_5_.refs_1_ = bf16[192,1536]{1,0:T(8,128)(2,1)S(1)} custom-call(s32[6]{0:T(128)S(1)} %stack.27.refs_0_, bf16[256,384]{1,0:T(8,128)(2,1)S(1)} %middle_grads.1.refs_1_.refs_3_, bf16[256,384]{1,0:T(8,128)(2,1)S(1)} %collective-permute-done.14.refs_2_.refs_5_, bf16[3,1536,384]{2,1,0:T(8,128)(2,1)S(1)} %bitcast.13, ...), custom_call_target="tpu_custom_call" | custom-call | flops 1 | bytes 1 | tf_op jit(solution)/shard_map/act_rows/pallas_call | solution.py:200
  58.4 0.9 collective-permute-start.16
  59.2 1.1 %collective-permute-done.18.refs_2_ = bf16[2,96,768]{2,1,0:T(8,128)(2,1)S(1)} collective-permute-done((bf16[2,96,768]{2,1,0:T(8,128)(2,1)S(1)}, bf16[2,96,768]{2,1,0:T(8,128)(2,1)S(1)}, u32[]{:S(2)}, u32[]{:S(2)}) %collective-permute-start.18) | collective-permute-done | bytes 294944 | tf_op jit(solution)/shard_map/ppermute | solution.py:34
  60.4 5.9 %collective-permute-done.20.refs_4_ = bf16[2,96,768]{2,1,0:T(8,128)(2,1)S(1)} collective-permute-done((bf16[2,96,768]{2,1,0:T(8,128)(2,1)S(1)}, bf16[2,96,768]{2,1,0:T(8,128)(2,1)S(1)}, u32[]{:S(2)}, u32[]{:S(2)}) %collective-permute-start.20) | collective-permute-done | bytes 294944 | tf_op jit(solution)/shard_map/ppermute | solution.py:34
  67.0 1.5 %tap_products.1 = (f32[2,96,768]{2,1,0:T(8,128)S(1)}, bf16[2,96,768]{2,1,0:T(8,128)(2,1)S(1)}, bf16[2,96,768]{2,1,0:T(8,128)(2,1)S(1)}, bf16[2,96,768]{2,1,0:T(8,128)(2,1)S(1)}) custom-call(s32[6]{0:T(128)S(1)} %stack.27.refs_0_, bf16[8,96,256]{2,1,0:T(8,128)(2,1)S(1)} %get-tuple-element.40.refs_3_.refs_1_, ...), custom_call_target="tpu_custom_call" | custom-call | flops 1 | bytes 1 | tf_op jit(solution)/shard_map/tap_products/pallas_call | solution.py:200
  69.2 2.9 %collective-permute-start.25 = (bf16[2,96,768]{2,1,0:T(8,128)(2,1)S(1)}, bf16[2,96,768]{2,1,0:T(8,128)(2,1)S(1)}, u32[]{:S(2)}, u32[]{:S(2)}) collective-permute-start(bf16[2,96,768]{2,1,0:T(8,128)(2,1)S(1)} %get-tuple-element.65), channel_id=1, source_target_pairs={{0,12},{4,8},{8,4},{12,0},{16,28},{20,24},{24,20},{28,16},{1,13},{... | collective-permute-start | bytes 884744 | tf_op jit(solution)/shard_map/ppermute | solution.py:34
  72.6 1.4 %act_rows.3.refs_7_.refs_3_ = bf16[64,1536]{1,0:T(8,128)(2,1)S(1)} custom-call(s32[6]{0:T(128)S(1)} %stack.27.refs_0_, bf16[256,384]{1,0:T(8,128)(2,1)S(1)} %middle_grads.1.refs_1_.refs_3_, bf16[256,384]{1,0:T(8,128)(2,1)S(1)} %collective-permute-done.14.refs_2_.refs_5_, bf16[3,1536,384]{2,1,0:T(8,128)(2,1)S(1)} %bitcast.14, ...), custom_call_target="tpu_custom_call" | custom-call | flops 1 | bytes 1 | tf_op jit(solution)/shard_map/act_rows/pallas_call | solution.py:200
  74.0 3.3 %collective-permute-done.22.refs_2_ = bf16[2,96,384]{2,1,0:T(8,128)(2,1)S(1)} collective-permute-done((bf16[2,96,384]{2,1,0:T(8,128)(2,1)S(1)}, bf16[2,96,384]{2,1,0:T(8,128)(2,1)S(1)}, u32[]{:S(2)}, u32[]{:S(2)}) %collective-permute-start.22) | collective-permute-done | bytes 147488 | tf_op jit(solution)/shard_map/ppermute | solution.py:34
  77.3 1.2 %collective-permute-done.23.refs_4_ = bf16[2,96,768]{2,1,0:T(8,128)(2,1)S(1)} collective-permute-done((bf16[2,96,768]{2,1,0:T(8,128)(2,1)S(1)}, bf16[2,96,768]{2,1,0:T(8,128)(2,1)S(1)}, u32[]{:S(2)}, u32[]{:S(2)}) %collective-permute-start.23) | collective-permute-done | bytes 294944 | tf_op jit(solution)/shard_map/ppermute | solution.py:34
  78.5 4.1 %collective-permute-done.24.refs_5_ = bf16[2,96,768]{2,1,0:T(8,128)(2,1)S(1)} collective-permute-done((bf16[2,96,768]{2,1,0:T(8,128)(2,1)S(1)}, bf16[2,96,768]{2,1,0:T(8,128)(2,1)S(1)}, u32[]{:S(2)}, u32[]{:S(2)}) %collective-permute-start.24) | collective-permute-done | bytes 294944 | tf_op jit(solution)/shard_map/ppermute | solution.py:34
  83.3 3.5 %collective-permute-start.26 = (bf16[96,1152]{1,0:T(8,128)(2,1)S(1)}, bf16[96,1152]{1,0:T(8,128)(2,1)S(1)}, u32[]{:S(2)}, u32[]{:S(2)}) collective-permute-start(bf16[96,1152]{1,0:T(8,128)(2,1)S(1)} %get-tuple-element.67), channel_id=1, source_target_pairs={{0,16},{4,20},{8,24},{12,28},{16,0},{20,4},{24,8},{28,12},{1,17},{... | collective-permute-start | bytes 663560 | tf_op jit(solution)/shard_map/ppermute | solution.py:34
  87.3 5.1 %collective-permute-done.21.refs_4_ = bf16[64,1536]{1,0:T(8,128)(2,1)S(1)} collective-permute-done((bf16[64,1536]{1,0:T(8,128)(2,1)S(1)}, bf16[64,1536]{1,0:T(8,128)(2,1)S(1)}, u32[]{:S(2)}, u32[]{:S(2)}) %collective-permute-start.21) | collective-permute-done | bytes 196640 | tf_op jit(solution)/shard_map/ppermute | solution.py:34
  92.5 1.7 %collective-permute-done.26.refs_6_ = bf16[96,1152]{1,0:T(8,128)(2,1)S(1)} collective-permute-done((bf16[96,1152]{1,0:T(8,128)(2,1)S(1)}, bf16[96,1152]{1,0:T(8,128)(2,1)S(1)}, u32[]{:S(2)}, u32[]{:S(2)}) %collective-permute-start.26) | collective-permute-done | bytes 221216 | tf_op jit(solution)/shard_map/ppermute | solution.py:34
  94.1 1.8 %finish.1 = (f32[3,96,384]{2,1,0:T(8,128)}, f32[96,384]{1,0:T(8,128)}, bf16[256,1536]{1,0:T(8,128)(2,1)}) custom-call(s32[6]{0:T(128)S(1)} %stack.27.refs_0_, bf16[192,1536]{1,0:T(8,128)(2,1)S(1)} %act_rows.2.refs_5_.refs_1_, bf16[192,1536]{1,0:T(8,128)(2,1)S(1)} %collective-permute-done.16.refs_2_, bf16[64,1536]{1,0:T(8,128)(2,1)S(1)} %act_rows.3.refs_7_.refs_3_, ...), custom_call_target="tpu_custom_call" | custom-call | flops 1 | bytes 1 | tf_op jit(solution)/shard_map/finish/pallas_call | solution.py:200
  (50 shorter events, 7.6 us)
Async XLA Ops:
  0.6 30.5 %collective-permute-start.2 = (bf16[768,1920]{1,0:T(8,128)(2,1)}, bf16[768,1920]{1,0:T(8,128)(2,1)S(1)}, u32[]{:S(2)}, u32[]{:S(2)}) collective-permute-start(bf16[768,1920]{1,0:T(8,128)(2,1)} %refs_3_.3), channel_id=1, source_target_pairs={{0,1},{1,0},{2,3},{3,2},{4,5},{5,4},{6,7},{7,6},{8,9},{9,8},{10,11... | collective-permute-start | bytes 8847368 | tf_op jit(solution)/shard_map/ppermute | solution.py:34
  1.2 10.0 %copy-start = (bf16[1536,3,384]{2,0,1:T(8,128)(2,1)S(1)}, bf16[1536,3,384]{2,0,1:T(8,128)(2,1)}, u32[]{:S(2)}) copy-start(bf16[1536,3,384]{2,0,1:T(8,128)(2,1)} %param.6) | copy-start | bytes 10616836
  3.1 18.8 %collective-permute-start.3 = (bf16[768,384]{1,0:T(8,128)(2,1)S(1)}, bf16[768,384]{1,0:T(8,128)(2,1)S(1)}, u32[]{:S(2)}, u32[]{:S(2)}) collective-permute-start(bf16[768,384]{1,0:T(8,128)(2,1)S(1)} %piece_of.1.refs_3_), channel_id=1, source_target_pairs={{0,2},{2,0},{1,3},{3,1},{4,6},{6,4},{5,7},{7,5},{8,10},{10,8},{9,1... | collective-permute-start | bytes 1769480 | tf_op jit(solution)/shard_map/ppermute | solution.py:34
  8.6 12.2 %collective-permute-start = (bf16[256,384]{1,0:T(8,128)(2,1)S(1)}, bf16[256,384]{1,0:T(8,128)(2,1)S(1)}, u32[]{:S(2)}, u32[]{:S(2)}) collective-permute-start(bf16[256,384]{1,0:T(8,128)(2,1)S(1)} %get-tuple-element.39), channel_id=1, source_target_pairs={{0,16},{4,20},{8,24},{12,28},{16,0},{20,4},{24,8},{28,12},{1,17},{... | collective-permute-start | bytes 589832 | tf_op jit(solution)/shard_map/ppermute | solution.py:486
  11.2 16.4 %copy-start.1 = (bf16[1536,384]{1,0:T(8,128)(2,1)S(1)}, bf16[1536,384]{1,0:T(8,128)(2,1)}, u32[]{:S(2)}) copy-start(bf16[1536,384]{1,0:T(8,128)(2,1)} %refs_6_.1) | copy-start | bytes 3538948
  11.3 16.4 %copy-start.2 = (bf16[1,256,1536]{2,1,0:T(8,128)(2,1)S(1)}, bf16[1,256,1536]{2,1,0:T(8,128)(2,1)}, u32[]{:S(2)}) copy-start(bf16[1,256,1536]{2,1,0:T(8,128)(2,1)} %param.5) | copy-start | bytes 2359300
  21.4 6.2 %collective-permute-start.1 = (bf16[256,384]{1,0:T(8,128)(2,1)S(1)}, bf16[256,384]{1,0:T(8,128)(2,1)S(1)}, u32[]{:S(2)}, u32[]{:S(2)}) collective-permute-start(bf16[256,384]{1,0:T(8,128)(2,1)S(1)} %get-tuple-element.43), channel_id=1, source_target_pairs={{0,2},{2,0},{1,3},{3,1},{4,6},{6,4},{5,7},{7,5},{8,10},{10,8},{9,1... | collective-permute-start | bytes 589832 | tf_op jit(solution)/shard_map/ppermute | solution.py:34
  22.0 6.9 %collective-permute-start.4 = (bf16[256,384]{1,0:T(8,128)(2,1)S(1)}, bf16[256,384]{1,0:T(8,128)(2,1)S(1)}, u32[]{:S(2)}, u32[]{:S(2)}) collective-permute-start(bf16[256,384]{1,0:T(8,128)(2,1)S(1)} %get-tuple-element.73), channel_id=1, source_target_pairs={{0,1},{1,0},{2,3},{3,2},{4,5},{5,4},{6,7},{7,6},{8,9},{9,8},{10,11... | collective-permute-start | bytes 589832 | tf_op jit(solution)/shard_map/ppermute | solution.py:34
  22.1 7.4 %collective-permute-start.5 = (bf16[256,384]{1,0:T(8,128)(2,1)S(1)}, bf16[256,384]{1,0:T(8,128)(2,1)S(1)}, u32[]{:S(2)}, u32[]{:S(2)}) collective-permute-start(bf16[256,384]{1,0:T(8,128)(2,1)S(1)} %get-tuple-element.72), channel_id=1, source_target_pairs={{0,1},{1,0},{2,3},{3,2},{4,5},{5,4},{6,7},{7,6},{8,9},{9,8},{10,11... | collective-permute-start | bytes 589832 | tf_op jit(solution)/shard_map/ppermute | solution.py:34
  22.6 17.2 %collective-permute-start.13 = (bf16[8,96,256]{2,1,0:T(8,128)(2,1)S(1)}, bf16[8,96,256]{2,1,0:T(8,128)(2,1)S(1)}, u32[]{:S(2)}, u32[]{:S(2)}) collective-permute-start(bf16[8,96,256]{2,1,0:T(8,128)(2,1)S(1)} %get-tuple-element.55), channel_id=1, source_target_pairs={{0,1},{1,0},{2,3},{3,2},{4,5},{5,4},{6,7},{7,6},{8,9},{9,8},{10,11... | collective-permute-start | bytes 1179656 | tf_op jit(solution)/shard_map/ppermute | solution.py:34
  27.6 3.5 %collective-permute-start.6 = (bf16[256,384]{1,0:T(8,128)(2,1)S(1)}, bf16[256,384]{1,0:T(8,128)(2,1)S(1)}, u32[]{:S(2)}, u32[]{:S(2)}) collective-permute-start(bf16[256,384]{1,0:T(8,128)(2,1)S(1)} %get-tuple-element.71), channel_id=1, source_target_pairs={{0,1},{1,0},{2,3},{3,2},{4,5},{5,4},{6,7},{7,6},{8,9},{9,8},{10,11... | collective-permute-start | bytes 589832 | tf_op jit(solution)/shard_map/ppermute | solution.py:34
  27.6 3.5 %copy-start.3 = (bf16[768,1920]{1,0:T(8,128)(2,1)S(1)}, bf16[768,1920]{1,0:T(8,128)(2,1)}, u32[]{:S(2)}) copy-start(bf16[768,1920]{1,0:T(8,128)(2,1)} %refs_3_.3) | copy-start | bytes 8847364
  27.7 3.5 %copy-start.4 = (bf16[1,256,1920]{2,1,0:T(8,128)(2,1)S(1)}, bf16[1,256,1920]{2,1,0:T(8,128)(2,1)}, u32[]{:S(2)}) copy-start(bf16[1,256,1920]{2,1,0:T(8,128)(2,1)} %param.9) | copy-start | bytes 2949124
  28.9 9.1 %collective-permute-start.9 = (bf16[256,384]{1,0:T(8,128)(2,1)S(1)}, bf16[256,384]{1,0:T(8,128)(2,1)S(1)}, u32[]{:S(2)}, u32[]{:S(2)}) collective-permute-start(bf16[256,384]{1,0:T(8,128)(2,1)S(1)} %get-tuple-element.48.refs_2_), channel_id=1, source_target_pairs={{0,1},{1,0},{2,3},{3,2},{4,5},{5,4},{6,7},{7,6},{8,9},{9,8},{10,11... | collective-permute-start | bytes 589832 | tf_op jit(solution)/shard_map/ppermute | solution.py:34
  29.5 8.6 %collective-permute-start.8 = (bf16[256,384]{1,0:T(8,128)(2,1)S(1)}, bf16[256,384]{1,0:T(8,128)(2,1)S(1)}, u32[]{:S(2)}, u32[]{:S(2)}) collective-permute-start(bf16[256,384]{1,0:T(8,128)(2,1)S(1)} %collective-permute-done.1.refs_2_), channel_id=1, source_target_pairs={{0,1},{1,0},{2,3},{3,2},{4,5},{5,4},{6,7},{7,6},{8,9},{9,8},{10,11... | collective-permute-start | bytes 589832 | tf_op jit(solution)/shard_map/ppermute | solution.py:34
  37.2 7.3 %collective-permute-start.7 = (bf16[256,384]{1,0:T(8,128)(2,1)S(1)}, bf16[256,384]{1,0:T(8,128)(2,1)S(1)}, u32[]{:S(2)}, u32[]{:S(2)}) collective-permute-start(bf16[256,384]{1,0:T(8,128)(2,1)S(1)} %get-tuple-element.45), channel_id=1, source_target_pairs={{0,2},{2,0},{1,3},{3,1},{4,6},{6,4},{5,7},{7,5},{8,10},{10,8},{9,1... | collective-permute-start | bytes 589832 | tf_op jit(solution)/shard_map/ppermute | solution.py:34
  39.0 1.9 %collective-permute-start.10 = (bf16[3,96,256]{2,1,0:T(8,128)(2,1)S(1)}, bf16[3,96,256]{2,1,0:T(8,128)(2,1)S(1)}, u32[]{:S(2)}, u32[]{:S(2)}) collective-permute-start(bf16[3,96,256]{2,1,0:T(8,128)(2,1)S(1)} %get-tuple-element.52), channel_id=1, source_target_pairs={{0,1},{1,0},{2,3},{3,2},{4,5},{5,4},{6,7},{7,6},{8,9},{9,8},{10,11... | collective-permute-start | bytes 442376 | tf_op jit(solution)/shard_map/ppermute | solution.py:34
  39.3 1.7 %collective-permute-start.11 = (bf16[3,96,256]{2,1,0:T(8,128)(2,1)S(1)}, bf16[3,96,256]{2,1,0:T(8,128)(2,1)S(1)}, u32[]{:S(2)}, u32[]{:S(2)}) collective-permute-start(bf16[3,96,256]{2,1,0:T(8,128)(2,1)S(1)} %get-tuple-element.53), channel_id=1, source_target_pairs={{0,1},{1,0},{2,3},{3,2},{4,5},{5,4},{6,7},{7,6},{8,9},{9,8},{10,11... | collective-permute-start | bytes 442376 | tf_op jit(solution)/shard_map/ppermute | solution.py:34
  39.6 1.3 %collective-permute-start.12 = (bf16[2,96,256]{2,1,0:T(8,128)(2,1)S(1)}, bf16[2,96,256]{2,1,0:T(8,128)(2,1)S(1)}, u32[]{:S(2)}, u32[]{:S(2)}) collective-permute-start(bf16[2,96,256]{2,1,0:T(8,128)(2,1)S(1)} %get-tuple-element.54), channel_id=1, source_target_pairs={{0,1},{1,0},{2,3},{3,2},{4,5},{5,4},{6,7},{7,6},{8,9},{9,8},{10,11... | collective-permute-start | bytes 294920 | tf_op jit(solution)/shard_map/ppermute | solution.py:34
  45.1 11.7 %collective-permute-start.14 = (bf16[256,384]{1,0:T(8,128)(2,1)S(1)}, bf16[256,384]{1,0:T(8,128)(2,1)S(1)}, u32[]{:S(2)}, u32[]{:S(2)}) collective-permute-start(bf16[256,384]{1,0:T(8,128)(2,1)S(1)} %middle_grads.1.refs_1_.refs_3_), channel_id=1, source_target_pairs={{0,16},{4,20},{8,24},{12,28},{16,0},{20,4},{24,8},{28,12},{1,17},{... | collective-permute-start | bytes 589832 | tf_op jit(solution)/shard_map/ppermute | solution.py:551
  45.2 15.2 %collective-permute-start.18 = (bf16[2,96,768]{2,1,0:T(8,128)(2,1)S(1)}, bf16[2,96,768]{2,1,0:T(8,128)(2,1)S(1)}, u32[]{:S(2)}, u32[]{:S(2)}) collective-permute-start(bf16[2,96,768]{2,1,0:T(8,128)(2,1)S(1)} %get-tuple-element.57), channel_id=1, source_target_pairs={{0,8},{4,12},{8,0},{12,4},{16,24},{20,28},{24,16},{28,20},{1,9},{5... | collective-permute-start | bytes 884744 | tf_op jit(solution)/shard_map/ppermute | solution.py:34
  49.9 10.5 %collective-permute-start.19 = (bf16[2,96,768]{2,1,0:T(8,128)(2,1)S(1)}, bf16[2,96,768]{2,1,0:T(8,128)(2,1)S(1)}, u32[]{:S(2)}, u32[]{:S(2)}) collective-permute-start(bf16[2,96,768]{2,1,0:T(8,128)(2,1)S(1)} %get-tuple-element.58), channel_id=1, source_target_pairs={{0,4},{4,0},{8,12},{12,8},{16,20},{20,16},{24,28},{28,24},{1,5},{5... | collective-permute-start | bytes 884744 | tf_op jit(solution)/shard_map/ppermute | solution.py:34
  51.4 14.9 %collective-permute-start.20 = (bf16[2,96,768]{2,1,0:T(8,128)(2,1)S(1)}, bf16[2,96,768]{2,1,0:T(8,128)(2,1)S(1)}, u32[]{:S(2)}, u32[]{:S(2)}) collective-permute-start(bf16[2,96,768]{2,1,0:T(8,128)(2,1)S(1)} %get-tuple-element.59), channel_id=1, source_target_pairs={{0,12},{4,8},{8,4},{12,0},{16,28},{20,24},{24,20},{28,16},{1,13},{... | collective-permute-start | bytes 884744 | tf_op jit(solution)/shard_map/ppermute | solution.py:34
  51.4 5.4 %collective-permute-start.15 = (bf16[256,384]{1,0:T(8,128)(2,1)S(1)}, bf16[256,384]{1,0:T(8,128)(2,1)S(1)}, u32[]{:S(2)}, u32[]{:S(2)}) collective-permute-start(bf16[256,384]{1,0:T(8,128)(2,1)S(1)} %middle_grads.1.refs_1_.refs_3_), channel_id=1, source_target_pairs={{0,1},{1,0},{2,3},{3,2},{4,5},{5,4},{6,7},{7,6},{8,9},{9,8},{10,11... | collective-permute-start | bytes 589832 | tf_op jit(solution)/shard_map/ppermute | solution.py:34
  56.8 10.1 %collective-permute-start.17 = (bf16[256,384]{1,0:T(8,128)(2,1)S(1)}, bf16[256,384]{1,0:T(8,128)(2,1)S(1)}, u32[]{:S(2)}, u32[]{:S(2)}) collective-permute-start(bf16[256,384]{1,0:T(8,128)(2,1)S(1)} %collective-permute-done.14.refs_2_.refs_5_), channel_id=1, source_target_pairs={{0,1},{1,0},{2,3},{3,2},{4,5},{5,4},{6,7},{7,6},{8,9},{9,8},{10,11... | collective-permute-start | bytes 589832 | tf_op jit(solution)/shard_map/ppermute | solution.py:34
  58.4 34.1 %collective-permute-start.16 = (bf16[192,1536]{1,0:T(8,128)(2,1)S(1)}, bf16[192,1536]{1,0:T(8,128)(2,1)S(1)}, u32[]{:S(2)}, u32[]{:S(2)}) collective-permute-start(bf16[192,1536]{1,0:T(8,128)(2,1)S(1)} %act_rows.2.refs_5_.refs_1_), channel_id=1, source_target_pairs={{0,2},{2,0},{1,3},{3,1},{4,6},{6,4},{5,7},{7,5},{8,10},{10,8},{9,1... | collective-permute-start | bytes 1769480 | tf_op jit(solution)/shard_map/ppermute | solution.py:34
  68.5 10.0 %collective-permute-start.23 = (bf16[2,96,768]{2,1,0:T(8,128)(2,1)S(1)}, bf16[2,96,768]{2,1,0:T(8,128)(2,1)S(1)}, u32[]{:S(2)}, u32[]{:S(2)}) collective-permute-start(bf16[2,96,768]{2,1,0:T(8,128)(2,1)S(1)} %get-tuple-element.63), channel_id=1, source_target_pairs={{0,8},{4,12},{8,0},{12,4},{16,24},{20,28},{24,16},{28,20},{1,9},{5... | collective-permute-start | bytes 884744 | tf_op jit(solution)/shard_map/ppermute | solution.py:34
  68.6 14.0 %collective-permute-start.24 = (bf16[2,96,768]{2,1,0:T(8,128)(2,1)S(1)}, bf16[2,96,768]{2,1,0:T(8,128)(2,1)S(1)}, u32[]{:S(2)}, u32[]{:S(2)}) collective-permute-start(bf16[2,96,768]{2,1,0:T(8,128)(2,1)S(1)} %get-tuple-element.64), channel_id=1, source_target_pairs={{0,4},{4,0},{8,12},{12,8},{16,20},{20,16},{24,28},{28,24},{1,5},{5... | collective-permute-start | bytes 884744 | tf_op jit(solution)/shard_map/ppermute | solution.py:34
  69.2 13.5 %collective-permute-start.25 = (bf16[2,96,768]{2,1,0:T(8,128)(2,1)S(1)}, bf16[2,96,768]{2,1,0:T(8,128)(2,1)S(1)}, u32[]{:S(2)}, u32[]{:S(2)}) collective-permute-start(bf16[2,96,768]{2,1,0:T(8,128)(2,1)S(1)} %get-tuple-element.65), channel_id=1, source_target_pairs={{0,12},{4,8},{8,4},{12,0},{16,28},{20,24},{24,20},{28,16},{1,13},{... | collective-permute-start | bytes 884744 | tf_op jit(solution)/shard_map/ppermute | solution.py:34
  72.1 5.3 %collective-permute-start.22 = (bf16[2,96,384]{2,1,0:T(8,128)(2,1)S(1)}, bf16[2,96,384]{2,1,0:T(8,128)(2,1)S(1)}, u32[]{:S(2)}, u32[]{:S(2)}) collective-permute-start(bf16[2,96,384]{2,1,0:T(8,128)(2,1)S(1)} %get-tuple-element.62), channel_id=1, source_target_pairs={{0,2},{2,0},{1,3},{3,1},{4,6},{6,4},{5,7},{7,5},{8,10},{10,8},{9,1... | collective-permute-start | bytes 442376 | tf_op jit(solution)/shard_map/ppermute | solution.py:34
  83.3 10.8 %collective-permute-start.26 = (bf16[96,1152]{1,0:T(8,128)(2,1)S(1)}, bf16[96,1152]{1,0:T(8,128)(2,1)S(1)}, u32[]{:S(2)}, u32[]{:S(2)}) collective-permute-start(bf16[96,1152]{1,0:T(8,128)(2,1)S(1)} %get-tuple-element.67), channel_id=1, source_target_pairs={{0,16},{4,20},{8,24},{12,28},{16,0},{20,4},{24,8},{28,12},{1,17},{... | collective-permute-start | bytes 663560 | tf_op jit(solution)/shard_map/ppermute | solution.py:34
  86.8 5.7 %collective-permute-start.21 = (bf16[64,1536]{1,0:T(8,128)(2,1)S(1)}, bf16[64,1536]{1,0:T(8,128)(2,1)S(1)}, u32[]{:S(2)}, u32[]{:S(2)}) collective-permute-start(bf16[64,1536]{1,0:T(8,128)(2,1)S(1)} %act_rows.3.refs_7_.refs_3_), channel_id=1, source_target_pairs={{0,2},{2,0},{1,3},{3,1},{4,6},{6,4},{5,7},{7,5},{8,10},{10,8},{9,1... | collective-permute-start | bytes 589832 | tf_op jit(solution)/shard_map/ppermute | solution.py:34

commit v7 on v6

--- a/solution.py
+++ b/solution.py
@@ -272,16 +272,18 @@
     sent[...] = value.astype(BF16)
 
 
-def own_hidden(place, middle, feat, point, hidden, block, slope):
+def own_hidden(place, middle, feat, point, near, hidden, block, slope, slope_feat, *pieces):
     value = middle[...]
     hid = gelu_value(value).astype(BF16)
     hidden[...] = hid
-    block[...] = wide(feat) + dot(hid, point[...], NT)
+    rows = wide(feat)
+    block[...] = rows + dot(hid, point[...], NT)
     slope[...] = gelu_slope(value)
-
-
-def feature_slope(place, feat, slope):
-    slope[...] = gelu_slope(wide(feat))
+    slope_feat[...] = gelu_slope(rows)
+    first = 0
+    for piece in pieces:
+        piece[...] = near[first : first + piece.shape[0]]
+        first += piece.shape[0]
 
 
 def tracks(place, block, other_middle, near, far, cotangent, point, *rest):
@@ -359,15 +361,17 @@
             out[:, :, k * width : (k + 1) * width] = value.astype(out.dtype).reshape(shape)
 
 
-def point_products(
-    place, outs, hidden, other_hidden, far_hidden, far_other, *rest
+def early_products(
+    place, acts, other_acts, middle_grad, outs, hidden, other_hidden, far_hidden, far_other, *rest
 ):
-    *pieces, keep, along, across, both, other_outs = rest
+    *pieces, first, second, keep, along, across, both, other_outs, other_grad = rest
     joined(pieces, other_outs)
+    joined((first, second), other_grad)
 
     def values(left):
         own, other = left(outs), left(other_outs)
         return (
+            dot(left(acts), middle_grad[...], NN) + dot(left(other_acts), other_grad[...], NN),
             dot(own, hidden[...], NN) + dot(other, far_hidden[...], NN),
             dot(own, other_hidden[...], NN) + dot(other, far_other[...], NN),
         )
@@ -375,28 +379,16 @@
     each_chip(place, keep, along, across, both, values)
 
 
-def tap_products(
-    place, acts, other_acts, middle_grad, other_middle_grad, moved, other_moved,
-    keep, along, across, both,
-):
+def outer_products(place, acts, other_acts, moved, other_moved, keep, along, across, both):
     def values(left):
-        own, other = left(acts), left(other_acts)
-        return (
-            dot(own, middle_grad[...], NN) + dot(other, other_middle_grad[...], NN),
-            dot(own, moved[...], NN) + dot(other, other_moved[...], NN),
-        )
+        return (dot(left(acts), moved[...], NN) + dot(left(other_acts), other_moved[...], NN),)
 
     each_chip(place, keep, along, across, both, values)
 
 
-def act_part(first):
-    def act_rows(place, middle_grad, moved, weight, part, slope, give):
-        rows = slice(first, first + give.shape[0])
-        value = dot(middle_grad[rows, :], weight[1], NT)
-        value += dot(moved[rows, :], weight[place[0]], NT)
-        give[...] = (part[rows, :].astype(F32) + value * slope[rows, :]).astype(BF16)
-
-    return act_rows
+def act_part(place, middle_grad, moved, weight, part, slope, give):
+    value = dot(middle_grad[...], weight[1], NT) + dot(moved[...], weight[place[0]], NT)
+    give[...] = (wide(part) + value * slope[...]).astype(BF16)
 
 
 def over_chips(at, kept, *arrived):
@@ -406,37 +398,33 @@
     return total
 
 
-def point_sum(place, kept, along, across, both, keep, give):
-    width = keep.shape[2]
+def early_sum(place, kept, along, across, both, keep, give):
+    two = keep.shape[2]
     for at in range(2):
         total = over_chips(at, kept, along, across, both)
-        keep[at] = total[:, :width]
-        give[at] = total[:, width:].astype(BF16)
-
-
-def last_sum(place, point_kept, point_got, *refs):
+        keep[at] = total[:, :two]
+        give[at] = total[:, two:].astype(BF16)
+
+
+def last_sum(place, early, point_got, *refs):
     *parts, keep, give = refs
     top = place[TOP]
     width = parts[0].shape[2]
-    for columns, terms in (
-        (slice(0, width), parts),
-        (slice(width, None), (point_kept, point_got)),
-    ):
-        keep[:, columns] = over_chips(top, *terms)
-        give[:, columns] = over_chips(1 - top, *terms).astype(BF16)
-
-
-def finish(place, one, one_got, two, two_got, kept, got, dilated, point, result):
+    for at, out in ((top, keep), (1 - top, give)):
+        rest = early[at]
+        point = rest[:, width:] + point_got[at].astype(F32)
+        out[:, :width] = over_chips(at, *parts).astype(out.dtype)
+        out[:, width : 2 * width] = rest[:, :width].astype(out.dtype)
+        out[:, 2 * width :] = point.astype(out.dtype)
+
+
+def finish(place, own, theirs, kept, got, dilated, point, result):
     width = point.shape[1]
-    dilated[1] = kept[:, :width] + got[:, :width].astype(F32)
-    dilated[place[0]] = kept[:, width : 2 * width]
-    dilated[2 - place[0]] = got[:, width : 2 * width].astype(F32)
+    dilated[place[0]] = kept[:, :width]
+    dilated[2 - place[0]] = got[:, :width].astype(F32)
+    dilated[1] = kept[:, width : 2 * width] + got[:, width : 2 * width].astype(F32)
     point[...] = kept[:, 2 * width :] + got[:, 2 * width :].astype(F32)
-    first = 0
-    for own, theirs in ((one, one_got), (two, two_got)):
-        rows = slice(first, first + own.shape[0])
-        result[rows, :] = (wide(own) + wide(theirs)).astype(BF16)
-        first += own.shape[0]
+    result[...] = (wide(own) + wide(theirs)).astype(BF16)
 
 
 def body(features, dilated_weight, point_weight, track_weight, track_cotangent):
@@ -468,8 +456,6 @@
         spaces={1: pltpu.HBM},
     )
     near = flip(own_piece, "head")
-    cut = piece // 3
-    points = [near] + [flip(near[k : k + cut], "sample") for k in range(0, piece, cut)]
     far_track = flip(track_weight, "sample")
     acted, term = kernel_call(
         outer_term,
@@ -496,14 +482,19 @@
         add_terms, [((rows, width), F32), ((rows, width), BF16)], [place, middle, arrived], acts
     )
     other_middle = flip(middle_b, "head")
-    hidden, block_part, slope = kernel_call(
+    cut = piece // 3
+    hidden, block_part, slope, slope_feat, *pieces = kernel_call(
         own_hidden,
-        [((rows, width), BF16), ((rows, channels), F32), ((rows, width), F32)],
-        [place, middle, feat, point_weight],
-    )
-    (slope_feat,) = kernel_call(
-        feature_slope, [((rows, channels), F32)], [place, feat], block_part
-    )
+        [
+            ((rows, width), BF16),
+            ((rows, channels), F32),
+            ((rows, width), F32),
+            ((rows, channels), F32),
+        ]
+        + [((cut, width), BF16)] * (piece // cut),
+        [place, middle, feat, point_weight, near],
+    )
+    points = [near] + [flip(part, "sample") for part in pieces]
     part, other_hidden, grad_kept, grad_given = kernel_call(
         tracks,
         [((rows, channels), BF16), ((rows, width), BF16), ((rows, width), F32), ((rows, width), BF16)],
@@ -511,7 +502,6 @@
             place, block_part, other_middle, track_weight, far_track, cotangent, point_weight,
             *points,
         ],
-        slope_feat,
         scratch=[
             pltpu.VMEM((n_sample, rows, piece), BF16),
             pltpu.VMEM((rows, tracks_here), BF16),
@@ -537,48 +527,42 @@
         far_hidden,
         scratch=[pltpu.VMEM((groups, block, rows), BF16)],
     )
-    points = traded(
-        point_products,
-        2 * width,
-        [outs, hidden, other_hidden, far_hidden, far_other]
-        + [flip(piece, "sample") for piece in outs_given],
-        other_acts,
-        scratch=[pltpu.VMEM((groups, block, rows), BF16)],
-    )
     (middle_grad,) = kernel_call(
-        middle_grads, [((rows, width), BF16)], [place, grad_kept, grad_got, slope], points[0]
+        middle_grads, [((rows, width), BF16)], [place, grad_kept, grad_got, slope], outs
     )
     moved = lax.ppermute(middle_grad, "seq", pairs)
-    ins = [place, middle_grad, moved, taps, part, slope_feat]
-    other_grad = flip(middle_grad, "sample")
-    most = rows * 3 // 4
-    (one,) = kernel_call(act_part(0), [((most, channels), BF16)], ins, other_grad)
-    point_kept, point_give = kernel_call(
-        point_sum,
-        [((2, block, width), F32), ((2, block, width), BF16)],
-        [place, *points],
-        one,
+    early = traded(
+        early_products,
+        3 * width,
+        [acts, other_acts, middle_grad, outs, hidden, other_hidden, far_hidden, far_other]
+        + [flip(piece, "sample") for piece in outs_given]
+        + [flip(middle_grad[k : k + half], "sample") for k in (0, half)],
+        scratch=[pltpu.VMEM((groups, block, rows), BF16), pltpu.VMEM((rows, width), BF16)],
+    )
+    (own,) = kernel_call(
+        act_part,
+        [((rows, channels), BF16)],
+        [place, middle_grad, moved, taps, part, slope_feat],
+        early[0],
+    )
+    kept, point_give = kernel_call(
+        early_sum,
+        [((2, block, 2 * width), F32), ((2, block, width), BF16)],
+        [place, *early],
+        own,
     )
     steps = traded(
-        tap_products,
-        2 * width,
-        [acts, other_acts, middle_grad, other_grad, moved, flip(moved, "sample")],
-        point_kept,
-    )
-    (two,) = kernel_call(act_part(most), [((rows - most, channels), BF16)], ins, steps[0])
+        outer_products, width, [acts, other_acts, moved, flip(moved, "sample")], kept
+    )
     kept, give = kernel_call(
         last_sum,
         [((block, 3 * width), F32), ((block, 3 * width), BF16)],
-        [place, point_kept, flip(point_give, "head"), *steps],
-        two,
+        [place, kept, flip(point_give, "head"), *steps],
     )
     dilated_grad, point_grad, input_grad = kernel_call(
         finish,
         [((3, block, width), F32), ((block, width), F32), ((rows, channels), BF16)],
-        [
-            place, one, flip(one, "head"), two, flip(two, "head"), kept,
-            flip(give, "seq", n_seq // 2),
-        ],
+        [place, own, flip(own, "head"), kept, flip(give, "seq", n_seq // 2)],
     )
     dilated_grad = jnp.transpose(dilated_grad, (1, 0, 2))
     return (input_grad.reshape(samples, positions, channels), dilated_grad, point_grad)

time: 96.1 us -> 98.6 us (1.026)
  waiting for transfers between devices: 44.5 us -> 50.9 us
  Pallas kernels: 25.9 us -> 23.8 us
  starting transfers between devices: 24.4 us -> 22.7 us
    ppermute x25, waiting for transfers between devices: 30.7 us -> 41.2 us  [flip(): return lax.ppermute(value, axis, [(i, i ^ step) for i in range(count)])]
    ppermute x1, waiting for transfers between devices: 5.42 us -> 1.36 us  [body(): moved = lax.ppermute(middle_grad, 'seq', pairs)]
    pallas_call x16 -> x14, Pallas kernels: 25.9 us -> 23.8 us  [kernel_call(): pl.pallas_call(run, out_shape=[jax.ShapeDtypeStruct(s, d) for s, d in out...]
    ppermute x25, starting transfers between devices: 21.7 us -> 20 us  [flip(): return lax.ppermute(value, axis, [(i, i ^ step) for i in range(count)])]
  transfers between devices with their start and end apart: 27 -> 27, of which waited for: 12 -> 11; matrix products, arithmetic and copies ran while one was open for 0% -> 0% of each run, Pallas kernels for 25% -> 22%
where the time goes in v7:
time: 98.6 us; the launch traced here: 98.4 us
  waiting for transfers between devices  50.9 us (52%)
  Pallas kernels  23.8 us (24%)
  starting transfers between devices  22.7 us (23%)
    ppermute x25, waiting for transfers between devices, flip(): return lax.ppermute(value, axis, [(i, i ^ step) for i in range(count)])  41.2 us
    pallas_call x14, Pallas kernels, kernel_call(): pl.pallas_call(run, out_shape=[jax.ShapeDtypeStruct(s, d) for s, d in out...  23.8 us
    ppermute x25, starting transfers between devices, flip(): return lax.ppermute(value, axis, [(i, i ^ step) for i in range(count)])  20 us
    ppermute x1, waiting for transfers between devices, body(): arrived = lax.ppermute(term, 'seq', pairs)  8.38 us
    ppermute x1, starting transfers between devices, body(): arrived = lax.ppermute(term, 'seq', pairs)  2.65 us
  transfers between devices with their start and end apart: 27, of which 11 were waited for; matrix products, arithmetic and copies ran while one was open for 0% of the time, Pallas kernels for 22%

profile of v7, /device:TPU:0, one launch (start us, length us, event | category | flops | bytes accessed | tf_op | source)
XLA Modules:
  0.0 98.4 jit_solution(5703212298429478729)
XLA Ops:
  1.2 1.9 %piece_of.1.refs_3_ = bf16[768,384]{1,0:T(8,128)(2,1)S(1)} custom-call(s32[6]{0:T(128)S(1)} %stack.27.refs_0_, bf16[1536,384]{1,0:T(8,128)(2,1)} %refs_6_.1), custom_call_target="tpu_custom_call" | custom-call | flops 1 | bytes 1 | tf_op jit(solution)/shard_map/piece_of/pallas_call | solution.py:200
  3.1 2.6 %collective-permute-start.1 = (bf16[768,384]{1,0:T(8,128)(2,1)S(1)}, bf16[768,384]{1,0:T(8,128)(2,1)S(1)}, u32[]{:S(2)}, u32[]{:S(2)}) collective-permute-start(bf16[768,384]{1,0:T(8,128)(2,1)S(1)} %piece_of.1.refs_3_), channel_id=1, source_target_pairs={{0,2},{2,0},{1,3},{3,1},{4,6},{6,4},{5,7},{7,5},{8,10},{10,8},{9,1... | collective-permute-start | bytes 1769480 | tf_op jit(solution)/shard_map/ppermute | solution.py:34
  5.7 2.9 %outer_term.1 = (bf16[256,1536]{1,0:T(8,128)(2,1)S(1)}, bf16[256,384]{1,0:T(8,128)(2,1)S(1)}) custom-call(s32[6]{0:T(128)S(1)} %stack.27.refs_0_, bf16[256,1536]{1,0:T(8,128)(2,1)} %bitcast.14, bf16[3,1536,384]{2,1,0:T(8,128)(2,1)} %bitcast.11, bf16[768,384]{1,0:T(8,128)(2,1)S(1)} %piece_of.1.refs_3_), custom_call_target="tpu_custom_call" | custom-call | flops 1 | bytes 1 | tf_op jit(solution)/shard_map/outer_term/pallas_call | solution.py:200
  8.6 2.7 %collective-permute-start = (bf16[256,384]{1,0:T(8,128)(2,1)S(1)}, bf16[256,384]{1,0:T(8,128)(2,1)S(1)}, u32[]{:S(2)}, u32[]{:S(2)}) collective-permute-start(bf16[256,384]{1,0:T(8,128)(2,1)S(1)} %get-tuple-element.43), channel_id=1, source_target_pairs={{0,16},{4,20},{8,24},{12,28},{16,0},{20,4},{24,8},{28,12},{1,17},{... | collective-permute-start | bytes 589832 | tf_op jit(solution)/shard_map/ppermute | solution.py:472
  11.3 1.1 %middle_term.1 = (f32[256,384]{1,0:T(8,128)S(1)}, bf16[8,96,256]{2,1,0:T(8,128)(2,1)S(1)}, bf16[8,96,256]{2,1,0:T(8,128)(2,1)S(1)}) custom-call(s32[6]{0:T(128)S(1)} %stack.27.refs_0_, bf16[256,1536]{1,0:T(8,128)(2,1)S(1)} %get-tuple-element.41.refs_1_, bf16[3,1536,384]{2,1,0:T(8,128)(2,1)S(1)} %bitcast.12), custom_call_target="tpu_custom_call" | custom-call | flops 1 | bytes 1 | tf_op jit(solution)/shard_map/middle_term/pallas_call | solution.py:200
  12.4 8.4 %collective-permute-done.refs_2_ = bf16[256,384]{1,0:T(8,128)(2,1)S(1)} collective-permute-done((bf16[256,384]{1,0:T(8,128)(2,1)S(1)}, bf16[256,384]{1,0:T(8,128)(2,1)S(1)}, u32[]{:S(2)}, u32[]{:S(2)}) %collective-permute-start) | collective-permute-done | bytes 196640 | tf_op jit(solution)/shard_map/ppermute | solution.py:472
  20.8 0.6 add_terms.1
  22.0 1.9 %own_hidden.1 = (bf16[256,384]{1,0:T(8,128)(2,1)S(1)}, f32[256,1536]{1,0:T(8,128)S(1)}, f32[256,384]{1,0:T(8,128)S(1)}, f32[256,1536]{1,0:T(8,128)S(1)}, bf16[25...) custom-call(s32[6]{0:T(128)S(1)} %stack.27.refs_0_, ...), custom_call_target="tpu_custom_call" | custom-call | flops 1 | bytes 1 | tf_op jit(solution)/shard_map/own_hidden/pallas_call | solution.py:200
  24.6 3.1 %collective-permute-done.2.refs_2_ = bf16[256,384]{1,0:T(8,128)(2,1)S(1)} collective-permute-done((bf16[256,384]{1,0:T(8,128)(2,1)S(1)}, bf16[256,384]{1,0:T(8,128)(2,1)S(1)}, u32[]{:S(2)}, u32[]{:S(2)}) %collective-permute-start.2) | collective-permute-done | bytes 196640 | tf_op jit(solution)/shard_map/ppermute | solution.py:34
  28.2 6.1 %tracks.1 = (bf16[256,1536]{1,0:T(8,128)(2,1)S(1)}, bf16[256,384]{1,0:T(8,128)(2,1)S(1)}, f32[256,384]{1,0:T(8,128)S(1)}, bf16[256,384]{1,0:T(8,128)(2,1)S(1)}) custom-call(s32[6]{0:T(128)S(1)} %stack.27.refs_0_, f32[256,1536]{1,0:T(8,128)S(1)} %get-tuple-element.46.refs_1_, bf16[256,384]{1,0:T(8,128)(2,1)S(1)} %collective-permute-done.2.refs_2_, ...), custom_call_target="tpu_custom_call" | custom-call | flops 1 | bytes 1 | tf_op jit(solution)/shard_map/tracks/pallas_call | solution.py:200
  34.3 0.9 collective-permute-start.7
  35.2 1.0 turn_parts.1
  37.2 4.0 %collective-permute-done.7.refs_2_ = bf16[256,384]{1,0:T(8,128)(2,1)S(1)} collective-permute-done((bf16[256,384]{1,0:T(8,128)(2,1)S(1)}, bf16[256,384]{1,0:T(8,128)(2,1)S(1)}, u32[]{:S(2)}, u32[]{:S(2)}) %collective-permute-start.7) | collective-permute-done | bytes 196640 | tf_op jit(solution)/shard_map/ppermute | solution.py:34
  42.5 0.8 collective-permute-done.15.refs_12_
  43.4 1.9 %early_products.1 = (f32[2,96,1152]{2,1,0:T(8,128)S(1)}, bf16[2,96,1152]{2,1,0:T(8,128)(2,1)S(1)}, bf16[2,96,1152]{2,1,0:T(8,128)(2,1)S(1)}, bf16[2,96,1152]{2,1,0:T(8,128)(2,1)S(1)}) custom-call(s32[6]{0:T(128)S(1)} %stack.27.refs_0_, bf16[8,96,256]{2,1,0:T(8,128)(2,1)S(1)} %get-tuple-element.44.refs_3_.refs_1_, ...), custom_call_target="tpu_custom_call" | custom-call | flops 1 | bytes 1 | tf_op jit(solution)/shard_map/early_products/pallas_call | solution.py:200
  45.4 4.8 %collective-permute-start.18 = (bf16[2,96,1152]{2,1,0:T(8,128)(2,1)S(1)}, bf16[2,96,1152]{2,1,0:T(8,128)(2,1)S(1)}, u32[]{:S(2)}, u32[]{:S(2)}) collective-permute-start(bf16[2,96,1152]{2,1,0:T(8,128)(2,1)S(1)} %get-tuple-element.65), channel_id=1, source_target_pairs={{0,8},{4,12},{8,0},{12,4},{16,24},{20,28},{24,16},{28,20},{1,9},{5... | collective-permute-start | bytes 1327112 | tf_op jit(solution)/shard_map/ppermute | solution.py:34
  50.1 1.5 %collective-permute-start.19 = (bf16[2,96,1152]{2,1,0:T(8,128)(2,1)S(1)}, bf16[2,96,1152]{2,1,0:T(8,128)(2,1)S(1)}, u32[]{:S(2)}, u32[]{:S(2)}) collective-permute-start(bf16[2,96,1152]{2,1,0:T(8,128)(2,1)S(1)} %get-tuple-element.66), channel_id=1, source_target_pairs={{0,4},{4,0},{8,12},{12,8},{16,20},{20,16},{24,28},{28,24},{1,5},{5... | collective-permute-start | bytes 1327112 | tf_op jit(solution)/shard_map/ppermute | solution.py:34
  51.7 1.4 %collective-permute-done.10.refs_2_.refs_3_ = bf16[256,384]{1,0:T(8,128)(2,1)S(1)} collective-permute-done((bf16[256,384]{1,0:T(8,128)(2,1)S(1)}, bf16[256,384]{1,0:T(8,128)(2,1)S(1)}, u32[]{:S(2)}, u32[]{:S(2)}) %collective-permute-start.10) | collective-permute-done | bytes 196640 | tf_op jit(solution)/shard_map/ppermute | solution.py:533
  53.0 1.6 %act_part.1.refs_5_.refs_1_ = bf16[256,1536]{1,0:T(8,128)(2,1)S(1)} custom-call(s32[6]{0:T(128)S(1)} %stack.27.refs_0_, bf16[256,384]{1,0:T(8,128)(2,1)S(1)} %middle_grads.1.refs_3_.refs_1_, bf16[256,384]{1,0:T(8,128)(2,1)S(1)} %collective-permute-done.10.refs_2_.refs_3_, bf16[3,1536,384]{2,1,0:T(8,128)(2,1)S(1)} %bitcast.13, ...), custom_call_target="tpu_custom_call" | custom-call | flops 1 | bytes 1 | tf_op jit(solution)/shard_map/act_part/pallas_call | solution.py:200
  54.6 0.9 collective-permute-start.17
  55.5 7.0 %collective-permute-done.18.refs_2_ = bf16[2,96,1152]{2,1,0:T(8,128)(2,1)S(1)} collective-permute-done((bf16[2,96,1152]{2,1,0:T(8,128)(2,1)S(1)}, bf16[2,96,1152]{2,1,0:T(8,128)(2,1)S(1)}, u32[]{:S(2)}, u32[]{:S(2)}) %collective-permute-start.18) | collective-permute-done | bytes 442400 | tf_op jit(solution)/shard_map/ppermute | solution.py:34
  62.4 10.4 %collective-permute-done.20.refs_4_ = bf16[2,96,1152]{2,1,0:T(8,128)(2,1)S(1)} collective-permute-done((bf16[2,96,1152]{2,1,0:T(8,128)(2,1)S(1)}, bf16[2,96,1152]{2,1,0:T(8,128)(2,1)S(1)}, u32[]{:S(2)}, u32[]{:S(2)}) %collective-permute-start.20) | collective-permute-done | bytes 442400 | tf_op jit(solution)/shard_map/ppermute | solution.py:34
  72.8 0.7 early_sum.1
  73.6 1.1 %outer_products.1 = (f32[2,96,384]{2,1,0:T(8,128)S(1)}, bf16[2,96,384]{2,1,0:T(8,128)(2,1)S(1)}, bf16[2,96,384]{2,1,0:T(8,128)(2,1)S(1)}, bf16[2,96,384]{2,1,0:T(8,128)(2,1)S(1)}) custom-call(s32[6]{0:T(128)S(1)} %stack.27.refs_0_, bf16[8,96,256]{2,1,0:T(8,128)(2,1)S(1)} %get-tuple-element.44.refs_3_.refs_1_, ...), custom_call_target="tpu_custom_call" | custom-call | flops 1 | bytes 1 | tf_op jit(solution)/shard_map/outer_products/pallas_call | solution.py:200
  74.9 0.6 collective-permute-start.24
  75.6 2.7 %collective-permute-start.25 = (bf16[2,96,384]{2,1,0:T(8,128)(2,1)S(1)}, bf16[2,96,384]{2,1,0:T(8,128)(2,1)S(1)}, u32[]{:S(2)}, u32[]{:S(2)}) collective-permute-start(bf16[2,96,384]{2,1,0:T(8,128)(2,1)S(1)} %get-tuple-element.73), channel_id=1, source_target_pairs={{0,12},{4,8},{8,4},{12,0},{16,28},{20,24},{24,20},{28,16},{1,13},{... | collective-permute-start | bytes 442376 | tf_op jit(solution)/shard_map/ppermute | solution.py:34
  78.8 2.7 %collective-permute-done.23.refs_4_ = bf16[2,96,384]{2,1,0:T(8,128)(2,1)S(1)} collective-permute-done((bf16[2,96,384]{2,1,0:T(8,128)(2,1)S(1)}, bf16[2,96,384]{2,1,0:T(8,128)(2,1)S(1)}, u32[]{:S(2)}, u32[]{:S(2)}) %collective-permute-start.23) | collective-permute-done | bytes 147488 | tf_op jit(solution)/shard_map/ppermute | solution.py:34
  81.5 2.4 %collective-permute-done.24.refs_5_ = bf16[2,96,384]{2,1,0:T(8,128)(2,1)S(1)} collective-permute-done((bf16[2,96,384]{2,1,0:T(8,128)(2,1)S(1)}, bf16[2,96,384]{2,1,0:T(8,128)(2,1)S(1)}, u32[]{:S(2)}, u32[]{:S(2)}) %collective-permute-start.24) | collective-permute-done | bytes 147488 | tf_op jit(solution)/shard_map/ppermute | solution.py:34
  83.8 0.7 last_sum.1
  84.5 1.4 %collective-permute-start.26 = (bf16[96,1152]{1,0:T(8,128)(2,1)S(1)}, bf16[96,1152]{1,0:T(8,128)(2,1)S(1)}, u32[]{:S(2)}, u32[]{:S(2)}) collective-permute-start(bf16[96,1152]{1,0:T(8,128)(2,1)S(1)} %get-tuple-element.75), channel_id=1, source_target_pairs={{0,16},{4,20},{8,24},{12,28},{16,0},{20,4},{24,8},{28,12},{1,17},{... | collective-permute-start | bytes 663560 | tf_op jit(solution)/shard_map/ppermute | solution.py:34
  85.9 10.7 %collective-permute-done.26.refs_4_ = bf16[96,1152]{1,0:T(8,128)(2,1)S(1)} collective-permute-done((bf16[96,1152]{1,0:T(8,128)(2,1)S(1)}, bf16[96,1152]{1,0:T(8,128)(2,1)S(1)}, u32[]{:S(2)}, u32[]{:S(2)}) %collective-permute-start.26) | collective-permute-done | bytes 221216 | tf_op jit(solution)/shard_map/ppermute | solution.py:34
  96.7 1.8 %finish.1 = (f32[3,96,384]{2,1,0:T(8,128)}, f32[96,384]{1,0:T(8,128)}, bf16[256,1536]{1,0:T(8,128)(2,1)}) custom-call(s32[6]{0:T(128)S(1)} %stack.27.refs_0_, bf16[256,1536]{1,0:T(8,128)(2,1)S(1)} %act_part.1.refs_5_.refs_1_, bf16[256,1536]{1,0:T(8,128)(2,1)S(1)} %collective-permute-done.17.refs_2_, f32[96,1152]{1,0:T(8,128)S(1)} %get-tuple-element.74.refs_3_, ...), custom_call_target="tpu_custom_call" | custom-call | flops 1 | bytes 1 | tf_op jit(solution)/shard_map/finish/pallas_call | solution.py:200
  (48 shorter events, 5.6 us)
Async XLA Ops:
  0.6 27.6 %collective-permute-start.3 = (bf16[768,1920]{1,0:T(8,128)(2,1)}, bf16[768,1920]{1,0:T(8,128)(2,1)S(1)}, u32[]{:S(2)}, u32[]{:S(2)}) collective-permute-start(bf16[768,1920]{1,0:T(8,128)(2,1)} %refs_3_.3), channel_id=1, source_target_pairs={{0,1},{1,0},{2,3},{3,2},{4,5},{5,4},{6,7},{7,6},{8,9},{9,8},{10,11... | collective-permute-start | bytes 8847368 | tf_op jit(solution)/shard_map/ppermute | solution.py:34
  1.2 10.0 %copy-start = (bf16[1536,3,384]{2,0,1:T(8,128)(2,1)S(1)}, bf16[1536,3,384]{2,0,1:T(8,128)(2,1)}, u32[]{:S(2)}) copy-start(bf16[1536,3,384]{2,0,1:T(8,128)(2,1)} %param.6) | copy-start | bytes 10616836
  3.1 18.8 %collective-permute-start.1 = (bf16[768,384]{1,0:T(8,128)(2,1)S(1)}, bf16[768,384]{1,0:T(8,128)(2,1)S(1)}, u32[]{:S(2)}, u32[]{:S(2)}) collective-permute-start(bf16[768,384]{1,0:T(8,128)(2,1)S(1)} %piece_of.1.refs_3_), channel_id=1, source_target_pairs={{0,2},{2,0},{1,3},{3,1},{4,6},{6,4},{5,7},{7,5},{8,10},{10,8},{9,1... | collective-permute-start | bytes 1769480 | tf_op jit(solution)/shard_map/ppermute | solution.py:34
  8.6 13.4 %copy-start.1 = (bf16[1536,384]{1,0:T(8,128)(2,1)S(1)}, bf16[1536,384]{1,0:T(8,128)(2,1)}, u32[]{:S(2)}) copy-start(bf16[1536,384]{1,0:T(8,128)(2,1)} %refs_6_.1) | copy-start | bytes 3538948
  8.6 13.4 %copy-start.2 = (bf16[1,256,1536]{2,1,0:T(8,128)(2,1)S(1)}, bf16[1,256,1536]{2,1,0:T(8,128)(2,1)}, u32[]{:S(2)}) copy-start(bf16[1,256,1536]{2,1,0:T(8,128)(2,1)} %param.5) | copy-start | bytes 2359300
  8.6 12.2 %collective-permute-start = (bf16[256,384]{1,0:T(8,128)(2,1)S(1)}, bf16[256,384]{1,0:T(8,128)(2,1)S(1)}, u32[]{:S(2)}, u32[]{:S(2)}) collective-permute-start(bf16[256,384]{1,0:T(8,128)(2,1)S(1)} %get-tuple-element.43), channel_id=1, source_target_pairs={{0,16},{4,20},{8,24},{12,28},{16,0},{20,4},{24,8},{28,12},{1,17},{... | collective-permute-start | bytes 589832 | tf_op jit(solution)/shard_map/ppermute | solution.py:472
  12.4 15.8 %copy-start.3 = (bf16[768,1920]{1,0:T(8,128)(2,1)S(1)}, bf16[768,1920]{1,0:T(8,128)(2,1)}, u32[]{:S(2)}) copy-start(bf16[768,1920]{1,0:T(8,128)(2,1)} %refs_3_.3) | copy-start | bytes 8847364
  12.4 15.8 %copy-start.4 = (bf16[1,256,1920]{2,1,0:T(8,128)(2,1)S(1)}, bf16[1,256,1920]{2,1,0:T(8,128)(2,1)}, u32[]{:S(2)}) copy-start(bf16[1,256,1920]{2,1,0:T(8,128)(2,1)} %param.9) | copy-start | bytes 2949124
  21.4 6.2 %collective-permute-start.2 = (bf16[256,384]{1,0:T(8,128)(2,1)S(1)}, bf16[256,384]{1,0:T(8,128)(2,1)S(1)}, u32[]{:S(2)}, u32[]{:S(2)}) collective-permute-start(bf16[256,384]{1,0:T(8,128)(2,1)S(1)} %get-tuple-element.47), channel_id=1, source_target_pairs={{0,2},{2,0},{1,3},{3,1},{4,6},{6,4},{5,7},{7,5},{8,10},{10,8},{9,1... | collective-permute-start | bytes 589832 | tf_op jit(solution)/shard_map/ppermute | solution.py:34
  23.9 3.8 %collective-permute-start.4 = (bf16[256,384]{1,0:T(8,128)(2,1)S(1)}, bf16[256,384]{1,0:T(8,128)(2,1)S(1)}, u32[]{:S(2)}, u32[]{:S(2)}) collective-permute-start(bf16[256,384]{1,0:T(8,128)(2,1)S(1)} %get-tuple-element.48), channel_id=1, source_target_pairs={{0,1},{1,0},{2,3},{3,2},{4,5},{5,4},{6,7},{7,6},{8,9},{9,8},{10,11... | collective-permute-start | bytes 589832 | tf_op jit(solution)/shard_map/ppermute | solution.py:34
  24.0 4.2 %collective-permute-start.5 = (bf16[256,384]{1,0:T(8,128)(2,1)S(1)}, bf16[256,384]{1,0:T(8,128)(2,1)S(1)}, u32[]{:S(2)}, u32[]{:S(2)}) collective-permute-start(bf16[256,384]{1,0:T(8,128)(2,1)S(1)} %get-tuple-element.49), channel_id=1, source_target_pairs={{0,1},{1,0},{2,3},{3,2},{4,5},{5,4},{6,7},{7,6},{8,9},{9,8},{10,11... | collective-permute-start | bytes 589832 | tf_op jit(solution)/shard_map/ppermute | solution.py:34
  24.5 3.7 %collective-permute-start.6 = (bf16[256,384]{1,0:T(8,128)(2,1)S(1)}, bf16[256,384]{1,0:T(8,128)(2,1)S(1)}, u32[]{:S(2)}, u32[]{:S(2)}) collective-permute-start(bf16[256,384]{1,0:T(8,128)(2,1)S(1)} %get-tuple-element.50), channel_id=1, source_target_pairs={{0,1},{1,0},{2,3},{3,2},{4,5},{5,4},{6,7},{7,6},{8,9},{9,8},{10,11... | collective-permute-start | bytes 589832 | tf_op jit(solution)/shard_map/ppermute | solution.py:34
  27.7 7.5 %collective-permute-start.8 = (bf16[256,384]{1,0:T(8,128)(2,1)S(1)}, bf16[256,384]{1,0:T(8,128)(2,1)S(1)}, u32[]{:S(2)}, u32[]{:S(2)}) collective-permute-start(bf16[256,384]{1,0:T(8,128)(2,1)S(1)} %collective-permute-done.2.refs_2_), channel_id=1, source_target_pairs={{0,1},{1,0},{2,3},{3,2},{4,5},{5,4},{6,7},{7,6},{8,9},{9,8},{10,11... | collective-permute-start | bytes 589832 | tf_op jit(solution)/shard_map/ppermute | solution.py:34
  27.7 7.5 %collective-permute-start.9 = (bf16[256,384]{1,0:T(8,128)(2,1)S(1)}, bf16[256,384]{1,0:T(8,128)(2,1)S(1)}, u32[]{:S(2)}, u32[]{:S(2)}) collective-permute-start(bf16[256,384]{1,0:T(8,128)(2,1)S(1)} %get-tuple-element.55.refs_5_), channel_id=1, source_target_pairs={{0,1},{1,0},{2,3},{3,2},{4,5},{5,4},{6,7},{7,6},{8,9},{9,8},{10,11... | collective-permute-start | bytes 589832 | tf_op jit(solution)/shard_map/ppermute | solution.py:34
  34.3 6.9 %collective-permute-start.7 = (bf16[256,384]{1,0:T(8,128)(2,1)S(1)}, bf16[256,384]{1,0:T(8,128)(2,1)S(1)}, u32[]{:S(2)}, u32[]{:S(2)}) collective-permute-start(bf16[256,384]{1,0:T(8,128)(2,1)S(1)} %get-tuple-element.52), channel_id=1, source_target_pairs={{0,2},{2,0},{1,3},{3,1},{4,6},{6,4},{5,7},{7,5},{8,10},{10,8},{9,1... | collective-permute-start | bytes 589832 | tf_op jit(solution)/shard_map/ppermute | solution.py:34
  35.1 6.7 %collective-permute-start.11 = (bf16[8,96,256]{2,1,0:T(8,128)(2,1)S(1)}, bf16[8,96,256]{2,1,0:T(8,128)(2,1)S(1)}, u32[]{:S(2)}, u32[]{:S(2)}) collective-permute-start(bf16[8,96,256]{2,1,0:T(8,128)(2,1)S(1)} %get-tuple-element.58), channel_id=1, source_target_pairs={{0,1},{1,0},{2,3},{3,2},{4,5},{5,4},{6,7},{7,6},{8,9},{9,8},{10,11... | collective-permute-start | bytes 1179656 | tf_op jit(solution)/shard_map/ppermute | solution.py:34
  36.1 6.3 %collective-permute-start.12 = (bf16[3,96,256]{2,1,0:T(8,128)(2,1)S(1)}, bf16[3,96,256]{2,1,0:T(8,128)(2,1)S(1)}, u32[]{:S(2)}, u32[]{:S(2)}) collective-permute-start(bf16[3,96,256]{2,1,0:T(8,128)(2,1)S(1)} %get-tuple-element.61), channel_id=1, source_target_pairs={{0,1},{1,0},{2,3},{3,2},{4,5},{5,4},{6,7},{7,6},{8,9},{9,8},{10,11... | collective-permute-start | bytes 442376 | tf_op jit(solution)/shard_map/ppermute | solution.py:34
  36.7 5.8 %collective-permute-start.13 = (bf16[3,96,256]{2,1,0:T(8,128)(2,1)S(1)}, bf16[3,96,256]{2,1,0:T(8,128)(2,1)S(1)}, u32[]{:S(2)}, u32[]{:S(2)}) collective-permute-start(bf16[3,96,256]{2,1,0:T(8,128)(2,1)S(1)} %get-tuple-element.62), channel_id=1, source_target_pairs={{0,1},{1,0},{2,3},{3,2},{4,5},{5,4},{6,7},{7,6},{8,9},{9,8},{10,11... | collective-permute-start | bytes 442376 | tf_op jit(solution)/shard_map/ppermute | solution.py:34
  36.8 5.2 %collective-permute-start.14 = (bf16[2,96,256]{2,1,0:T(8,128)(2,1)S(1)}, bf16[2,96,256]{2,1,0:T(8,128)(2,1)S(1)}, u32[]{:S(2)}, u32[]{:S(2)}) collective-permute-start(bf16[2,96,256]{2,1,0:T(8,128)(2,1)S(1)} %get-tuple-element.63), channel_id=1, source_target_pairs={{0,1},{1,0},{2,3},{3,2},{4,5},{5,4},{6,7},{7,6},{8,9},{9,8},{10,11... | collective-permute-start | bytes 294920 | tf_op jit(solution)/shard_map/ppermute | solution.py:34
  41.8 11.3 %collective-permute-start.10 = (bf16[256,384]{1,0:T(8,128)(2,1)S(1)}, bf16[256,384]{1,0:T(8,128)(2,1)S(1)}, u32[]{:S(2)}, u32[]{:S(2)}) collective-permute-start(bf16[256,384]{1,0:T(8,128)(2,1)S(1)} %middle_grads.1.refs_3_.refs_1_), channel_id=1, source_target_pairs={{0,16},{4,20},{8,24},{12,28},{16,0},{20,4},{24,8},{28,12},{1,17},{... | collective-permute-start | bytes 589832 | tf_op jit(solution)/shard_map/ppermute | solution.py:533
  41.9 1.4 %collective-permute-start.15 = (bf16[128,384]{1,0:T(8,128)(2,1)S(1)}, bf16[128,384]{1,0:T(8,128)(2,1)S(1)}, u32[]{:S(2)}, u32[]{:S(2)}) collective-permute-start(bf16[128,384]{1,0:T(8,128)(2,1)S(1)} %get-tuple-element.80), channel_id=1, source_target_pairs={{0,1},{1,0},{2,3},{3,2},{4,5},{5,4},{6,7},{7,6},{8,9},{9,8},{10,11... | collective-permute-start | bytes 294920 | tf_op jit(solution)/shard_map/ppermute | solution.py:34
  42.0 1.4 %collective-permute-start.16 = (bf16[128,384]{1,0:T(8,128)(2,1)S(1)}, bf16[128,384]{1,0:T(8,128)(2,1)S(1)}, u32[]{:S(2)}, u32[]{:S(2)}) collective-permute-start(bf16[128,384]{1,0:T(8,128)(2,1)S(1)} %get-tuple-element.79), channel_id=1, source_target_pairs={{0,1},{1,0},{2,3},{3,2},{4,5},{5,4},{6,7},{7,6},{8,9},{9,8},{10,11... | collective-permute-start | bytes 294920 | tf_op jit(solution)/shard_map/ppermute | solution.py:34
  45.4 17.1 %collective-permute-start.18 = (bf16[2,96,1152]{2,1,0:T(8,128)(2,1)S(1)}, bf16[2,96,1152]{2,1,0:T(8,128)(2,1)S(1)}, u32[]{:S(2)}, u32[]{:S(2)}) collective-permute-start(bf16[2,96,1152]{2,1,0:T(8,128)(2,1)S(1)} %get-tuple-element.65), channel_id=1, source_target_pairs={{0,8},{4,12},{8,0},{12,4},{16,24},{20,28},{24,16},{28,20},{1,9},{5... | collective-permute-start | bytes 1327112 | tf_op jit(solution)/shard_map/ppermute | solution.py:34
  50.1 12.3 %collective-permute-start.19 = (bf16[2,96,1152]{2,1,0:T(8,128)(2,1)S(1)}, bf16[2,96,1152]{2,1,0:T(8,128)(2,1)S(1)}, u32[]{:S(2)}, u32[]{:S(2)}) collective-permute-start(bf16[2,96,1152]{2,1,0:T(8,128)(2,1)S(1)} %get-tuple-element.66), channel_id=1, source_target_pairs={{0,4},{4,0},{8,12},{12,8},{16,20},{20,16},{24,28},{28,24},{1,5},{5... | collective-permute-start | bytes 1327112 | tf_op jit(solution)/shard_map/ppermute | solution.py:34
  51.6 21.2 %collective-permute-start.20 = (bf16[2,96,1152]{2,1,0:T(8,128)(2,1)S(1)}, bf16[2,96,1152]{2,1,0:T(8,128)(2,1)S(1)}, u32[]{:S(2)}, u32[]{:S(2)}) collective-permute-start(bf16[2,96,1152]{2,1,0:T(8,128)(2,1)S(1)} %get-tuple-element.67), channel_id=1, source_target_pairs={{0,12},{4,8},{8,4},{12,0},{16,28},{20,24},{24,20},{28,16},{1,13},{... | collective-permute-start | bytes 1327112 | tf_op jit(solution)/shard_map/ppermute | solution.py:34
  54.6 42.1 %collective-permute-start.17 = (bf16[256,1536]{1,0:T(8,128)(2,1)S(1)}, bf16[256,1536]{1,0:T(8,128)(2,1)S(1)}, u32[]{:S(2)}, u32[]{:S(2)}) collective-permute-start(bf16[256,1536]{1,0:T(8,128)(2,1)S(1)} %act_part.1.refs_5_.refs_1_), channel_id=1, source_target_pairs={{0,2},{2,0},{1,3},{3,1},{4,6},{6,4},{5,7},{7,5},{8,10},{10,8},{9,1... | collective-permute-start | bytes 2359304 | tf_op jit(solution)/shard_map/ppermute | solution.py:34
  55.5 18.1 %collective-permute-start.22 = (bf16[256,384]{1,0:T(8,128)(2,1)S(1)}, bf16[256,384]{1,0:T(8,128)(2,1)S(1)}, u32[]{:S(2)}, u32[]{:S(2)}) collective-permute-start(bf16[256,384]{1,0:T(8,128)(2,1)S(1)} %collective-permute-done.10.refs_2_.refs_3_), channel_id=1, source_target_pairs={{0,1},{1,0},{2,3},{3,2},{4,5},{5,4},{6,7},{7,6},{8,9},{9,8},{10,11... | collective-permute-start | bytes 589832 | tf_op jit(solution)/shard_map/ppermute | solution.py:34
  74.7 6.8 %collective-permute-start.23 = (bf16[2,96,384]{2,1,0:T(8,128)(2,1)S(1)}, bf16[2,96,384]{2,1,0:T(8,128)(2,1)S(1)}, u32[]{:S(2)}, u32[]{:S(2)}) collective-permute-start(bf16[2,96,384]{2,1,0:T(8,128)(2,1)S(1)} %get-tuple-element.71), channel_id=1, source_target_pairs={{0,8},{4,12},{8,0},{12,4},{16,24},{20,28},{24,16},{28,20},{1,9},{5... | collective-permute-start | bytes 442376 | tf_op jit(solution)/shard_map/ppermute | solution.py:34
  74.9 8.9 %collective-permute-start.24 = (bf16[2,96,384]{2,1,0:T(8,128)(2,1)S(1)}, bf16[2,96,384]{2,1,0:T(8,128)(2,1)S(1)}, u32[]{:S(2)}, u32[]{:S(2)}) collective-permute-start(bf16[2,96,384]{2,1,0:T(8,128)(2,1)S(1)} %get-tuple-element.72), channel_id=1, source_target_pairs={{0,4},{4,0},{8,12},{12,8},{16,20},{20,16},{24,28},{28,24},{1,5},{5... | collective-permute-start | bytes 442376 | tf_op jit(solution)/shard_map/ppermute | solution.py:34
  75.6 8.3 %collective-permute-start.25 = (bf16[2,96,384]{2,1,0:T(8,128)(2,1)S(1)}, bf16[2,96,384]{2,1,0:T(8,128)(2,1)S(1)}, u32[]{:S(2)}, u32[]{:S(2)}) collective-permute-start(bf16[2,96,384]{2,1,0:T(8,128)(2,1)S(1)} %get-tuple-element.73), channel_id=1, source_target_pairs={{0,12},{4,8},{8,4},{12,0},{16,28},{20,24},{24,20},{28,16},{1,13},{... | collective-permute-start | bytes 442376 | tf_op jit(solution)/shard_map/ppermute | solution.py:34
  78.3 5.6 %collective-permute-start.21 = (bf16[2,96,384]{2,1,0:T(8,128)(2,1)S(1)}, bf16[2,96,384]{2,1,0:T(8,128)(2,1)S(1)}, u32[]{:S(2)}, u32[]{:S(2)}) collective-permute-start(bf16[2,96,384]{2,1,0:T(8,128)(2,1)S(1)} %get-tuple-element.69), channel_id=1, source_target_pairs={{0,2},{2,0},{1,3},{3,1},{4,6},{6,4},{5,7},{7,5},{8,10},{10,8},{9,1... | collective-permute-start | bytes 442376 | tf_op jit(solution)/shard_map/ppermute | solution.py:34
  84.5 12.2 %collective-permute-start.26 = (bf16[96,1152]{1,0:T(8,128)(2,1)S(1)}, bf16[96,1152]{1,0:T(8,128)(2,1)S(1)}, u32[]{:S(2)}, u32[]{:S(2)}) collective-permute-start(bf16[96,1152]{1,0:T(8,128)(2,1)S(1)} %get-tuple-element.75), channel_id=1, source_target_pairs={{0,16},{4,20},{8,24},{12,28},{16,0},{20,4},{24,8},{28,12},{1,17},{... | collective-permute-start | bytes 663560 | tf_op jit(solution)/shard_map/ppermute | solution.py:34

commit v8 on v7

--- a/solution.py
+++ b/solution.py
@@ -182,15 +182,15 @@
     return ref[...].astype(F32)
 
 
-def kernel_call(kernel, outs, ins, after=None, scratch=(), spaces={}):
+def kernel_call(kernel, outs, ins, after=(), scratch=(), spaces={}):
     place, arrays = ins[0], list(ins[1:])
     in_specs = [pl.BlockSpec(memory_space=pltpu.SMEM)]
     in_specs += [
         pl.BlockSpec(memory_space=spaces.get(k + 1, pltpu.VMEM)) for k in range(len(arrays))
     ]
     number = len(arrays) + 1
-    if after is not None:
-        arrays.append(after)
+    for value in after:
+        arrays.append(value)
         in_specs.append(pl.BlockSpec(memory_space=pl.ANY))
 
     def run(*refs):
@@ -331,8 +331,18 @@
         first += piece.shape[0]
 
 
-def middle_grads(place, kept, got, slope, middle_grad):
+def other_points(place, outs, other_hidden, far_other, *rest):
+    *pieces, share, other_outs = rest
+    joined(pieces, other_outs)
+    groups, block, rows = outs.shape
+    value = dot(outs[...].reshape(groups * block, rows), other_hidden[...], NN)
+    value += dot(other_outs[...].reshape(groups * block, rows), far_other[...], NN)
+    share[...] = value.astype(BF16).reshape(share.shape)
+
+
+def middle_grads(place, kept, got, slope, share, middle_grad, give):
     middle_grad[...] = ((kept[...] + wide(got)) * slope[...]).astype(BF16)
+    give[...] = share[...]
 
 
 def joined(pieces, whole):
@@ -361,34 +371,38 @@
             out[:, :, k * width : (k + 1) * width] = value.astype(out.dtype).reshape(shape)
 
 
-def early_products(
-    place, acts, other_acts, middle_grad, outs, hidden, other_hidden, far_hidden, far_other, *rest
+def middle_products(place, acts, other_acts, field, *rest):
+    *pieces, keep, along, across, both, other = rest
+    joined(pieces, other)
+
+    def values(left):
+        return (dot(left(acts), field[...], NN) + dot(left(other_acts), other[...], NN),)
+
+    each_chip(place, keep, along, across, both, values)
+
+
+def late_products(
+    place, acts, other_acts, moved, other_moved, outs, other_outs, hidden, far_hidden, shares,
+    keep, along, across, both,
 ):
-    *pieces, first, second, keep, along, across, both, other_outs, other_grad = rest
-    joined(pieces, other_outs)
-    joined((first, second), other_grad)
-
     def values(left):
-        own, other = left(outs), left(other_outs)
+        point = dot(left(outs), hidden[...], NN) + dot(left(other_outs), far_hidden[...], NN)
         return (
-            dot(left(acts), middle_grad[...], NN) + dot(left(other_acts), other_grad[...], NN),
-            dot(own, hidden[...], NN) + dot(other, far_hidden[...], NN),
-            dot(own, other_hidden[...], NN) + dot(other, far_other[...], NN),
+            dot(left(acts), moved[...], NN) + dot(left(other_acts), other_moved[...], NN),
+            point + left(shares).astype(F32),
         )
 
     each_chip(place, keep, along, across, both, values)
 
 
-def outer_products(place, acts, other_acts, moved, other_moved, keep, along, across, both):
-    def values(left):
-        return (dot(left(acts), moved[...], NN) + dot(left(other_acts), other_moved[...], NN),)
-
-    each_chip(place, keep, along, across, both, values)
-
-
-def act_part(place, middle_grad, moved, weight, part, slope, give):
-    value = dot(middle_grad[...], weight[1], NT) + dot(moved[...], weight[place[0]], NT)
-    give[...] = (wide(part) + value * slope[...]).astype(BF16)
+def act_part(first):
+    def act_rows(place, middle_grad, moved, weight, part, slope, give):
+        rows = slice(first, first + give.shape[0])
+        value = dot(middle_grad[rows, :], weight[1], NT)
+        value += dot(moved[rows, :], weight[place[0]], NT)
+        give[...] = (part[rows, :].astype(F32) + value * slope[rows, :]).astype(BF16)
+
+    return act_rows
 
 
 def over_chips(at, kept, *arrived):
@@ -398,33 +412,26 @@
     return total
 
 
-def early_sum(place, kept, along, across, both, keep, give):
-    two = keep.shape[2]
-    for at in range(2):
-        total = over_chips(at, kept, along, across, both)
-        keep[at] = total[:, :two]
-        give[at] = total[:, two:].astype(BF16)
-
-
-def last_sum(place, early, point_got, *refs):
+def chips_sum(place, *refs):
     *parts, keep, give = refs
     top = place[TOP]
-    width = parts[0].shape[2]
-    for at, out in ((top, keep), (1 - top, give)):
-        rest = early[at]
-        point = rest[:, width:] + point_got[at].astype(F32)
-        out[:, :width] = over_chips(at, *parts).astype(out.dtype)
-        out[:, width : 2 * width] = rest[:, :width].astype(out.dtype)
-        out[:, 2 * width :] = point.astype(out.dtype)
-
-
-def finish(place, own, theirs, kept, got, dilated, point, result):
+    keep[...] = over_chips(top, *parts)
+    give[...] = over_chips(1 - top, *parts).astype(BF16)
+
+
+def finish(
+    place, one, one_got, two, two_got, mid_kept, mid_got, kept, got, dilated, point, result
+):
     width = point.shape[1]
+    dilated[1] = mid_kept[...] + wide(mid_got)
     dilated[place[0]] = kept[:, :width]
     dilated[2 - place[0]] = got[:, :width].astype(F32)
-    dilated[1] = kept[:, width : 2 * width] + got[:, width : 2 * width].astype(F32)
-    point[...] = kept[:, 2 * width :] + got[:, 2 * width :].astype(F32)
-    result[...] = (wide(own) + wide(theirs)).astype(BF16)
+    point[...] = kept[:, width:] + got[:, width:].astype(F32)
+    first = 0
+    for own, theirs in ((one, one_got), (two, two_got)):
+        rows = slice(first, first + own.shape[0])
+        result[rows, :] = (wide(own) + wide(theirs)).astype(BF16)
+        first += own.shape[0]
 
 
 def body(features, dilated_weight, point_weight, track_weight, track_cotangent):
@@ -461,7 +468,7 @@
         outer_term,
         [((rows, channels), BF16), ((rows, width), BF16)],
         [place, in_hbm(feat), in_hbm(taps)],
-        own_piece,
+        [own_piece],
         scratch=[
             pltpu.VMEM((rows, channels), BF16),
             pltpu.VMEM((channels, width), BF16),
@@ -479,10 +486,11 @@
         [place, acted, taps],
     )
     middle, middle_b = kernel_call(
-        add_terms, [((rows, width), F32), ((rows, width), BF16)], [place, middle, arrived], acts
+        add_terms, [((rows, width), F32), ((rows, width), BF16)], [place, middle, arrived], [acts]
     )
     other_middle = flip(middle_b, "head")
     cut = piece // 3
+    other_acts = flip(acts_given, "sample")
     hidden, block_part, slope, slope_feat, *pieces = kernel_call(
         own_hidden,
         [
@@ -509,9 +517,9 @@
         ],
     )
     grad_got = flip(grad_given, "head")
-    far_hidden, other_acts = flip(hidden, "sample"), flip(acts_given, "sample")
-
-    def traded(kernel, columns, ins, after=None, scratch=()):
+    far_hidden = flip(hidden, "sample")
+
+    def traded(kernel, columns, ins, after=(), scratch=()):
         shape = (2, block, columns)
         keep, *gives = kernel_call(
             kernel, [(shape, F32)] + [(shape, BF16)] * 3, [place, *ins], after, scratch
@@ -524,45 +532,56 @@
         [turned, ((rows, width), BF16)]
         + [((min(third, groups - k), block, rows), BF16) for k in range(0, groups, third)],
         [place, part, flip(other_middle, "sample")],
-        far_hidden,
+        [far_hidden],
         scratch=[pltpu.VMEM((groups, block, rows), BF16)],
     )
-    (middle_grad,) = kernel_call(
-        middle_grads, [((rows, width), BF16)], [place, grad_kept, grad_got, slope], outs
+    shares = ((groups, block, width), BF16)
+    share, other_outs = kernel_call(
+        other_points,
+        [shares, turned],
+        [place, outs, other_hidden, far_other] + [flip(piece, "sample") for piece in outs_given],
+    )
+    middle_grad, share = kernel_call(
+        middle_grads,
+        [((rows, width), BF16), shares],
+        [place, grad_kept, grad_got, slope, share],
     )
     moved = lax.ppermute(middle_grad, "seq", pairs)
+    share_got = flip(share, "head")
+    cuts = [0, rows * 3 // 8, rows * 3 // 4, rows]
     early = traded(
-        early_products,
-        3 * width,
-        [acts, other_acts, middle_grad, outs, hidden, other_hidden, far_hidden, far_other]
-        + [flip(piece, "sample") for piece in outs_given]
-        + [flip(middle_grad[k : k + half], "sample") for k in (0, half)],
-        scratch=[pltpu.VMEM((groups, block, rows), BF16), pltpu.VMEM((rows, width), BF16)],
-    )
-    (own,) = kernel_call(
-        act_part,
-        [((rows, channels), BF16)],
-        [place, middle_grad, moved, taps, part, slope_feat],
-        early[0],
-    )
-    kept, point_give = kernel_call(
-        early_sum,
-        [((2, block, 2 * width), F32), ((2, block, width), BF16)],
-        [place, *early],
-        own,
-    )
-    steps = traded(
-        outer_products, width, [acts, other_acts, moved, flip(moved, "sample")], kept
-    )
-    kept, give = kernel_call(
-        last_sum,
-        [((block, 3 * width), F32), ((block, 3 * width), BF16)],
-        [place, kept, flip(point_give, "head"), *steps],
-    )
+        middle_products,
+        width,
+        [acts, other_acts, middle_grad]
+        + [flip(middle_grad[i:j], "sample") for i, j in zip(cuts[:-1], cuts[1:])],
+        scratch=[pltpu.VMEM((rows, width), BF16)],
+    )
+
+    def halved(terms, columns, after):
+        kept, give = kernel_call(
+            chips_sum, [((block, columns), F32), ((block, columns), BF16)], [place, *terms], after
+        )
+        return kept, flip(give, "seq", n_seq // 2)
+
+    mid_kept, mid_got = halved(early, width, [share_got])
+    most = rows * 3 // 4
+    ins = [place, middle_grad, moved, taps, part, slope_feat]
+    (one,) = kernel_call(act_part(0), [((most, channels), BF16)], ins, [mid_kept])
+    late = traded(
+        late_products,
+        2 * width,
+        [
+            acts, other_acts, moved, flip(moved, "sample"), outs, other_outs, hidden, far_hidden,
+            share_got,
+        ],
+        [one],
+    )
+    (two,) = kernel_call(act_part(most), [((rows - most, channels), BF16)], ins, [late[0]])
+    kept, got = halved(late, 2 * width, [two, mid_got])
     dilated_grad, point_grad, input_grad = kernel_call(
         finish,
         [((3, block, width), F32), ((block, width), F32), ((rows, channels), BF16)],
-        [place, own, flip(own, "head"), kept, flip(give, "seq", n_seq // 2)],
+        [place, one, flip(one, "head"), two, flip(two, "head"), mid_kept, mid_got, kept, got],
     )
     dilated_grad = jnp.transpose(dilated_grad, (1, 0, 2))
     return (input_grad.reshape(samples, positions, channels), dilated_grad, point_grad)

time: 98.6 us -> 93.6 us (0.949)
  waiting for transfers between devices: 50.9 us -> 42.2 us
  starting transfers between devices: 22.7 us -> 24.6 us
  Pallas kernels: 23.8 us -> 25.7 us
    ppermute x25 -> x28, waiting for transfers between devices: 41.2 us -> 32 us  [flip(): return lax.ppermute(value, axis, [(i, i ^ step) for i in range(count)])]
    pallas_call x14 -> x16, Pallas kernels: 23.8 us -> 25.7 us  [kernel_call(): pl.pallas_call(run, out_shape=[jax.ShapeDtypeStruct(s, d) for s, d in out...]
    ppermute x25 -> x28, starting transfers between devices: 20 us -> 21.9 us  [flip(): return lax.ppermute(value, axis, [(i, i ^ step) for i in range(count)])]
  transfers between devices with their start and end apart: 27 -> 30, of which waited for: 11 -> 12; matrix products, arithmetic and copies ran while one was open for 0% -> 0% of each run, Pallas kernels for 22% -> 26%
where the time goes in v8:
time: 93.6 us; the launch traced here: 93.5 us
  waiting for transfers between devices  42.2 us (45%)
  Pallas kernels  25.7 us (27%)
  starting transfers between devices  24.6 us (26%)
    ppermute x28, waiting for transfers between devices, flip(): return lax.ppermute(value, axis, [(i, i ^ step) for i in range(count)])  32 us
    pallas_call x16, Pallas kernels, kernel_call(): pl.pallas_call(run, out_shape=[jax.ShapeDtypeStruct(s, d) for s, d in out...  25.7 us
    ppermute x28, starting transfers between devices, flip(): return lax.ppermute(value, axis, [(i, i ^ step) for i in range(count)])  21.9 us
    ppermute x1, waiting for transfers between devices, body(): arrived = lax.ppermute(term, 'seq', pairs)  8.38 us
    ppermute x1, starting transfers between devices, body(): arrived = lax.ppermute(term, 'seq', pairs)  2.65 us
  transfers between devices with their start and end apart: 30, of which 12 were waited for; matrix products, arithmetic and copies ran while one was open for 0% of the time, Pallas kernels for 26%

profile of v8, /device:TPU:0, one launch (start us, length us, event | category | flops | bytes accessed | tf_op | source)
XLA Modules:
  0.0 93.5 jit_solution(253317663111254640)
XLA Ops:
  1.2 1.9 %piece_of.1.refs_3_ = bf16[768,384]{1,0:T(8,128)(2,1)S(1)} custom-call(s32[6]{0:T(128)S(1)} %stack.27.refs_0_, bf16[1536,384]{1,0:T(8,128)(2,1)} %refs_6_.1), custom_call_target="tpu_custom_call" | custom-call | flops 1 | bytes 1 | tf_op jit(solution)/shard_map/piece_of/pallas_call | solution.py:200
  3.1 2.6 %collective-permute-start.1 = (bf16[768,384]{1,0:T(8,128)(2,1)S(1)}, bf16[768,384]{1,0:T(8,128)(2,1)S(1)}, u32[]{:S(2)}, u32[]{:S(2)}) collective-permute-start(bf16[768,384]{1,0:T(8,128)(2,1)S(1)} %piece_of.1.refs_3_), channel_id=1, source_target_pairs={{0,2},{2,0},{1,3},{3,1},{4,6},{6,4},{5,7},{7,5},{8,10},{10,8},{9,1... | collective-permute-start | bytes 1769480 | tf_op jit(solution)/shard_map/ppermute | solution.py:34
  5.7 2.9 %outer_term.1 = (bf16[256,1536]{1,0:T(8,128)(2,1)S(1)}, bf16[256,384]{1,0:T(8,128)(2,1)S(1)}) custom-call(s32[6]{0:T(128)S(1)} %stack.27.refs_0_, bf16[256,1536]{1,0:T(8,128)(2,1)} %bitcast.15, bf16[3,1536,384]{2,1,0:T(8,128)(2,1)} %bitcast.11, bf16[768,384]{1,0:T(8,128)(2,1)S(1)} %piece_of.1.refs_3_), custom_call_target="tpu_custom_call" | custom-call | flops 1 | bytes 1 | tf_op jit(solution)/shard_map/outer_term/pallas_call | solution.py:200
  8.6 2.7 %collective-permute-start = (bf16[256,384]{1,0:T(8,128)(2,1)S(1)}, bf16[256,384]{1,0:T(8,128)(2,1)S(1)}, u32[]{:S(2)}, u32[]{:S(2)}) collective-permute-start(bf16[256,384]{1,0:T(8,128)(2,1)S(1)} %get-tuple-element.47), channel_id=1, source_target_pairs={{0,16},{4,20},{8,24},{12,28},{16,0},{20,4},{24,8},{28,12},{1,17},{... | collective-permute-start | bytes 589832 | tf_op jit(solution)/shard_map/ppermute | solution.py:479
  11.3 1.1 %middle_term.1 = (f32[256,384]{1,0:T(8,128)S(1)}, bf16[8,96,256]{2,1,0:T(8,128)(2,1)S(1)}, bf16[8,96,256]{2,1,0:T(8,128)(2,1)S(1)}) custom-call(s32[6]{0:T(128)S(1)} %stack.27.refs_0_, bf16[256,1536]{1,0:T(8,128)(2,1)S(1)} %get-tuple-element.45.refs_1_, bf16[3,1536,384]{2,1,0:T(8,128)(2,1)S(1)} %bitcast.12), custom_call_target="tpu_custom_call" | custom-call | flops 1 | bytes 1 | tf_op jit(solution)/shard_map/middle_term/pallas_call | solution.py:200
  12.4 8.4 %collective-permute-done.refs_2_ = bf16[256,384]{1,0:T(8,128)(2,1)S(1)} collective-permute-done((bf16[256,384]{1,0:T(8,128)(2,1)S(1)}, bf16[256,384]{1,0:T(8,128)(2,1)S(1)}, u32[]{:S(2)}, u32[]{:S(2)}) %collective-permute-start) | collective-permute-done | bytes 196640 | tf_op jit(solution)/shard_map/ppermute | solution.py:479
  22.0 1.9 %own_hidden.1 = (bf16[256,384]{1,0:T(8,128)(2,1)S(1)}, f32[256,1536]{1,0:T(8,128)S(1)}, f32[256,384]{1,0:T(8,128)S(1)}, f32[256,1536]{1,0:T(8,128)S(1)}, bf16[25...) custom-call(s32[6]{0:T(128)S(1)} %stack.27.refs_0_, ...), custom_call_target="tpu_custom_call" | custom-call | flops 1 | bytes 1 | tf_op jit(solution)/shard_map/own_hidden/pallas_call | solution.py:200
  24.6 3.1 %collective-permute-done.2.refs_2_ = bf16[256,384]{1,0:T(8,128)(2,1)S(1)} collective-permute-done((bf16[256,384]{1,0:T(8,128)(2,1)S(1)}, bf16[256,384]{1,0:T(8,128)(2,1)S(1)}, u32[]{:S(2)}, u32[]{:S(2)}) %collective-permute-start.2) | collective-permute-done | bytes 196640 | tf_op jit(solution)/shard_map/ppermute | solution.py:34
  28.2 6.1 %tracks.1 = (bf16[256,1536]{1,0:T(8,128)(2,1)S(1)}, bf16[256,384]{1,0:T(8,128)(2,1)S(1)}, f32[256,384]{1,0:T(8,128)S(1)}, bf16[256,384]{1,0:T(8,128)(2,1)S(1)}) custom-call(s32[6]{0:T(128)S(1)} %stack.27.refs_0_, f32[256,1536]{1,0:T(8,128)S(1)} %get-tuple-element.50.refs_1_, bf16[256,384]{1,0:T(8,128)(2,1)S(1)} %collective-permute-done.2.refs_2_, ...), custom_call_target="tpu_custom_call" | custom-call | flops 1 | bytes 1 | tf_op jit(solution)/shard_map/tracks/pallas_call | solution.py:200
  34.3 0.9 collective-permute-start.7
  35.2 1.0 %turn_parts.1 = (bf16[8,96,256]{2,1,0:T(8,128)(2,1)S(1)}, bf16[256,384]{1,0:T(8,128)(2,1)S(1)}, bf16[3,96,256]{2,1,0:T(8,128)(2,1)S(1)}, bf16[3,96,256]{2,1,0:T(8,128)(2,1)S(1)}, bf16[2,96,256]{2,1,0:T(8,128)(2,1)S(1)}) custom-call(s32[6]{0:T(128)S(1)} %stack.27.refs_0_, bf16[256,1536]{1,0:T(8,128)(2,1)S(1)} %get-tuple-element.58.refs_1_.refs_4_, ...), custom_call_target="tpu_custom_call" | custom-call | flops 1 | bytes 1 | tf_op jit(solution)/shard_map/turn_parts/pallas_call | solution.py:200
  38.0 1.1 %other_points.1 = (bf16[8,96,384]{2,1,0:T(8,128)(2,1)S(1)}, bf16[8,96,256]{2,1,0:T(8,128)(2,1)S(1)}) custom-call(s32[6]{0:T(128)S(1)} %stack.27.refs_0_, bf16[8,96,256]{2,1,0:T(8,128)(2,1)S(1)} %get-tuple-element.60.refs_1_.refs_5_, bf16[256,384]{1,0:T(8,128)(2,1)S(1)} %get-tuple-element.61.refs_2_, bf16[256,384]{1,0:T(8,128)(2,1)S(1)} %get-tuple-element.62.refs_3_, ...), custom_call_target="tpu_custom_call" | custom-call | flops 1 | bytes 1 | tf_op jit(solution)/shard_map/other_points/pallas_call | solution.py:200
  39.1 2.0 %collective-permute-done.7.refs_2_ = bf16[256,384]{1,0:T(8,128)(2,1)S(1)} collective-permute-done((bf16[256,384]{1,0:T(8,128)(2,1)S(1)}, bf16[256,384]{1,0:T(8,128)(2,1)S(1)}, u32[]{:S(2)}, u32[]{:S(2)}) %collective-permute-start.7) | collective-permute-done | bytes 196640 | tf_op jit(solution)/shard_map/ppermute | solution.py:34
  41.8 0.9 collective-permute-start.21
  43.4 1.2 %collective-permute-done.17.refs_6_ = bf16[64,384]{1,0:T(8,128)(2,1)S(1)} collective-permute-done((bf16[64,384]{1,0:T(8,128)(2,1)S(1)}, bf16[64,384]{1,0:T(8,128)(2,1)S(1)}, u32[]{:S(2)}, u32[]{:S(2)}) %collective-permute-start.17) | collective-permute-done | bytes 49184 | tf_op jit(solution)/shard_map/ppermute | solution.py:34
  44.6 1.1 %middle_products.1 = (f32[2,96,384]{2,1,0:T(8,128)S(1)}, bf16[2,96,384]{2,1,0:T(8,128)(2,1)S(1)}, bf16[2,96,384]{2,1,0:T(8,128)(2,1)S(1)}, bf16[2,96,384]{2,1,0:T(8,128)(2,1)S(1)}) custom-call(s32[6]{0:T(128)S(1)} %stack.27.refs_0_, bf16[8,96,256]{2,1,0:T(8,128)(2,1)S(1)} %get-tuple-element.48.refs_3_.refs_1_, ...), custom_call_target="tpu_custom_call" | custom-call | flops 1 | bytes 1 | tf_op jit(solution)/shard_map/middle_products/pallas_call | solution.py:200
  45.7 4.5 %collective-permute-start.18 = (bf16[2,96,384]{2,1,0:T(8,128)(2,1)S(1)}, bf16[2,96,384]{2,1,0:T(8,128)(2,1)S(1)}, u32[]{:S(2)}, u32[]{:S(2)}) collective-permute-start(bf16[2,96,384]{2,1,0:T(8,128)(2,1)S(1)} %get-tuple-element.71), channel_id=1, source_target_pairs={{0,8},{4,12},{8,0},{12,4},{16,24},{20,28},{24,16},{28,20},{1,9},{5... | collective-permute-start | bytes 442376 | tf_op jit(solution)/shard_map/ppermute | solution.py:34
  50.2 1.5 %collective-permute-start.19 = (bf16[2,96,384]{2,1,0:T(8,128)(2,1)S(1)}, bf16[2,96,384]{2,1,0:T(8,128)(2,1)S(1)}, u32[]{:S(2)}, u32[]{:S(2)}) collective-permute-start(bf16[2,96,384]{2,1,0:T(8,128)(2,1)S(1)} %get-tuple-element.72), channel_id=1, source_target_pairs={{0,4},{4,0},{8,12},{12,8},{16,20},{20,16},{24,28},{28,24},{1,5},{5... | collective-permute-start | bytes 442376 | tf_op jit(solution)/shard_map/ppermute | solution.py:34
  51.8 1.8 %collective-permute-done.13.refs_2_.refs_3_ = bf16[256,384]{1,0:T(8,128)(2,1)S(1)} collective-permute-done((bf16[256,384]{1,0:T(8,128)(2,1)S(1)}, bf16[256,384]{1,0:T(8,128)(2,1)S(1)}, u32[]{:S(2)}, u32[]{:S(2)}) %collective-permute-start.13) | collective-permute-done | bytes 196640 | tf_op jit(solution)/shard_map/ppermute | solution.py:549
  53.6 3.1 %collective-permute-done.18.refs_2_ = bf16[2,96,384]{2,1,0:T(8,128)(2,1)S(1)} collective-permute-done((bf16[2,96,384]{2,1,0:T(8,128)(2,1)S(1)}, bf16[2,96,384]{2,1,0:T(8,128)(2,1)S(1)}, u32[]{:S(2)}, u32[]{:S(2)}) %collective-permute-start.18) | collective-permute-done | bytes 147488 | tf_op jit(solution)/shard_map/ppermute | solution.py:34
  56.7 3.8 %collective-permute-done.20.refs_4_ = bf16[2,96,384]{2,1,0:T(8,128)(2,1)S(1)} collective-permute-done((bf16[2,96,384]{2,1,0:T(8,128)(2,1)S(1)}, bf16[2,96,384]{2,1,0:T(8,128)(2,1)S(1)}, u32[]{:S(2)}, u32[]{:S(2)}) %collective-permute-start.20) | collective-permute-done | bytes 147488 | tf_op jit(solution)/shard_map/ppermute | solution.py:34
  61.1 1.5 %act_rows.2.refs_10_.refs_1_ = bf16[192,1536]{1,0:T(8,128)(2,1)S(1)} custom-call(s32[6]{0:T(128)S(1)} %stack.27.refs_0_, bf16[256,384]{1,0:T(8,128)(2,1)S(1)} %get-tuple-element.67.refs_3_.refs_1_, bf16[256,384]{1,0:T(8,128)(2,1)S(1)} %collective-permute-done.13.refs_2_.refs_3_, bf16[3,1536,384]{2,1,0:T(8,128)(2,1)S(1)} %bitcast.13, ...), custom_call_target="tpu_custom_call" | custom-call | flops 1 | bytes 1 | tf_op jit(solution)/shard_map/act_rows/pallas_call | solution.py:200
  62.7 1.6 %collective-permute-start.22 = (bf16[192,1536]{1,0:T(8,128)(2,1)S(1)}, bf16[192,1536]{1,0:T(8,128)(2,1)S(1)}, u32[]{:S(2)}, u32[]{:S(2)}) collective-permute-start(bf16[192,1536]{1,0:T(8,128)(2,1)S(1)} %act_rows.2.refs_10_.refs_1_), channel_id=1, source_target_pairs={{0,2},{2,0},{1,3},{3,1},{4,6},{6,4},{5,7},{7,5},{8,10},{10,8},{9,1... | collective-permute-start | bytes 1769480 | tf_op jit(solution)/shard_map/ppermute | solution.py:34
  64.2 1.5 %late_products.1 = (f32[2,96,768]{2,1,0:T(8,128)S(1)}, bf16[2,96,768]{2,1,0:T(8,128)(2,1)S(1)}, bf16[2,96,768]{2,1,0:T(8,128)(2,1)S(1)}, bf16[2,96,768]{2,1,0:T(8,128)(2,1)S(1)}) custom-call(s32[6]{0:T(128)S(1)} %stack.27.refs_0_, bf16[8,96,256]{2,1,0:T(8,128)(2,1)S(1)} %get-tuple-element.48.refs_3_.refs_1_, ...), custom_call_target="tpu_custom_call" | custom-call | flops 1 | bytes 1 | tf_op jit(solution)/shard_map/late_products/pallas_call | solution.py:200
  66.4 2.9 %collective-permute-start.28 = (bf16[2,96,768]{2,1,0:T(8,128)(2,1)S(1)}, bf16[2,96,768]{2,1,0:T(8,128)(2,1)S(1)}, u32[]{:S(2)}, u32[]{:S(2)}) collective-permute-start(bf16[2,96,768]{2,1,0:T(8,128)(2,1)S(1)} %get-tuple-element.81), channel_id=1, source_target_pairs={{0,12},{4,8},{8,4},{12,0},{16,28},{20,24},{24,20},{28,16},{1,13},{... | collective-permute-start | bytes 884744 | tf_op jit(solution)/shard_map/ppermute | solution.py:34
  69.3 1.4 %act_rows.3.refs_5_.refs_3_ = bf16[64,1536]{1,0:T(8,128)(2,1)S(1)} custom-call(s32[6]{0:T(128)S(1)} %stack.27.refs_0_, bf16[256,384]{1,0:T(8,128)(2,1)S(1)} %get-tuple-element.67.refs_3_.refs_1_, bf16[256,384]{1,0:T(8,128)(2,1)S(1)} %collective-permute-done.13.refs_2_.refs_3_, bf16[3,1536,384]{2,1,0:T(8,128)(2,1)S(1)} %bitcast.14, ...), custom_call_target="tpu_custom_call" | custom-call | flops 1 | bytes 1 | tf_op jit(solution)/shard_map/act_rows/pallas_call | solution.py:200
  70.7 9.6 %collective-permute-done.25.refs_6_ = bf16[96,384]{1,0:T(8,128)(2,1)S(1)} collective-permute-done((bf16[96,384]{1,0:T(8,128)(2,1)S(1)}, bf16[96,384]{1,0:T(8,128)(2,1)S(1)}, u32[]{:S(2)}, u32[]{:S(2)}) %collective-permute-start.25) | collective-permute-done | bytes 73760 | tf_op jit(solution)/shard_map/ppermute | solution.py:34
  80.8 1.5 %collective-permute-done.28.refs_4_ = bf16[2,96,768]{2,1,0:T(8,128)(2,1)S(1)} collective-permute-done((bf16[2,96,768]{2,1,0:T(8,128)(2,1)S(1)}, bf16[2,96,768]{2,1,0:T(8,128)(2,1)S(1)}, u32[]{:S(2)}, u32[]{:S(2)}) %collective-permute-start.28) | collective-permute-done | bytes 294944 | tf_op jit(solution)/shard_map/ppermute | solution.py:34
  83.0 1.9 %collective-permute-start.29 = (bf16[96,768]{1,0:T(8,128)(2,1)S(1)}, bf16[96,768]{1,0:T(8,128)(2,1)S(1)}, u32[]{:S(2)}, u32[]{:S(2)}) collective-permute-start(bf16[96,768]{1,0:T(8,128)(2,1)S(1)} %get-tuple-element.83), channel_id=1, source_target_pairs={{0,16},{4,20},{8,24},{12,28},{16,0},{20,4},{24,8},{28,12},{1,17},{... | collective-permute-start | bytes 442376 | tf_op jit(solution)/shard_map/ppermute | solution.py:34
  84.9 1.4 %collective-permute-done.24.refs_4_ = bf16[64,1536]{1,0:T(8,128)(2,1)S(1)} collective-permute-done((bf16[64,1536]{1,0:T(8,128)(2,1)S(1)}, bf16[64,1536]{1,0:T(8,128)(2,1)S(1)}, u32[]{:S(2)}, u32[]{:S(2)}) %collective-permute-start.24) | collective-permute-done | bytes 196640 | tf_op jit(solution)/shard_map/ppermute | solution.py:34
  86.3 5.5 %collective-permute-done.29.refs_8_ = bf16[96,768]{1,0:T(8,128)(2,1)S(1)} collective-permute-done((bf16[96,768]{1,0:T(8,128)(2,1)S(1)}, bf16[96,768]{1,0:T(8,128)(2,1)S(1)}, u32[]{:S(2)}, u32[]{:S(2)}) %collective-permute-start.29) | collective-permute-done | bytes 147488 | tf_op jit(solution)/shard_map/ppermute | solution.py:34
  91.8 1.7 %finish.1 = (f32[3,96,384]{2,1,0:T(8,128)}, f32[96,384]{1,0:T(8,128)}, bf16[256,1536]{1,0:T(8,128)(2,1)}) custom-call(s32[6]{0:T(128)S(1)} %stack.27.refs_0_, bf16[192,1536]{1,0:T(8,128)(2,1)S(1)} %act_rows.2.refs_10_.refs_1_, bf16[192,1536]{1,0:T(8,128)(2,1)S(1)} %collective-permute-done.22.refs_2_, bf16[64,1536]{1,0:T(8,128)(2,1)S(1)} %act_rows.3.refs_5_.refs_3_, ...), custom_call_target="tpu_custom_call" | custom-call | flops 1 | bytes 1 | tf_op jit(solution)/shard_map/finish/pallas_call | solution.py:200
  (57 shorter events, 8.7 us)
Async XLA Ops:
  0.6 27.6 %collective-permute-start.3 = (bf16[768,1920]{1,0:T(8,128)(2,1)}, bf16[768,1920]{1,0:T(8,128)(2,1)S(1)}, u32[]{:S(2)}, u32[]{:S(2)}) collective-permute-start(bf16[768,1920]{1,0:T(8,128)(2,1)} %refs_3_.3), channel_id=1, source_target_pairs={{0,1},{1,0},{2,3},{3,2},{4,5},{5,4},{6,7},{7,6},{8,9},{9,8},{10,11... | collective-permute-start | bytes 8847368 | tf_op jit(solution)/shard_map/ppermute | solution.py:34
  3.1 18.8 %collective-permute-start.1 = (bf16[768,384]{1,0:T(8,128)(2,1)S(1)}, bf16[768,384]{1,0:T(8,128)(2,1)S(1)}, u32[]{:S(2)}, u32[]{:S(2)}) collective-permute-start(bf16[768,384]{1,0:T(8,128)(2,1)S(1)} %piece_of.1.refs_3_), channel_id=1, source_target_pairs={{0,2},{2,0},{1,3},{3,1},{4,6},{6,4},{5,7},{7,5},{8,10},{10,8},{9,1... | collective-permute-start | bytes 1769480 | tf_op jit(solution)/shard_map/ppermute | solution.py:34
  8.6 12.2 %collective-permute-start = (bf16[256,384]{1,0:T(8,128)(2,1)S(1)}, bf16[256,384]{1,0:T(8,128)(2,1)S(1)}, u32[]{:S(2)}, u32[]{:S(2)}) collective-permute-start(bf16[256,384]{1,0:T(8,128)(2,1)S(1)} %get-tuple-element.47), channel_id=1, source_target_pairs={{0,16},{4,20},{8,24},{12,28},{16,0},{20,4},{24,8},{28,12},{1,17},{... | collective-permute-start | bytes 589832 | tf_op jit(solution)/shard_map/ppermute | solution.py:479
  12.4 15.8 %copy-start.3 = (bf16[768,1920]{1,0:T(8,128)(2,1)S(1)}, bf16[768,1920]{1,0:T(8,128)(2,1)}, u32[]{:S(2)}) copy-start(bf16[768,1920]{1,0:T(8,128)(2,1)} %refs_3_.3) | copy-start | bytes 8847364
  12.4 15.8 %copy-start.4 = (bf16[1,256,1920]{2,1,0:T(8,128)(2,1)S(1)}, bf16[1,256,1920]{2,1,0:T(8,128)(2,1)}, u32[]{:S(2)}) copy-start(bf16[1,256,1920]{2,1,0:T(8,128)(2,1)} %param.9) | copy-start | bytes 2949124
  21.4 6.2 %collective-permute-start.2 = (bf16[256,384]{1,0:T(8,128)(2,1)S(1)}, bf16[256,384]{1,0:T(8,128)(2,1)S(1)}, u32[]{:S(2)}, u32[]{:S(2)}) collective-permute-start(bf16[256,384]{1,0:T(8,128)(2,1)S(1)} %get-tuple-element.51), channel_id=1, source_target_pairs={{0,2},{2,0},{1,3},{3,1},{4,6},{6,4},{5,7},{7,5},{8,10},{10,8},{9,1... | collective-permute-start | bytes 589832 | tf_op jit(solution)/shard_map/ppermute | solution.py:34
  23.9 3.8 %collective-permute-start.4 = (bf16[256,384]{1,0:T(8,128)(2,1)S(1)}, bf16[256,384]{1,0:T(8,128)(2,1)S(1)}, u32[]{:S(2)}, u32[]{:S(2)}) collective-permute-start(bf16[256,384]{1,0:T(8,128)(2,1)S(1)} %get-tuple-element.52), channel_id=1, source_target_pairs={{0,1},{1,0},{2,3},{3,2},{4,5},{5,4},{6,7},{7,6},{8,9},{9,8},{10,11... | collective-permute-start | bytes 589832 | tf_op jit(solution)/shard_map/ppermute | solution.py:34
  24.0 4.2 %collective-permute-start.5 = (bf16[256,384]{1,0:T(8,128)(2,1)S(1)}, bf16[256,384]{1,0:T(8,128)(2,1)S(1)}, u32[]{:S(2)}, u32[]{:S(2)}) collective-permute-start(bf16[256,384]{1,0:T(8,128)(2,1)S(1)} %get-tuple-element.53), channel_id=1, source_target_pairs={{0,1},{1,0},{2,3},{3,2},{4,5},{5,4},{6,7},{7,6},{8,9},{9,8},{10,11... | collective-permute-start | bytes 589832 | tf_op jit(solution)/shard_map/ppermute | solution.py:34
  24.5 3.7 %collective-permute-start.6 = (bf16[256,384]{1,0:T(8,128)(2,1)S(1)}, bf16[256,384]{1,0:T(8,128)(2,1)S(1)}, u32[]{:S(2)}, u32[]{:S(2)}) collective-permute-start(bf16[256,384]{1,0:T(8,128)(2,1)S(1)} %get-tuple-element.54), channel_id=1, source_target_pairs={{0,1},{1,0},{2,3},{3,2},{4,5},{5,4},{6,7},{7,6},{8,9},{9,8},{10,11... | collective-permute-start | bytes 589832 | tf_op jit(solution)/shard_map/ppermute | solution.py:34
  27.7 7.5 %collective-permute-start.8 = (bf16[256,384]{1,0:T(8,128)(2,1)S(1)}, bf16[256,384]{1,0:T(8,128)(2,1)S(1)}, u32[]{:S(2)}, u32[]{:S(2)}) collective-permute-start(bf16[256,384]{1,0:T(8,128)(2,1)S(1)} %collective-permute-done.2.refs_2_), channel_id=1, source_target_pairs={{0,1},{1,0},{2,3},{3,2},{4,5},{5,4},{6,7},{7,6},{8,9},{9,8},{10,11... | collective-permute-start | bytes 589832 | tf_op jit(solution)/shard_map/ppermute | solution.py:34
  27.7 7.5 %collective-permute-start.9 = (bf16[256,384]{1,0:T(8,128)(2,1)S(1)}, bf16[256,384]{1,0:T(8,128)(2,1)S(1)}, u32[]{:S(2)}, u32[]{:S(2)}) collective-permute-start(bf16[256,384]{1,0:T(8,128)(2,1)S(1)} %get-tuple-element.59.refs_7_), channel_id=1, source_target_pairs={{0,1},{1,0},{2,3},{3,2},{4,5},{5,4},{6,7},{7,6},{8,9},{9,8},{10,11... | collective-permute-start | bytes 589832 | tf_op jit(solution)/shard_map/ppermute | solution.py:34
  34.3 6.9 %collective-permute-start.7 = (bf16[256,384]{1,0:T(8,128)(2,1)S(1)}, bf16[256,384]{1,0:T(8,128)(2,1)S(1)}, u32[]{:S(2)}, u32[]{:S(2)}) collective-permute-start(bf16[256,384]{1,0:T(8,128)(2,1)S(1)} %get-tuple-element.56), channel_id=1, source_target_pairs={{0,2},{2,0},{1,3},{3,1},{4,6},{6,4},{5,7},{7,5},{8,10},{10,8},{9,1... | collective-permute-start | bytes 589832 | tf_op jit(solution)/shard_map/ppermute | solution.py:34
  36.1 1.9 %collective-permute-start.10 = (bf16[3,96,256]{2,1,0:T(8,128)(2,1)S(1)}, bf16[3,96,256]{2,1,0:T(8,128)(2,1)S(1)}, u32[]{:S(2)}, u32[]{:S(2)}) collective-permute-start(bf16[3,96,256]{2,1,0:T(8,128)(2,1)S(1)} %get-tuple-element.63), channel_id=1, source_target_pairs={{0,1},{1,0},{2,3},{3,2},{4,5},{5,4},{6,7},{7,6},{8,9},{9,8},{10,11... | collective-permute-start | bytes 442376 | tf_op jit(solution)/shard_map/ppermute | solution.py:34
  36.2 1.8 %collective-permute-start.11 = (bf16[3,96,256]{2,1,0:T(8,128)(2,1)S(1)}, bf16[3,96,256]{2,1,0:T(8,128)(2,1)S(1)}, u32[]{:S(2)}, u32[]{:S(2)}) collective-permute-start(bf16[3,96,256]{2,1,0:T(8,128)(2,1)S(1)} %get-tuple-element.64), channel_id=1, source_target_pairs={{0,1},{1,0},{2,3},{3,2},{4,5},{5,4},{6,7},{7,6},{8,9},{9,8},{10,11... | collective-permute-start | bytes 442376 | tf_op jit(solution)/shard_map/ppermute | solution.py:34
  36.7 1.3 %collective-permute-start.12 = (bf16[2,96,256]{2,1,0:T(8,128)(2,1)S(1)}, bf16[2,96,256]{2,1,0:T(8,128)(2,1)S(1)}, u32[]{:S(2)}, u32[]{:S(2)}) collective-permute-start(bf16[2,96,256]{2,1,0:T(8,128)(2,1)S(1)} %get-tuple-element.65), channel_id=1, source_target_pairs={{0,1},{1,0},{2,3},{3,2},{4,5},{5,4},{6,7},{7,6},{8,9},{9,8},{10,11... | collective-permute-start | bytes 294920 | tf_op jit(solution)/shard_map/ppermute | solution.py:34
  36.8 6.5 %collective-permute-start.14 = (bf16[8,96,256]{2,1,0:T(8,128)(2,1)S(1)}, bf16[8,96,256]{2,1,0:T(8,128)(2,1)S(1)}, u32[]{:S(2)}, u32[]{:S(2)}) collective-permute-start(bf16[8,96,256]{2,1,0:T(8,128)(2,1)S(1)} %get-tuple-element.69), channel_id=1, source_target_pairs={{0,1},{1,0},{2,3},{3,2},{4,5},{5,4},{6,7},{7,6},{8,9},{9,8},{10,11... | collective-permute-start | bytes 1179656 | tf_op jit(solution)/shard_map/ppermute | solution.py:34
  41.8 18.7 %collective-permute-start.21 = (bf16[8,96,384]{2,1,0:T(8,128)(2,1)S(1)}, bf16[8,96,384]{2,1,0:T(8,128)(2,1)S(1)}, u32[]{:S(2)}, u32[]{:S(2)}) collective-permute-start(bf16[8,96,384]{2,1,0:T(8,128)(2,1)S(1)} %get-tuple-element.74), channel_id=1, source_target_pairs={{0,2},{2,0},{1,3},{3,1},{4,6},{6,4},{5,7},{7,5},{8,10},{10,8},{9,1... | collective-permute-start | bytes 1769480 | tf_op jit(solution)/shard_map/ppermute | solution.py:34
  42.7 10.9 %collective-permute-start.13 = (bf16[256,384]{1,0:T(8,128)(2,1)S(1)}, bf16[256,384]{1,0:T(8,128)(2,1)S(1)}, u32[]{:S(2)}, u32[]{:S(2)}) collective-permute-start(bf16[256,384]{1,0:T(8,128)(2,1)S(1)} %get-tuple-element.67.refs_3_.refs_1_), channel_id=1, source_target_pairs={{0,16},{4,20},{8,24},{12,28},{16,0},{20,4},{24,8},{28,12},{1,17},{... | collective-permute-start | bytes 589832 | tf_op jit(solution)/shard_map/ppermute | solution.py:549
  42.7 1.9 %collective-permute-start.15 = (bf16[96,384]{1,0:T(8,128)(2,1)S(1)}, bf16[96,384]{1,0:T(8,128)(2,1)S(1)}, u32[]{:S(2)}, u32[]{:S(2)}) collective-permute-start(bf16[96,384]{1,0:T(8,128)(2,1)S(1)} %get-tuple-element.88), channel_id=1, source_target_pairs={{0,1},{1,0},{2,3},{3,2},{4,5},{5,4},{6,7},{7,6},{8,9},{9,8},{10,11... | collective-permute-start | bytes 221192 | tf_op jit(solution)/shard_map/ppermute | solution.py:34
  42.8 1.8 %collective-permute-start.16 = (bf16[96,384]{1,0:T(8,128)(2,1)S(1)}, bf16[96,384]{1,0:T(8,128)(2,1)S(1)}, u32[]{:S(2)}, u32[]{:S(2)}) collective-permute-start(bf16[96,384]{1,0:T(8,128)(2,1)S(1)} %get-tuple-element.87), channel_id=1, source_target_pairs={{0,1},{1,0},{2,3},{3,2},{4,5},{5,4},{6,7},{7,6},{8,9},{9,8},{10,11... | collective-permute-start | bytes 221192 | tf_op jit(solution)/shard_map/ppermute | solution.py:34
  43.3 1.3 %collective-permute-start.17 = (bf16[64,384]{1,0:T(8,128)(2,1)S(1)}, bf16[64,384]{1,0:T(8,128)(2,1)S(1)}, u32[]{:S(2)}, u32[]{:S(2)}) collective-permute-start(bf16[64,384]{1,0:T(8,128)(2,1)S(1)} %slice.11), channel_id=1, source_target_pairs={{0,1},{1,0},{2,3},{3,2},{4,5},{5,4},{6,7},{7,6},{8,9},{9,8},{10,11... | collective-permute-start | bytes 147464 | tf_op jit(solution)/shard_map/ppermute | solution.py:34
  45.7 11.0 %collective-permute-start.18 = (bf16[2,96,384]{2,1,0:T(8,128)(2,1)S(1)}, bf16[2,96,384]{2,1,0:T(8,128)(2,1)S(1)}, u32[]{:S(2)}, u32[]{:S(2)}) collective-permute-start(bf16[2,96,384]{2,1,0:T(8,128)(2,1)S(1)} %get-tuple-element.71), channel_id=1, source_target_pairs={{0,8},{4,12},{8,0},{12,4},{16,24},{20,28},{24,16},{28,20},{1,9},{5... | collective-permute-start | bytes 442376 | tf_op jit(solution)/shard_map/ppermute | solution.py:34
  50.2 6.5 %collective-permute-start.19 = (bf16[2,96,384]{2,1,0:T(8,128)(2,1)S(1)}, bf16[2,96,384]{2,1,0:T(8,128)(2,1)S(1)}, u32[]{:S(2)}, u32[]{:S(2)}) collective-permute-start(bf16[2,96,384]{2,1,0:T(8,128)(2,1)S(1)} %get-tuple-element.72), channel_id=1, source_target_pairs={{0,4},{4,0},{8,12},{12,8},{16,20},{20,16},{24,28},{28,24},{1,5},{5... | collective-permute-start | bytes 442376 | tf_op jit(solution)/shard_map/ppermute | solution.py:34
  51.7 8.8 %collective-permute-start.20 = (bf16[2,96,384]{2,1,0:T(8,128)(2,1)S(1)}, bf16[2,96,384]{2,1,0:T(8,128)(2,1)S(1)}, u32[]{:S(2)}, u32[]{:S(2)}) collective-permute-start(bf16[2,96,384]{2,1,0:T(8,128)(2,1)S(1)} %get-tuple-element.73), channel_id=1, source_target_pairs={{0,12},{4,8},{8,4},{12,0},{16,28},{20,24},{24,20},{28,16},{1,13},{... | collective-permute-start | bytes 442376 | tf_op jit(solution)/shard_map/ppermute | solution.py:34
  53.6 10.6 %collective-permute-start.23 = (bf16[256,384]{1,0:T(8,128)(2,1)S(1)}, bf16[256,384]{1,0:T(8,128)(2,1)S(1)}, u32[]{:S(2)}, u32[]{:S(2)}) collective-permute-start(bf16[256,384]{1,0:T(8,128)(2,1)S(1)} %collective-permute-done.13.refs_2_.refs_3_), channel_id=1, source_target_pairs={{0,1},{1,0},{2,3},{3,2},{4,5},{5,4},{6,7},{7,6},{8,9},{9,8},{10,11... | collective-permute-start | bytes 589832 | tf_op jit(solution)/shard_map/ppermute | solution.py:34
  62.7 29.2 %collective-permute-start.22 = (bf16[192,1536]{1,0:T(8,128)(2,1)S(1)}, bf16[192,1536]{1,0:T(8,128)(2,1)S(1)}, u32[]{:S(2)}, u32[]{:S(2)}) collective-permute-start(bf16[192,1536]{1,0:T(8,128)(2,1)S(1)} %act_rows.2.refs_10_.refs_1_), channel_id=1, source_target_pairs={{0,2},{2,0},{1,3},{3,1},{4,6},{6,4},{5,7},{7,5},{8,10},{10,8},{9,1... | collective-permute-start | bytes 1769480 | tf_op jit(solution)/shard_map/ppermute | solution.py:34
  65.7 15.1 %collective-permute-start.26 = (bf16[2,96,768]{2,1,0:T(8,128)(2,1)S(1)}, bf16[2,96,768]{2,1,0:T(8,128)(2,1)S(1)}, u32[]{:S(2)}, u32[]{:S(2)}) collective-permute-start(bf16[2,96,768]{2,1,0:T(8,128)(2,1)S(1)} %get-tuple-element.79), channel_id=1, source_target_pairs={{0,8},{4,12},{8,0},{12,4},{16,24},{20,28},{24,16},{28,20},{1,9},{5... | collective-permute-start | bytes 884744 | tf_op jit(solution)/shard_map/ppermute | solution.py:34
  65.8 15.0 %collective-permute-start.27 = (bf16[2,96,768]{2,1,0:T(8,128)(2,1)S(1)}, bf16[2,96,768]{2,1,0:T(8,128)(2,1)S(1)}, u32[]{:S(2)}, u32[]{:S(2)}) collective-permute-start(bf16[2,96,768]{2,1,0:T(8,128)(2,1)S(1)} %get-tuple-element.80), channel_id=1, source_target_pairs={{0,4},{4,0},{8,12},{12,8},{16,20},{20,16},{24,28},{28,24},{1,5},{5... | collective-permute-start | bytes 884744 | tf_op jit(solution)/shard_map/ppermute | solution.py:34
  66.4 16.0 %collective-permute-start.28 = (bf16[2,96,768]{2,1,0:T(8,128)(2,1)S(1)}, bf16[2,96,768]{2,1,0:T(8,128)(2,1)S(1)}, u32[]{:S(2)}, u32[]{:S(2)}) collective-permute-start(bf16[2,96,768]{2,1,0:T(8,128)(2,1)S(1)} %get-tuple-element.81), channel_id=1, source_target_pairs={{0,12},{4,8},{8,4},{12,0},{16,28},{20,24},{24,20},{28,16},{1,13},{... | collective-permute-start | bytes 884744 | tf_op jit(solution)/shard_map/ppermute | solution.py:34
  69.3 11.0 %collective-permute-start.25 = (bf16[96,384]{1,0:T(8,128)(2,1)S(1)}, bf16[96,384]{1,0:T(8,128)(2,1)S(1)}, u32[]{:S(2)}, u32[]{:S(2)}) collective-permute-start(bf16[96,384]{1,0:T(8,128)(2,1)S(1)} %get-tuple-element.78), channel_id=1, source_target_pairs={{0,16},{4,20},{8,24},{12,28},{16,0},{20,4},{24,8},{28,12},{1,17},{... | collective-permute-start | bytes 221192 | tf_op jit(solution)/shard_map/ppermute | solution.py:34
  80.3 6.0 %collective-permute-start.24 = (bf16[64,1536]{1,0:T(8,128)(2,1)S(1)}, bf16[64,1536]{1,0:T(8,128)(2,1)S(1)}, u32[]{:S(2)}, u32[]{:S(2)}) collective-permute-start(bf16[64,1536]{1,0:T(8,128)(2,1)S(1)} %act_rows.3.refs_5_.refs_3_), channel_id=1, source_target_pairs={{0,2},{2,0},{1,3},{3,1},{4,6},{6,4},{5,7},{7,5},{8,10},{10,8},{9,1... | collective-permute-start | bytes 589832 | tf_op jit(solution)/shard_map/ppermute | solution.py:34
  83.0 8.8 %collective-permute-start.29 = (bf16[96,768]{1,0:T(8,128)(2,1)S(1)}, bf16[96,768]{1,0:T(8,128)(2,1)S(1)}, u32[]{:S(2)}, u32[]{:S(2)}) collective-permute-start(bf16[96,768]{1,0:T(8,128)(2,1)S(1)} %get-tuple-element.83), channel_id=1, source_target_pairs={{0,16},{4,20},{8,24},{12,28},{16,0},{20,4},{24,8},{28,12},{1,17},{... | collective-permute-start | bytes 442376 | tf_op jit(solution)/shard_map/ppermute | solution.py:34
  (3 other events, 36.8 us)

commit v9 on v8

--- a/solution.py
+++ b/solution.py
@@ -372,7 +372,7 @@
 
 
 def middle_products(place, acts, other_acts, field, *rest):
-    *pieces, keep, along, across, both, other = rest
+    *pieces, keep, across, along, both, other = rest
     joined(pieces, other)
 
     def values(left):
@@ -382,9 +382,11 @@
 
 
 def late_products(
-    place, acts, other_acts, moved, other_moved, outs, other_outs, hidden, far_hidden, shares,
-    keep, along, across, both,
+    place, acts, other_acts, moved, outs, other_outs, hidden, far_hidden, shares, first, second,
+    keep, across, along, both, other_moved,
 ):
+    joined((first, second), other_moved)
+
     def values(left):
         point = dot(left(outs), hidden[...], NN) + dot(left(other_outs), far_hidden[...], NN)
         return (
@@ -524,7 +526,7 @@
         keep, *gives = kernel_call(
             kernel, [(shape, F32)] + [(shape, BF16)] * 3, [place, *ins], after, scratch
         )
-        return keep, *[flip(value, "seq", step) for value, step in zip(gives, (2, 1, 3))]
+        return keep, *[flip(value, "seq", step) for value, step in zip(gives, (1, 2, 3))]
 
     third = -(-groups // 3)
     outs, far_other, *outs_given = kernel_call(
@@ -548,7 +550,7 @@
     )
     moved = lax.ppermute(middle_grad, "seq", pairs)
     share_got = flip(share, "head")
-    cuts = [0, rows * 3 // 8, rows * 3 // 4, rows]
+    cuts = [k * rows // 4 for k in range(5)]
     early = traded(
         middle_products,
         width,
@@ -557,26 +559,24 @@
         scratch=[pltpu.VMEM((rows, width), BF16)],
     )
 
-    def halved(terms, columns, after):
+    def halved(terms, columns, after=()):
         kept, give = kernel_call(
             chips_sum, [((block, columns), F32), ((block, columns), BF16)], [place, *terms], after
         )
         return kept, flip(give, "seq", n_seq // 2)
 
-    mid_kept, mid_got = halved(early, width, [share_got])
-    most = rows * 3 // 4
-    ins = [place, middle_grad, moved, taps, part, slope_feat]
-    (one,) = kernel_call(act_part(0), [((most, channels), BF16)], ins, [mid_kept])
+    mid_kept, mid_got = halved(early, width)
     late = traded(
         late_products,
         2 * width,
-        [
-            acts, other_acts, moved, flip(moved, "sample"), outs, other_outs, hidden, far_hidden,
-            share_got,
-        ],
-        [one],
-    )
-    (two,) = kernel_call(act_part(most), [((rows - most, channels), BF16)], ins, [late[0]])
+        [acts, other_acts, moved, outs, other_outs, hidden, far_hidden, share_got]
+        + [flip(moved[k : k + half], "sample") for k in (0, half)],
+        [mid_kept],
+        scratch=[pltpu.VMEM((rows, width), BF16)],
+    )
+    ins = [place, middle_grad, moved, taps, part, slope_feat]
+    (one,) = kernel_call(act_part(0), [((half, channels), BF16)], ins, [late[0]])
+    (two,) = kernel_call(act_part(half), [((half, channels), BF16)], ins, [one])
     kept, got = halved(late, 2 * width, [two, mid_got])
     dilated_grad, point_grad, input_grad = kernel_call(
         finish,

time: 93.6 us -> 91.2 us (0.974)
  waiting for transfers between devices: 42.2 us -> 38.6 us
  starting transfers between devices: 24.6 us -> 25.9 us
    ppermute x28 -> x30, waiting for transfers between devices: 32 us -> 29 us  [flip(): return lax.ppermute(value, axis, [(i, i ^ step) for i in range(count)])]
    ppermute x28 -> x30, starting transfers between devices: 21.9 us -> 23.2 us  [flip(): return lax.ppermute(value, axis, [(i, i ^ step) for i in range(count)])]
  transfers between devices with their start and end apart: 30 -> 32, of which waited for: 12 -> 15; matrix products, arithmetic and copies ran while one was open for 0% -> 0% of each run, Pallas kernels for 26% -> 26%
where the time goes in v9:
time: 91.2 us; the launch traced here: 91 us
  waiting for transfers between devices  38.6 us (42%)
  starting transfers between devices  25.9 us (28%)
  Pallas kernels  25.6 us (28%)
    ppermute x30, waiting for transfers between devices, flip(): return lax.ppermute(value, axis, [(i, i ^ step) for i in range(count)])  29 us
    pallas_call x16, Pallas kernels, kernel_call(): pl.pallas_call(run, out_shape=[jax.ShapeDtypeStruct(s, d) for s, d in out...  25.6 us
    ppermute x30, starting transfers between devices, flip(): return lax.ppermute(value, axis, [(i, i ^ step) for i in range(count)])  23.2 us
    ppermute x1, waiting for transfers between devices, body(): arrived = lax.ppermute(term, 'seq', pairs)  8.38 us
    ppermute x1, starting transfers between devices, body(): arrived = lax.ppermute(term, 'seq', pairs)  2.65 us
  transfers between devices with their start and end apart: 32, of which 15 were waited for; matrix products, arithmetic and copies ran while one was open for 0% of the time, Pallas kernels for 26%

profile of v9, /device:TPU:0, one launch (start us, length us, event | category | flops | bytes accessed | tf_op | source)
XLA Modules:
  0.0 91.0 jit_solution(2161197999719294466)
XLA Ops:
  1.2 1.9 %piece_of.1.refs_3_ = bf16[768,384]{1,0:T(8,128)(2,1)S(1)} custom-call(s32[6]{0:T(128)S(1)} %stack.27.refs_0_, bf16[1536,384]{1,0:T(8,128)(2,1)} %refs_6_.1), custom_call_target="tpu_custom_call" | custom-call | flops 1 | bytes 1 | tf_op jit(solution)/shard_map/piece_of/pallas_call | solution.py:200
  3.1 2.6 %collective-permute-start.1 = (bf16[768,384]{1,0:T(8,128)(2,1)S(1)}, bf16[768,384]{1,0:T(8,128)(2,1)S(1)}, u32[]{:S(2)}, u32[]{:S(2)}) collective-permute-start(bf16[768,384]{1,0:T(8,128)(2,1)S(1)} %piece_of.1.refs_3_), channel_id=1, source_target_pairs={{0,2},{2,0},{1,3},{3,1},{4,6},{6,4},{5,7},{7,5},{8,10},{10,8},{9,1... | collective-permute-start | bytes 1769480 | tf_op jit(solution)/shard_map/ppermute | solution.py:34
  5.7 2.9 %outer_term.1 = (bf16[256,1536]{1,0:T(8,128)(2,1)S(1)}, bf16[256,384]{1,0:T(8,128)(2,1)S(1)}) custom-call(s32[6]{0:T(128)S(1)} %stack.27.refs_0_, bf16[256,1536]{1,0:T(8,128)(2,1)} %bitcast.15, bf16[3,1536,384]{2,1,0:T(8,128)(2,1)} %bitcast.11, bf16[768,384]{1,0:T(8,128)(2,1)S(1)} %piece_of.1.refs_3_), custom_call_target="tpu_custom_call" | custom-call | flops 1 | bytes 1 | tf_op jit(solution)/shard_map/outer_term/pallas_call | solution.py:200
  8.6 2.7 %collective-permute-start = (bf16[256,384]{1,0:T(8,128)(2,1)S(1)}, bf16[256,384]{1,0:T(8,128)(2,1)S(1)}, u32[]{:S(2)}, u32[]{:S(2)}) collective-permute-start(bf16[256,384]{1,0:T(8,128)(2,1)S(1)} %get-tuple-element.47), channel_id=1, source_target_pairs={{0,16},{4,20},{8,24},{12,28},{16,0},{20,4},{24,8},{28,12},{1,17},{... | collective-permute-start | bytes 589832 | tf_op jit(solution)/shard_map/ppermute | solution.py:481
  11.3 1.1 %middle_term.1 = (f32[256,384]{1,0:T(8,128)S(1)}, bf16[8,96,256]{2,1,0:T(8,128)(2,1)S(1)}, bf16[8,96,256]{2,1,0:T(8,128)(2,1)S(1)}) custom-call(s32[6]{0:T(128)S(1)} %stack.27.refs_0_, bf16[256,1536]{1,0:T(8,128)(2,1)S(1)} %get-tuple-element.45.refs_1_, bf16[3,1536,384]{2,1,0:T(8,128)(2,1)S(1)} %bitcast.12), custom_call_target="tpu_custom_call" | custom-call | flops 1 | bytes 1 | tf_op jit(solution)/shard_map/middle_term/pallas_call | solution.py:200
  12.4 8.4 %collective-permute-done.refs_2_ = bf16[256,384]{1,0:T(8,128)(2,1)S(1)} collective-permute-done((bf16[256,384]{1,0:T(8,128)(2,1)S(1)}, bf16[256,384]{1,0:T(8,128)(2,1)S(1)}, u32[]{:S(2)}, u32[]{:S(2)}) %collective-permute-start) | collective-permute-done | bytes 196640 | tf_op jit(solution)/shard_map/ppermute | solution.py:481
  22.0 1.9 %own_hidden.1 = (bf16[256,384]{1,0:T(8,128)(2,1)S(1)}, f32[256,1536]{1,0:T(8,128)S(1)}, f32[256,384]{1,0:T(8,128)S(1)}, f32[256,1536]{1,0:T(8,128)S(1)}, bf16[25...) custom-call(s32[6]{0:T(128)S(1)} %stack.27.refs_0_, ...), custom_call_target="tpu_custom_call" | custom-call | flops 1 | bytes 1 | tf_op jit(solution)/shard_map/own_hidden/pallas_call | solution.py:200
  24.6 3.1 %collective-permute-done.2.refs_2_ = bf16[256,384]{1,0:T(8,128)(2,1)S(1)} collective-permute-done((bf16[256,384]{1,0:T(8,128)(2,1)S(1)}, bf16[256,384]{1,0:T(8,128)(2,1)S(1)}, u32[]{:S(2)}, u32[]{:S(2)}) %collective-permute-start.2) | collective-permute-done | bytes 196640 | tf_op jit(solution)/shard_map/ppermute | solution.py:34
  28.2 6.1 %tracks.1 = (bf16[256,1536]{1,0:T(8,128)(2,1)S(1)}, bf16[256,384]{1,0:T(8,128)(2,1)S(1)}, f32[256,384]{1,0:T(8,128)S(1)}, bf16[256,384]{1,0:T(8,128)(2,1)S(1)}) custom-call(s32[6]{0:T(128)S(1)} %stack.27.refs_0_, f32[256,1536]{1,0:T(8,128)S(1)} %get-tuple-element.50.refs_1_, bf16[256,384]{1,0:T(8,128)(2,1)S(1)} %collective-permute-done.2.refs_2_, ...), custom_call_target="tpu_custom_call" | custom-call | flops 1 | bytes 1 | tf_op jit(solution)/shard_map/tracks/pallas_call | solution.py:200
  35.2 1.0 %turn_parts.1 = (bf16[8,96,256]{2,1,0:T(8,128)(2,1)S(1)}, bf16[256,384]{1,0:T(8,128)(2,1)S(1)}, bf16[3,96,256]{2,1,0:T(8,128)(2,1)S(1)}, bf16[3,96,256]{2,1,0:T(8,128)(2,1)S(1)}, bf16[2,96,256]{2,1,0:T(8,128)(2,1)S(1)}) custom-call(s32[6]{0:T(128)S(1)} %stack.27.refs_0_, bf16[256,1536]{1,0:T(8,128)(2,1)S(1)} %get-tuple-element.58.refs_1_.refs_4_, ...), custom_call_target="tpu_custom_call" | custom-call | flops 1 | bytes 1 | tf_op jit(solution)/shard_map/turn_parts/pallas_call | solution.py:200
  37.2 1.4 %collective-permute-done.12.refs_6_ = bf16[2,96,256]{2,1,0:T(8,128)(2,1)S(1)} collective-permute-done((bf16[2,96,256]{2,1,0:T(8,128)(2,1)S(1)}, bf16[2,96,256]{2,1,0:T(8,128)(2,1)S(1)}, u32[]{:S(2)}, u32[]{:S(2)}) %collective-permute-start.12) | collective-permute-done | bytes 98336 | tf_op jit(solution)/shard_map/ppermute | solution.py:34
  38.6 1.1 %other_points.1 = (bf16[8,96,384]{2,1,0:T(8,128)(2,1)S(1)}, bf16[8,96,256]{2,1,0:T(8,128)(2,1)S(1)}) custom-call(s32[6]{0:T(128)S(1)} %stack.27.refs_0_, bf16[8,96,256]{2,1,0:T(8,128)(2,1)S(1)} %get-tuple-element.60.refs_1_.refs_4_, bf16[256,384]{1,0:T(8,128)(2,1)S(1)} %get-tuple-element.61.refs_2_, bf16[256,384]{1,0:T(8,128)(2,1)S(1)} %get-tuple-element.62.refs_3_, ...), custom_call_target="tpu_custom_call" | custom-call | flops 1 | bytes 1 | tf_op jit(solution)/shard_map/other_points/pallas_call | solution.py:200
  39.7 1.5 %collective-permute-done.7.refs_2_ = bf16[256,384]{1,0:T(8,128)(2,1)S(1)} collective-permute-done((bf16[256,384]{1,0:T(8,128)(2,1)S(1)}, bf16[256,384]{1,0:T(8,128)(2,1)S(1)}, u32[]{:S(2)}, u32[]{:S(2)}) %collective-permute-start.7) | collective-permute-done | bytes 196640 | tf_op jit(solution)/shard_map/ppermute | solution.py:34
  41.8 0.9 collective-permute-start.15
  45.2 1.1 %middle_products.1 = (f32[2,96,384]{2,1,0:T(8,128)S(1)}, bf16[2,96,384]{2,1,0:T(8,128)(2,1)S(1)}, bf16[2,96,384]{2,1,0:T(8,128)(2,1)S(1)}, bf16[2,96,384]{2,1,0:T(8,128)(2,1)S(1)}) custom-call(s32[6]{0:T(128)S(1)} %stack.27.refs_0_, bf16[8,96,256]{2,1,0:T(8,128)(2,1)S(1)} %get-tuple-element.48.refs_3_.refs_1_, ...), custom_call_target="tpu_custom_call" | custom-call | flops 1 | bytes 1 | tf_op jit(solution)/shard_map/middle_products/pallas_call | solution.py:200
  46.4 1.3 %collective-permute-start.22 = (bf16[2,96,384]{2,1,0:T(8,128)(2,1)S(1)}, bf16[2,96,384]{2,1,0:T(8,128)(2,1)S(1)}, u32[]{:S(2)}, u32[]{:S(2)}) collective-permute-start(bf16[2,96,384]{2,1,0:T(8,128)(2,1)S(1)} %get-tuple-element.73), channel_id=1, source_target_pairs={{0,4},{4,0},{8,12},{12,8},{16,20},{20,16},{24,28},{28,24},{1,5},{5... | collective-permute-start | bytes 442376 | tf_op jit(solution)/shard_map/ppermute | solution.py:34
  47.7 4.7 %collective-permute-start.23 = (bf16[2,96,384]{2,1,0:T(8,128)(2,1)S(1)}, bf16[2,96,384]{2,1,0:T(8,128)(2,1)S(1)}, u32[]{:S(2)}, u32[]{:S(2)}) collective-permute-start(bf16[2,96,384]{2,1,0:T(8,128)(2,1)S(1)} %get-tuple-element.74), channel_id=1, source_target_pairs={{0,8},{4,12},{8,0},{12,4},{16,24},{20,28},{24,16},{28,20},{1,9},{5... | collective-permute-start | bytes 442376 | tf_op jit(solution)/shard_map/ppermute | solution.py:34
  52.4 1.1 %collective-permute-done.13.refs_3_.refs_2_ = bf16[256,384]{1,0:T(8,128)(2,1)S(1)} collective-permute-done((bf16[256,384]{1,0:T(8,128)(2,1)S(1)}, bf16[256,384]{1,0:T(8,128)(2,1)S(1)}, u32[]{:S(2)}, u32[]{:S(2)}) %collective-permute-start.13) | collective-permute-done | bytes 196640 | tf_op jit(solution)/shard_map/ppermute | solution.py:551
  54.1 2.9 %collective-permute-done.23.refs_3_ = bf16[2,96,384]{2,1,0:T(8,128)(2,1)S(1)} collective-permute-done((bf16[2,96,384]{2,1,0:T(8,128)(2,1)S(1)}, bf16[2,96,384]{2,1,0:T(8,128)(2,1)S(1)}, u32[]{:S(2)}, u32[]{:S(2)}) %collective-permute-start.23) | collective-permute-done | bytes 147488 | tf_op jit(solution)/shard_map/ppermute | solution.py:34
  57.1 3.7 %collective-permute-done.24.refs_4_ = bf16[2,96,384]{2,1,0:T(8,128)(2,1)S(1)} collective-permute-done((bf16[2,96,384]{2,1,0:T(8,128)(2,1)S(1)}, bf16[2,96,384]{2,1,0:T(8,128)(2,1)S(1)}, u32[]{:S(2)}, u32[]{:S(2)}) %collective-permute-start.24) | collective-permute-done | bytes 147488 | tf_op jit(solution)/shard_map/ppermute | solution.py:34
  61.5 1.5 %late_products.1 = (f32[2,96,768]{2,1,0:T(8,128)S(1)}, bf16[2,96,768]{2,1,0:T(8,128)(2,1)S(1)}, bf16[2,96,768]{2,1,0:T(8,128)(2,1)S(1)}, bf16[2,96,768]{2,1,0:T(8,128)(2,1)S(1)}) custom-call(s32[6]{0:T(128)S(1)} %stack.27.refs_0_, bf16[8,96,256]{2,1,0:T(8,128)(2,1)S(1)} %get-tuple-element.48.refs_3_.refs_1_, ...), custom_call_target="tpu_custom_call" | custom-call | flops 1 | bytes 1 | tf_op jit(solution)/shard_map/late_products/pallas_call | solution.py:200
  63.6 1.7 %collective-permute-start.29 = (bf16[2,96,768]{2,1,0:T(8,128)(2,1)S(1)}, bf16[2,96,768]{2,1,0:T(8,128)(2,1)S(1)}, u32[]{:S(2)}, u32[]{:S(2)}) collective-permute-start(bf16[2,96,768]{2,1,0:T(8,128)(2,1)S(1)} %get-tuple-element.80), channel_id=1, source_target_pairs={{0,8},{4,12},{8,0},{12,4},{16,24},{20,28},{24,16},{28,20},{1,9},{5... | collective-permute-start | bytes 884744 | tf_op jit(solution)/shard_map/ppermute | solution.py:34
  65.3 1.3 %collective-permute-start.30 = (bf16[2,96,768]{2,1,0:T(8,128)(2,1)S(1)}, bf16[2,96,768]{2,1,0:T(8,128)(2,1)S(1)}, u32[]{:S(2)}, u32[]{:S(2)}) collective-permute-start(bf16[2,96,768]{2,1,0:T(8,128)(2,1)S(1)} %get-tuple-element.81), channel_id=1, source_target_pairs={{0,12},{4,8},{8,4},{12,0},{16,28},{20,24},{24,20},{28,16},{1,13},{... | collective-permute-start | bytes 884744 | tf_op jit(solution)/shard_map/ppermute | solution.py:34
  66.6 1.4 %act_rows.2.refs_6_.refs_1_ = bf16[128,1536]{1,0:T(8,128)(2,1)S(1)} custom-call(s32[6]{0:T(128)S(1)} %stack.27.refs_0_, bf16[256,384]{1,0:T(8,128)(2,1)S(1)} %get-tuple-element.67.refs_3_.refs_1_, bf16[256,384]{1,0:T(8,128)(2,1)S(1)} %collective-permute-done.13.refs_3_.refs_2_, bf16[3,1536,384]{2,1,0:T(8,128)(2,1)S(1)} %bitcast.13, ...), custom_call_target="tpu_custom_call" | custom-call | flops 1 | bytes 1 | tf_op jit(solution)/shard_map/act_rows/pallas_call | solution.py:200
  68.0 1.4 %act_rows.3.refs_5_.refs_3_ = bf16[128,1536]{1,0:T(8,128)(2,1)S(1)} custom-call(s32[6]{0:T(128)S(1)} %stack.27.refs_0_, bf16[256,384]{1,0:T(8,128)(2,1)S(1)} %get-tuple-element.67.refs_3_.refs_1_, bf16[256,384]{1,0:T(8,128)(2,1)S(1)} %collective-permute-done.13.refs_3_.refs_2_, bf16[3,1536,384]{2,1,0:T(8,128)(2,1)S(1)} %bitcast.14, ...), custom_call_target="tpu_custom_call" | custom-call | flops 1 | bytes 1 | tf_op jit(solution)/shard_map/act_rows/pallas_call | solution.py:200
  69.4 1.3 %collective-permute-start.26 = (bf16[128,1536]{1,0:T(8,128)(2,1)S(1)}, bf16[128,1536]{1,0:T(8,128)(2,1)S(1)}, u32[]{:S(2)}, u32[]{:S(2)}) collective-permute-start(bf16[128,1536]{1,0:T(8,128)(2,1)S(1)} %act_rows.3.refs_5_.refs_3_), channel_id=1, source_target_pairs={{0,2},{2,0},{1,3},{3,1},{4,6},{6,4},{5,7},{7,5},{8,10},{10,8},{9,1... | collective-permute-start | bytes 1179656 | tf_op jit(solution)/shard_map/ppermute | solution.py:34
  72.1 1.8 %collective-permute-done.29.refs_3_ = bf16[2,96,768]{2,1,0:T(8,128)(2,1)S(1)} collective-permute-done((bf16[2,96,768]{2,1,0:T(8,128)(2,1)S(1)}, bf16[2,96,768]{2,1,0:T(8,128)(2,1)S(1)}, u32[]{:S(2)}, u32[]{:S(2)}) %collective-permute-start.29) | collective-permute-done | bytes 294944 | tf_op jit(solution)/shard_map/ppermute | solution.py:34
  73.8 5.9 %collective-permute-done.30.refs_4_ = bf16[2,96,768]{2,1,0:T(8,128)(2,1)S(1)} collective-permute-done((bf16[2,96,768]{2,1,0:T(8,128)(2,1)S(1)}, bf16[2,96,768]{2,1,0:T(8,128)(2,1)S(1)}, u32[]{:S(2)}, u32[]{:S(2)}) %collective-permute-start.30) | collective-permute-done | bytes 294944 | tf_op jit(solution)/shard_map/ppermute | solution.py:34
  80.4 2.5 %collective-permute-start.31 = (bf16[96,768]{1,0:T(8,128)(2,1)S(1)}, bf16[96,768]{1,0:T(8,128)(2,1)S(1)}, u32[]{:S(2)}, u32[]{:S(2)}) collective-permute-start(bf16[96,768]{1,0:T(8,128)(2,1)S(1)} %get-tuple-element.83), channel_id=1, source_target_pairs={{0,16},{4,20},{8,24},{12,28},{16,0},{20,4},{24,8},{28,12},{1,17},{... | collective-permute-start | bytes 442376 | tf_op jit(solution)/shard_map/ppermute | solution.py:34
  82.9 5.2 %collective-permute-done.25.refs_2_ = bf16[128,1536]{1,0:T(8,128)(2,1)S(1)} collective-permute-done((bf16[128,1536]{1,0:T(8,128)(2,1)S(1)}, bf16[128,1536]{1,0:T(8,128)(2,1)S(1)}, u32[]{:S(2)}, u32[]{:S(2)}) %collective-permute-start.25) | collective-permute-done | bytes 393248 | tf_op jit(solution)/shard_map/ppermute | solution.py:34
  88.1 1.3 %collective-permute-done.31.refs_8_ = bf16[96,768]{1,0:T(8,128)(2,1)S(1)} collective-permute-done((bf16[96,768]{1,0:T(8,128)(2,1)S(1)}, bf16[96,768]{1,0:T(8,128)(2,1)S(1)}, u32[]{:S(2)}, u32[]{:S(2)}) %collective-permute-start.31) | collective-permute-done | bytes 147488 | tf_op jit(solution)/shard_map/ppermute | solution.py:34
  89.4 1.7 %finish.1 = (f32[3,96,384]{2,1,0:T(8,128)}, f32[96,384]{1,0:T(8,128)}, bf16[256,1536]{1,0:T(8,128)(2,1)}) custom-call(s32[6]{0:T(128)S(1)} %stack.27.refs_0_, bf16[128,1536]{1,0:T(8,128)(2,1)S(1)} %act_rows.2.refs_6_.refs_1_, bf16[128,1536]{1,0:T(8,128)(2,1)S(1)} %collective-permute-done.25.refs_2_, bf16[128,1536]{1,0:T(8,128)(2,1)S(1)} %act_rows.3.refs_5_.refs_3_, ...), custom_call_target="tpu_custom_call" | custom-call | flops 1 | bytes 1 | tf_op jit(solution)/shard_map/finish/pallas_call | solution.py:200
  (61 shorter events, 11.9 us)
Async XLA Ops:
  0.6 27.6 %collective-permute-start.3 = (bf16[768,1920]{1,0:T(8,128)(2,1)}, bf16[768,1920]{1,0:T(8,128)(2,1)S(1)}, u32[]{:S(2)}, u32[]{:S(2)}) collective-permute-start(bf16[768,1920]{1,0:T(8,128)(2,1)} %refs_3_.3), channel_id=1, source_target_pairs={{0,1},{1,0},{2,3},{3,2},{4,5},{5,4},{6,7},{7,6},{8,9},{9,8},{10,11... | collective-permute-start | bytes 8847368 | tf_op jit(solution)/shard_map/ppermute | solution.py:34
  3.1 18.8 %collective-permute-start.1 = (bf16[768,384]{1,0:T(8,128)(2,1)S(1)}, bf16[768,384]{1,0:T(8,128)(2,1)S(1)}, u32[]{:S(2)}, u32[]{:S(2)}) collective-permute-start(bf16[768,384]{1,0:T(8,128)(2,1)S(1)} %piece_of.1.refs_3_), channel_id=1, source_target_pairs={{0,2},{2,0},{1,3},{3,1},{4,6},{6,4},{5,7},{7,5},{8,10},{10,8},{9,1... | collective-permute-start | bytes 1769480 | tf_op jit(solution)/shard_map/ppermute | solution.py:34
  8.6 12.2 %collective-permute-start = (bf16[256,384]{1,0:T(8,128)(2,1)S(1)}, bf16[256,384]{1,0:T(8,128)(2,1)S(1)}, u32[]{:S(2)}, u32[]{:S(2)}) collective-permute-start(bf16[256,384]{1,0:T(8,128)(2,1)S(1)} %get-tuple-element.47), channel_id=1, source_target_pairs={{0,16},{4,20},{8,24},{12,28},{16,0},{20,4},{24,8},{28,12},{1,17},{... | collective-permute-start | bytes 589832 | tf_op jit(solution)/shard_map/ppermute | solution.py:481
  21.4 6.2 %collective-permute-start.2 = (bf16[256,384]{1,0:T(8,128)(2,1)S(1)}, bf16[256,384]{1,0:T(8,128)(2,1)S(1)}, u32[]{:S(2)}, u32[]{:S(2)}) collective-permute-start(bf16[256,384]{1,0:T(8,128)(2,1)S(1)} %get-tuple-element.51), channel_id=1, source_target_pairs={{0,2},{2,0},{1,3},{3,1},{4,6},{6,4},{5,7},{7,5},{8,10},{10,8},{9,1... | collective-permute-start | bytes 589832 | tf_op jit(solution)/shard_map/ppermute | solution.py:34
  23.9 3.8 %collective-permute-start.4 = (bf16[256,384]{1,0:T(8,128)(2,1)S(1)}, bf16[256,384]{1,0:T(8,128)(2,1)S(1)}, u32[]{:S(2)}, u32[]{:S(2)}) collective-permute-start(bf16[256,384]{1,0:T(8,128)(2,1)S(1)} %get-tuple-element.52), channel_id=1, source_target_pairs={{0,1},{1,0},{2,3},{3,2},{4,5},{5,4},{6,7},{7,6},{8,9},{9,8},{10,11... | collective-permute-start | bytes 589832 | tf_op jit(solution)/shard_map/ppermute | solution.py:34
  24.0 4.2 %collective-permute-start.5 = (bf16[256,384]{1,0:T(8,128)(2,1)S(1)}, bf16[256,384]{1,0:T(8,128)(2,1)S(1)}, u32[]{:S(2)}, u32[]{:S(2)}) collective-permute-start(bf16[256,384]{1,0:T(8,128)(2,1)S(1)} %get-tuple-element.53), channel_id=1, source_target_pairs={{0,1},{1,0},{2,3},{3,2},{4,5},{5,4},{6,7},{7,6},{8,9},{9,8},{10,11... | collective-permute-start | bytes 589832 | tf_op jit(solution)/shard_map/ppermute | solution.py:34
  24.5 3.7 %collective-permute-start.6 = (bf16[256,384]{1,0:T(8,128)(2,1)S(1)}, bf16[256,384]{1,0:T(8,128)(2,1)S(1)}, u32[]{:S(2)}, u32[]{:S(2)}) collective-permute-start(bf16[256,384]{1,0:T(8,128)(2,1)S(1)} %get-tuple-element.54), channel_id=1, source_target_pairs={{0,1},{1,0},{2,3},{3,2},{4,5},{5,4},{6,7},{7,6},{8,9},{9,8},{10,11... | collective-permute-start | bytes 589832 | tf_op jit(solution)/shard_map/ppermute | solution.py:34
  27.7 7.5 %collective-permute-start.8 = (bf16[256,384]{1,0:T(8,128)(2,1)S(1)}, bf16[256,384]{1,0:T(8,128)(2,1)S(1)}, u32[]{:S(2)}, u32[]{:S(2)}) collective-permute-start(bf16[256,384]{1,0:T(8,128)(2,1)S(1)} %collective-permute-done.2.refs_2_), channel_id=1, source_target_pairs={{0,1},{1,0},{2,3},{3,2},{4,5},{5,4},{6,7},{7,6},{8,9},{9,8},{10,11... | collective-permute-start | bytes 589832 | tf_op jit(solution)/shard_map/ppermute | solution.py:34
  27.7 7.5 %collective-permute-start.9 = (bf16[256,384]{1,0:T(8,128)(2,1)S(1)}, bf16[256,384]{1,0:T(8,128)(2,1)S(1)}, u32[]{:S(2)}, u32[]{:S(2)}) collective-permute-start(bf16[256,384]{1,0:T(8,128)(2,1)S(1)} %get-tuple-element.59.refs_6_), channel_id=1, source_target_pairs={{0,1},{1,0},{2,3},{3,2},{4,5},{5,4},{6,7},{7,6},{8,9},{9,8},{10,11... | collective-permute-start | bytes 589832 | tf_op jit(solution)/shard_map/ppermute | solution.py:34
  34.3 6.9 %collective-permute-start.7 = (bf16[256,384]{1,0:T(8,128)(2,1)S(1)}, bf16[256,384]{1,0:T(8,128)(2,1)S(1)}, u32[]{:S(2)}, u32[]{:S(2)}) collective-permute-start(bf16[256,384]{1,0:T(8,128)(2,1)S(1)} %get-tuple-element.56), channel_id=1, source_target_pairs={{0,2},{2,0},{1,3},{3,1},{4,6},{6,4},{5,7},{7,5},{8,10},{10,8},{9,1... | collective-permute-start | bytes 589832 | tf_op jit(solution)/shard_map/ppermute | solution.py:34
  36.1 2.4 %collective-permute-start.10 = (bf16[3,96,256]{2,1,0:T(8,128)(2,1)S(1)}, bf16[3,96,256]{2,1,0:T(8,128)(2,1)S(1)}, u32[]{:S(2)}, u32[]{:S(2)}) collective-permute-start(bf16[3,96,256]{2,1,0:T(8,128)(2,1)S(1)} %get-tuple-element.63), channel_id=1, source_target_pairs={{0,1},{1,0},{2,3},{3,2},{4,5},{5,4},{6,7},{7,6},{8,9},{9,8},{10,11... | collective-permute-start | bytes 442376 | tf_op jit(solution)/shard_map/ppermute | solution.py:34
  36.2 2.4 %collective-permute-start.11 = (bf16[3,96,256]{2,1,0:T(8,128)(2,1)S(1)}, bf16[3,96,256]{2,1,0:T(8,128)(2,1)S(1)}, u32[]{:S(2)}, u32[]{:S(2)}) collective-permute-start(bf16[3,96,256]{2,1,0:T(8,128)(2,1)S(1)} %get-tuple-element.64), channel_id=1, source_target_pairs={{0,1},{1,0},{2,3},{3,2},{4,5},{5,4},{6,7},{7,6},{8,9},{9,8},{10,11... | collective-permute-start | bytes 442376 | tf_op jit(solution)/shard_map/ppermute | solution.py:34
  36.7 6.6 %collective-permute-start.14 = (bf16[8,96,256]{2,1,0:T(8,128)(2,1)S(1)}, bf16[8,96,256]{2,1,0:T(8,128)(2,1)S(1)}, u32[]{:S(2)}, u32[]{:S(2)}) collective-permute-start(bf16[8,96,256]{2,1,0:T(8,128)(2,1)S(1)} %get-tuple-element.69), channel_id=1, source_target_pairs={{0,1},{1,0},{2,3},{3,2},{4,5},{5,4},{6,7},{7,6},{8,9},{9,8},{10,11... | collective-permute-start | bytes 1179656 | tf_op jit(solution)/shard_map/ppermute | solution.py:34
  36.8 1.8 %collective-permute-start.12 = (bf16[2,96,256]{2,1,0:T(8,128)(2,1)S(1)}, bf16[2,96,256]{2,1,0:T(8,128)(2,1)S(1)}, u32[]{:S(2)}, u32[]{:S(2)}) collective-permute-start(bf16[2,96,256]{2,1,0:T(8,128)(2,1)S(1)} %get-tuple-element.65), channel_id=1, source_target_pairs={{0,1},{1,0},{2,3},{3,2},{4,5},{5,4},{6,7},{7,6},{8,9},{9,8},{10,11... | collective-permute-start | bytes 294920 | tf_op jit(solution)/shard_map/ppermute | solution.py:34
  41.8 19.7 %collective-permute-start.15 = (bf16[8,96,384]{2,1,0:T(8,128)(2,1)S(1)}, bf16[8,96,384]{2,1,0:T(8,128)(2,1)S(1)}, u32[]{:S(2)}, u32[]{:S(2)}) collective-permute-start(bf16[8,96,384]{2,1,0:T(8,128)(2,1)S(1)} %get-tuple-element.71), channel_id=1, source_target_pairs={{0,2},{2,0},{1,3},{3,1},{4,6},{6,4},{5,7},{7,5},{8,10},{10,8},{9,1... | collective-permute-start | bytes 1769480 | tf_op jit(solution)/shard_map/ppermute | solution.py:34
  42.7 10.8 %collective-permute-start.13 = (bf16[256,384]{1,0:T(8,128)(2,1)S(1)}, bf16[256,384]{1,0:T(8,128)(2,1)S(1)}, u32[]{:S(2)}, u32[]{:S(2)}) collective-permute-start(bf16[256,384]{1,0:T(8,128)(2,1)S(1)} %get-tuple-element.67.refs_3_.refs_1_), channel_id=1, source_target_pairs={{0,16},{4,20},{8,24},{12,28},{16,0},{20,4},{24,8},{28,12},{1,17},{... | collective-permute-start | bytes 589832 | tf_op jit(solution)/shard_map/ppermute | solution.py:551
  42.7 1.3 %collective-permute-start.18 = (bf16[64,384]{1,0:T(8,128)(2,1)S(1)}, bf16[64,384]{1,0:T(8,128)(2,1)S(1)}, u32[]{:S(2)}, u32[]{:S(2)}) collective-permute-start(bf16[64,384]{1,0:T(8,128)(2,1)S(1)} %get-tuple-element.90), channel_id=1, source_target_pairs={{0,1},{1,0},{2,3},{3,2},{4,5},{5,4},{6,7},{7,6},{8,9},{9,8},{10,11... | collective-permute-start | bytes 147464 | tf_op jit(solution)/shard_map/ppermute | solution.py:34
  42.8 1.4 %collective-permute-start.19 = (bf16[64,384]{1,0:T(8,128)(2,1)S(1)}, bf16[64,384]{1,0:T(8,128)(2,1)S(1)}, u32[]{:S(2)}, u32[]{:S(2)}) collective-permute-start(bf16[64,384]{1,0:T(8,128)(2,1)S(1)} %get-tuple-element.89), channel_id=1, source_target_pairs={{0,1},{1,0},{2,3},{3,2},{4,5},{5,4},{6,7},{7,6},{8,9},{9,8},{10,11... | collective-permute-start | bytes 147464 | tf_op jit(solution)/shard_map/ppermute | solution.py:34
  43.3 1.2 %collective-permute-start.20 = (bf16[64,384]{1,0:T(8,128)(2,1)S(1)}, bf16[64,384]{1,0:T(8,128)(2,1)S(1)}, u32[]{:S(2)}, u32[]{:S(2)}) collective-permute-start(bf16[64,384]{1,0:T(8,128)(2,1)S(1)} %get-tuple-element.88), channel_id=1, source_target_pairs={{0,1},{1,0},{2,3},{3,2},{4,5},{5,4},{6,7},{7,6},{8,9},{9,8},{10,11... | collective-permute-start | bytes 147464 | tf_op jit(solution)/shard_map/ppermute | solution.py:34
  44.0 1.2 %collective-permute-start.21 = (bf16[64,384]{1,0:T(8,128)(2,1)S(1)}, bf16[64,384]{1,0:T(8,128)(2,1)S(1)}, u32[]{:S(2)}, u32[]{:S(2)}) collective-permute-start(bf16[64,384]{1,0:T(8,128)(2,1)S(1)} %get-tuple-element.87), channel_id=1, source_target_pairs={{0,1},{1,0},{2,3},{3,2},{4,5},{5,4},{6,7},{7,6},{8,9},{9,8},{10,11... | collective-permute-start | bytes 147464 | tf_op jit(solution)/shard_map/ppermute | solution.py:34
  46.4 7.3 %collective-permute-start.22 = (bf16[2,96,384]{2,1,0:T(8,128)(2,1)S(1)}, bf16[2,96,384]{2,1,0:T(8,128)(2,1)S(1)}, u32[]{:S(2)}, u32[]{:S(2)}) collective-permute-start(bf16[2,96,384]{2,1,0:T(8,128)(2,1)S(1)} %get-tuple-element.73), channel_id=1, source_target_pairs={{0,4},{4,0},{8,12},{12,8},{16,20},{20,16},{24,28},{28,24},{1,5},{5... | collective-permute-start | bytes 442376 | tf_op jit(solution)/shard_map/ppermute | solution.py:34
  47.7 9.3 %collective-permute-start.23 = (bf16[2,96,384]{2,1,0:T(8,128)(2,1)S(1)}, bf16[2,96,384]{2,1,0:T(8,128)(2,1)S(1)}, u32[]{:S(2)}, u32[]{:S(2)}) collective-permute-start(bf16[2,96,384]{2,1,0:T(8,128)(2,1)S(1)} %get-tuple-element.74), channel_id=1, source_target_pairs={{0,8},{4,12},{8,0},{12,4},{16,24},{20,28},{24,16},{28,20},{1,9},{5... | collective-permute-start | bytes 442376 | tf_op jit(solution)/shard_map/ppermute | solution.py:34
  52.4 8.4 %collective-permute-start.24 = (bf16[2,96,384]{2,1,0:T(8,128)(2,1)S(1)}, bf16[2,96,384]{2,1,0:T(8,128)(2,1)S(1)}, u32[]{:S(2)}, u32[]{:S(2)}) collective-permute-start(bf16[2,96,384]{2,1,0:T(8,128)(2,1)S(1)} %get-tuple-element.75), channel_id=1, source_target_pairs={{0,12},{4,8},{8,4},{12,0},{16,28},{20,24},{24,20},{28,16},{1,13},{... | collective-permute-start | bytes 442376 | tf_op jit(solution)/shard_map/ppermute | solution.py:34
  53.6 7.9 %collective-permute-start.16 = (bf16[128,384]{1,0:T(8,128)(2,1)S(1)}, bf16[128,384]{1,0:T(8,128)(2,1)S(1)}, u32[]{:S(2)}, u32[]{:S(2)}) collective-permute-start(bf16[128,384]{1,0:T(8,128)(2,1)S(1)} %get-tuple-element.92), channel_id=1, source_target_pairs={{0,1},{1,0},{2,3},{3,2},{4,5},{5,4},{6,7},{7,6},{8,9},{9,8},{10,11... | collective-permute-start | bytes 294920 | tf_op jit(solution)/shard_map/ppermute | solution.py:34
  53.6 7.8 %collective-permute-start.17 = (bf16[128,384]{1,0:T(8,128)(2,1)S(1)}, bf16[128,384]{1,0:T(8,128)(2,1)S(1)}, u32[]{:S(2)}, u32[]{:S(2)}) collective-permute-start(bf16[128,384]{1,0:T(8,128)(2,1)S(1)} %get-tuple-element.91), channel_id=1, source_target_pairs={{0,1},{1,0},{2,3},{3,2},{4,5},{5,4},{6,7},{7,6},{8,9},{9,8},{10,11... | collective-permute-start | bytes 294920 | tf_op jit(solution)/shard_map/ppermute | solution.py:34
  61.4 9.3 %collective-permute-start.27 = (bf16[96,384]{1,0:T(8,128)(2,1)S(1)}, bf16[96,384]{1,0:T(8,128)(2,1)S(1)}, u32[]{:S(2)}, u32[]{:S(2)}) collective-permute-start(bf16[96,384]{1,0:T(8,128)(2,1)S(1)} %get-tuple-element.78), channel_id=1, source_target_pairs={{0,16},{4,20},{8,24},{12,28},{16,0},{20,4},{24,8},{28,12},{1,17},{... | collective-permute-start | bytes 221192 | tf_op jit(solution)/shard_map/ppermute | solution.py:34
  63.0 9.0 %collective-permute-start.28 = (bf16[2,96,768]{2,1,0:T(8,128)(2,1)S(1)}, bf16[2,96,768]{2,1,0:T(8,128)(2,1)S(1)}, u32[]{:S(2)}, u32[]{:S(2)}) collective-permute-start(bf16[2,96,768]{2,1,0:T(8,128)(2,1)S(1)} %get-tuple-element.79), channel_id=1, source_target_pairs={{0,4},{4,0},{8,12},{12,8},{16,20},{20,16},{24,28},{28,24},{1,5},{5... | collective-permute-start | bytes 884744 | tf_op jit(solution)/shard_map/ppermute | solution.py:34
  63.6 10.2 %collective-permute-start.29 = (bf16[2,96,768]{2,1,0:T(8,128)(2,1)S(1)}, bf16[2,96,768]{2,1,0:T(8,128)(2,1)S(1)}, u32[]{:S(2)}, u32[]{:S(2)}) collective-permute-start(bf16[2,96,768]{2,1,0:T(8,128)(2,1)S(1)} %get-tuple-element.80), channel_id=1, source_target_pairs={{0,8},{4,12},{8,0},{12,4},{16,24},{20,28},{24,16},{28,20},{1,9},{5... | collective-permute-start | bytes 884744 | tf_op jit(solution)/shard_map/ppermute | solution.py:34
  65.3 14.4 %collective-permute-start.30 = (bf16[2,96,768]{2,1,0:T(8,128)(2,1)S(1)}, bf16[2,96,768]{2,1,0:T(8,128)(2,1)S(1)}, u32[]{:S(2)}, u32[]{:S(2)}) collective-permute-start(bf16[2,96,768]{2,1,0:T(8,128)(2,1)S(1)} %get-tuple-element.81), channel_id=1, source_target_pairs={{0,12},{4,8},{8,4},{12,0},{16,28},{20,24},{24,20},{28,16},{1,13},{... | collective-permute-start | bytes 884744 | tf_op jit(solution)/shard_map/ppermute | solution.py:34
  69.4 13.5 %collective-permute-start.26 = (bf16[128,1536]{1,0:T(8,128)(2,1)S(1)}, bf16[128,1536]{1,0:T(8,128)(2,1)S(1)}, u32[]{:S(2)}, u32[]{:S(2)}) collective-permute-start(bf16[128,1536]{1,0:T(8,128)(2,1)S(1)} %act_rows.3.refs_5_.refs_3_), channel_id=1, source_target_pairs={{0,2},{2,0},{1,3},{3,1},{4,6},{6,4},{5,7},{7,5},{8,10},{10,8},{9,1... | collective-permute-start | bytes 1179656 | tf_op jit(solution)/shard_map/ppermute | solution.py:34
  70.7 17.4 %collective-permute-start.25 = (bf16[128,1536]{1,0:T(8,128)(2,1)S(1)}, bf16[128,1536]{1,0:T(8,128)(2,1)S(1)}, u32[]{:S(2)}, u32[]{:S(2)}) collective-permute-start(bf16[128,1536]{1,0:T(8,128)(2,1)S(1)} %act_rows.2.refs_6_.refs_1_), channel_id=1, source_target_pairs={{0,2},{2,0},{1,3},{3,1},{4,6},{6,4},{5,7},{7,5},{8,10},{10,8},{9,1... | collective-permute-start | bytes 1179656 | tf_op jit(solution)/shard_map/ppermute | solution.py:34
  80.4 9.0 %collective-permute-start.31 = (bf16[96,768]{1,0:T(8,128)(2,1)S(1)}, bf16[96,768]{1,0:T(8,128)(2,1)S(1)}, u32[]{:S(2)}, u32[]{:S(2)}) collective-permute-start(bf16[96,768]{1,0:T(8,128)(2,1)S(1)} %get-tuple-element.83), channel_id=1, source_target_pairs={{0,16},{4,20},{8,24},{12,28},{16,0},{20,4},{24,8},{28,12},{1,17},{... | collective-permute-start | bytes 442376 | tf_op jit(solution)/shard_map/ppermute | solution.py:34
  (5 other events, 68.3 us)

commit v10 on v9

--- a/solution.py
+++ b/solution.py
@@ -372,7 +372,7 @@
 
 
 def middle_products(place, acts, other_acts, field, *rest):
-    *pieces, keep, across, along, both, other = rest
+    *pieces, keep, both, across, along, other = rest
     joined(pieces, other)
 
     def values(left):
@@ -383,7 +383,7 @@
 
 def late_products(
     place, acts, other_acts, moved, outs, other_outs, hidden, far_hidden, shares, first, second,
-    keep, across, along, both, other_moved,
+    keep, both, across, along, other_moved,
 ):
     joined((first, second), other_moved)
 
@@ -397,14 +397,13 @@
     each_chip(place, keep, along, across, both, values)
 
 
-def act_part(first):
-    def act_rows(place, middle_grad, moved, weight, part, slope, give):
-        rows = slice(first, first + give.shape[0])
-        value = dot(middle_grad[rows, :], weight[1], NT)
-        value += dot(moved[rows, :], weight[place[0]], NT)
-        give[...] = (part[rows, :].astype(F32) + value * slope[rows, :]).astype(BF16)
-
-    return act_rows
+def act_part(place, middle_grad, moved, weight, part, slope, *halves):
+    value = dot(middle_grad[...], weight[1], NT) + dot(moved[...], weight[place[0]], NT)
+    value = wide(part) + value * slope[...]
+    first = 0
+    for out in halves:
+        out[...] = value[first : first + out.shape[0]].astype(BF16)
+        first += out.shape[0]
 
 
 def over_chips(at, kept, *arrived):
@@ -526,7 +525,7 @@
         keep, *gives = kernel_call(
             kernel, [(shape, F32)] + [(shape, BF16)] * 3, [place, *ins], after, scratch
         )
-        return keep, *[flip(value, "seq", step) for value, step in zip(gives, (1, 2, 3))]
+        return keep, *[flip(value, "seq", step) for value, step in zip(gives, (3, 1, 2))]
 
     third = -(-groups // 3)
     outs, far_other, *outs_given = kernel_call(
@@ -575,8 +574,7 @@
         scratch=[pltpu.VMEM((rows, width), BF16)],
     )
     ins = [place, middle_grad, moved, taps, part, slope_feat]
-    (one,) = kernel_call(act_part(0), [((half, channels), BF16)], ins, [late[0]])
-    (two,) = kernel_call(act_part(half), [((half, channels), BF16)], ins, [one])
+    one, two = kernel_call(act_part, [((half, channels), BF16)] * 2, ins, [late[0]])
     kept, got = halved(late, 2 * width, [two, mid_got])
     dilated_grad, point_grad, input_grad = kernel_call(
         finish,

time: 91.2 us -> 91.1 us (level)
  waiting for transfers between devices: 38.6 us -> 40.7 us
  Pallas kernels: 25.6 us -> 24.3 us
  starting transfers between devices: 25.9 us -> 24.9 us
    ppermute x30, waiting for transfers between devices: 29 us -> 31.2 us  [flip(): return lax.ppermute(value, axis, [(i, i ^ step) for i in range(count)])]
    pallas_call x16 -> x15, Pallas kernels: 25.6 us -> 24.3 us  [kernel_call(): pl.pallas_call(run, out_shape=[jax.ShapeDtypeStruct(s, d) for s, d in out...]
    ppermute x30, starting transfers between devices: 23.2 us -> 22.2 us  [flip(): return lax.ppermute(value, axis, [(i, i ^ step) for i in range(count)])]
  transfers between devices with their start and end apart: 32 -> 32, of which waited for: 15 -> 15; matrix products, arithmetic and copies ran while one was open for 0% -> 0% of each run, Pallas kernels for 26% -> 25%
where the time goes in v10:
time: 91.1 us; the launch traced here: 91 us
  waiting for transfers between devices  40.7 us (45%)
  starting transfers between devices  24.9 us (27%)
  Pallas kernels  24.3 us (27%)
    ppermute x30, waiting for transfers between devices, flip(): return lax.ppermute(value, axis, [(i, i ^ step) for i in range(count)])  31.2 us
    pallas_call x15, Pallas kernels, kernel_call(): pl.pallas_call(run, out_shape=[jax.ShapeDtypeStruct(s, d) for s, d in out...  24.3 us
    ppermute x30, starting transfers between devices, flip(): return lax.ppermute(value, axis, [(i, i ^ step) for i in range(count)])  22.2 us
    ppermute x1, waiting for transfers between devices, body(): arrived = lax.ppermute(term, 'seq', pairs)  8.38 us
    ppermute x1, starting transfers between devices, body(): arrived = lax.ppermute(term, 'seq', pairs)  2.65 us
  transfers between devices with their start and end apart: 32, of which 15 were waited for; matrix products, arithmetic and copies ran while one was open for 0% of the time, Pallas kernels for 25%

profile of v10, /device:TPU:0, one launch (start us, length us, event | category | flops | bytes accessed | tf_op | source)
XLA Modules:
  0.0 91.0 jit_solution(10152466925452544244)
XLA Ops:
  1.2 1.9 %piece_of.1.refs_3_ = bf16[768,384]{1,0:T(8,128)(2,1)S(1)} custom-call(s32[6]{0:T(128)S(1)} %stack.27.refs_0_, bf16[1536,384]{1,0:T(8,128)(2,1)} %refs_6_.1), custom_call_target="tpu_custom_call" | custom-call | flops 1 | bytes 1 | tf_op jit(solution)/shard_map/piece_of/pallas_call | solution.py:200
  3.1 2.6 %collective-permute-start.1 = (bf16[768,384]{1,0:T(8,128)(2,1)S(1)}, bf16[768,384]{1,0:T(8,128)(2,1)S(1)}, u32[]{:S(2)}, u32[]{:S(2)}) collective-permute-start(bf16[768,384]{1,0:T(8,128)(2,1)S(1)} %piece_of.1.refs_3_), channel_id=1, source_target_pairs={{0,2},{2,0},{1,3},{3,1},{4,6},{6,4},{5,7},{7,5},{8,10},{10,8},{9,1... | collective-permute-start | bytes 1769480 | tf_op jit(solution)/shard_map/ppermute | solution.py:34
  5.7 2.9 %outer_term.1 = (bf16[256,1536]{1,0:T(8,128)(2,1)S(1)}, bf16[256,384]{1,0:T(8,128)(2,1)S(1)}) custom-call(s32[6]{0:T(128)S(1)} %stack.27.refs_0_, bf16[256,1536]{1,0:T(8,128)(2,1)} %bitcast.14, bf16[3,1536,384]{2,1,0:T(8,128)(2,1)} %bitcast.11, bf16[768,384]{1,0:T(8,128)(2,1)S(1)} %piece_of.1.refs_3_), custom_call_target="tpu_custom_call" | custom-call | flops 1 | bytes 1 | tf_op jit(solution)/shard_map/outer_term/pallas_call | solution.py:200
  8.6 2.7 %collective-permute-start = (bf16[256,384]{1,0:T(8,128)(2,1)S(1)}, bf16[256,384]{1,0:T(8,128)(2,1)S(1)}, u32[]{:S(2)}, u32[]{:S(2)}) collective-permute-start(bf16[256,384]{1,0:T(8,128)(2,1)S(1)} %get-tuple-element.49), channel_id=1, source_target_pairs={{0,16},{4,20},{8,24},{12,28},{16,0},{20,4},{24,8},{28,12},{1,17},{... | collective-permute-start | bytes 589832 | tf_op jit(solution)/shard_map/ppermute | solution.py:480
  11.3 1.1 %middle_term.1 = (f32[256,384]{1,0:T(8,128)S(1)}, bf16[8,96,256]{2,1,0:T(8,128)(2,1)S(1)}, bf16[8,96,256]{2,1,0:T(8,128)(2,1)S(1)}) custom-call(s32[6]{0:T(128)S(1)} %stack.27.refs_0_, bf16[256,1536]{1,0:T(8,128)(2,1)S(1)} %get-tuple-element.47.refs_1_, bf16[3,1536,384]{2,1,0:T(8,128)(2,1)S(1)} %bitcast.12), custom_call_target="tpu_custom_call" | custom-call | flops 1 | bytes 1 | tf_op jit(solution)/shard_map/middle_term/pallas_call | solution.py:200
  12.4 8.4 %collective-permute-done.refs_2_ = bf16[256,384]{1,0:T(8,128)(2,1)S(1)} collective-permute-done((bf16[256,384]{1,0:T(8,128)(2,1)S(1)}, bf16[256,384]{1,0:T(8,128)(2,1)S(1)}, u32[]{:S(2)}, u32[]{:S(2)}) %collective-permute-start) | collective-permute-done | bytes 196640 | tf_op jit(solution)/shard_map/ppermute | solution.py:480
  22.0 1.9 %own_hidden.1 = (bf16[256,384]{1,0:T(8,128)(2,1)S(1)}, f32[256,1536]{1,0:T(8,128)S(1)}, f32[256,384]{1,0:T(8,128)S(1)}, f32[256,1536]{1,0:T(8,128)S(1)}, bf16[25...) custom-call(s32[6]{0:T(128)S(1)} %stack.27.refs_0_, ...), custom_call_target="tpu_custom_call" | custom-call | flops 1 | bytes 1 | tf_op jit(solution)/shard_map/own_hidden/pallas_call | solution.py:200
  24.6 3.1 %collective-permute-done.2.refs_2_ = bf16[256,384]{1,0:T(8,128)(2,1)S(1)} collective-permute-done((bf16[256,384]{1,0:T(8,128)(2,1)S(1)}, bf16[256,384]{1,0:T(8,128)(2,1)S(1)}, u32[]{:S(2)}, u32[]{:S(2)}) %collective-permute-start.2) | collective-permute-done | bytes 196640 | tf_op jit(solution)/shard_map/ppermute | solution.py:34
  28.2 6.1 %tracks.1 = (bf16[256,1536]{1,0:T(8,128)(2,1)S(1)}, bf16[256,384]{1,0:T(8,128)(2,1)S(1)}, f32[256,384]{1,0:T(8,128)S(1)}, bf16[256,384]{1,0:T(8,128)(2,1)S(1)}) custom-call(s32[6]{0:T(128)S(1)} %stack.27.refs_0_, f32[256,1536]{1,0:T(8,128)S(1)} %get-tuple-element.52.refs_1_, bf16[256,384]{1,0:T(8,128)(2,1)S(1)} %collective-permute-done.2.refs_2_, ...), custom_call_target="tpu_custom_call" | custom-call | flops 1 | bytes 1 | tf_op jit(solution)/shard_map/tracks/pallas_call | solution.py:200
  34.3 0.9 collective-permute-start.7
  35.2 1.0 %turn_parts.1 = (bf16[8,96,256]{2,1,0:T(8,128)(2,1)S(1)}, bf16[256,384]{1,0:T(8,128)(2,1)S(1)}, bf16[3,96,256]{2,1,0:T(8,128)(2,1)S(1)}, bf16[3,96,256]{2,1,0:T(8,128)(2,1)S(1)}, bf16[2,96,256]{2,1,0:T(8,128)(2,1)S(1)}) custom-call(s32[6]{0:T(128)S(1)} %stack.27.refs_0_, bf16[256,1536]{1,0:T(8,128)(2,1)S(1)} %get-tuple-element.60.refs_1_.refs_4_, ...), custom_call_target="tpu_custom_call" | custom-call | flops 1 | bytes 1 | tf_op jit(solution)/shard_map/turn_parts/pallas_call | solution.py:200
  37.2 1.4 %collective-permute-done.12.refs_6_ = bf16[2,96,256]{2,1,0:T(8,128)(2,1)S(1)} collective-permute-done((bf16[2,96,256]{2,1,0:T(8,128)(2,1)S(1)}, bf16[2,96,256]{2,1,0:T(8,128)(2,1)S(1)}, u32[]{:S(2)}, u32[]{:S(2)}) %collective-permute-start.12) | collective-permute-done | bytes 98336 | tf_op jit(solution)/shard_map/ppermute | solution.py:34
  38.6 1.1 %other_points.1 = (bf16[8,96,384]{2,1,0:T(8,128)(2,1)S(1)}, bf16[8,96,256]{2,1,0:T(8,128)(2,1)S(1)}) custom-call(s32[6]{0:T(128)S(1)} %stack.27.refs_0_, bf16[8,96,256]{2,1,0:T(8,128)(2,1)S(1)} %get-tuple-element.62.refs_1_.refs_4_, bf16[256,384]{1,0:T(8,128)(2,1)S(1)} %get-tuple-element.63.refs_2_, bf16[256,384]{1,0:T(8,128)(2,1)S(1)} %get-tuple-element.64.refs_3_, ...), custom_call_target="tpu_custom_call" | custom-call | flops 1 | bytes 1 | tf_op jit(solution)/shard_map/other_points/pallas_call | solution.py:200
  39.7 1.5 %collective-permute-done.7.refs_2_ = bf16[256,384]{1,0:T(8,128)(2,1)S(1)} collective-permute-done((bf16[256,384]{1,0:T(8,128)(2,1)S(1)}, bf16[256,384]{1,0:T(8,128)(2,1)S(1)}, u32[]{:S(2)}, u32[]{:S(2)}) %collective-permute-start.7) | collective-permute-done | bytes 196640 | tf_op jit(solution)/shard_map/ppermute | solution.py:34
  41.8 0.9 collective-permute-start.15
  44.5 0.7 collective-permute-done.21.refs_7_
  45.2 1.1 %middle_products.1 = (f32[2,96,384]{2,1,0:T(8,128)S(1)}, bf16[2,96,384]{2,1,0:T(8,128)(2,1)S(1)}, bf16[2,96,384]{2,1,0:T(8,128)(2,1)S(1)}, bf16[2,96,384]{2,1,0:T(8,128)(2,1)S(1)}) custom-call(s32[6]{0:T(128)S(1)} %stack.27.refs_0_, bf16[8,96,256]{2,1,0:T(8,128)(2,1)S(1)} %get-tuple-element.50.refs_3_.refs_1_, ...), custom_call_target="tpu_custom_call" | custom-call | flops 1 | bytes 1 | tf_op jit(solution)/shard_map/middle_products/pallas_call | solution.py:200
  46.4 5.5 %collective-permute-start.22 = (bf16[2,96,384]{2,1,0:T(8,128)(2,1)S(1)}, bf16[2,96,384]{2,1,0:T(8,128)(2,1)S(1)}, u32[]{:S(2)}, u32[]{:S(2)}) collective-permute-start(bf16[2,96,384]{2,1,0:T(8,128)(2,1)S(1)} %get-tuple-element.75), channel_id=1, source_target_pairs={{0,12},{4,8},{8,4},{12,0},{16,28},{20,24},{24,20},{28,16},{1,13},{... | collective-permute-start | bytes 442376 | tf_op jit(solution)/shard_map/ppermute | solution.py:34
  52.5 1.1 %collective-permute-done.13.refs_3_.refs_2_ = bf16[256,384]{1,0:T(8,128)(2,1)S(1)} collective-permute-done((bf16[256,384]{1,0:T(8,128)(2,1)S(1)}, bf16[256,384]{1,0:T(8,128)(2,1)S(1)}, u32[]{:S(2)}, u32[]{:S(2)}) %collective-permute-start.13) | collective-permute-done | bytes 196640 | tf_op jit(solution)/shard_map/ppermute | solution.py:550
  53.7 4.0 %collective-permute-done.22.refs_2_ = bf16[2,96,384]{2,1,0:T(8,128)(2,1)S(1)} collective-permute-done((bf16[2,96,384]{2,1,0:T(8,128)(2,1)S(1)}, bf16[2,96,384]{2,1,0:T(8,128)(2,1)S(1)}, u32[]{:S(2)}, u32[]{:S(2)}) %collective-permute-start.22) | collective-permute-done | bytes 147488 | tf_op jit(solution)/shard_map/ppermute | solution.py:34
  57.7 2.8 %collective-permute-done.23.refs_3_ = bf16[2,96,384]{2,1,0:T(8,128)(2,1)S(1)} collective-permute-done((bf16[2,96,384]{2,1,0:T(8,128)(2,1)S(1)}, bf16[2,96,384]{2,1,0:T(8,128)(2,1)S(1)}, u32[]{:S(2)}, u32[]{:S(2)}) %collective-permute-start.23) | collective-permute-done | bytes 147488 | tf_op jit(solution)/shard_map/ppermute | solution.py:34
  61.3 1.5 %late_products.1 = (f32[2,96,768]{2,1,0:T(8,128)S(1)}, bf16[2,96,768]{2,1,0:T(8,128)(2,1)S(1)}, bf16[2,96,768]{2,1,0:T(8,128)(2,1)S(1)}, bf16[2,96,768]{2,1,0:T(8,128)(2,1)S(1)}) custom-call(s32[6]{0:T(128)S(1)} %stack.27.refs_0_, bf16[8,96,256]{2,1,0:T(8,128)(2,1)S(1)} %get-tuple-element.50.refs_3_.refs_1_, ...), custom_call_target="tpu_custom_call" | custom-call | flops 1 | bytes 1 | tf_op jit(solution)/shard_map/late_products/pallas_call | solution.py:200
  62.8 2.1 %collective-permute-start.28 = (bf16[2,96,768]{2,1,0:T(8,128)(2,1)S(1)}, bf16[2,96,768]{2,1,0:T(8,128)(2,1)S(1)}, u32[]{:S(2)}, u32[]{:S(2)}) collective-permute-start(bf16[2,96,768]{2,1,0:T(8,128)(2,1)S(1)} %get-tuple-element.83), channel_id=1, source_target_pairs={{0,12},{4,8},{8,4},{12,0},{16,28},{20,24},{24,20},{28,16},{1,13},{... | collective-permute-start | bytes 884744 | tf_op jit(solution)/shard_map/ppermute | solution.py:34
  65.4 1.0 %collective-permute-start.30 = (bf16[2,96,768]{2,1,0:T(8,128)(2,1)S(1)}, bf16[2,96,768]{2,1,0:T(8,128)(2,1)S(1)}, u32[]{:S(2)}, u32[]{:S(2)}) collective-permute-start(bf16[2,96,768]{2,1,0:T(8,128)(2,1)S(1)} %get-tuple-element.85), channel_id=1, source_target_pairs={{0,8},{4,12},{8,0},{12,4},{16,24},{20,28},{24,16},{28,20},{1,9},{5... | collective-permute-start | bytes 884744 | tf_op jit(solution)/shard_map/ppermute | solution.py:34
  66.4 1.6 %act_part.1 = (bf16[128,1536]{1,0:T(8,128)(2,1)S(1)}, bf16[128,1536]{1,0:T(8,128)(2,1)S(1)}) custom-call(s32[6]{0:T(128)S(1)} %stack.27.refs_0_, bf16[256,384]{1,0:T(8,128)(2,1)S(1)} %get-tuple-element.69.refs_3_.refs_1_, bf16[256,384]{1,0:T(8,128)(2,1)S(1)} %collective-permute-done.13.refs_3_.refs_2_, bf16[3,1536,384]{2,1,0:T(8,128)(2,1)S(1)} %bitcast.13, ...), custom_call_target="tpu_custom_call" | custom-call | flops 1 | bytes 1 | tf_op jit(solution)/shard_map/act_part/pallas_call | solution.py:200
  67.9 1.5 %collective-permute-start.25 = (bf16[128,1536]{1,0:T(8,128)(2,1)S(1)}, bf16[128,1536]{1,0:T(8,128)(2,1)S(1)}, u32[]{:S(2)}, u32[]{:S(2)}) collective-permute-start(bf16[128,1536]{1,0:T(8,128)(2,1)S(1)} %get-tuple-element.80.refs_1_), channel_id=1, source_target_pairs={{0,2},{2,0},{1,3},{3,1},{4,6},{6,4},{5,7},{7,5},{8,10},{10,8},{9,1... | collective-permute-start | bytes 1179656 | tf_op jit(solution)/shard_map/ppermute | solution.py:34
  70.0 3.9 %collective-permute-done.28.refs_2_ = bf16[2,96,768]{2,1,0:T(8,128)(2,1)S(1)} collective-permute-done((bf16[2,96,768]{2,1,0:T(8,128)(2,1)S(1)}, bf16[2,96,768]{2,1,0:T(8,128)(2,1)S(1)}, u32[]{:S(2)}, u32[]{:S(2)}) %collective-permute-start.28) | collective-permute-done | bytes 294944 | tf_op jit(solution)/shard_map/ppermute | solution.py:34
  73.9 5.2 %collective-permute-done.29.refs_3_ = bf16[2,96,768]{2,1,0:T(8,128)(2,1)S(1)} collective-permute-done((bf16[2,96,768]{2,1,0:T(8,128)(2,1)S(1)}, bf16[2,96,768]{2,1,0:T(8,128)(2,1)S(1)}, u32[]{:S(2)}, u32[]{:S(2)}) %collective-permute-start.29) | collective-permute-done | bytes 294944 | tf_op jit(solution)/shard_map/ppermute | solution.py:34
  79.9 1.9 %collective-permute-start.31 = (bf16[96,768]{1,0:T(8,128)(2,1)S(1)}, bf16[96,768]{1,0:T(8,128)(2,1)S(1)}, u32[]{:S(2)}, u32[]{:S(2)}) collective-permute-start(bf16[96,768]{1,0:T(8,128)(2,1)S(1)} %get-tuple-element.87), channel_id=1, source_target_pairs={{0,16},{4,20},{8,24},{12,28},{16,0},{20,4},{24,8},{28,12},{1,17},{... | collective-permute-start | bytes 442376 | tf_op jit(solution)/shard_map/ppermute | solution.py:34
  81.8 4.5 %collective-permute-done.26.refs_4_ = bf16[128,1536]{1,0:T(8,128)(2,1)S(1)} collective-permute-done((bf16[128,1536]{1,0:T(8,128)(2,1)S(1)}, bf16[128,1536]{1,0:T(8,128)(2,1)S(1)}, u32[]{:S(2)}, u32[]{:S(2)}) %collective-permute-start.26) | collective-permute-done | bytes 393248 | tf_op jit(solution)/shard_map/ppermute | solution.py:34
  86.4 3.0 %collective-permute-done.31.refs_8_ = bf16[96,768]{1,0:T(8,128)(2,1)S(1)} collective-permute-done((bf16[96,768]{1,0:T(8,128)(2,1)S(1)}, bf16[96,768]{1,0:T(8,128)(2,1)S(1)}, u32[]{:S(2)}, u32[]{:S(2)}) %collective-permute-start.31) | collective-permute-done | bytes 147488 | tf_op jit(solution)/shard_map/ppermute | solution.py:34
  89.3 1.7 %finish.1 = (f32[3,96,384]{2,1,0:T(8,128)}, f32[96,384]{1,0:T(8,128)}, bf16[256,1536]{1,0:T(8,128)(2,1)}) custom-call(s32[6]{0:T(128)S(1)} %stack.27.refs_0_, bf16[128,1536]{1,0:T(8,128)(2,1)S(1)} %get-tuple-element.80.refs_1_, bf16[128,1536]{1,0:T(8,128)(2,1)S(1)} %collective-permute-done.25.refs_2_, ...), custom_call_target="tpu_custom_call" | custom-call | flops 1 | bytes 1 | tf_op jit(solution)/shard_map/finish/pallas_call | solution.py:200
  (60 shorter events, 9.8 us)
Async XLA Ops:
  0.6 27.6 %collective-permute-start.3 = (bf16[768,1920]{1,0:T(8,128)(2,1)}, bf16[768,1920]{1,0:T(8,128)(2,1)S(1)}, u32[]{:S(2)}, u32[]{:S(2)}) collective-permute-start(bf16[768,1920]{1,0:T(8,128)(2,1)} %refs_3_.3), channel_id=1, source_target_pairs={{0,1},{1,0},{2,3},{3,2},{4,5},{5,4},{6,7},{7,6},{8,9},{9,8},{10,11... | collective-permute-start | bytes 8847368 | tf_op jit(solution)/shard_map/ppermute | solution.py:34
  3.1 18.8 %collective-permute-start.1 = (bf16[768,384]{1,0:T(8,128)(2,1)S(1)}, bf16[768,384]{1,0:T(8,128)(2,1)S(1)}, u32[]{:S(2)}, u32[]{:S(2)}) collective-permute-start(bf16[768,384]{1,0:T(8,128)(2,1)S(1)} %piece_of.1.refs_3_), channel_id=1, source_target_pairs={{0,2},{2,0},{1,3},{3,1},{4,6},{6,4},{5,7},{7,5},{8,10},{10,8},{9,1... | collective-permute-start | bytes 1769480 | tf_op jit(solution)/shard_map/ppermute | solution.py:34
  8.6 12.2 %collective-permute-start = (bf16[256,384]{1,0:T(8,128)(2,1)S(1)}, bf16[256,384]{1,0:T(8,128)(2,1)S(1)}, u32[]{:S(2)}, u32[]{:S(2)}) collective-permute-start(bf16[256,384]{1,0:T(8,128)(2,1)S(1)} %get-tuple-element.49), channel_id=1, source_target_pairs={{0,16},{4,20},{8,24},{12,28},{16,0},{20,4},{24,8},{28,12},{1,17},{... | collective-permute-start | bytes 589832 | tf_op jit(solution)/shard_map/ppermute | solution.py:480
  21.4 6.2 %collective-permute-start.2 = (bf16[256,384]{1,0:T(8,128)(2,1)S(1)}, bf16[256,384]{1,0:T(8,128)(2,1)S(1)}, u32[]{:S(2)}, u32[]{:S(2)}) collective-permute-start(bf16[256,384]{1,0:T(8,128)(2,1)S(1)} %get-tuple-element.53), channel_id=1, source_target_pairs={{0,2},{2,0},{1,3},{3,1},{4,6},{6,4},{5,7},{7,5},{8,10},{10,8},{9,1... | collective-permute-start | bytes 589832 | tf_op jit(solution)/shard_map/ppermute | solution.py:34
  23.9 3.8 %collective-permute-start.4 = (bf16[256,384]{1,0:T(8,128)(2,1)S(1)}, bf16[256,384]{1,0:T(8,128)(2,1)S(1)}, u32[]{:S(2)}, u32[]{:S(2)}) collective-permute-start(bf16[256,384]{1,0:T(8,128)(2,1)S(1)} %get-tuple-element.54), channel_id=1, source_target_pairs={{0,1},{1,0},{2,3},{3,2},{4,5},{5,4},{6,7},{7,6},{8,9},{9,8},{10,11... | collective-permute-start | bytes 589832 | tf_op jit(solution)/shard_map/ppermute | solution.py:34
  24.0 4.2 %collective-permute-start.5 = (bf16[256,384]{1,0:T(8,128)(2,1)S(1)}, bf16[256,384]{1,0:T(8,128)(2,1)S(1)}, u32[]{:S(2)}, u32[]{:S(2)}) collective-permute-start(bf16[256,384]{1,0:T(8,128)(2,1)S(1)} %get-tuple-element.55), channel_id=1, source_target_pairs={{0,1},{1,0},{2,3},{3,2},{4,5},{5,4},{6,7},{7,6},{8,9},{9,8},{10,11... | collective-permute-start | bytes 589832 | tf_op jit(solution)/shard_map/ppermute | solution.py:34
  24.5 3.7 %collective-permute-start.6 = (bf16[256,384]{1,0:T(8,128)(2,1)S(1)}, bf16[256,384]{1,0:T(8,128)(2,1)S(1)}, u32[]{:S(2)}, u32[]{:S(2)}) collective-permute-start(bf16[256,384]{1,0:T(8,128)(2,1)S(1)} %get-tuple-element.56), channel_id=1, source_target_pairs={{0,1},{1,0},{2,3},{3,2},{4,5},{5,4},{6,7},{7,6},{8,9},{9,8},{10,11... | collective-permute-start | bytes 589832 | tf_op jit(solution)/shard_map/ppermute | solution.py:34
  27.7 7.5 %collective-permute-start.8 = (bf16[256,384]{1,0:T(8,128)(2,1)S(1)}, bf16[256,384]{1,0:T(8,128)(2,1)S(1)}, u32[]{:S(2)}, u32[]{:S(2)}) collective-permute-start(bf16[256,384]{1,0:T(8,128)(2,1)S(1)} %collective-permute-done.2.refs_2_), channel_id=1, source_target_pairs={{0,1},{1,0},{2,3},{3,2},{4,5},{5,4},{6,7},{7,6},{8,9},{9,8},{10,11... | collective-permute-start | bytes 589832 | tf_op jit(solution)/shard_map/ppermute | solution.py:34
  27.7 7.5 %collective-permute-start.9 = (bf16[256,384]{1,0:T(8,128)(2,1)S(1)}, bf16[256,384]{1,0:T(8,128)(2,1)S(1)}, u32[]{:S(2)}, u32[]{:S(2)}) collective-permute-start(bf16[256,384]{1,0:T(8,128)(2,1)S(1)} %get-tuple-element.61.refs_6_), channel_id=1, source_target_pairs={{0,1},{1,0},{2,3},{3,2},{4,5},{5,4},{6,7},{7,6},{8,9},{9,8},{10,11... | collective-permute-start | bytes 589832 | tf_op jit(solution)/shard_map/ppermute | solution.py:34
  34.3 6.9 %collective-permute-start.7 = (bf16[256,384]{1,0:T(8,128)(2,1)S(1)}, bf16[256,384]{1,0:T(8,128)(2,1)S(1)}, u32[]{:S(2)}, u32[]{:S(2)}) collective-permute-start(bf16[256,384]{1,0:T(8,128)(2,1)S(1)} %get-tuple-element.58), channel_id=1, source_target_pairs={{0,2},{2,0},{1,3},{3,1},{4,6},{6,4},{5,7},{7,5},{8,10},{10,8},{9,1... | collective-permute-start | bytes 589832 | tf_op jit(solution)/shard_map/ppermute | solution.py:34
  36.1 2.4 %collective-permute-start.10 = (bf16[3,96,256]{2,1,0:T(8,128)(2,1)S(1)}, bf16[3,96,256]{2,1,0:T(8,128)(2,1)S(1)}, u32[]{:S(2)}, u32[]{:S(2)}) collective-permute-start(bf16[3,96,256]{2,1,0:T(8,128)(2,1)S(1)} %get-tuple-element.65), channel_id=1, source_target_pairs={{0,1},{1,0},{2,3},{3,2},{4,5},{5,4},{6,7},{7,6},{8,9},{9,8},{10,11... | collective-permute-start | bytes 442376 | tf_op jit(solution)/shard_map/ppermute | solution.py:34
  36.2 2.4 %collective-permute-start.11 = (bf16[3,96,256]{2,1,0:T(8,128)(2,1)S(1)}, bf16[3,96,256]{2,1,0:T(8,128)(2,1)S(1)}, u32[]{:S(2)}, u32[]{:S(2)}) collective-permute-start(bf16[3,96,256]{2,1,0:T(8,128)(2,1)S(1)} %get-tuple-element.66), channel_id=1, source_target_pairs={{0,1},{1,0},{2,3},{3,2},{4,5},{5,4},{6,7},{7,6},{8,9},{9,8},{10,11... | collective-permute-start | bytes 442376 | tf_op jit(solution)/shard_map/ppermute | solution.py:34
  36.7 6.6 %collective-permute-start.14 = (bf16[8,96,256]{2,1,0:T(8,128)(2,1)S(1)}, bf16[8,96,256]{2,1,0:T(8,128)(2,1)S(1)}, u32[]{:S(2)}, u32[]{:S(2)}) collective-permute-start(bf16[8,96,256]{2,1,0:T(8,128)(2,1)S(1)} %get-tuple-element.71), channel_id=1, source_target_pairs={{0,1},{1,0},{2,3},{3,2},{4,5},{5,4},{6,7},{7,6},{8,9},{9,8},{10,11... | collective-permute-start | bytes 1179656 | tf_op jit(solution)/shard_map/ppermute | solution.py:34
  36.8 1.8 %collective-permute-start.12 = (bf16[2,96,256]{2,1,0:T(8,128)(2,1)S(1)}, bf16[2,96,256]{2,1,0:T(8,128)(2,1)S(1)}, u32[]{:S(2)}, u32[]{:S(2)}) collective-permute-start(bf16[2,96,256]{2,1,0:T(8,128)(2,1)S(1)} %get-tuple-element.67), channel_id=1, source_target_pairs={{0,1},{1,0},{2,3},{3,2},{4,5},{5,4},{6,7},{7,6},{8,9},{9,8},{10,11... | collective-permute-start | bytes 294920 | tf_op jit(solution)/shard_map/ppermute | solution.py:34
  41.8 19.4 %collective-permute-start.15 = (bf16[8,96,384]{2,1,0:T(8,128)(2,1)S(1)}, bf16[8,96,384]{2,1,0:T(8,128)(2,1)S(1)}, u32[]{:S(2)}, u32[]{:S(2)}) collective-permute-start(bf16[8,96,384]{2,1,0:T(8,128)(2,1)S(1)} %get-tuple-element.73), channel_id=1, source_target_pairs={{0,2},{2,0},{1,3},{3,1},{4,6},{6,4},{5,7},{7,5},{8,10},{10,8},{9,1... | collective-permute-start | bytes 1769480 | tf_op jit(solution)/shard_map/ppermute | solution.py:34
  42.7 10.9 %collective-permute-start.13 = (bf16[256,384]{1,0:T(8,128)(2,1)S(1)}, bf16[256,384]{1,0:T(8,128)(2,1)S(1)}, u32[]{:S(2)}, u32[]{:S(2)}) collective-permute-start(bf16[256,384]{1,0:T(8,128)(2,1)S(1)} %get-tuple-element.69.refs_3_.refs_1_), channel_id=1, source_target_pairs={{0,16},{4,20},{8,24},{12,28},{16,0},{20,4},{24,8},{28,12},{1,17},{... | collective-permute-start | bytes 589832 | tf_op jit(solution)/shard_map/ppermute | solution.py:550
  42.7 1.3 %collective-permute-start.18 = (bf16[64,384]{1,0:T(8,128)(2,1)S(1)}, bf16[64,384]{1,0:T(8,128)(2,1)S(1)}, u32[]{:S(2)}, u32[]{:S(2)}) collective-permute-start(bf16[64,384]{1,0:T(8,128)(2,1)S(1)} %get-tuple-element.94), channel_id=1, source_target_pairs={{0,1},{1,0},{2,3},{3,2},{4,5},{5,4},{6,7},{7,6},{8,9},{9,8},{10,11... | collective-permute-start | bytes 147464 | tf_op jit(solution)/shard_map/ppermute | solution.py:34
  42.8 1.4 %collective-permute-start.19 = (bf16[64,384]{1,0:T(8,128)(2,1)S(1)}, bf16[64,384]{1,0:T(8,128)(2,1)S(1)}, u32[]{:S(2)}, u32[]{:S(2)}) collective-permute-start(bf16[64,384]{1,0:T(8,128)(2,1)S(1)} %get-tuple-element.93), channel_id=1, source_target_pairs={{0,1},{1,0},{2,3},{3,2},{4,5},{5,4},{6,7},{7,6},{8,9},{9,8},{10,11... | collective-permute-start | bytes 147464 | tf_op jit(solution)/shard_map/ppermute | solution.py:34
  43.3 1.2 %collective-permute-start.20 = (bf16[64,384]{1,0:T(8,128)(2,1)S(1)}, bf16[64,384]{1,0:T(8,128)(2,1)S(1)}, u32[]{:S(2)}, u32[]{:S(2)}) collective-permute-start(bf16[64,384]{1,0:T(8,128)(2,1)S(1)} %get-tuple-element.92), channel_id=1, source_target_pairs={{0,1},{1,0},{2,3},{3,2},{4,5},{5,4},{6,7},{7,6},{8,9},{9,8},{10,11... | collective-permute-start | bytes 147464 | tf_op jit(solution)/shard_map/ppermute | solution.py:34
  44.0 1.2 %collective-permute-start.21 = (bf16[64,384]{1,0:T(8,128)(2,1)S(1)}, bf16[64,384]{1,0:T(8,128)(2,1)S(1)}, u32[]{:S(2)}, u32[]{:S(2)}) collective-permute-start(bf16[64,384]{1,0:T(8,128)(2,1)S(1)} %get-tuple-element.91), channel_id=1, source_target_pairs={{0,1},{1,0},{2,3},{3,2},{4,5},{5,4},{6,7},{7,6},{8,9},{9,8},{10,11... | collective-permute-start | bytes 147464 | tf_op jit(solution)/shard_map/ppermute | solution.py:34
  46.4 11.4 %collective-permute-start.22 = (bf16[2,96,384]{2,1,0:T(8,128)(2,1)S(1)}, bf16[2,96,384]{2,1,0:T(8,128)(2,1)S(1)}, u32[]{:S(2)}, u32[]{:S(2)}) collective-permute-start(bf16[2,96,384]{2,1,0:T(8,128)(2,1)S(1)} %get-tuple-element.75), channel_id=1, source_target_pairs={{0,12},{4,8},{8,4},{12,0},{16,28},{20,24},{24,20},{28,16},{1,13},{... | collective-permute-start | bytes 442376 | tf_op jit(solution)/shard_map/ppermute | solution.py:34
  51.8 8.7 %collective-permute-start.23 = (bf16[2,96,384]{2,1,0:T(8,128)(2,1)S(1)}, bf16[2,96,384]{2,1,0:T(8,128)(2,1)S(1)}, u32[]{:S(2)}, u32[]{:S(2)}) collective-permute-start(bf16[2,96,384]{2,1,0:T(8,128)(2,1)S(1)} %get-tuple-element.76), channel_id=1, source_target_pairs={{0,4},{4,0},{8,12},{12,8},{16,20},{20,16},{24,28},{28,24},{1,5},{5... | collective-permute-start | bytes 442376 | tf_op jit(solution)/shard_map/ppermute | solution.py:34
  52.3 8.2 %collective-permute-start.24 = (bf16[2,96,384]{2,1,0:T(8,128)(2,1)S(1)}, bf16[2,96,384]{2,1,0:T(8,128)(2,1)S(1)}, u32[]{:S(2)}, u32[]{:S(2)}) collective-permute-start(bf16[2,96,384]{2,1,0:T(8,128)(2,1)S(1)} %get-tuple-element.77), channel_id=1, source_target_pairs={{0,8},{4,12},{8,0},{12,4},{16,24},{20,28},{24,16},{28,20},{1,9},{5... | collective-permute-start | bytes 442376 | tf_op jit(solution)/shard_map/ppermute | solution.py:34
  53.6 7.6 %collective-permute-start.16 = (bf16[128,384]{1,0:T(8,128)(2,1)S(1)}, bf16[128,384]{1,0:T(8,128)(2,1)S(1)}, u32[]{:S(2)}, u32[]{:S(2)}) collective-permute-start(bf16[128,384]{1,0:T(8,128)(2,1)S(1)} %get-tuple-element.96), channel_id=1, source_target_pairs={{0,1},{1,0},{2,3},{3,2},{4,5},{5,4},{6,7},{7,6},{8,9},{9,8},{10,11... | collective-permute-start | bytes 294920 | tf_op jit(solution)/shard_map/ppermute | solution.py:34
  57.7 3.5 %collective-permute-start.17 = (bf16[128,384]{1,0:T(8,128)(2,1)S(1)}, bf16[128,384]{1,0:T(8,128)(2,1)S(1)}, u32[]{:S(2)}, u32[]{:S(2)}) collective-permute-start(bf16[128,384]{1,0:T(8,128)(2,1)S(1)} %get-tuple-element.95), channel_id=1, source_target_pairs={{0,1},{1,0},{2,3},{3,2},{4,5},{5,4},{6,7},{7,6},{8,9},{9,8},{10,11... | collective-permute-start | bytes 294920 | tf_op jit(solution)/shard_map/ppermute | solution.py:34
  61.1 8.3 %collective-permute-start.27 = (bf16[96,384]{1,0:T(8,128)(2,1)S(1)}, bf16[96,384]{1,0:T(8,128)(2,1)S(1)}, u32[]{:S(2)}, u32[]{:S(2)}) collective-permute-start(bf16[96,384]{1,0:T(8,128)(2,1)S(1)} %get-tuple-element.82), channel_id=1, source_target_pairs={{0,16},{4,20},{8,24},{12,28},{16,0},{20,4},{24,8},{28,12},{1,17},{... | collective-permute-start | bytes 221192 | tf_op jit(solution)/shard_map/ppermute | solution.py:34
  62.8 11.1 %collective-permute-start.28 = (bf16[2,96,768]{2,1,0:T(8,128)(2,1)S(1)}, bf16[2,96,768]{2,1,0:T(8,128)(2,1)S(1)}, u32[]{:S(2)}, u32[]{:S(2)}) collective-permute-start(bf16[2,96,768]{2,1,0:T(8,128)(2,1)S(1)} %get-tuple-element.83), channel_id=1, source_target_pairs={{0,12},{4,8},{8,4},{12,0},{16,28},{20,24},{24,20},{28,16},{1,13},{... | collective-permute-start | bytes 884744 | tf_op jit(solution)/shard_map/ppermute | solution.py:34
  64.9 14.3 %collective-permute-start.29 = (bf16[2,96,768]{2,1,0:T(8,128)(2,1)S(1)}, bf16[2,96,768]{2,1,0:T(8,128)(2,1)S(1)}, u32[]{:S(2)}, u32[]{:S(2)}) collective-permute-start(bf16[2,96,768]{2,1,0:T(8,128)(2,1)S(1)} %get-tuple-element.84), channel_id=1, source_target_pairs={{0,4},{4,0},{8,12},{12,8},{16,20},{20,16},{24,28},{28,24},{1,5},{5... | collective-permute-start | bytes 884744 | tf_op jit(solution)/shard_map/ppermute | solution.py:34
  65.4 13.9 %collective-permute-start.30 = (bf16[2,96,768]{2,1,0:T(8,128)(2,1)S(1)}, bf16[2,96,768]{2,1,0:T(8,128)(2,1)S(1)}, u32[]{:S(2)}, u32[]{:S(2)}) collective-permute-start(bf16[2,96,768]{2,1,0:T(8,128)(2,1)S(1)} %get-tuple-element.85), channel_id=1, source_target_pairs={{0,8},{4,12},{8,0},{12,4},{16,24},{20,28},{24,16},{28,20},{1,9},{5... | collective-permute-start | bytes 884744 | tf_op jit(solution)/shard_map/ppermute | solution.py:34
  67.9 13.9 %collective-permute-start.25 = (bf16[128,1536]{1,0:T(8,128)(2,1)S(1)}, bf16[128,1536]{1,0:T(8,128)(2,1)S(1)}, u32[]{:S(2)}, u32[]{:S(2)}) collective-permute-start(bf16[128,1536]{1,0:T(8,128)(2,1)S(1)} %get-tuple-element.80.refs_1_), channel_id=1, source_target_pairs={{0,2},{2,0},{1,3},{3,1},{4,6},{6,4},{5,7},{7,5},{8,10},{10,8},{9,1... | collective-permute-start | bytes 1179656 | tf_op jit(solution)/shard_map/ppermute | solution.py:34
  69.5 16.9 %collective-permute-start.26 = (bf16[128,1536]{1,0:T(8,128)(2,1)S(1)}, bf16[128,1536]{1,0:T(8,128)(2,1)S(1)}, u32[]{:S(2)}, u32[]{:S(2)}) collective-permute-start(bf16[128,1536]{1,0:T(8,128)(2,1)S(1)} %get-tuple-element.81.refs_5_.refs_3_), channel_id=1, source_target_pairs={{0,2},{2,0},{1,3},{3,1},{4,6},{6,4},{5,7},{7,5},{8,10},{10,8},{9,1... | collective-permute-start | bytes 1179656 | tf_op jit(solution)/shard_map/ppermute | solution.py:34
  79.9 9.4 %collective-permute-start.31 = (bf16[96,768]{1,0:T(8,128)(2,1)S(1)}, bf16[96,768]{1,0:T(8,128)(2,1)S(1)}, u32[]{:S(2)}, u32[]{:S(2)}) collective-permute-start(bf16[96,768]{1,0:T(8,128)(2,1)S(1)} %get-tuple-element.87), channel_id=1, source_target_pairs={{0,16},{4,20},{8,24},{12,28},{16,0},{20,4},{24,8},{28,12},{1,17},{... | collective-permute-start | bytes 442376 | tf_op jit(solution)/shard_map/ppermute | solution.py:34
  (5 other events, 68.3 us)

commit v11 on v10

--- a/solution.py
+++ b/solution.py
@@ -242,14 +242,6 @@
         value = dot(act, weight[part, :], NN)
         total = value if total is None else total + value
     term[...] = total.astype(BF16)
-
-
-def piece_of(place, point, piece, sem):
-    number = piece.shape[0]
-    own = pl.ds(pl.multiple_of(place[SAMPLE] * number, number), number)
-    copy = pltpu.make_async_copy(point.at[own], piece, sem)
-    copy.start()
-    copy.wait()
 
 
 def middle_term(place, acted, weight, middle, kept, given):
@@ -456,13 +448,7 @@
     cotangent = track_cotangent.reshape(rows, tracks_here)
     pairs = [(i, (i + dist) % n_seq) for i in range(n_seq)]
 
-    (own_piece,) = kernel_call(
-        piece_of,
-        [((piece, width), BF16)],
-        [place, in_hbm(point_weight)],
-        scratch=[pltpu.SemaphoreType.DMA],
-        spaces={1: pltpu.HBM},
-    )
+    own_piece = lax.dynamic_slice_in_dim(point_weight, sample * piece, piece, 0)
     near = flip(own_piece, "head")
     far_track = flip(track_weight, "sample")
     acted, term = kernel_call(
@@ -473,7 +459,7 @@
         scratch=[
             pltpu.VMEM((rows, channels), BF16),
             pltpu.VMEM((channels, width), BF16),
-            pltpu.SemaphoreType.DMA((2, 3)),
+            pltpu.SemaphoreType.DMA((2, 6)),
         ],
         spaces={1: pltpu.HBM, 2: pltpu.HBM},
     )

time: 91.1 us -> 91.7 us (level)
  local copies, waits for them, and re-layouts: 0.15 us -> 1.27 us
    dynamic_slice x0 -> x1, local copies, waits for them, and re-layouts: none -> 1.12 us  [body(): own_piece = lax.dynamic_slice_in_dim(point_weight, sample * piece, piece, 0)]
    pallas_call x15 -> x14, Pallas kernels: 24.3 us -> 24.5 us  [kernel_call(): pl.pallas_call(run, out_shape=[jax.ShapeDtypeStruct(s, d) for s, d in out...]
  transfers between devices with their start and end apart: 32 -> 32, of which waited for: 15 -> 15; matrix products, arithmetic and copies ran while one was open for 0% -> 1% of each run, Pallas kernels for 25% -> 25%
where the time goes in v11:
time: 91.7 us; the launch traced here: 91.5 us
  waiting for transfers between devices  39.9 us (44%)
  starting transfers between devices  24.9 us (27%)
  Pallas kernels  24.5 us (27%)
  local copies, waits for them, and re-layouts  1.27 us (1%)
    ppermute x30, waiting for transfers between devices, flip(): return lax.ppermute(value, axis, [(i, i ^ step) for i in range(count)])  30.4 us
    pallas_call x14, Pallas kernels, kernel_call(): pl.pallas_call(run, out_shape=[jax.ShapeDtypeStruct(s, d) for s, d in out...  24.5 us
    ppermute x30, starting transfers between devices, flip(): return lax.ppermute(value, axis, [(i, i ^ step) for i in range(count)])  22.2 us
    ppermute x1, waiting for transfers between devices, body(): arrived = lax.ppermute(term, 'seq', pairs)  8.4 us
    ppermute x1, starting transfers between devices, body(): arrived = lax.ppermute(term, 'seq', pairs)  2.66 us
  transfers between devices with their start and end apart: 32, of which 15 were waited for; matrix products, arithmetic and copies ran while one was open for 1% of the time, Pallas kernels for 25%

profile of v11, /device:TPU:0, one launch (start us, length us, event | category | flops | bytes accessed | tf_op | source)
XLA Modules:
  0.0 91.5 jit_solution(2018181812033939540)
XLA Ops:
  1.1 1.1 %constant_dynamic-slice_fusion.refs_3_ = bf16[768,384]{1,0:T(8,128)(2,1)S(1)} fusion(bf16[1536,384]{1,0:T(8,128)(2,1)} %refs_6_.1, s32[]{:T(128)S(6)} %select_n.8), kind=kLoop, calls=%fused_computation | loop fusion | bytes 1179652 | tf_op jit(solution)/shard_map/dynamic_slice | solution.py:451
  2.3 2.6 %collective-permute-start.1 = (bf16[768,384]{1,0:T(8,128)(2,1)S(1)}, bf16[768,384]{1,0:T(8,128)(2,1)}, u32[]{:S(2)}, u32[]{:S(2)}) collective-permute-start(bf16[768,384]{1,0:T(8,128)(2,1)S(1)} %constant_dynamic-slice_fusion.refs_3_), channel_id=1, source_target_pairs={{0,2},{2,0},{1,3},{3,1},{4,6},{6,4},{5,7},{7,5},{8,10},{10,8},{9,1... | collective-permute-start | bytes 1769480 | tf_op jit(solution)/shard_map/ppermute | solution.py:34
  4.9 3.6 %outer_term.1 = (bf16[256,1536]{1,0:T(8,128)(2,1)S(1)}, bf16[256,384]{1,0:T(8,128)(2,1)S(1)}) custom-call(s32[6]{0:T(128)S(1)} %stack.27.refs_0_, bf16[256,1536]{1,0:T(8,128)(2,1)} %bitcast.14, bf16[3,1536,384]{2,1,0:T(8,128)(2,1)} %bitcast.11, bf16[768,384]{1,0:T(8,128)(2,1)S(1)} %constant_dynamic-slice_fusion.refs_3_), custom_call_target="tpu_custom_call" | custom-call | flops 1 | bytes 1 | tf_op jit(solution)/shard_map/outer_term/pallas_call | solution.py:200
  8.6 2.7 %collective-permute-start = (bf16[256,384]{1,0:T(8,128)(2,1)S(1)}, bf16[256,384]{1,0:T(8,128)(2,1)S(1)}, u32[]{:S(2)}, u32[]{:S(2)}) collective-permute-start(bf16[256,384]{1,0:T(8,128)(2,1)S(1)} %get-tuple-element.49), channel_id=1, source_target_pairs={{0,16},{4,20},{8,24},{12,28},{16,0},{20,4},{24,8},{28,12},{1,17},{... | collective-permute-start | bytes 589832 | tf_op jit(solution)/shard_map/ppermute | solution.py:466
  11.2 1.1 %middle_term.1 = (f32[256,384]{1,0:T(8,128)S(1)}, bf16[8,96,256]{2,1,0:T(8,128)(2,1)S(1)}, bf16[8,96,256]{2,1,0:T(8,128)(2,1)S(1)}) custom-call(s32[6]{0:T(128)S(1)} %stack.27.refs_0_, bf16[256,1536]{1,0:T(8,128)(2,1)S(1)} %get-tuple-element.47.refs_1_, bf16[3,1536,384]{2,1,0:T(8,128)(2,1)S(1)} %bitcast.12), custom_call_target="tpu_custom_call" | custom-call | flops 1 | bytes 1 | tf_op jit(solution)/shard_map/middle_term/pallas_call | solution.py:200
  12.3 8.4 %collective-permute-done.refs_2_ = bf16[256,384]{1,0:T(8,128)(2,1)S(1)} collective-permute-done((bf16[256,384]{1,0:T(8,128)(2,1)S(1)}, bf16[256,384]{1,0:T(8,128)(2,1)S(1)}, u32[]{:S(2)}, u32[]{:S(2)}) %collective-permute-start) | collective-permute-done | bytes 196640 | tf_op jit(solution)/shard_map/ppermute | solution.py:466
  21.9 2.8 %own_hidden.1 = (bf16[256,384]{1,0:T(8,128)(2,1)S(1)}, f32[256,1536]{1,0:T(8,128)S(1)}, f32[256,384]{1,0:T(8,128)S(1)}, f32[256,1536]{1,0:T(8,128)S(1)}, bf16[25...) custom-call(s32[6]{0:T(128)S(1)} %stack.27.refs_0_, ...), custom_call_target="tpu_custom_call" | custom-call | flops 1 | bytes 1 | tf_op jit(solution)/shard_map/own_hidden/pallas_call | solution.py:200
  25.3 2.3 %collective-permute-done.2.refs_2_ = bf16[256,384]{1,0:T(8,128)(2,1)S(1)} collective-permute-done((bf16[256,384]{1,0:T(8,128)(2,1)S(1)}, bf16[256,384]{1,0:T(8,128)(2,1)S(1)}, u32[]{:S(2)}, u32[]{:S(2)}) %collective-permute-start.2) | collective-permute-done | bytes 196640 | tf_op jit(solution)/shard_map/ppermute | solution.py:34
  28.2 6.6 %tracks.1 = (bf16[256,1536]{1,0:T(8,128)(2,1)S(1)}, bf16[256,384]{1,0:T(8,128)(2,1)S(1)}, f32[256,384]{1,0:T(8,128)S(1)}, bf16[256,384]{1,0:T(8,128)(2,1)S(1)}) custom-call(s32[6]{0:T(128)S(1)} %stack.27.refs_0_, f32[256,1536]{1,0:T(8,128)S(1)} %get-tuple-element.52.refs_1_, bf16[256,384]{1,0:T(8,128)(2,1)S(1)} %collective-permute-done.2.refs_2_, ...), custom_call_target="tpu_custom_call" | custom-call | flops 1 | bytes 1 | tf_op jit(solution)/shard_map/tracks/pallas_call | solution.py:200
  34.8 0.9 collective-permute-start.7
  35.6 1.0 %turn_parts.1 = (bf16[8,96,256]{2,1,0:T(8,128)(2,1)S(1)}, bf16[256,384]{1,0:T(8,128)(2,1)S(1)}, bf16[3,96,256]{2,1,0:T(8,128)(2,1)S(1)}, bf16[3,96,256]{2,1,0:T(8,128)(2,1)S(1)}, bf16[2,96,256]{2,1,0:T(8,128)(2,1)S(1)}) custom-call(s32[6]{0:T(128)S(1)} %stack.27.refs_0_, bf16[256,1536]{1,0:T(8,128)(2,1)S(1)} %get-tuple-element.60.refs_1_.refs_4_, ...), custom_call_target="tpu_custom_call" | custom-call | flops 1 | bytes 1 | tf_op jit(solution)/shard_map/turn_parts/pallas_call | solution.py:200
  37.7 1.4 %collective-permute-done.12.refs_6_ = bf16[2,96,256]{2,1,0:T(8,128)(2,1)S(1)} collective-permute-done((bf16[2,96,256]{2,1,0:T(8,128)(2,1)S(1)}, bf16[2,96,256]{2,1,0:T(8,128)(2,1)S(1)}, u32[]{:S(2)}, u32[]{:S(2)}) %collective-permute-start.12) | collective-permute-done | bytes 98336 | tf_op jit(solution)/shard_map/ppermute | solution.py:34
  39.1 1.1 %other_points.1 = (bf16[8,96,384]{2,1,0:T(8,128)(2,1)S(1)}, bf16[8,96,256]{2,1,0:T(8,128)(2,1)S(1)}) custom-call(s32[6]{0:T(128)S(1)} %stack.27.refs_0_, bf16[8,96,256]{2,1,0:T(8,128)(2,1)S(1)} %get-tuple-element.62.refs_1_.refs_4_, bf16[256,384]{1,0:T(8,128)(2,1)S(1)} %get-tuple-element.63.refs_2_, bf16[256,384]{1,0:T(8,128)(2,1)S(1)} %get-tuple-element.64.refs_3_, ...), custom_call_target="tpu_custom_call" | custom-call | flops 1 | bytes 1 | tf_op jit(solution)/shard_map/other_points/pallas_call | solution.py:200
  40.2 1.5 %collective-permute-done.7.refs_2_ = bf16[256,384]{1,0:T(8,128)(2,1)S(1)} collective-permute-done((bf16[256,384]{1,0:T(8,128)(2,1)S(1)}, bf16[256,384]{1,0:T(8,128)(2,1)S(1)}, u32[]{:S(2)}, u32[]{:S(2)}) %collective-permute-start.7) | collective-permute-done | bytes 196640 | tf_op jit(solution)/shard_map/ppermute | solution.py:34
  42.3 0.9 collective-permute-start.15
  45.0 0.7 collective-permute-done.21.refs_7_
  45.7 1.1 %middle_products.1 = (f32[2,96,384]{2,1,0:T(8,128)S(1)}, bf16[2,96,384]{2,1,0:T(8,128)(2,1)S(1)}, bf16[2,96,384]{2,1,0:T(8,128)(2,1)S(1)}, bf16[2,96,384]{2,1,0:T(8,128)(2,1)S(1)}) custom-call(s32[6]{0:T(128)S(1)} %stack.27.refs_0_, bf16[8,96,256]{2,1,0:T(8,128)(2,1)S(1)} %get-tuple-element.50.refs_3_.refs_1_, ...), custom_call_target="tpu_custom_call" | custom-call | flops 1 | bytes 1 | tf_op jit(solution)/shard_map/middle_products/pallas_call | solution.py:200
  46.8 5.5 %collective-permute-start.22 = (bf16[2,96,384]{2,1,0:T(8,128)(2,1)S(1)}, bf16[2,96,384]{2,1,0:T(8,128)(2,1)S(1)}, u32[]{:S(2)}, u32[]{:S(2)}) collective-permute-start(bf16[2,96,384]{2,1,0:T(8,128)(2,1)S(1)} %get-tuple-element.75), channel_id=1, source_target_pairs={{0,12},{4,8},{8,4},{12,0},{16,28},{20,24},{24,20},{28,16},{1,13},{... | collective-permute-start | bytes 442376 | tf_op jit(solution)/shard_map/ppermute | solution.py:34
  53.0 1.1 %collective-permute-done.13.refs_3_.refs_2_ = bf16[256,384]{1,0:T(8,128)(2,1)S(1)} collective-permute-done((bf16[256,384]{1,0:T(8,128)(2,1)S(1)}, bf16[256,384]{1,0:T(8,128)(2,1)S(1)}, u32[]{:S(2)}, u32[]{:S(2)}) %collective-permute-start.13) | collective-permute-done | bytes 196640 | tf_op jit(solution)/shard_map/ppermute | solution.py:536
  54.2 4.0 %collective-permute-done.22.refs_2_ = bf16[2,96,384]{2,1,0:T(8,128)(2,1)S(1)} collective-permute-done((bf16[2,96,384]{2,1,0:T(8,128)(2,1)S(1)}, bf16[2,96,384]{2,1,0:T(8,128)(2,1)S(1)}, u32[]{:S(2)}, u32[]{:S(2)}) %collective-permute-start.22) | collective-permute-done | bytes 147488 | tf_op jit(solution)/shard_map/ppermute | solution.py:34
  58.2 2.8 %collective-permute-done.23.refs_3_ = bf16[2,96,384]{2,1,0:T(8,128)(2,1)S(1)} collective-permute-done((bf16[2,96,384]{2,1,0:T(8,128)(2,1)S(1)}, bf16[2,96,384]{2,1,0:T(8,128)(2,1)S(1)}, u32[]{:S(2)}, u32[]{:S(2)}) %collective-permute-start.23) | collective-permute-done | bytes 147488 | tf_op jit(solution)/shard_map/ppermute | solution.py:34
  61.8 1.5 %late_products.1 = (f32[2,96,768]{2,1,0:T(8,128)S(1)}, bf16[2,96,768]{2,1,0:T(8,128)(2,1)S(1)}, bf16[2,96,768]{2,1,0:T(8,128)(2,1)S(1)}, bf16[2,96,768]{2,1,0:T(8,128)(2,1)S(1)}) custom-call(s32[6]{0:T(128)S(1)} %stack.27.refs_0_, bf16[8,96,256]{2,1,0:T(8,128)(2,1)S(1)} %get-tuple-element.50.refs_3_.refs_1_, ...), custom_call_target="tpu_custom_call" | custom-call | flops 1 | bytes 1 | tf_op jit(solution)/shard_map/late_products/pallas_call | solution.py:200
  63.3 2.1 %collective-permute-start.28 = (bf16[2,96,768]{2,1,0:T(8,128)(2,1)S(1)}, bf16[2,96,768]{2,1,0:T(8,128)(2,1)S(1)}, u32[]{:S(2)}, u32[]{:S(2)}) collective-permute-start(bf16[2,96,768]{2,1,0:T(8,128)(2,1)S(1)} %get-tuple-element.83), channel_id=1, source_target_pairs={{0,12},{4,8},{8,4},{12,0},{16,28},{20,24},{24,20},{28,16},{1,13},{... | collective-permute-start | bytes 884744 | tf_op jit(solution)/shard_map/ppermute | solution.py:34
  65.9 1.0 %collective-permute-start.30 = (bf16[2,96,768]{2,1,0:T(8,128)(2,1)S(1)}, bf16[2,96,768]{2,1,0:T(8,128)(2,1)S(1)}, u32[]{:S(2)}, u32[]{:S(2)}) collective-permute-start(bf16[2,96,768]{2,1,0:T(8,128)(2,1)S(1)} %get-tuple-element.85), channel_id=1, source_target_pairs={{0,8},{4,12},{8,0},{12,4},{16,24},{20,28},{24,16},{28,20},{1,9},{5... | collective-permute-start | bytes 884744 | tf_op jit(solution)/shard_map/ppermute | solution.py:34
  66.8 1.5 %act_part.1 = (bf16[128,1536]{1,0:T(8,128)(2,1)S(1)}, bf16[128,1536]{1,0:T(8,128)(2,1)S(1)}) custom-call(s32[6]{0:T(128)S(1)} %stack.27.refs_0_, bf16[256,384]{1,0:T(8,128)(2,1)S(1)} %get-tuple-element.69.refs_3_.refs_1_, bf16[256,384]{1,0:T(8,128)(2,1)S(1)} %collective-permute-done.13.refs_3_.refs_2_, bf16[3,1536,384]{2,1,0:T(8,128)(2,1)S(1)} %bitcast.13, ...), custom_call_target="tpu_custom_call" | custom-call | flops 1 | bytes 1 | tf_op jit(solution)/shard_map/act_part/pallas_call | solution.py:200
  68.4 1.5 %collective-permute-start.25 = (bf16[128,1536]{1,0:T(8,128)(2,1)S(1)}, bf16[128,1536]{1,0:T(8,128)(2,1)S(1)}, u32[]{:S(2)}, u32[]{:S(2)}) collective-permute-start(bf16[128,1536]{1,0:T(8,128)(2,1)S(1)} %get-tuple-element.80.refs_1_), channel_id=1, source_target_pairs={{0,2},{2,0},{1,3},{3,1},{4,6},{6,4},{5,7},{7,5},{8,10},{10,8},{9,1... | collective-permute-start | bytes 1179656 | tf_op jit(solution)/shard_map/ppermute | solution.py:34
  70.5 3.9 %collective-permute-done.28.refs_2_ = bf16[2,96,768]{2,1,0:T(8,128)(2,1)S(1)} collective-permute-done((bf16[2,96,768]{2,1,0:T(8,128)(2,1)S(1)}, bf16[2,96,768]{2,1,0:T(8,128)(2,1)S(1)}, u32[]{:S(2)}, u32[]{:S(2)}) %collective-permute-start.28) | collective-permute-done | bytes 294944 | tf_op jit(solution)/shard_map/ppermute | solution.py:34
  74.4 5.2 %collective-permute-done.29.refs_3_ = bf16[2,96,768]{2,1,0:T(8,128)(2,1)S(1)} collective-permute-done((bf16[2,96,768]{2,1,0:T(8,128)(2,1)S(1)}, bf16[2,96,768]{2,1,0:T(8,128)(2,1)S(1)}, u32[]{:S(2)}, u32[]{:S(2)}) %collective-permute-start.29) | collective-permute-done | bytes 294944 | tf_op jit(solution)/shard_map/ppermute | solution.py:34
  80.4 1.9 %collective-permute-start.31 = (bf16[96,768]{1,0:T(8,128)(2,1)S(1)}, bf16[96,768]{1,0:T(8,128)(2,1)S(1)}, u32[]{:S(2)}, u32[]{:S(2)}) collective-permute-start(bf16[96,768]{1,0:T(8,128)(2,1)S(1)} %get-tuple-element.87), channel_id=1, source_target_pairs={{0,16},{4,20},{8,24},{12,28},{16,0},{20,4},{24,8},{28,12},{1,17},{... | collective-permute-start | bytes 442376 | tf_op jit(solution)/shard_map/ppermute | solution.py:34
  82.3 4.5 %collective-permute-done.26.refs_4_ = bf16[128,1536]{1,0:T(8,128)(2,1)S(1)} collective-permute-done((bf16[128,1536]{1,0:T(8,128)(2,1)S(1)}, bf16[128,1536]{1,0:T(8,128)(2,1)S(1)}, u32[]{:S(2)}, u32[]{:S(2)}) %collective-permute-start.26) | collective-permute-done | bytes 393248 | tf_op jit(solution)/shard_map/ppermute | solution.py:34
  86.8 3.0 %collective-permute-done.31.refs_8_ = bf16[96,768]{1,0:T(8,128)(2,1)S(1)} collective-permute-done((bf16[96,768]{1,0:T(8,128)(2,1)S(1)}, bf16[96,768]{1,0:T(8,128)(2,1)S(1)}, u32[]{:S(2)}, u32[]{:S(2)}) %collective-permute-start.31) | collective-permute-done | bytes 147488 | tf_op jit(solution)/shard_map/ppermute | solution.py:34
  89.8 1.7 %finish.1 = (f32[3,96,384]{2,1,0:T(8,128)}, f32[96,384]{1,0:T(8,128)}, bf16[256,1536]{1,0:T(8,128)(2,1)}) custom-call(s32[6]{0:T(128)S(1)} %stack.27.refs_0_, bf16[128,1536]{1,0:T(8,128)(2,1)S(1)} %get-tuple-element.80.refs_1_, bf16[128,1536]{1,0:T(8,128)(2,1)S(1)} %collective-permute-done.25.refs_2_, ...), custom_call_target="tpu_custom_call" | custom-call | flops 1 | bytes 1 | tf_op jit(solution)/shard_map/finish/pallas_call | solution.py:200
  (60 shorter events, 9.8 us)
Async XLA Ops:
  0.6 27.5 %collective-permute-start.3 = (bf16[768,1920]{1,0:T(8,128)(2,1)}, bf16[768,1920]{1,0:T(8,128)(2,1)S(1)}, u32[]{:S(2)}, u32[]{:S(2)}) collective-permute-start(bf16[768,1920]{1,0:T(8,128)(2,1)} %refs_3_.3), channel_id=1, source_target_pairs={{0,1},{1,0},{2,3},{3,2},{4,5},{5,4},{6,7},{7,6},{8,9},{9,8},{10,11... | collective-permute-start | bytes 8847368 | tf_op jit(solution)/shard_map/ppermute | solution.py:34
  2.3 19.6 %collective-permute-start.1 = (bf16[768,384]{1,0:T(8,128)(2,1)S(1)}, bf16[768,384]{1,0:T(8,128)(2,1)}, u32[]{:S(2)}, u32[]{:S(2)}) collective-permute-start(bf16[768,384]{1,0:T(8,128)(2,1)S(1)} %constant_dynamic-slice_fusion.refs_3_), channel_id=1, source_target_pairs={{0,2},{2,0},{1,3},{3,1},{4,6},{6,4},{5,7},{7,5},{8,10},{10,8},{9,1... | collective-permute-start | bytes 1769480 | tf_op jit(solution)/shard_map/ppermute | solution.py:34
  8.6 12.2 %collective-permute-start = (bf16[256,384]{1,0:T(8,128)(2,1)S(1)}, bf16[256,384]{1,0:T(8,128)(2,1)S(1)}, u32[]{:S(2)}, u32[]{:S(2)}) collective-permute-start(bf16[256,384]{1,0:T(8,128)(2,1)S(1)} %get-tuple-element.49), channel_id=1, source_target_pairs={{0,16},{4,20},{8,24},{12,28},{16,0},{20,4},{24,8},{28,12},{1,17},{... | collective-permute-start | bytes 589832 | tf_op jit(solution)/shard_map/ppermute | solution.py:466
  21.4 6.3 %collective-permute-start.2 = (bf16[256,384]{1,0:T(8,128)(2,1)S(1)}, bf16[256,384]{1,0:T(8,128)(2,1)S(1)}, u32[]{:S(2)}, u32[]{:S(2)}) collective-permute-start(bf16[256,384]{1,0:T(8,128)(2,1)S(1)} %get-tuple-element.53), channel_id=1, source_target_pairs={{0,2},{2,0},{1,3},{3,1},{4,6},{6,4},{5,7},{7,5},{8,10},{10,8},{9,1... | collective-permute-start | bytes 589832 | tf_op jit(solution)/shard_map/ppermute | solution.py:34
  24.7 2.9 %collective-permute-start.4 = (bf16[256,384]{1,0:T(8,128)(2,1)S(1)}, bf16[256,384]{1,0:T(8,128)(2,1)S(1)}, u32[]{:S(2)}, u32[]{:S(2)}) collective-permute-start(bf16[256,384]{1,0:T(8,128)(2,1)S(1)} %get-tuple-element.54), channel_id=1, source_target_pairs={{0,1},{1,0},{2,3},{3,2},{4,5},{5,4},{6,7},{7,6},{8,9},{9,8},{10,11... | collective-permute-start | bytes 589832 | tf_op jit(solution)/shard_map/ppermute | solution.py:34
  24.8 3.4 %collective-permute-start.5 = (bf16[256,384]{1,0:T(8,128)(2,1)S(1)}, bf16[256,384]{1,0:T(8,128)(2,1)S(1)}, u32[]{:S(2)}, u32[]{:S(2)}) collective-permute-start(bf16[256,384]{1,0:T(8,128)(2,1)S(1)} %get-tuple-element.55), channel_id=1, source_target_pairs={{0,1},{1,0},{2,3},{3,2},{4,5},{5,4},{6,7},{7,6},{8,9},{9,8},{10,11... | collective-permute-start | bytes 589832 | tf_op jit(solution)/shard_map/ppermute | solution.py:34
  25.3 2.9 %collective-permute-start.6 = (bf16[256,384]{1,0:T(8,128)(2,1)S(1)}, bf16[256,384]{1,0:T(8,128)(2,1)S(1)}, u32[]{:S(2)}, u32[]{:S(2)}) collective-permute-start(bf16[256,384]{1,0:T(8,128)(2,1)S(1)} %get-tuple-element.56), channel_id=1, source_target_pairs={{0,1},{1,0},{2,3},{3,2},{4,5},{5,4},{6,7},{7,6},{8,9},{9,8},{10,11... | collective-permute-start | bytes 589832 | tf_op jit(solution)/shard_map/ppermute | solution.py:34
  27.6 8.0 %collective-permute-start.8 = (bf16[256,384]{1,0:T(8,128)(2,1)S(1)}, bf16[256,384]{1,0:T(8,128)(2,1)S(1)}, u32[]{:S(2)}, u32[]{:S(2)}) collective-permute-start(bf16[256,384]{1,0:T(8,128)(2,1)S(1)} %collective-permute-done.2.refs_2_), channel_id=1, source_target_pairs={{0,1},{1,0},{2,3},{3,2},{4,5},{5,4},{6,7},{7,6},{8,9},{9,8},{10,11... | collective-permute-start | bytes 589832 | tf_op jit(solution)/shard_map/ppermute | solution.py:34
  27.6 8.0 %collective-permute-start.9 = (bf16[256,384]{1,0:T(8,128)(2,1)S(1)}, bf16[256,384]{1,0:T(8,128)(2,1)S(1)}, u32[]{:S(2)}, u32[]{:S(2)}) collective-permute-start(bf16[256,384]{1,0:T(8,128)(2,1)S(1)} %get-tuple-element.61.refs_6_), channel_id=1, source_target_pairs={{0,1},{1,0},{2,3},{3,2},{4,5},{5,4},{6,7},{7,6},{8,9},{9,8},{10,11... | collective-permute-start | bytes 589832 | tf_op jit(solution)/shard_map/ppermute | solution.py:34
  34.8 6.9 %collective-permute-start.7 = (bf16[256,384]{1,0:T(8,128)(2,1)S(1)}, bf16[256,384]{1,0:T(8,128)(2,1)S(1)}, u32[]{:S(2)}, u32[]{:S(2)}) collective-permute-start(bf16[256,384]{1,0:T(8,128)(2,1)S(1)} %get-tuple-element.58), channel_id=1, source_target_pairs={{0,2},{2,0},{1,3},{3,1},{4,6},{6,4},{5,7},{7,5},{8,10},{10,8},{9,1... | collective-permute-start | bytes 589832 | tf_op jit(solution)/shard_map/ppermute | solution.py:34
  36.6 2.4 %collective-permute-start.10 = (bf16[3,96,256]{2,1,0:T(8,128)(2,1)S(1)}, bf16[3,96,256]{2,1,0:T(8,128)(2,1)S(1)}, u32[]{:S(2)}, u32[]{:S(2)}) collective-permute-start(bf16[3,96,256]{2,1,0:T(8,128)(2,1)S(1)} %get-tuple-element.65), channel_id=1, source_target_pairs={{0,1},{1,0},{2,3},{3,2},{4,5},{5,4},{6,7},{7,6},{8,9},{9,8},{10,11... | collective-permute-start | bytes 442376 | tf_op jit(solution)/shard_map/ppermute | solution.py:34
  36.7 2.4 %collective-permute-start.11 = (bf16[3,96,256]{2,1,0:T(8,128)(2,1)S(1)}, bf16[3,96,256]{2,1,0:T(8,128)(2,1)S(1)}, u32[]{:S(2)}, u32[]{:S(2)}) collective-permute-start(bf16[3,96,256]{2,1,0:T(8,128)(2,1)S(1)} %get-tuple-element.66), channel_id=1, source_target_pairs={{0,1},{1,0},{2,3},{3,2},{4,5},{5,4},{6,7},{7,6},{8,9},{9,8},{10,11... | collective-permute-start | bytes 442376 | tf_op jit(solution)/shard_map/ppermute | solution.py:34
  37.2 6.6 %collective-permute-start.14 = (bf16[8,96,256]{2,1,0:T(8,128)(2,1)S(1)}, bf16[8,96,256]{2,1,0:T(8,128)(2,1)S(1)}, u32[]{:S(2)}, u32[]{:S(2)}) collective-permute-start(bf16[8,96,256]{2,1,0:T(8,128)(2,1)S(1)} %get-tuple-element.71), channel_id=1, source_target_pairs={{0,1},{1,0},{2,3},{3,2},{4,5},{5,4},{6,7},{7,6},{8,9},{9,8},{10,11... | collective-permute-start | bytes 1179656 | tf_op jit(solution)/shard_map/ppermute | solution.py:34
  37.3 1.8 %collective-permute-start.12 = (bf16[2,96,256]{2,1,0:T(8,128)(2,1)S(1)}, bf16[2,96,256]{2,1,0:T(8,128)(2,1)S(1)}, u32[]{:S(2)}, u32[]{:S(2)}) collective-permute-start(bf16[2,96,256]{2,1,0:T(8,128)(2,1)S(1)} %get-tuple-element.67), channel_id=1, source_target_pairs={{0,1},{1,0},{2,3},{3,2},{4,5},{5,4},{6,7},{7,6},{8,9},{9,8},{10,11... | collective-permute-start | bytes 294920 | tf_op jit(solution)/shard_map/ppermute | solution.py:34
  42.3 19.4 %collective-permute-start.15 = (bf16[8,96,384]{2,1,0:T(8,128)(2,1)S(1)}, bf16[8,96,384]{2,1,0:T(8,128)(2,1)S(1)}, u32[]{:S(2)}, u32[]{:S(2)}) collective-permute-start(bf16[8,96,384]{2,1,0:T(8,128)(2,1)S(1)} %get-tuple-element.73), channel_id=1, source_target_pairs={{0,2},{2,0},{1,3},{3,1},{4,6},{6,4},{5,7},{7,5},{8,10},{10,8},{9,1... | collective-permute-start | bytes 1769480 | tf_op jit(solution)/shard_map/ppermute | solution.py:34
  43.2 10.9 %collective-permute-start.13 = (bf16[256,384]{1,0:T(8,128)(2,1)S(1)}, bf16[256,384]{1,0:T(8,128)(2,1)S(1)}, u32[]{:S(2)}, u32[]{:S(2)}) collective-permute-start(bf16[256,384]{1,0:T(8,128)(2,1)S(1)} %get-tuple-element.69.refs_3_.refs_1_), channel_id=1, source_target_pairs={{0,16},{4,20},{8,24},{12,28},{16,0},{20,4},{24,8},{28,12},{1,17},{... | collective-permute-start | bytes 589832 | tf_op jit(solution)/shard_map/ppermute | solution.py:536
  43.2 1.3 %collective-permute-start.18 = (bf16[64,384]{1,0:T(8,128)(2,1)S(1)}, bf16[64,384]{1,0:T(8,128)(2,1)S(1)}, u32[]{:S(2)}, u32[]{:S(2)}) collective-permute-start(bf16[64,384]{1,0:T(8,128)(2,1)S(1)} %get-tuple-element.94), channel_id=1, source_target_pairs={{0,1},{1,0},{2,3},{3,2},{4,5},{5,4},{6,7},{7,6},{8,9},{9,8},{10,11... | collective-permute-start | bytes 147464 | tf_op jit(solution)/shard_map/ppermute | solution.py:34
  43.3 1.4 %collective-permute-start.19 = (bf16[64,384]{1,0:T(8,128)(2,1)S(1)}, bf16[64,384]{1,0:T(8,128)(2,1)S(1)}, u32[]{:S(2)}, u32[]{:S(2)}) collective-permute-start(bf16[64,384]{1,0:T(8,128)(2,1)S(1)} %get-tuple-element.93), channel_id=1, source_target_pairs={{0,1},{1,0},{2,3},{3,2},{4,5},{5,4},{6,7},{7,6},{8,9},{9,8},{10,11... | collective-permute-start | bytes 147464 | tf_op jit(solution)/shard_map/ppermute | solution.py:34
  43.8 1.2 %collective-permute-start.20 = (bf16[64,384]{1,0:T(8,128)(2,1)S(1)}, bf16[64,384]{1,0:T(8,128)(2,1)S(1)}, u32[]{:S(2)}, u32[]{:S(2)}) collective-permute-start(bf16[64,384]{1,0:T(8,128)(2,1)S(1)} %get-tuple-element.92), channel_id=1, source_target_pairs={{0,1},{1,0},{2,3},{3,2},{4,5},{5,4},{6,7},{7,6},{8,9},{9,8},{10,11... | collective-permute-start | bytes 147464 | tf_op jit(solution)/shard_map/ppermute | solution.py:34
  44.5 1.2 %collective-permute-start.21 = (bf16[64,384]{1,0:T(8,128)(2,1)S(1)}, bf16[64,384]{1,0:T(8,128)(2,1)S(1)}, u32[]{:S(2)}, u32[]{:S(2)}) collective-permute-start(bf16[64,384]{1,0:T(8,128)(2,1)S(1)} %get-tuple-element.91), channel_id=1, source_target_pairs={{0,1},{1,0},{2,3},{3,2},{4,5},{5,4},{6,7},{7,6},{8,9},{9,8},{10,11... | collective-permute-start | bytes 147464 | tf_op jit(solution)/shard_map/ppermute | solution.py:34
  46.8 11.4 %collective-permute-start.22 = (bf16[2,96,384]{2,1,0:T(8,128)(2,1)S(1)}, bf16[2,96,384]{2,1,0:T(8,128)(2,1)S(1)}, u32[]{:S(2)}, u32[]{:S(2)}) collective-permute-start(bf16[2,96,384]{2,1,0:T(8,128)(2,1)S(1)} %get-tuple-element.75), channel_id=1, source_target_pairs={{0,12},{4,8},{8,4},{12,0},{16,28},{20,24},{24,20},{28,16},{1,13},{... | collective-permute-start | bytes 442376 | tf_op jit(solution)/shard_map/ppermute | solution.py:34
  52.3 8.7 %collective-permute-start.23 = (bf16[2,96,384]{2,1,0:T(8,128)(2,1)S(1)}, bf16[2,96,384]{2,1,0:T(8,128)(2,1)S(1)}, u32[]{:S(2)}, u32[]{:S(2)}) collective-permute-start(bf16[2,96,384]{2,1,0:T(8,128)(2,1)S(1)} %get-tuple-element.76), channel_id=1, source_target_pairs={{0,4},{4,0},{8,12},{12,8},{16,20},{20,16},{24,28},{28,24},{1,5},{5... | collective-permute-start | bytes 442376 | tf_op jit(solution)/shard_map/ppermute | solution.py:34
  52.8 8.2 %collective-permute-start.24 = (bf16[2,96,384]{2,1,0:T(8,128)(2,1)S(1)}, bf16[2,96,384]{2,1,0:T(8,128)(2,1)S(1)}, u32[]{:S(2)}, u32[]{:S(2)}) collective-permute-start(bf16[2,96,384]{2,1,0:T(8,128)(2,1)S(1)} %get-tuple-element.77), channel_id=1, source_target_pairs={{0,8},{4,12},{8,0},{12,4},{16,24},{20,28},{24,16},{28,20},{1,9},{5... | collective-permute-start | bytes 442376 | tf_op jit(solution)/shard_map/ppermute | solution.py:34
  54.1 7.6 %collective-permute-start.16 = (bf16[128,384]{1,0:T(8,128)(2,1)S(1)}, bf16[128,384]{1,0:T(8,128)(2,1)S(1)}, u32[]{:S(2)}, u32[]{:S(2)}) collective-permute-start(bf16[128,384]{1,0:T(8,128)(2,1)S(1)} %get-tuple-element.96), channel_id=1, source_target_pairs={{0,1},{1,0},{2,3},{3,2},{4,5},{5,4},{6,7},{7,6},{8,9},{9,8},{10,11... | collective-permute-start | bytes 294920 | tf_op jit(solution)/shard_map/ppermute | solution.py:34
  58.2 3.5 %collective-permute-start.17 = (bf16[128,384]{1,0:T(8,128)(2,1)S(1)}, bf16[128,384]{1,0:T(8,128)(2,1)S(1)}, u32[]{:S(2)}, u32[]{:S(2)}) collective-permute-start(bf16[128,384]{1,0:T(8,128)(2,1)S(1)} %get-tuple-element.95), channel_id=1, source_target_pairs={{0,1},{1,0},{2,3},{3,2},{4,5},{5,4},{6,7},{7,6},{8,9},{9,8},{10,11... | collective-permute-start | bytes 294920 | tf_op jit(solution)/shard_map/ppermute | solution.py:34
  61.6 8.3 %collective-permute-start.27 = (bf16[96,384]{1,0:T(8,128)(2,1)S(1)}, bf16[96,384]{1,0:T(8,128)(2,1)S(1)}, u32[]{:S(2)}, u32[]{:S(2)}) collective-permute-start(bf16[96,384]{1,0:T(8,128)(2,1)S(1)} %get-tuple-element.82), channel_id=1, source_target_pairs={{0,16},{4,20},{8,24},{12,28},{16,0},{20,4},{24,8},{28,12},{1,17},{... | collective-permute-start | bytes 221192 | tf_op jit(solution)/shard_map/ppermute | solution.py:34
  63.3 11.1 %collective-permute-start.28 = (bf16[2,96,768]{2,1,0:T(8,128)(2,1)S(1)}, bf16[2,96,768]{2,1,0:T(8,128)(2,1)S(1)}, u32[]{:S(2)}, u32[]{:S(2)}) collective-permute-start(bf16[2,96,768]{2,1,0:T(8,128)(2,1)S(1)} %get-tuple-element.83), channel_id=1, source_target_pairs={{0,12},{4,8},{8,4},{12,0},{16,28},{20,24},{24,20},{28,16},{1,13},{... | collective-permute-start | bytes 884744 | tf_op jit(solution)/shard_map/ppermute | solution.py:34
  65.4 14.3 %collective-permute-start.29 = (bf16[2,96,768]{2,1,0:T(8,128)(2,1)S(1)}, bf16[2,96,768]{2,1,0:T(8,128)(2,1)S(1)}, u32[]{:S(2)}, u32[]{:S(2)}) collective-permute-start(bf16[2,96,768]{2,1,0:T(8,128)(2,1)S(1)} %get-tuple-element.84), channel_id=1, source_target_pairs={{0,4},{4,0},{8,12},{12,8},{16,20},{20,16},{24,28},{28,24},{1,5},{5... | collective-permute-start | bytes 884744 | tf_op jit(solution)/shard_map/ppermute | solution.py:34
  65.9 13.9 %collective-permute-start.30 = (bf16[2,96,768]{2,1,0:T(8,128)(2,1)S(1)}, bf16[2,96,768]{2,1,0:T(8,128)(2,1)S(1)}, u32[]{:S(2)}, u32[]{:S(2)}) collective-permute-start(bf16[2,96,768]{2,1,0:T(8,128)(2,1)S(1)} %get-tuple-element.85), channel_id=1, source_target_pairs={{0,8},{4,12},{8,0},{12,4},{16,24},{20,28},{24,16},{28,20},{1,9},{5... | collective-permute-start | bytes 884744 | tf_op jit(solution)/shard_map/ppermute | solution.py:34
  68.4 13.9 %collective-permute-start.25 = (bf16[128,1536]{1,0:T(8,128)(2,1)S(1)}, bf16[128,1536]{1,0:T(8,128)(2,1)S(1)}, u32[]{:S(2)}, u32[]{:S(2)}) collective-permute-start(bf16[128,1536]{1,0:T(8,128)(2,1)S(1)} %get-tuple-element.80.refs_1_), channel_id=1, source_target_pairs={{0,2},{2,0},{1,3},{3,1},{4,6},{6,4},{5,7},{7,5},{8,10},{10,8},{9,1... | collective-permute-start | bytes 1179656 | tf_op jit(solution)/shard_map/ppermute | solution.py:34
  70.0 16.9 %collective-permute-start.26 = (bf16[128,1536]{1,0:T(8,128)(2,1)S(1)}, bf16[128,1536]{1,0:T(8,128)(2,1)S(1)}, u32[]{:S(2)}, u32[]{:S(2)}) collective-permute-start(bf16[128,1536]{1,0:T(8,128)(2,1)S(1)} %get-tuple-element.81.refs_5_.refs_3_), channel_id=1, source_target_pairs={{0,2},{2,0},{1,3},{3,1},{4,6},{6,4},{5,7},{7,5},{8,10},{10,8},{9,1... | collective-permute-start | bytes 1179656 | tf_op jit(solution)/shard_map/ppermute | solution.py:34
  80.4 9.4 %collective-permute-start.31 = (bf16[96,768]{1,0:T(8,128)(2,1)S(1)}, bf16[96,768]{1,0:T(8,128)(2,1)S(1)}, u32[]{:S(2)}, u32[]{:S(2)}) collective-permute-start(bf16[96,768]{1,0:T(8,128)(2,1)S(1)} %get-tuple-element.87), channel_id=1, source_target_pairs={{0,16},{4,20},{8,24},{12,28},{16,0},{20,4},{24,8},{28,12},{1,17},{... | collective-permute-start | bytes 442376 | tf_op jit(solution)/shard_map/ppermute | solution.py:34
  (5 other events, 41.9 us)

commit v12 on v11

--- a/solution.py
+++ b/solution.py
@@ -459,7 +459,7 @@
         scratch=[
             pltpu.VMEM((rows, channels), BF16),
             pltpu.VMEM((channels, width), BF16),
-            pltpu.SemaphoreType.DMA((2, 6)),
+            pltpu.SemaphoreType.DMA((2, 3)),
         ],
         spaces={1: pltpu.HBM, 2: pltpu.HBM},
     )

time: 91.7 us -> 91.2 us (level)
  no operation moved by 1% of the time
where the time goes in v12:
time: 91.2 us; the launch traced here: 91 us
  waiting for transfers between devices  39.9 us (44%)
  starting transfers between devices  24.9 us (27%)
  Pallas kernels  24.1 us (26%)
  local copies, waits for them, and re-layouts  1.27 us (1%)
    ppermute x30, waiting for transfers between devices, flip(): return lax.ppermute(value, axis, [(i, i ^ step) for i in range(count)])  30.4 us
    pallas_call x14, Pallas kernels, kernel_call(): pl.pallas_call(run, out_shape=[jax.ShapeDtypeStruct(s, d) for s, d in out...  24.1 us
    ppermute x30, starting transfers between devices, flip(): return lax.ppermute(value, axis, [(i, i ^ step) for i in range(count)])  22.2 us
    ppermute x1, waiting for transfers between devices, body(): arrived = lax.ppermute(term, 'seq', pairs)  8.4 us
    ppermute x1, starting transfers between devices, body(): arrived = lax.ppermute(term, 'seq', pairs)  2.66 us
  transfers between devices with their start and end apart: 32, of which 15 were waited for; matrix products, arithmetic and copies ran while one was open for 1% of the time, Pallas kernels for 25%

profile of v12, /device:TPU:0, one launch (start us, length us, event | category | flops | bytes accessed | tf_op | source)
XLA Modules:
  0.0 91.0 jit_solution(12861445054663028796)
XLA Ops:
  1.1 1.1 %constant_dynamic-slice_fusion.refs_3_ = bf16[768,384]{1,0:T(8,128)(2,1)S(1)} fusion(bf16[1536,384]{1,0:T(8,128)(2,1)} %refs_6_.1, s32[]{:T(128)S(6)} %select_n.8), kind=kLoop, calls=%fused_computation | loop fusion | bytes 1179652 | tf_op jit(solution)/shard_map/dynamic_slice | solution.py:451
  2.3 2.6 %collective-permute-start.1 = (bf16[768,384]{1,0:T(8,128)(2,1)S(1)}, bf16[768,384]{1,0:T(8,128)(2,1)}, u32[]{:S(2)}, u32[]{:S(2)}) collective-permute-start(bf16[768,384]{1,0:T(8,128)(2,1)S(1)} %constant_dynamic-slice_fusion.refs_3_), channel_id=1, source_target_pairs={{0,2},{2,0},{1,3},{3,1},{4,6},{6,4},{5,7},{7,5},{8,10},{10,8},{9,1... | collective-permute-start | bytes 1769480 | tf_op jit(solution)/shard_map/ppermute | solution.py:34
  4.9 3.1 %outer_term.1 = (bf16[256,1536]{1,0:T(8,128)(2,1)S(1)}, bf16[256,384]{1,0:T(8,128)(2,1)S(1)}) custom-call(s32[6]{0:T(128)S(1)} %stack.27.refs_0_, bf16[256,1536]{1,0:T(8,128)(2,1)} %bitcast.14, bf16[3,1536,384]{2,1,0:T(8,128)(2,1)} %bitcast.11, bf16[768,384]{1,0:T(8,128)(2,1)S(1)} %constant_dynamic-slice_fusion.refs_3_), custom_call_target="tpu_custom_call" | custom-call | flops 1 | bytes 1 | tf_op jit(solution)/shard_map/outer_term/pallas_call | solution.py:200
  8.1 2.7 %collective-permute-start = (bf16[256,384]{1,0:T(8,128)(2,1)S(1)}, bf16[256,384]{1,0:T(8,128)(2,1)S(1)}, u32[]{:S(2)}, u32[]{:S(2)}) collective-permute-start(bf16[256,384]{1,0:T(8,128)(2,1)S(1)} %get-tuple-element.49), channel_id=1, source_target_pairs={{0,16},{4,20},{8,24},{12,28},{16,0},{20,4},{24,8},{28,12},{1,17},{... | collective-permute-start | bytes 589832 | tf_op jit(solution)/shard_map/ppermute | solution.py:466
  10.8 1.1 %middle_term.1 = (f32[256,384]{1,0:T(8,128)S(1)}, bf16[8,96,256]{2,1,0:T(8,128)(2,1)S(1)}, bf16[8,96,256]{2,1,0:T(8,128)(2,1)S(1)}) custom-call(s32[6]{0:T(128)S(1)} %stack.27.refs_0_, bf16[256,1536]{1,0:T(8,128)(2,1)S(1)} %get-tuple-element.47.refs_1_, bf16[3,1536,384]{2,1,0:T(8,128)(2,1)S(1)} %bitcast.12), custom_call_target="tpu_custom_call" | custom-call | flops 1 | bytes 1 | tf_op jit(solution)/shard_map/middle_term/pallas_call | solution.py:200
  11.9 8.4 %collective-permute-done.refs_2_ = bf16[256,384]{1,0:T(8,128)(2,1)S(1)} collective-permute-done((bf16[256,384]{1,0:T(8,128)(2,1)S(1)}, bf16[256,384]{1,0:T(8,128)(2,1)S(1)}, u32[]{:S(2)}, u32[]{:S(2)}) %collective-permute-start) | collective-permute-done | bytes 196640 | tf_op jit(solution)/shard_map/ppermute | solution.py:466
  21.5 2.8 %own_hidden.1 = (bf16[256,384]{1,0:T(8,128)(2,1)S(1)}, f32[256,1536]{1,0:T(8,128)S(1)}, f32[256,384]{1,0:T(8,128)S(1)}, f32[256,1536]{1,0:T(8,128)S(1)}, bf16[25...) custom-call(s32[6]{0:T(128)S(1)} %stack.27.refs_0_, ...), custom_call_target="tpu_custom_call" | custom-call | flops 1 | bytes 1 | tf_op jit(solution)/shard_map/own_hidden/pallas_call | solution.py:200
  24.9 2.3 %collective-permute-done.2.refs_2_ = bf16[256,384]{1,0:T(8,128)(2,1)S(1)} collective-permute-done((bf16[256,384]{1,0:T(8,128)(2,1)S(1)}, bf16[256,384]{1,0:T(8,128)(2,1)S(1)}, u32[]{:S(2)}, u32[]{:S(2)}) %collective-permute-start.2) | collective-permute-done | bytes 196640 | tf_op jit(solution)/shard_map/ppermute | solution.py:34
  27.7 6.6 %tracks.1 = (bf16[256,1536]{1,0:T(8,128)(2,1)S(1)}, bf16[256,384]{1,0:T(8,128)(2,1)S(1)}, f32[256,384]{1,0:T(8,128)S(1)}, bf16[256,384]{1,0:T(8,128)(2,1)S(1)}) custom-call(s32[6]{0:T(128)S(1)} %stack.27.refs_0_, f32[256,1536]{1,0:T(8,128)S(1)} %get-tuple-element.52.refs_1_, bf16[256,384]{1,0:T(8,128)(2,1)S(1)} %collective-permute-done.2.refs_2_, ...), custom_call_target="tpu_custom_call" | custom-call | flops 1 | bytes 1 | tf_op jit(solution)/shard_map/tracks/pallas_call | solution.py:200
  34.3 0.9 collective-permute-start.7
  35.2 1.0 %turn_parts.1 = (bf16[8,96,256]{2,1,0:T(8,128)(2,1)S(1)}, bf16[256,384]{1,0:T(8,128)(2,1)S(1)}, bf16[3,96,256]{2,1,0:T(8,128)(2,1)S(1)}, bf16[3,96,256]{2,1,0:T(8,128)(2,1)S(1)}, bf16[2,96,256]{2,1,0:T(8,128)(2,1)S(1)}) custom-call(s32[6]{0:T(128)S(1)} %stack.27.refs_0_, bf16[256,1536]{1,0:T(8,128)(2,1)S(1)} %get-tuple-element.60.refs_1_.refs_4_, ...), custom_call_target="tpu_custom_call" | custom-call | flops 1 | bytes 1 | tf_op jit(solution)/shard_map/turn_parts/pallas_call | solution.py:200
  37.3 1.4 %collective-permute-done.12.refs_6_ = bf16[2,96,256]{2,1,0:T(8,128)(2,1)S(1)} collective-permute-done((bf16[2,96,256]{2,1,0:T(8,128)(2,1)S(1)}, bf16[2,96,256]{2,1,0:T(8,128)(2,1)S(1)}, u32[]{:S(2)}, u32[]{:S(2)}) %collective-permute-start.12) | collective-permute-done | bytes 98336 | tf_op jit(solution)/shard_map/ppermute | solution.py:34
  38.6 1.1 %other_points.1 = (bf16[8,96,384]{2,1,0:T(8,128)(2,1)S(1)}, bf16[8,96,256]{2,1,0:T(8,128)(2,1)S(1)}) custom-call(s32[6]{0:T(128)S(1)} %stack.27.refs_0_, bf16[8,96,256]{2,1,0:T(8,128)(2,1)S(1)} %get-tuple-element.62.refs_1_.refs_4_, bf16[256,384]{1,0:T(8,128)(2,1)S(1)} %get-tuple-element.63.refs_2_, bf16[256,384]{1,0:T(8,128)(2,1)S(1)} %get-tuple-element.64.refs_3_, ...), custom_call_target="tpu_custom_call" | custom-call | flops 1 | bytes 1 | tf_op jit(solution)/shard_map/other_points/pallas_call | solution.py:200
  39.7 1.5 %collective-permute-done.7.refs_2_ = bf16[256,384]{1,0:T(8,128)(2,1)S(1)} collective-permute-done((bf16[256,384]{1,0:T(8,128)(2,1)S(1)}, bf16[256,384]{1,0:T(8,128)(2,1)S(1)}, u32[]{:S(2)}, u32[]{:S(2)}) %collective-permute-start.7) | collective-permute-done | bytes 196640 | tf_op jit(solution)/shard_map/ppermute | solution.py:34
  41.8 0.9 collective-permute-start.15
  44.6 0.7 collective-permute-done.21.refs_7_
  45.3 1.1 %middle_products.1 = (f32[2,96,384]{2,1,0:T(8,128)S(1)}, bf16[2,96,384]{2,1,0:T(8,128)(2,1)S(1)}, bf16[2,96,384]{2,1,0:T(8,128)(2,1)S(1)}, bf16[2,96,384]{2,1,0:T(8,128)(2,1)S(1)}) custom-call(s32[6]{0:T(128)S(1)} %stack.27.refs_0_, bf16[8,96,256]{2,1,0:T(8,128)(2,1)S(1)} %get-tuple-element.50.refs_3_.refs_1_, ...), custom_call_target="tpu_custom_call" | custom-call | flops 1 | bytes 1 | tf_op jit(solution)/shard_map/middle_products/pallas_call | solution.py:200
  46.4 5.5 %collective-permute-start.22 = (bf16[2,96,384]{2,1,0:T(8,128)(2,1)S(1)}, bf16[2,96,384]{2,1,0:T(8,128)(2,1)S(1)}, u32[]{:S(2)}, u32[]{:S(2)}) collective-permute-start(bf16[2,96,384]{2,1,0:T(8,128)(2,1)S(1)} %get-tuple-element.75), channel_id=1, source_target_pairs={{0,12},{4,8},{8,4},{12,0},{16,28},{20,24},{24,20},{28,16},{1,13},{... | collective-permute-start | bytes 442376 | tf_op jit(solution)/shard_map/ppermute | solution.py:34
  52.5 1.1 %collective-permute-done.13.refs_3_.refs_2_ = bf16[256,384]{1,0:T(8,128)(2,1)S(1)} collective-permute-done((bf16[256,384]{1,0:T(8,128)(2,1)S(1)}, bf16[256,384]{1,0:T(8,128)(2,1)S(1)}, u32[]{:S(2)}, u32[]{:S(2)}) %collective-permute-start.13) | collective-permute-done | bytes 196640 | tf_op jit(solution)/shard_map/ppermute | solution.py:536
  53.7 4.0 %collective-permute-done.22.refs_2_ = bf16[2,96,384]{2,1,0:T(8,128)(2,1)S(1)} collective-permute-done((bf16[2,96,384]{2,1,0:T(8,128)(2,1)S(1)}, bf16[2,96,384]{2,1,0:T(8,128)(2,1)S(1)}, u32[]{:S(2)}, u32[]{:S(2)}) %collective-permute-start.22) | collective-permute-done | bytes 147488 | tf_op jit(solution)/shard_map/ppermute | solution.py:34
  57.7 2.8 %collective-permute-done.23.refs_3_ = bf16[2,96,384]{2,1,0:T(8,128)(2,1)S(1)} collective-permute-done((bf16[2,96,384]{2,1,0:T(8,128)(2,1)S(1)}, bf16[2,96,384]{2,1,0:T(8,128)(2,1)S(1)}, u32[]{:S(2)}, u32[]{:S(2)}) %collective-permute-start.23) | collective-permute-done | bytes 147488 | tf_op jit(solution)/shard_map/ppermute | solution.py:34
  61.3 1.5 %late_products.1 = (f32[2,96,768]{2,1,0:T(8,128)S(1)}, bf16[2,96,768]{2,1,0:T(8,128)(2,1)S(1)}, bf16[2,96,768]{2,1,0:T(8,128)(2,1)S(1)}, bf16[2,96,768]{2,1,0:T(8,128)(2,1)S(1)}) custom-call(s32[6]{0:T(128)S(1)} %stack.27.refs_0_, bf16[8,96,256]{2,1,0:T(8,128)(2,1)S(1)} %get-tuple-element.50.refs_3_.refs_1_, ...), custom_call_target="tpu_custom_call" | custom-call | flops 1 | bytes 1 | tf_op jit(solution)/shard_map/late_products/pallas_call | solution.py:200
  62.8 2.1 %collective-permute-start.28 = (bf16[2,96,768]{2,1,0:T(8,128)(2,1)S(1)}, bf16[2,96,768]{2,1,0:T(8,128)(2,1)S(1)}, u32[]{:S(2)}, u32[]{:S(2)}) collective-permute-start(bf16[2,96,768]{2,1,0:T(8,128)(2,1)S(1)} %get-tuple-element.83), channel_id=1, source_target_pairs={{0,12},{4,8},{8,4},{12,0},{16,28},{20,24},{24,20},{28,16},{1,13},{... | collective-permute-start | bytes 884744 | tf_op jit(solution)/shard_map/ppermute | solution.py:34
  65.4 1.0 %collective-permute-start.30 = (bf16[2,96,768]{2,1,0:T(8,128)(2,1)S(1)}, bf16[2,96,768]{2,1,0:T(8,128)(2,1)S(1)}, u32[]{:S(2)}, u32[]{:S(2)}) collective-permute-start(bf16[2,96,768]{2,1,0:T(8,128)(2,1)S(1)} %get-tuple-element.85), channel_id=1, source_target_pairs={{0,8},{4,12},{8,0},{12,4},{16,24},{20,28},{24,16},{28,20},{1,9},{5... | collective-permute-start | bytes 884744 | tf_op jit(solution)/shard_map/ppermute | solution.py:34
  66.4 1.6 %act_part.1 = (bf16[128,1536]{1,0:T(8,128)(2,1)S(1)}, bf16[128,1536]{1,0:T(8,128)(2,1)S(1)}) custom-call(s32[6]{0:T(128)S(1)} %stack.27.refs_0_, bf16[256,384]{1,0:T(8,128)(2,1)S(1)} %get-tuple-element.69.refs_3_.refs_1_, bf16[256,384]{1,0:T(8,128)(2,1)S(1)} %collective-permute-done.13.refs_3_.refs_2_, bf16[3,1536,384]{2,1,0:T(8,128)(2,1)S(1)} %bitcast.13, ...), custom_call_target="tpu_custom_call" | custom-call | flops 1 | bytes 1 | tf_op jit(solution)/shard_map/act_part/pallas_call | solution.py:200
  67.9 1.5 %collective-permute-start.25 = (bf16[128,1536]{1,0:T(8,128)(2,1)S(1)}, bf16[128,1536]{1,0:T(8,128)(2,1)S(1)}, u32[]{:S(2)}, u32[]{:S(2)}) collective-permute-start(bf16[128,1536]{1,0:T(8,128)(2,1)S(1)} %get-tuple-element.80.refs_1_), channel_id=1, source_target_pairs={{0,2},{2,0},{1,3},{3,1},{4,6},{6,4},{5,7},{7,5},{8,10},{10,8},{9,1... | collective-permute-start | bytes 1179656 | tf_op jit(solution)/shard_map/ppermute | solution.py:34
  70.0 3.9 %collective-permute-done.28.refs_2_ = bf16[2,96,768]{2,1,0:T(8,128)(2,1)S(1)} collective-permute-done((bf16[2,96,768]{2,1,0:T(8,128)(2,1)S(1)}, bf16[2,96,768]{2,1,0:T(8,128)(2,1)S(1)}, u32[]{:S(2)}, u32[]{:S(2)}) %collective-permute-start.28) | collective-permute-done | bytes 294944 | tf_op jit(solution)/shard_map/ppermute | solution.py:34
  73.9 5.2 %collective-permute-done.29.refs_3_ = bf16[2,96,768]{2,1,0:T(8,128)(2,1)S(1)} collective-permute-done((bf16[2,96,768]{2,1,0:T(8,128)(2,1)S(1)}, bf16[2,96,768]{2,1,0:T(8,128)(2,1)S(1)}, u32[]{:S(2)}, u32[]{:S(2)}) %collective-permute-start.29) | collective-permute-done | bytes 294944 | tf_op jit(solution)/shard_map/ppermute | solution.py:34
  80.0 1.9 %collective-permute-start.31 = (bf16[96,768]{1,0:T(8,128)(2,1)S(1)}, bf16[96,768]{1,0:T(8,128)(2,1)S(1)}, u32[]{:S(2)}, u32[]{:S(2)}) collective-permute-start(bf16[96,768]{1,0:T(8,128)(2,1)S(1)} %get-tuple-element.87), channel_id=1, source_target_pairs={{0,16},{4,20},{8,24},{12,28},{16,0},{20,4},{24,8},{28,12},{1,17},{... | collective-permute-start | bytes 442376 | tf_op jit(solution)/shard_map/ppermute | solution.py:34
  81.9 4.5 %collective-permute-done.26.refs_4_ = bf16[128,1536]{1,0:T(8,128)(2,1)S(1)} collective-permute-done((bf16[128,1536]{1,0:T(8,128)(2,1)S(1)}, bf16[128,1536]{1,0:T(8,128)(2,1)S(1)}, u32[]{:S(2)}, u32[]{:S(2)}) %collective-permute-start.26) | collective-permute-done | bytes 393248 | tf_op jit(solution)/shard_map/ppermute | solution.py:34
  86.4 2.9 %collective-permute-done.31.refs_8_ = bf16[96,768]{1,0:T(8,128)(2,1)S(1)} collective-permute-done((bf16[96,768]{1,0:T(8,128)(2,1)S(1)}, bf16[96,768]{1,0:T(8,128)(2,1)S(1)}, u32[]{:S(2)}, u32[]{:S(2)}) %collective-permute-start.31) | collective-permute-done | bytes 147488 | tf_op jit(solution)/shard_map/ppermute | solution.py:34
  89.3 1.7 %finish.1 = (f32[3,96,384]{2,1,0:T(8,128)}, f32[96,384]{1,0:T(8,128)}, bf16[256,1536]{1,0:T(8,128)(2,1)}) custom-call(s32[6]{0:T(128)S(1)} %stack.27.refs_0_, bf16[128,1536]{1,0:T(8,128)(2,1)S(1)} %get-tuple-element.80.refs_1_, bf16[128,1536]{1,0:T(8,128)(2,1)S(1)} %collective-permute-done.25.refs_2_, ...), custom_call_target="tpu_custom_call" | custom-call | flops 1 | bytes 1 | tf_op jit(solution)/shard_map/finish/pallas_call | solution.py:200
  (60 shorter events, 9.8 us)
Async XLA Ops:
  0.6 27.1 %collective-permute-start.3 = (bf16[768,1920]{1,0:T(8,128)(2,1)}, bf16[768,1920]{1,0:T(8,128)(2,1)S(1)}, u32[]{:S(2)}, u32[]{:S(2)}) collective-permute-start(bf16[768,1920]{1,0:T(8,128)(2,1)} %refs_3_.3), channel_id=1, source_target_pairs={{0,1},{1,0},{2,3},{3,2},{4,5},{5,4},{6,7},{7,6},{8,9},{9,8},{10,11... | collective-permute-start | bytes 8847368 | tf_op jit(solution)/shard_map/ppermute | solution.py:34
  2.3 19.2 %collective-permute-start.1 = (bf16[768,384]{1,0:T(8,128)(2,1)S(1)}, bf16[768,384]{1,0:T(8,128)(2,1)}, u32[]{:S(2)}, u32[]{:S(2)}) collective-permute-start(bf16[768,384]{1,0:T(8,128)(2,1)S(1)} %constant_dynamic-slice_fusion.refs_3_), channel_id=1, source_target_pairs={{0,2},{2,0},{1,3},{3,1},{4,6},{6,4},{5,7},{7,5},{8,10},{10,8},{9,1... | collective-permute-start | bytes 1769480 | tf_op jit(solution)/shard_map/ppermute | solution.py:34
  8.1 12.2 %collective-permute-start = (bf16[256,384]{1,0:T(8,128)(2,1)S(1)}, bf16[256,384]{1,0:T(8,128)(2,1)S(1)}, u32[]{:S(2)}, u32[]{:S(2)}) collective-permute-start(bf16[256,384]{1,0:T(8,128)(2,1)S(1)} %get-tuple-element.49), channel_id=1, source_target_pairs={{0,16},{4,20},{8,24},{12,28},{16,0},{20,4},{24,8},{28,12},{1,17},{... | collective-permute-start | bytes 589832 | tf_op jit(solution)/shard_map/ppermute | solution.py:466
  20.9 6.3 %collective-permute-start.2 = (bf16[256,384]{1,0:T(8,128)(2,1)S(1)}, bf16[256,384]{1,0:T(8,128)(2,1)S(1)}, u32[]{:S(2)}, u32[]{:S(2)}) collective-permute-start(bf16[256,384]{1,0:T(8,128)(2,1)S(1)} %get-tuple-element.53), channel_id=1, source_target_pairs={{0,2},{2,0},{1,3},{3,1},{4,6},{6,4},{5,7},{7,5},{8,10},{10,8},{9,1... | collective-permute-start | bytes 589832 | tf_op jit(solution)/shard_map/ppermute | solution.py:34
  24.2 2.9 %collective-permute-start.4 = (bf16[256,384]{1,0:T(8,128)(2,1)S(1)}, bf16[256,384]{1,0:T(8,128)(2,1)S(1)}, u32[]{:S(2)}, u32[]{:S(2)}) collective-permute-start(bf16[256,384]{1,0:T(8,128)(2,1)S(1)} %get-tuple-element.54), channel_id=1, source_target_pairs={{0,1},{1,0},{2,3},{3,2},{4,5},{5,4},{6,7},{7,6},{8,9},{9,8},{10,11... | collective-permute-start | bytes 589832 | tf_op jit(solution)/shard_map/ppermute | solution.py:34
  24.3 3.4 %collective-permute-start.5 = (bf16[256,384]{1,0:T(8,128)(2,1)S(1)}, bf16[256,384]{1,0:T(8,128)(2,1)S(1)}, u32[]{:S(2)}, u32[]{:S(2)}) collective-permute-start(bf16[256,384]{1,0:T(8,128)(2,1)S(1)} %get-tuple-element.55), channel_id=1, source_target_pairs={{0,1},{1,0},{2,3},{3,2},{4,5},{5,4},{6,7},{7,6},{8,9},{9,8},{10,11... | collective-permute-start | bytes 589832 | tf_op jit(solution)/shard_map/ppermute | solution.py:34
  24.8 2.9 %collective-permute-start.6 = (bf16[256,384]{1,0:T(8,128)(2,1)S(1)}, bf16[256,384]{1,0:T(8,128)(2,1)S(1)}, u32[]{:S(2)}, u32[]{:S(2)}) collective-permute-start(bf16[256,384]{1,0:T(8,128)(2,1)S(1)} %get-tuple-element.56), channel_id=1, source_target_pairs={{0,1},{1,0},{2,3},{3,2},{4,5},{5,4},{6,7},{7,6},{8,9},{9,8},{10,11... | collective-permute-start | bytes 589832 | tf_op jit(solution)/shard_map/ppermute | solution.py:34
  27.2 8.0 %collective-permute-start.8 = (bf16[256,384]{1,0:T(8,128)(2,1)S(1)}, bf16[256,384]{1,0:T(8,128)(2,1)S(1)}, u32[]{:S(2)}, u32[]{:S(2)}) collective-permute-start(bf16[256,384]{1,0:T(8,128)(2,1)S(1)} %collective-permute-done.2.refs_2_), channel_id=1, source_target_pairs={{0,1},{1,0},{2,3},{3,2},{4,5},{5,4},{6,7},{7,6},{8,9},{9,8},{10,11... | collective-permute-start | bytes 589832 | tf_op jit(solution)/shard_map/ppermute | solution.py:34
  27.2 8.0 %collective-permute-start.9 = (bf16[256,384]{1,0:T(8,128)(2,1)S(1)}, bf16[256,384]{1,0:T(8,128)(2,1)S(1)}, u32[]{:S(2)}, u32[]{:S(2)}) collective-permute-start(bf16[256,384]{1,0:T(8,128)(2,1)S(1)} %get-tuple-element.61.refs_6_), channel_id=1, source_target_pairs={{0,1},{1,0},{2,3},{3,2},{4,5},{5,4},{6,7},{7,6},{8,9},{9,8},{10,11... | collective-permute-start | bytes 589832 | tf_op jit(solution)/shard_map/ppermute | solution.py:34
  34.3 6.9 %collective-permute-start.7 = (bf16[256,384]{1,0:T(8,128)(2,1)S(1)}, bf16[256,384]{1,0:T(8,128)(2,1)S(1)}, u32[]{:S(2)}, u32[]{:S(2)}) collective-permute-start(bf16[256,384]{1,0:T(8,128)(2,1)S(1)} %get-tuple-element.58), channel_id=1, source_target_pairs={{0,2},{2,0},{1,3},{3,1},{4,6},{6,4},{5,7},{7,5},{8,10},{10,8},{9,1... | collective-permute-start | bytes 589832 | tf_op jit(solution)/shard_map/ppermute | solution.py:34
  36.2 2.4 %collective-permute-start.10 = (bf16[3,96,256]{2,1,0:T(8,128)(2,1)S(1)}, bf16[3,96,256]{2,1,0:T(8,128)(2,1)S(1)}, u32[]{:S(2)}, u32[]{:S(2)}) collective-permute-start(bf16[3,96,256]{2,1,0:T(8,128)(2,1)S(1)} %get-tuple-element.65), channel_id=1, source_target_pairs={{0,1},{1,0},{2,3},{3,2},{4,5},{5,4},{6,7},{7,6},{8,9},{9,8},{10,11... | collective-permute-start | bytes 442376 | tf_op jit(solution)/shard_map/ppermute | solution.py:34
  36.2 2.4 %collective-permute-start.11 = (bf16[3,96,256]{2,1,0:T(8,128)(2,1)S(1)}, bf16[3,96,256]{2,1,0:T(8,128)(2,1)S(1)}, u32[]{:S(2)}, u32[]{:S(2)}) collective-permute-start(bf16[3,96,256]{2,1,0:T(8,128)(2,1)S(1)} %get-tuple-element.66), channel_id=1, source_target_pairs={{0,1},{1,0},{2,3},{3,2},{4,5},{5,4},{6,7},{7,6},{8,9},{9,8},{10,11... | collective-permute-start | bytes 442376 | tf_op jit(solution)/shard_map/ppermute | solution.py:34
  36.7 6.6 %collective-permute-start.14 = (bf16[8,96,256]{2,1,0:T(8,128)(2,1)S(1)}, bf16[8,96,256]{2,1,0:T(8,128)(2,1)S(1)}, u32[]{:S(2)}, u32[]{:S(2)}) collective-permute-start(bf16[8,96,256]{2,1,0:T(8,128)(2,1)S(1)} %get-tuple-element.71), channel_id=1, source_target_pairs={{0,1},{1,0},{2,3},{3,2},{4,5},{5,4},{6,7},{7,6},{8,9},{9,8},{10,11... | collective-permute-start | bytes 1179656 | tf_op jit(solution)/shard_map/ppermute | solution.py:34
  36.8 1.8 %collective-permute-start.12 = (bf16[2,96,256]{2,1,0:T(8,128)(2,1)S(1)}, bf16[2,96,256]{2,1,0:T(8,128)(2,1)S(1)}, u32[]{:S(2)}, u32[]{:S(2)}) collective-permute-start(bf16[2,96,256]{2,1,0:T(8,128)(2,1)S(1)} %get-tuple-element.67), channel_id=1, source_target_pairs={{0,1},{1,0},{2,3},{3,2},{4,5},{5,4},{6,7},{7,6},{8,9},{9,8},{10,11... | collective-permute-start | bytes 294920 | tf_op jit(solution)/shard_map/ppermute | solution.py:34
  41.8 19.4 %collective-permute-start.15 = (bf16[8,96,384]{2,1,0:T(8,128)(2,1)S(1)}, bf16[8,96,384]{2,1,0:T(8,128)(2,1)S(1)}, u32[]{:S(2)}, u32[]{:S(2)}) collective-permute-start(bf16[8,96,384]{2,1,0:T(8,128)(2,1)S(1)} %get-tuple-element.73), channel_id=1, source_target_pairs={{0,2},{2,0},{1,3},{3,1},{4,6},{6,4},{5,7},{7,5},{8,10},{10,8},{9,1... | collective-permute-start | bytes 1769480 | tf_op jit(solution)/shard_map/ppermute | solution.py:34
  42.7 10.9 %collective-permute-start.13 = (bf16[256,384]{1,0:T(8,128)(2,1)S(1)}, bf16[256,384]{1,0:T(8,128)(2,1)S(1)}, u32[]{:S(2)}, u32[]{:S(2)}) collective-permute-start(bf16[256,384]{1,0:T(8,128)(2,1)S(1)} %get-tuple-element.69.refs_3_.refs_1_), channel_id=1, source_target_pairs={{0,16},{4,20},{8,24},{12,28},{16,0},{20,4},{24,8},{28,12},{1,17},{... | collective-permute-start | bytes 589832 | tf_op jit(solution)/shard_map/ppermute | solution.py:536
  42.8 1.3 %collective-permute-start.18 = (bf16[64,384]{1,0:T(8,128)(2,1)S(1)}, bf16[64,384]{1,0:T(8,128)(2,1)S(1)}, u32[]{:S(2)}, u32[]{:S(2)}) collective-permute-start(bf16[64,384]{1,0:T(8,128)(2,1)S(1)} %get-tuple-element.94), channel_id=1, source_target_pairs={{0,1},{1,0},{2,3},{3,2},{4,5},{5,4},{6,7},{7,6},{8,9},{9,8},{10,11... | collective-permute-start | bytes 147464 | tf_op jit(solution)/shard_map/ppermute | solution.py:34
  42.8 1.4 %collective-permute-start.19 = (bf16[64,384]{1,0:T(8,128)(2,1)S(1)}, bf16[64,384]{1,0:T(8,128)(2,1)S(1)}, u32[]{:S(2)}, u32[]{:S(2)}) collective-permute-start(bf16[64,384]{1,0:T(8,128)(2,1)S(1)} %get-tuple-element.93), channel_id=1, source_target_pairs={{0,1},{1,0},{2,3},{3,2},{4,5},{5,4},{6,7},{7,6},{8,9},{9,8},{10,11... | collective-permute-start | bytes 147464 | tf_op jit(solution)/shard_map/ppermute | solution.py:34
  43.3 1.2 %collective-permute-start.20 = (bf16[64,384]{1,0:T(8,128)(2,1)S(1)}, bf16[64,384]{1,0:T(8,128)(2,1)S(1)}, u32[]{:S(2)}, u32[]{:S(2)}) collective-permute-start(bf16[64,384]{1,0:T(8,128)(2,1)S(1)} %get-tuple-element.92), channel_id=1, source_target_pairs={{0,1},{1,0},{2,3},{3,2},{4,5},{5,4},{6,7},{7,6},{8,9},{9,8},{10,11... | collective-permute-start | bytes 147464 | tf_op jit(solution)/shard_map/ppermute | solution.py:34
  44.0 1.2 %collective-permute-start.21 = (bf16[64,384]{1,0:T(8,128)(2,1)S(1)}, bf16[64,384]{1,0:T(8,128)(2,1)S(1)}, u32[]{:S(2)}, u32[]{:S(2)}) collective-permute-start(bf16[64,384]{1,0:T(8,128)(2,1)S(1)} %get-tuple-element.91), channel_id=1, source_target_pairs={{0,1},{1,0},{2,3},{3,2},{4,5},{5,4},{6,7},{7,6},{8,9},{9,8},{10,11... | collective-permute-start | bytes 147464 | tf_op jit(solution)/shard_map/ppermute | solution.py:34
  46.4 11.3 %collective-permute-start.22 = (bf16[2,96,384]{2,1,0:T(8,128)(2,1)S(1)}, bf16[2,96,384]{2,1,0:T(8,128)(2,1)S(1)}, u32[]{:S(2)}, u32[]{:S(2)}) collective-permute-start(bf16[2,96,384]{2,1,0:T(8,128)(2,1)S(1)} %get-tuple-element.75), channel_id=1, source_target_pairs={{0,12},{4,8},{8,4},{12,0},{16,28},{20,24},{24,20},{28,16},{1,13},{... | collective-permute-start | bytes 442376 | tf_op jit(solution)/shard_map/ppermute | solution.py:34
  51.9 8.7 %collective-permute-start.23 = (bf16[2,96,384]{2,1,0:T(8,128)(2,1)S(1)}, bf16[2,96,384]{2,1,0:T(8,128)(2,1)S(1)}, u32[]{:S(2)}, u32[]{:S(2)}) collective-permute-start(bf16[2,96,384]{2,1,0:T(8,128)(2,1)S(1)} %get-tuple-element.76), channel_id=1, source_target_pairs={{0,4},{4,0},{8,12},{12,8},{16,20},{20,16},{24,28},{28,24},{1,5},{5... | collective-permute-start | bytes 442376 | tf_op jit(solution)/shard_map/ppermute | solution.py:34
  52.4 8.2 %collective-permute-start.24 = (bf16[2,96,384]{2,1,0:T(8,128)(2,1)S(1)}, bf16[2,96,384]{2,1,0:T(8,128)(2,1)S(1)}, u32[]{:S(2)}, u32[]{:S(2)}) collective-permute-start(bf16[2,96,384]{2,1,0:T(8,128)(2,1)S(1)} %get-tuple-element.77), channel_id=1, source_target_pairs={{0,8},{4,12},{8,0},{12,4},{16,24},{20,28},{24,16},{28,20},{1,9},{5... | collective-permute-start | bytes 442376 | tf_op jit(solution)/shard_map/ppermute | solution.py:34
  53.7 7.6 %collective-permute-start.16 = (bf16[128,384]{1,0:T(8,128)(2,1)S(1)}, bf16[128,384]{1,0:T(8,128)(2,1)S(1)}, u32[]{:S(2)}, u32[]{:S(2)}) collective-permute-start(bf16[128,384]{1,0:T(8,128)(2,1)S(1)} %get-tuple-element.96), channel_id=1, source_target_pairs={{0,1},{1,0},{2,3},{3,2},{4,5},{5,4},{6,7},{7,6},{8,9},{9,8},{10,11... | collective-permute-start | bytes 294920 | tf_op jit(solution)/shard_map/ppermute | solution.py:34
  57.7 3.5 %collective-permute-start.17 = (bf16[128,384]{1,0:T(8,128)(2,1)S(1)}, bf16[128,384]{1,0:T(8,128)(2,1)S(1)}, u32[]{:S(2)}, u32[]{:S(2)}) collective-permute-start(bf16[128,384]{1,0:T(8,128)(2,1)S(1)} %get-tuple-element.95), channel_id=1, source_target_pairs={{0,1},{1,0},{2,3},{3,2},{4,5},{5,4},{6,7},{7,6},{8,9},{9,8},{10,11... | collective-permute-start | bytes 294920 | tf_op jit(solution)/shard_map/ppermute | solution.py:34
  61.2 8.3 %collective-permute-start.27 = (bf16[96,384]{1,0:T(8,128)(2,1)S(1)}, bf16[96,384]{1,0:T(8,128)(2,1)S(1)}, u32[]{:S(2)}, u32[]{:S(2)}) collective-permute-start(bf16[96,384]{1,0:T(8,128)(2,1)S(1)} %get-tuple-element.82), channel_id=1, source_target_pairs={{0,16},{4,20},{8,24},{12,28},{16,0},{20,4},{24,8},{28,12},{1,17},{... | collective-permute-start | bytes 221192 | tf_op jit(solution)/shard_map/ppermute | solution.py:34
  62.8 11.1 %collective-permute-start.28 = (bf16[2,96,768]{2,1,0:T(8,128)(2,1)S(1)}, bf16[2,96,768]{2,1,0:T(8,128)(2,1)S(1)}, u32[]{:S(2)}, u32[]{:S(2)}) collective-permute-start(bf16[2,96,768]{2,1,0:T(8,128)(2,1)S(1)} %get-tuple-element.83), channel_id=1, source_target_pairs={{0,12},{4,8},{8,4},{12,0},{16,28},{20,24},{24,20},{28,16},{1,13},{... | collective-permute-start | bytes 884744 | tf_op jit(solution)/shard_map/ppermute | solution.py:34
  64.9 14.3 %collective-permute-start.29 = (bf16[2,96,768]{2,1,0:T(8,128)(2,1)S(1)}, bf16[2,96,768]{2,1,0:T(8,128)(2,1)S(1)}, u32[]{:S(2)}, u32[]{:S(2)}) collective-permute-start(bf16[2,96,768]{2,1,0:T(8,128)(2,1)S(1)} %get-tuple-element.84), channel_id=1, source_target_pairs={{0,4},{4,0},{8,12},{12,8},{16,20},{20,16},{24,28},{28,24},{1,5},{5... | collective-permute-start | bytes 884744 | tf_op jit(solution)/shard_map/ppermute | solution.py:34
  65.4 13.9 %collective-permute-start.30 = (bf16[2,96,768]{2,1,0:T(8,128)(2,1)S(1)}, bf16[2,96,768]{2,1,0:T(8,128)(2,1)S(1)}, u32[]{:S(2)}, u32[]{:S(2)}) collective-permute-start(bf16[2,96,768]{2,1,0:T(8,128)(2,1)S(1)} %get-tuple-element.85), channel_id=1, source_target_pairs={{0,8},{4,12},{8,0},{12,4},{16,24},{20,28},{24,16},{28,20},{1,9},{5... | collective-permute-start | bytes 884744 | tf_op jit(solution)/shard_map/ppermute | solution.py:34
  67.9 13.9 %collective-permute-start.25 = (bf16[128,1536]{1,0:T(8,128)(2,1)S(1)}, bf16[128,1536]{1,0:T(8,128)(2,1)S(1)}, u32[]{:S(2)}, u32[]{:S(2)}) collective-permute-start(bf16[128,1536]{1,0:T(8,128)(2,1)S(1)} %get-tuple-element.80.refs_1_), channel_id=1, source_target_pairs={{0,2},{2,0},{1,3},{3,1},{4,6},{6,4},{5,7},{7,5},{8,10},{10,8},{9,1... | collective-permute-start | bytes 1179656 | tf_op jit(solution)/shard_map/ppermute | solution.py:34
  69.5 16.9 %collective-permute-start.26 = (bf16[128,1536]{1,0:T(8,128)(2,1)S(1)}, bf16[128,1536]{1,0:T(8,128)(2,1)S(1)}, u32[]{:S(2)}, u32[]{:S(2)}) collective-permute-start(bf16[128,1536]{1,0:T(8,128)(2,1)S(1)} %get-tuple-element.81.refs_5_.refs_3_), channel_id=1, source_target_pairs={{0,2},{2,0},{1,3},{3,1},{4,6},{6,4},{5,7},{7,5},{8,10},{10,8},{9,1... | collective-permute-start | bytes 1179656 | tf_op jit(solution)/shard_map/ppermute | solution.py:34
  80.0 9.4 %collective-permute-start.31 = (bf16[96,768]{1,0:T(8,128)(2,1)S(1)}, bf16[96,768]{1,0:T(8,128)(2,1)S(1)}, u32[]{:S(2)}, u32[]{:S(2)}) collective-permute-start(bf16[96,768]{1,0:T(8,128)(2,1)S(1)} %get-tuple-element.87), channel_id=1, source_target_pairs={{0,16},{4,20},{8,24},{12,28},{16,0},{20,4},{24,8},{28,12},{1,17},{... | collective-permute-start | bytes 442376 | tf_op jit(solution)/shard_map/ppermute | solution.py:34
  (5 other events, 41.4 us)

commit v13 on v12

--- a/solution.py
+++ b/solution.py
@@ -459,7 +459,7 @@
         scratch=[
             pltpu.VMEM((rows, channels), BF16),
             pltpu.VMEM((channels, width), BF16),
-            pltpu.SemaphoreType.DMA((2, 3)),
+            pltpu.SemaphoreType.DMA((2, 2)),
         ],
         spaces={1: pltpu.HBM, 2: pltpu.HBM},
     )

time: 91.2 us -> 91.1 us (level)
  no operation moved by 1% of the time
where the time goes in v13:
time: 91.1 us; the launch traced here: 90.9 us
  waiting for transfers between devices  39.9 us (44%)
  starting transfers between devices  24.9 us (27%)
  Pallas kernels  24 us (26%)
  local copies, waits for them, and re-layouts  1.27 us (1%)
    ppermute x30, waiting for transfers between devices, flip(): return lax.ppermute(value, axis, [(i, i ^ step) for i in range(count)])  30.4 us
    pallas_call x14, Pallas kernels, kernel_call(): pl.pallas_call(run, out_shape=[jax.ShapeDtypeStruct(s, d) for s, d in out...  24 us
    ppermute x30, starting transfers between devices, flip(): return lax.ppermute(value, axis, [(i, i ^ step) for i in range(count)])  22.2 us
    ppermute x1, waiting for transfers between devices, body(): arrived = lax.ppermute(term, 'seq', pairs)  8.4 us
    ppermute x1, starting transfers between devices, body(): arrived = lax.ppermute(term, 'seq', pairs)  2.66 us
  transfers between devices with their start and end apart: 32, of which 15 were waited for; matrix products, arithmetic and copies ran while one was open for 1% of the time, Pallas kernels for 25%

profile of v13, /device:TPU:0, one launch (start us, length us, event | category | flops | bytes accessed | tf_op | source)
XLA Modules:
  0.0 90.9 jit_solution(2895546965104118462)
XLA Ops:
  1.1 1.1 %constant_dynamic-slice_fusion.refs_3_ = bf16[768,384]{1,0:T(8,128)(2,1)S(1)} fusion(bf16[1536,384]{1,0:T(8,128)(2,1)} %refs_6_.1, s32[]{:T(128)S(6)} %select_n.8), kind=kLoop, calls=%fused_computation | loop fusion | bytes 1179652 | tf_op jit(solution)/shard_map/dynamic_slice | solution.py:451
  2.3 2.6 %collective-permute-start.1 = (bf16[768,384]{1,0:T(8,128)(2,1)S(1)}, bf16[768,384]{1,0:T(8,128)(2,1)}, u32[]{:S(2)}, u32[]{:S(2)}) collective-permute-start(bf16[768,384]{1,0:T(8,128)(2,1)S(1)} %constant_dynamic-slice_fusion.refs_3_), channel_id=1, source_target_pairs={{0,2},{2,0},{1,3},{3,1},{4,6},{6,4},{5,7},{7,5},{8,10},{10,8},{9,1... | collective-permute-start | bytes 1769480 | tf_op jit(solution)/shard_map/ppermute | solution.py:34
  4.9 3.0 %outer_term.1 = (bf16[256,1536]{1,0:T(8,128)(2,1)S(1)}, bf16[256,384]{1,0:T(8,128)(2,1)S(1)}) custom-call(s32[6]{0:T(128)S(1)} %stack.27.refs_0_, bf16[256,1536]{1,0:T(8,128)(2,1)} %bitcast.14, bf16[3,1536,384]{2,1,0:T(8,128)(2,1)} %bitcast.11, bf16[768,384]{1,0:T(8,128)(2,1)S(1)} %constant_dynamic-slice_fusion.refs_3_), custom_call_target="tpu_custom_call" | custom-call | flops 1 | bytes 1 | tf_op jit(solution)/shard_map/outer_term/pallas_call | solution.py:200
  8.0 2.7 %collective-permute-start = (bf16[256,384]{1,0:T(8,128)(2,1)S(1)}, bf16[256,384]{1,0:T(8,128)(2,1)S(1)}, u32[]{:S(2)}, u32[]{:S(2)}) collective-permute-start(bf16[256,384]{1,0:T(8,128)(2,1)S(1)} %get-tuple-element.49), channel_id=1, source_target_pairs={{0,16},{4,20},{8,24},{12,28},{16,0},{20,4},{24,8},{28,12},{1,17},{... | collective-permute-start | bytes 589832 | tf_op jit(solution)/shard_map/ppermute | solution.py:466
  10.7 1.1 %middle_term.1 = (f32[256,384]{1,0:T(8,128)S(1)}, bf16[8,96,256]{2,1,0:T(8,128)(2,1)S(1)}, bf16[8,96,256]{2,1,0:T(8,128)(2,1)S(1)}) custom-call(s32[6]{0:T(128)S(1)} %stack.27.refs_0_, bf16[256,1536]{1,0:T(8,128)(2,1)S(1)} %get-tuple-element.47.refs_1_, bf16[3,1536,384]{2,1,0:T(8,128)(2,1)S(1)} %bitcast.12), custom_call_target="tpu_custom_call" | custom-call | flops 1 | bytes 1 | tf_op jit(solution)/shard_map/middle_term/pallas_call | solution.py:200
  11.8 8.4 %collective-permute-done.refs_2_ = bf16[256,384]{1,0:T(8,128)(2,1)S(1)} collective-permute-done((bf16[256,384]{1,0:T(8,128)(2,1)S(1)}, bf16[256,384]{1,0:T(8,128)(2,1)S(1)}, u32[]{:S(2)}, u32[]{:S(2)}) %collective-permute-start) | collective-permute-done | bytes 196640 | tf_op jit(solution)/shard_map/ppermute | solution.py:466
  21.4 2.8 %own_hidden.1 = (bf16[256,384]{1,0:T(8,128)(2,1)S(1)}, f32[256,1536]{1,0:T(8,128)S(1)}, f32[256,384]{1,0:T(8,128)S(1)}, f32[256,1536]{1,0:T(8,128)S(1)}, bf16[25...) custom-call(s32[6]{0:T(128)S(1)} %stack.27.refs_0_, ...), custom_call_target="tpu_custom_call" | custom-call | flops 1 | bytes 1 | tf_op jit(solution)/shard_map/own_hidden/pallas_call | solution.py:200
  24.8 2.3 %collective-permute-done.2.refs_2_ = bf16[256,384]{1,0:T(8,128)(2,1)S(1)} collective-permute-done((bf16[256,384]{1,0:T(8,128)(2,1)S(1)}, bf16[256,384]{1,0:T(8,128)(2,1)S(1)}, u32[]{:S(2)}, u32[]{:S(2)}) %collective-permute-start.2) | collective-permute-done | bytes 196640 | tf_op jit(solution)/shard_map/ppermute | solution.py:34
  27.6 6.6 %tracks.1 = (bf16[256,1536]{1,0:T(8,128)(2,1)S(1)}, bf16[256,384]{1,0:T(8,128)(2,1)S(1)}, f32[256,384]{1,0:T(8,128)S(1)}, bf16[256,384]{1,0:T(8,128)(2,1)S(1)}) custom-call(s32[6]{0:T(128)S(1)} %stack.27.refs_0_, f32[256,1536]{1,0:T(8,128)S(1)} %get-tuple-element.52.refs_1_, bf16[256,384]{1,0:T(8,128)(2,1)S(1)} %collective-permute-done.2.refs_2_, ...), custom_call_target="tpu_custom_call" | custom-call | flops 1 | bytes 1 | tf_op jit(solution)/shard_map/tracks/pallas_call | solution.py:200
  34.2 0.9 collective-permute-start.7
  35.1 1.0 %turn_parts.1 = (bf16[8,96,256]{2,1,0:T(8,128)(2,1)S(1)}, bf16[256,384]{1,0:T(8,128)(2,1)S(1)}, bf16[3,96,256]{2,1,0:T(8,128)(2,1)S(1)}, bf16[3,96,256]{2,1,0:T(8,128)(2,1)S(1)}, bf16[2,96,256]{2,1,0:T(8,128)(2,1)S(1)}) custom-call(s32[6]{0:T(128)S(1)} %stack.27.refs_0_, bf16[256,1536]{1,0:T(8,128)(2,1)S(1)} %get-tuple-element.60.refs_1_.refs_4_, ...), custom_call_target="tpu_custom_call" | custom-call | flops 1 | bytes 1 | tf_op jit(solution)/shard_map/turn_parts/pallas_call | solution.py:200
  37.1 1.4 %collective-permute-done.12.refs_6_ = bf16[2,96,256]{2,1,0:T(8,128)(2,1)S(1)} collective-permute-done((bf16[2,96,256]{2,1,0:T(8,128)(2,1)S(1)}, bf16[2,96,256]{2,1,0:T(8,128)(2,1)S(1)}, u32[]{:S(2)}, u32[]{:S(2)}) %collective-permute-start.12) | collective-permute-done | bytes 98336 | tf_op jit(solution)/shard_map/ppermute | solution.py:34
  38.5 1.1 %other_points.1 = (bf16[8,96,384]{2,1,0:T(8,128)(2,1)S(1)}, bf16[8,96,256]{2,1,0:T(8,128)(2,1)S(1)}) custom-call(s32[6]{0:T(128)S(1)} %stack.27.refs_0_, bf16[8,96,256]{2,1,0:T(8,128)(2,1)S(1)} %get-tuple-element.62.refs_1_.refs_4_, bf16[256,384]{1,0:T(8,128)(2,1)S(1)} %get-tuple-element.63.refs_2_, bf16[256,384]{1,0:T(8,128)(2,1)S(1)} %get-tuple-element.64.refs_3_, ...), custom_call_target="tpu_custom_call" | custom-call | flops 1 | bytes 1 | tf_op jit(solution)/shard_map/other_points/pallas_call | solution.py:200
  39.6 1.5 %collective-permute-done.7.refs_2_ = bf16[256,384]{1,0:T(8,128)(2,1)S(1)} collective-permute-done((bf16[256,384]{1,0:T(8,128)(2,1)S(1)}, bf16[256,384]{1,0:T(8,128)(2,1)S(1)}, u32[]{:S(2)}, u32[]{:S(2)}) %collective-permute-start.7) | collective-permute-done | bytes 196640 | tf_op jit(solution)/shard_map/ppermute | solution.py:34
  41.7 0.9 collective-permute-start.15
  44.5 0.7 collective-permute-done.21.refs_7_
  45.2 1.1 %middle_products.1 = (f32[2,96,384]{2,1,0:T(8,128)S(1)}, bf16[2,96,384]{2,1,0:T(8,128)(2,1)S(1)}, bf16[2,96,384]{2,1,0:T(8,128)(2,1)S(1)}, bf16[2,96,384]{2,1,0:T(8,128)(2,1)S(1)}) custom-call(s32[6]{0:T(128)S(1)} %stack.27.refs_0_, bf16[8,96,256]{2,1,0:T(8,128)(2,1)S(1)} %get-tuple-element.50.refs_3_.refs_1_, ...), custom_call_target="tpu_custom_call" | custom-call | flops 1 | bytes 1 | tf_op jit(solution)/shard_map/middle_products/pallas_call | solution.py:200
  46.3 5.5 %collective-permute-start.22 = (bf16[2,96,384]{2,1,0:T(8,128)(2,1)S(1)}, bf16[2,96,384]{2,1,0:T(8,128)(2,1)S(1)}, u32[]{:S(2)}, u32[]{:S(2)}) collective-permute-start(bf16[2,96,384]{2,1,0:T(8,128)(2,1)S(1)} %get-tuple-element.75), channel_id=1, source_target_pairs={{0,12},{4,8},{8,4},{12,0},{16,28},{20,24},{24,20},{28,16},{1,13},{... | collective-permute-start | bytes 442376 | tf_op jit(solution)/shard_map/ppermute | solution.py:34
  52.4 1.1 %collective-permute-done.13.refs_3_.refs_2_ = bf16[256,384]{1,0:T(8,128)(2,1)S(1)} collective-permute-done((bf16[256,384]{1,0:T(8,128)(2,1)S(1)}, bf16[256,384]{1,0:T(8,128)(2,1)S(1)}, u32[]{:S(2)}, u32[]{:S(2)}) %collective-permute-start.13) | collective-permute-done | bytes 196640 | tf_op jit(solution)/shard_map/ppermute | solution.py:536
  53.6 4.0 %collective-permute-done.22.refs_2_ = bf16[2,96,384]{2,1,0:T(8,128)(2,1)S(1)} collective-permute-done((bf16[2,96,384]{2,1,0:T(8,128)(2,1)S(1)}, bf16[2,96,384]{2,1,0:T(8,128)(2,1)S(1)}, u32[]{:S(2)}, u32[]{:S(2)}) %collective-permute-start.22) | collective-permute-done | bytes 147488 | tf_op jit(solution)/shard_map/ppermute | solution.py:34
  57.6 2.8 %collective-permute-done.23.refs_3_ = bf16[2,96,384]{2,1,0:T(8,128)(2,1)S(1)} collective-permute-done((bf16[2,96,384]{2,1,0:T(8,128)(2,1)S(1)}, bf16[2,96,384]{2,1,0:T(8,128)(2,1)S(1)}, u32[]{:S(2)}, u32[]{:S(2)}) %collective-permute-start.23) | collective-permute-done | bytes 147488 | tf_op jit(solution)/shard_map/ppermute | solution.py:34
  61.2 1.5 %late_products.1 = (f32[2,96,768]{2,1,0:T(8,128)S(1)}, bf16[2,96,768]{2,1,0:T(8,128)(2,1)S(1)}, bf16[2,96,768]{2,1,0:T(8,128)(2,1)S(1)}, bf16[2,96,768]{2,1,0:T(8,128)(2,1)S(1)}) custom-call(s32[6]{0:T(128)S(1)} %stack.27.refs_0_, bf16[8,96,256]{2,1,0:T(8,128)(2,1)S(1)} %get-tuple-element.50.refs_3_.refs_1_, ...), custom_call_target="tpu_custom_call" | custom-call | flops 1 | bytes 1 | tf_op jit(solution)/shard_map/late_products/pallas_call | solution.py:200
  62.7 2.0 %collective-permute-start.28 = (bf16[2,96,768]{2,1,0:T(8,128)(2,1)S(1)}, bf16[2,96,768]{2,1,0:T(8,128)(2,1)S(1)}, u32[]{:S(2)}, u32[]{:S(2)}) collective-permute-start(bf16[2,96,768]{2,1,0:T(8,128)(2,1)S(1)} %get-tuple-element.83), channel_id=1, source_target_pairs={{0,12},{4,8},{8,4},{12,0},{16,28},{20,24},{24,20},{28,16},{1,13},{... | collective-permute-start | bytes 884744 | tf_op jit(solution)/shard_map/ppermute | solution.py:34
  65.3 1.0 %collective-permute-start.30 = (bf16[2,96,768]{2,1,0:T(8,128)(2,1)S(1)}, bf16[2,96,768]{2,1,0:T(8,128)(2,1)S(1)}, u32[]{:S(2)}, u32[]{:S(2)}) collective-permute-start(bf16[2,96,768]{2,1,0:T(8,128)(2,1)S(1)} %get-tuple-element.85), channel_id=1, source_target_pairs={{0,8},{4,12},{8,0},{12,4},{16,24},{20,28},{24,16},{28,20},{1,9},{5... | collective-permute-start | bytes 884744 | tf_op jit(solution)/shard_map/ppermute | solution.py:34
  66.3 1.5 %act_part.1 = (bf16[128,1536]{1,0:T(8,128)(2,1)S(1)}, bf16[128,1536]{1,0:T(8,128)(2,1)S(1)}) custom-call(s32[6]{0:T(128)S(1)} %stack.27.refs_0_, bf16[256,384]{1,0:T(8,128)(2,1)S(1)} %get-tuple-element.69.refs_3_.refs_1_, bf16[256,384]{1,0:T(8,128)(2,1)S(1)} %collective-permute-done.13.refs_3_.refs_2_, bf16[3,1536,384]{2,1,0:T(8,128)(2,1)S(1)} %bitcast.13, ...), custom_call_target="tpu_custom_call" | custom-call | flops 1 | bytes 1 | tf_op jit(solution)/shard_map/act_part/pallas_call | solution.py:200
  67.8 1.5 %collective-permute-start.25 = (bf16[128,1536]{1,0:T(8,128)(2,1)S(1)}, bf16[128,1536]{1,0:T(8,128)(2,1)S(1)}, u32[]{:S(2)}, u32[]{:S(2)}) collective-permute-start(bf16[128,1536]{1,0:T(8,128)(2,1)S(1)} %get-tuple-element.80.refs_1_), channel_id=1, source_target_pairs={{0,2},{2,0},{1,3},{3,1},{4,6},{6,4},{5,7},{7,5},{8,10},{10,8},{9,1... | collective-permute-start | bytes 1179656 | tf_op jit(solution)/shard_map/ppermute | solution.py:34
  69.9 3.9 %collective-permute-done.28.refs_2_ = bf16[2,96,768]{2,1,0:T(8,128)(2,1)S(1)} collective-permute-done((bf16[2,96,768]{2,1,0:T(8,128)(2,1)S(1)}, bf16[2,96,768]{2,1,0:T(8,128)(2,1)S(1)}, u32[]{:S(2)}, u32[]{:S(2)}) %collective-permute-start.28) | collective-permute-done | bytes 294944 | tf_op jit(solution)/shard_map/ppermute | solution.py:34
  73.8 5.2 %collective-permute-done.29.refs_3_ = bf16[2,96,768]{2,1,0:T(8,128)(2,1)S(1)} collective-permute-done((bf16[2,96,768]{2,1,0:T(8,128)(2,1)S(1)}, bf16[2,96,768]{2,1,0:T(8,128)(2,1)S(1)}, u32[]{:S(2)}, u32[]{:S(2)}) %collective-permute-start.29) | collective-permute-done | bytes 294944 | tf_op jit(solution)/shard_map/ppermute | solution.py:34
  79.9 1.9 %collective-permute-start.31 = (bf16[96,768]{1,0:T(8,128)(2,1)S(1)}, bf16[96,768]{1,0:T(8,128)(2,1)S(1)}, u32[]{:S(2)}, u32[]{:S(2)}) collective-permute-start(bf16[96,768]{1,0:T(8,128)(2,1)S(1)} %get-tuple-element.87), channel_id=1, source_target_pairs={{0,16},{4,20},{8,24},{12,28},{16,0},{20,4},{24,8},{28,12},{1,17},{... | collective-permute-start | bytes 442376 | tf_op jit(solution)/shard_map/ppermute | solution.py:34
  81.8 4.5 %collective-permute-done.26.refs_4_ = bf16[128,1536]{1,0:T(8,128)(2,1)S(1)} collective-permute-done((bf16[128,1536]{1,0:T(8,128)(2,1)S(1)}, bf16[128,1536]{1,0:T(8,128)(2,1)S(1)}, u32[]{:S(2)}, u32[]{:S(2)}) %collective-permute-start.26) | collective-permute-done | bytes 393248 | tf_op jit(solution)/shard_map/ppermute | solution.py:34
  86.3 2.9 %collective-permute-done.31.refs_8_ = bf16[96,768]{1,0:T(8,128)(2,1)S(1)} collective-permute-done((bf16[96,768]{1,0:T(8,128)(2,1)S(1)}, bf16[96,768]{1,0:T(8,128)(2,1)S(1)}, u32[]{:S(2)}, u32[]{:S(2)}) %collective-permute-start.31) | collective-permute-done | bytes 147488 | tf_op jit(solution)/shard_map/ppermute | solution.py:34
  89.2 1.7 %finish.1 = (f32[3,96,384]{2,1,0:T(8,128)}, f32[96,384]{1,0:T(8,128)}, bf16[256,1536]{1,0:T(8,128)(2,1)}) custom-call(s32[6]{0:T(128)S(1)} %stack.27.refs_0_, bf16[128,1536]{1,0:T(8,128)(2,1)S(1)} %get-tuple-element.80.refs_1_, bf16[128,1536]{1,0:T(8,128)(2,1)S(1)} %collective-permute-done.25.refs_2_, ...), custom_call_target="tpu_custom_call" | custom-call | flops 1 | bytes 1 | tf_op jit(solution)/shard_map/finish/pallas_call | solution.py:200
  (60 shorter events, 9.8 us)
Async XLA Ops:
  0.6 26.9 %collective-permute-start.3 = (bf16[768,1920]{1,0:T(8,128)(2,1)}, bf16[768,1920]{1,0:T(8,128)(2,1)S(1)}, u32[]{:S(2)}, u32[]{:S(2)}) collective-permute-start(bf16[768,1920]{1,0:T(8,128)(2,1)} %refs_3_.3), channel_id=1, source_target_pairs={{0,1},{1,0},{2,3},{3,2},{4,5},{5,4},{6,7},{7,6},{8,9},{9,8},{10,11... | collective-permute-start | bytes 8847368 | tf_op jit(solution)/shard_map/ppermute | solution.py:34
  2.3 19.1 %collective-permute-start.1 = (bf16[768,384]{1,0:T(8,128)(2,1)S(1)}, bf16[768,384]{1,0:T(8,128)(2,1)}, u32[]{:S(2)}, u32[]{:S(2)}) collective-permute-start(bf16[768,384]{1,0:T(8,128)(2,1)S(1)} %constant_dynamic-slice_fusion.refs_3_), channel_id=1, source_target_pairs={{0,2},{2,0},{1,3},{3,1},{4,6},{6,4},{5,7},{7,5},{8,10},{10,8},{9,1... | collective-permute-start | bytes 1769480 | tf_op jit(solution)/shard_map/ppermute | solution.py:34
  8.0 12.2 %collective-permute-start = (bf16[256,384]{1,0:T(8,128)(2,1)S(1)}, bf16[256,384]{1,0:T(8,128)(2,1)S(1)}, u32[]{:S(2)}, u32[]{:S(2)}) collective-permute-start(bf16[256,384]{1,0:T(8,128)(2,1)S(1)} %get-tuple-element.49), channel_id=1, source_target_pairs={{0,16},{4,20},{8,24},{12,28},{16,0},{20,4},{24,8},{28,12},{1,17},{... | collective-permute-start | bytes 589832 | tf_op jit(solution)/shard_map/ppermute | solution.py:466
  20.8 6.3 %collective-permute-start.2 = (bf16[256,384]{1,0:T(8,128)(2,1)S(1)}, bf16[256,384]{1,0:T(8,128)(2,1)S(1)}, u32[]{:S(2)}, u32[]{:S(2)}) collective-permute-start(bf16[256,384]{1,0:T(8,128)(2,1)S(1)} %get-tuple-element.53), channel_id=1, source_target_pairs={{0,2},{2,0},{1,3},{3,1},{4,6},{6,4},{5,7},{7,5},{8,10},{10,8},{9,1... | collective-permute-start | bytes 589832 | tf_op jit(solution)/shard_map/ppermute | solution.py:34
  24.1 2.9 %collective-permute-start.4 = (bf16[256,384]{1,0:T(8,128)(2,1)S(1)}, bf16[256,384]{1,0:T(8,128)(2,1)S(1)}, u32[]{:S(2)}, u32[]{:S(2)}) collective-permute-start(bf16[256,384]{1,0:T(8,128)(2,1)S(1)} %get-tuple-element.54), channel_id=1, source_target_pairs={{0,1},{1,0},{2,3},{3,2},{4,5},{5,4},{6,7},{7,6},{8,9},{9,8},{10,11... | collective-permute-start | bytes 589832 | tf_op jit(solution)/shard_map/ppermute | solution.py:34
  24.2 3.4 %collective-permute-start.5 = (bf16[256,384]{1,0:T(8,128)(2,1)S(1)}, bf16[256,384]{1,0:T(8,128)(2,1)S(1)}, u32[]{:S(2)}, u32[]{:S(2)}) collective-permute-start(bf16[256,384]{1,0:T(8,128)(2,1)S(1)} %get-tuple-element.55), channel_id=1, source_target_pairs={{0,1},{1,0},{2,3},{3,2},{4,5},{5,4},{6,7},{7,6},{8,9},{9,8},{10,11... | collective-permute-start | bytes 589832 | tf_op jit(solution)/shard_map/ppermute | solution.py:34
  24.7 2.9 %collective-permute-start.6 = (bf16[256,384]{1,0:T(8,128)(2,1)S(1)}, bf16[256,384]{1,0:T(8,128)(2,1)S(1)}, u32[]{:S(2)}, u32[]{:S(2)}) collective-permute-start(bf16[256,384]{1,0:T(8,128)(2,1)S(1)} %get-tuple-element.56), channel_id=1, source_target_pairs={{0,1},{1,0},{2,3},{3,2},{4,5},{5,4},{6,7},{7,6},{8,9},{9,8},{10,11... | collective-permute-start | bytes 589832 | tf_op jit(solution)/shard_map/ppermute | solution.py:34
  27.1 8.0 %collective-permute-start.8 = (bf16[256,384]{1,0:T(8,128)(2,1)S(1)}, bf16[256,384]{1,0:T(8,128)(2,1)S(1)}, u32[]{:S(2)}, u32[]{:S(2)}) collective-permute-start(bf16[256,384]{1,0:T(8,128)(2,1)S(1)} %collective-permute-done.2.refs_2_), channel_id=1, source_target_pairs={{0,1},{1,0},{2,3},{3,2},{4,5},{5,4},{6,7},{7,6},{8,9},{9,8},{10,11... | collective-permute-start | bytes 589832 | tf_op jit(solution)/shard_map/ppermute | solution.py:34
  27.1 8.0 %collective-permute-start.9 = (bf16[256,384]{1,0:T(8,128)(2,1)S(1)}, bf16[256,384]{1,0:T(8,128)(2,1)S(1)}, u32[]{:S(2)}, u32[]{:S(2)}) collective-permute-start(bf16[256,384]{1,0:T(8,128)(2,1)S(1)} %get-tuple-element.61.refs_6_), channel_id=1, source_target_pairs={{0,1},{1,0},{2,3},{3,2},{4,5},{5,4},{6,7},{7,6},{8,9},{9,8},{10,11... | collective-permute-start | bytes 589832 | tf_op jit(solution)/shard_map/ppermute | solution.py:34
  34.2 6.9 %collective-permute-start.7 = (bf16[256,384]{1,0:T(8,128)(2,1)S(1)}, bf16[256,384]{1,0:T(8,128)(2,1)S(1)}, u32[]{:S(2)}, u32[]{:S(2)}) collective-permute-start(bf16[256,384]{1,0:T(8,128)(2,1)S(1)} %get-tuple-element.58), channel_id=1, source_target_pairs={{0,2},{2,0},{1,3},{3,1},{4,6},{6,4},{5,7},{7,5},{8,10},{10,8},{9,1... | collective-permute-start | bytes 589832 | tf_op jit(solution)/shard_map/ppermute | solution.py:34
  36.1 2.4 %collective-permute-start.10 = (bf16[3,96,256]{2,1,0:T(8,128)(2,1)S(1)}, bf16[3,96,256]{2,1,0:T(8,128)(2,1)S(1)}, u32[]{:S(2)}, u32[]{:S(2)}) collective-permute-start(bf16[3,96,256]{2,1,0:T(8,128)(2,1)S(1)} %get-tuple-element.65), channel_id=1, source_target_pairs={{0,1},{1,0},{2,3},{3,2},{4,5},{5,4},{6,7},{7,6},{8,9},{9,8},{10,11... | collective-permute-start | bytes 442376 | tf_op jit(solution)/shard_map/ppermute | solution.py:34
  36.1 2.4 %collective-permute-start.11 = (bf16[3,96,256]{2,1,0:T(8,128)(2,1)S(1)}, bf16[3,96,256]{2,1,0:T(8,128)(2,1)S(1)}, u32[]{:S(2)}, u32[]{:S(2)}) collective-permute-start(bf16[3,96,256]{2,1,0:T(8,128)(2,1)S(1)} %get-tuple-element.66), channel_id=1, source_target_pairs={{0,1},{1,0},{2,3},{3,2},{4,5},{5,4},{6,7},{7,6},{8,9},{9,8},{10,11... | collective-permute-start | bytes 442376 | tf_op jit(solution)/shard_map/ppermute | solution.py:34
  36.6 6.6 %collective-permute-start.14 = (bf16[8,96,256]{2,1,0:T(8,128)(2,1)S(1)}, bf16[8,96,256]{2,1,0:T(8,128)(2,1)S(1)}, u32[]{:S(2)}, u32[]{:S(2)}) collective-permute-start(bf16[8,96,256]{2,1,0:T(8,128)(2,1)S(1)} %get-tuple-element.71), channel_id=1, source_target_pairs={{0,1},{1,0},{2,3},{3,2},{4,5},{5,4},{6,7},{7,6},{8,9},{9,8},{10,11... | collective-permute-start | bytes 1179656 | tf_op jit(solution)/shard_map/ppermute | solution.py:34
  36.7 1.8 %collective-permute-start.12 = (bf16[2,96,256]{2,1,0:T(8,128)(2,1)S(1)}, bf16[2,96,256]{2,1,0:T(8,128)(2,1)S(1)}, u32[]{:S(2)}, u32[]{:S(2)}) collective-permute-start(bf16[2,96,256]{2,1,0:T(8,128)(2,1)S(1)} %get-tuple-element.67), channel_id=1, source_target_pairs={{0,1},{1,0},{2,3},{3,2},{4,5},{5,4},{6,7},{7,6},{8,9},{9,8},{10,11... | collective-permute-start | bytes 294920 | tf_op jit(solution)/shard_map/ppermute | solution.py:34
  41.7 19.4 %collective-permute-start.15 = (bf16[8,96,384]{2,1,0:T(8,128)(2,1)S(1)}, bf16[8,96,384]{2,1,0:T(8,128)(2,1)S(1)}, u32[]{:S(2)}, u32[]{:S(2)}) collective-permute-start(bf16[8,96,384]{2,1,0:T(8,128)(2,1)S(1)} %get-tuple-element.73), channel_id=1, source_target_pairs={{0,2},{2,0},{1,3},{3,1},{4,6},{6,4},{5,7},{7,5},{8,10},{10,8},{9,1... | collective-permute-start | bytes 1769480 | tf_op jit(solution)/shard_map/ppermute | solution.py:34
  42.6 10.9 %collective-permute-start.13 = (bf16[256,384]{1,0:T(8,128)(2,1)S(1)}, bf16[256,384]{1,0:T(8,128)(2,1)S(1)}, u32[]{:S(2)}, u32[]{:S(2)}) collective-permute-start(bf16[256,384]{1,0:T(8,128)(2,1)S(1)} %get-tuple-element.69.refs_3_.refs_1_), channel_id=1, source_target_pairs={{0,16},{4,20},{8,24},{12,28},{16,0},{20,4},{24,8},{28,12},{1,17},{... | collective-permute-start | bytes 589832 | tf_op jit(solution)/shard_map/ppermute | solution.py:536
  42.6 1.3 %collective-permute-start.18 = (bf16[64,384]{1,0:T(8,128)(2,1)S(1)}, bf16[64,384]{1,0:T(8,128)(2,1)S(1)}, u32[]{:S(2)}, u32[]{:S(2)}) collective-permute-start(bf16[64,384]{1,0:T(8,128)(2,1)S(1)} %get-tuple-element.94), channel_id=1, source_target_pairs={{0,1},{1,0},{2,3},{3,2},{4,5},{5,4},{6,7},{7,6},{8,9},{9,8},{10,11... | collective-permute-start | bytes 147464 | tf_op jit(solution)/shard_map/ppermute | solution.py:34
  42.7 1.4 %collective-permute-start.19 = (bf16[64,384]{1,0:T(8,128)(2,1)S(1)}, bf16[64,384]{1,0:T(8,128)(2,1)S(1)}, u32[]{:S(2)}, u32[]{:S(2)}) collective-permute-start(bf16[64,384]{1,0:T(8,128)(2,1)S(1)} %get-tuple-element.93), channel_id=1, source_target_pairs={{0,1},{1,0},{2,3},{3,2},{4,5},{5,4},{6,7},{7,6},{8,9},{9,8},{10,11... | collective-permute-start | bytes 147464 | tf_op jit(solution)/shard_map/ppermute | solution.py:34
  43.2 1.2 %collective-permute-start.20 = (bf16[64,384]{1,0:T(8,128)(2,1)S(1)}, bf16[64,384]{1,0:T(8,128)(2,1)S(1)}, u32[]{:S(2)}, u32[]{:S(2)}) collective-permute-start(bf16[64,384]{1,0:T(8,128)(2,1)S(1)} %get-tuple-element.92), channel_id=1, source_target_pairs={{0,1},{1,0},{2,3},{3,2},{4,5},{5,4},{6,7},{7,6},{8,9},{9,8},{10,11... | collective-permute-start | bytes 147464 | tf_op jit(solution)/shard_map/ppermute | solution.py:34
  43.9 1.2 %collective-permute-start.21 = (bf16[64,384]{1,0:T(8,128)(2,1)S(1)}, bf16[64,384]{1,0:T(8,128)(2,1)S(1)}, u32[]{:S(2)}, u32[]{:S(2)}) collective-permute-start(bf16[64,384]{1,0:T(8,128)(2,1)S(1)} %get-tuple-element.91), channel_id=1, source_target_pairs={{0,1},{1,0},{2,3},{3,2},{4,5},{5,4},{6,7},{7,6},{8,9},{9,8},{10,11... | collective-permute-start | bytes 147464 | tf_op jit(solution)/shard_map/ppermute | solution.py:34
  46.3 11.3 %collective-permute-start.22 = (bf16[2,96,384]{2,1,0:T(8,128)(2,1)S(1)}, bf16[2,96,384]{2,1,0:T(8,128)(2,1)S(1)}, u32[]{:S(2)}, u32[]{:S(2)}) collective-permute-start(bf16[2,96,384]{2,1,0:T(8,128)(2,1)S(1)} %get-tuple-element.75), channel_id=1, source_target_pairs={{0,12},{4,8},{8,4},{12,0},{16,28},{20,24},{24,20},{28,16},{1,13},{... | collective-permute-start | bytes 442376 | tf_op jit(solution)/shard_map/ppermute | solution.py:34
  51.8 8.7 %collective-permute-start.23 = (bf16[2,96,384]{2,1,0:T(8,128)(2,1)S(1)}, bf16[2,96,384]{2,1,0:T(8,128)(2,1)S(1)}, u32[]{:S(2)}, u32[]{:S(2)}) collective-permute-start(bf16[2,96,384]{2,1,0:T(8,128)(2,1)S(1)} %get-tuple-element.76), channel_id=1, source_target_pairs={{0,4},{4,0},{8,12},{12,8},{16,20},{20,16},{24,28},{28,24},{1,5},{5... | collective-permute-start | bytes 442376 | tf_op jit(solution)/shard_map/ppermute | solution.py:34
  52.3 8.2 %collective-permute-start.24 = (bf16[2,96,384]{2,1,0:T(8,128)(2,1)S(1)}, bf16[2,96,384]{2,1,0:T(8,128)(2,1)S(1)}, u32[]{:S(2)}, u32[]{:S(2)}) collective-permute-start(bf16[2,96,384]{2,1,0:T(8,128)(2,1)S(1)} %get-tuple-element.77), channel_id=1, source_target_pairs={{0,8},{4,12},{8,0},{12,4},{16,24},{20,28},{24,16},{28,20},{1,9},{5... | collective-permute-start | bytes 442376 | tf_op jit(solution)/shard_map/ppermute | solution.py:34
  53.5 7.6 %collective-permute-start.16 = (bf16[128,384]{1,0:T(8,128)(2,1)S(1)}, bf16[128,384]{1,0:T(8,128)(2,1)S(1)}, u32[]{:S(2)}, u32[]{:S(2)}) collective-permute-start(bf16[128,384]{1,0:T(8,128)(2,1)S(1)} %get-tuple-element.96), channel_id=1, source_target_pairs={{0,1},{1,0},{2,3},{3,2},{4,5},{5,4},{6,7},{7,6},{8,9},{9,8},{10,11... | collective-permute-start | bytes 294920 | tf_op jit(solution)/shard_map/ppermute | solution.py:34
  57.6 3.5 %collective-permute-start.17 = (bf16[128,384]{1,0:T(8,128)(2,1)S(1)}, bf16[128,384]{1,0:T(8,128)(2,1)S(1)}, u32[]{:S(2)}, u32[]{:S(2)}) collective-permute-start(bf16[128,384]{1,0:T(8,128)(2,1)S(1)} %get-tuple-element.95), channel_id=1, source_target_pairs={{0,1},{1,0},{2,3},{3,2},{4,5},{5,4},{6,7},{7,6},{8,9},{9,8},{10,11... | collective-permute-start | bytes 294920 | tf_op jit(solution)/shard_map/ppermute | solution.py:34
  61.1 8.3 %collective-permute-start.27 = (bf16[96,384]{1,0:T(8,128)(2,1)S(1)}, bf16[96,384]{1,0:T(8,128)(2,1)S(1)}, u32[]{:S(2)}, u32[]{:S(2)}) collective-permute-start(bf16[96,384]{1,0:T(8,128)(2,1)S(1)} %get-tuple-element.82), channel_id=1, source_target_pairs={{0,16},{4,20},{8,24},{12,28},{16,0},{20,4},{24,8},{28,12},{1,17},{... | collective-permute-start | bytes 221192 | tf_op jit(solution)/shard_map/ppermute | solution.py:34
  62.7 11.1 %collective-permute-start.28 = (bf16[2,96,768]{2,1,0:T(8,128)(2,1)S(1)}, bf16[2,96,768]{2,1,0:T(8,128)(2,1)S(1)}, u32[]{:S(2)}, u32[]{:S(2)}) collective-permute-start(bf16[2,96,768]{2,1,0:T(8,128)(2,1)S(1)} %get-tuple-element.83), channel_id=1, source_target_pairs={{0,12},{4,8},{8,4},{12,0},{16,28},{20,24},{24,20},{28,16},{1,13},{... | collective-permute-start | bytes 884744 | tf_op jit(solution)/shard_map/ppermute | solution.py:34
  64.8 14.3 %collective-permute-start.29 = (bf16[2,96,768]{2,1,0:T(8,128)(2,1)S(1)}, bf16[2,96,768]{2,1,0:T(8,128)(2,1)S(1)}, u32[]{:S(2)}, u32[]{:S(2)}) collective-permute-start(bf16[2,96,768]{2,1,0:T(8,128)(2,1)S(1)} %get-tuple-element.84), channel_id=1, source_target_pairs={{0,4},{4,0},{8,12},{12,8},{16,20},{20,16},{24,28},{28,24},{1,5},{5... | collective-permute-start | bytes 884744 | tf_op jit(solution)/shard_map/ppermute | solution.py:34
  65.3 13.9 %collective-permute-start.30 = (bf16[2,96,768]{2,1,0:T(8,128)(2,1)S(1)}, bf16[2,96,768]{2,1,0:T(8,128)(2,1)S(1)}, u32[]{:S(2)}, u32[]{:S(2)}) collective-permute-start(bf16[2,96,768]{2,1,0:T(8,128)(2,1)S(1)} %get-tuple-element.85), channel_id=1, source_target_pairs={{0,8},{4,12},{8,0},{12,4},{16,24},{20,28},{24,16},{28,20},{1,9},{5... | collective-permute-start | bytes 884744 | tf_op jit(solution)/shard_map/ppermute | solution.py:34
  67.8 13.9 %collective-permute-start.25 = (bf16[128,1536]{1,0:T(8,128)(2,1)S(1)}, bf16[128,1536]{1,0:T(8,128)(2,1)S(1)}, u32[]{:S(2)}, u32[]{:S(2)}) collective-permute-start(bf16[128,1536]{1,0:T(8,128)(2,1)S(1)} %get-tuple-element.80.refs_1_), channel_id=1, source_target_pairs={{0,2},{2,0},{1,3},{3,1},{4,6},{6,4},{5,7},{7,5},{8,10},{10,8},{9,1... | collective-permute-start | bytes 1179656 | tf_op jit(solution)/shard_map/ppermute | solution.py:34
  69.4 16.9 %collective-permute-start.26 = (bf16[128,1536]{1,0:T(8,128)(2,1)S(1)}, bf16[128,1536]{1,0:T(8,128)(2,1)S(1)}, u32[]{:S(2)}, u32[]{:S(2)}) collective-permute-start(bf16[128,1536]{1,0:T(8,128)(2,1)S(1)} %get-tuple-element.81.refs_5_.refs_3_), channel_id=1, source_target_pairs={{0,2},{2,0},{1,3},{3,1},{4,6},{6,4},{5,7},{7,5},{8,10},{10,8},{9,1... | collective-permute-start | bytes 1179656 | tf_op jit(solution)/shard_map/ppermute | solution.py:34
  79.9 9.4 %collective-permute-start.31 = (bf16[96,768]{1,0:T(8,128)(2,1)S(1)}, bf16[96,768]{1,0:T(8,128)(2,1)S(1)}, u32[]{:S(2)}, u32[]{:S(2)}) collective-permute-start(bf16[96,768]{1,0:T(8,128)(2,1)S(1)} %get-tuple-element.87), channel_id=1, source_target_pairs={{0,16},{4,20},{8,24},{12,28},{16,0},{20,4},{24,8},{28,12},{1,17},{... | collective-permute-start | bytes 442376 | tf_op jit(solution)/shard_map/ppermute | solution.py:34
  (5 other events, 41.3 us)
